TPU v7x, 32 devices: a whole 2x2x4 slice. The times are simulated.
32 devices in a mesh: ctx: 8 (over y, x, core), tp: 4 (over z).
Axes of the slice: x: 2, y: 2, z: 4, core: 2. Of those that a mesh axis runs over, the one named last changes fastest.
Arguments:
- hidden_in: bfloat16 [3072, 1024], P('ctx'), may hold values from -6 to 6
- doc_starts: int32 [8], replicated, may hold values from 0 to 3071, as said below
- norm1_gain: float32 [1024], replicated, may hold values from 0.5 to 1.5
- w_query: bfloat16 [1024, 1024], P(None, 'tp'), may hold values from -0.1875 to 0.1875
- w_key: bfloat16 [1024, 512], P(None, 'tp'), may hold values from -0.1875 to 0.1875
- w_value: bfloat16 [1024, 512], P(None, 'tp'), may hold values from -0.1875 to 0.1875
- query_gain: float32 [64], replicated, may hold values from 1 to 2
- key_gain: float32 [64], replicated, may hold values from 0.25 to 1.75
- w_out: bfloat16 [1024, 1024], P('tp'), may hold values from -1.25 to 1.25
- norm2_gain: float32 [1024], replicated, may hold values from 0.5 to 1.5
- w_gate: bfloat16 [1024, 4608], P(None, 'tp'), may hold values from -0.1875 to 0.1875
- w_up: bfloat16 [1024, 4608], P(None, 'tp'), may hold values from -0.1875 to 0.1875
- w_down: bfloat16 [4608, 1024], P('tp'), may hold values from -0.09375 to 0.09375
- out_grad: bfloat16 [3072, 1024], P('ctx'), may hold values from -6 to 6
Outputs:
- layer_out: bfloat16 [3072, 1024], P('ctx')
- input_grad: float32 [3072, 1024], P('ctx')
- norm1_gain_grad: float32 [1024], P('ctx')
- w_query_grad: float32 [1024, 1024], P('ctx', 'tp')
- w_key_grad: float32 [1024, 512], P('ctx', 'tp')
- w_value_grad: float32 [1024, 512], P('ctx', 'tp')
- query_gain_grad: float32 [64], replicated
- key_gain_grad: float32 [64], replicated
- w_out_grad: float32 [1024, 1024], P('tp', 'ctx')
- norm2_gain_grad: float32 [1024], P('ctx')
- w_gate_grad: float32 [1024, 4608], P('ctx', 'tp')
- w_up_grad: float32 [1024, 4608], P('ctx', 'tp')
- w_down_grad: float32 [4608, 1024], P('tp', 'ctx')
Inputs may be any that keep to these rules, and one draw needn't show every extreme that they name: doc_starts[0] is 0, the last entry is 3071, and the entries rise strictly; the first 4 entries are below 384 and the others above 2688, so one document runs from the first block of the stream into the last.
All inputs are finite; a program needn't handle non-finite values.
Results may differ from a plain program's by a relative error of at most 0.023.
Values may be sent and summed in bfloat16 or wider, within the bound.
No kernel may reach another device: no remote copies, remote signals or barrier semaphores. Data moves between devices by JAX's collectives and lax.ppermute only.
A program may use at most 192 MiB of HBM per device.

v0:
```python
import jax
import jax.numpy as jnp
from jax import lax
from jax.sharding import PartitionSpec as P

norm_eps = 1e-05
rope_base = 1000000.0
masked_score = -1e30


def doc_info(positions, doc_starts):
    inside = doc_starts[None, :] <= positions[:, None]
    doc_ids = jnp.sum(inside.astype(jnp.int32), axis=1) - 1
    doc_begin = jnp.max(jnp.where(inside, doc_starts[None, :], 0), axis=1)
    return (doc_ids, doc_begin)


def rope_tables(relative, head_dim):
    frequency = rope_base ** (-2.0 * jnp.arange(head_dim // 2, dtype=jnp.float32) / head_dim)
    angles = relative.astype(jnp.float32)[:, None] * frequency[None, :]
    return (jnp.cos(angles)[:, None, :], jnp.sin(angles)[:, None, :])


def rotate(values, cosine, sine):
    halfway = values.shape[-1] // 2
    first_half = values[..., :halfway]
    second_half = values[..., halfway:]
    return jnp.concatenate(
        [first_half * cosine - second_half * sine, second_half * cosine + first_half * sine],
        axis=-1,
    )


def rotate_back(grads, cosine, sine):
    halfway = grads.shape[-1] // 2
    first_half = grads[..., :halfway]
    second_half = grads[..., halfway:]
    return jnp.concatenate(
        [first_half * cosine + second_half * sine, second_half * cosine - first_half * sine],
        axis=-1,
    )


def rms_forward(values, gain):
    inverse = lax.rsqrt(jnp.mean(values * values, axis=-1, keepdims=True) + norm_eps)
    return (values * inverse * gain, inverse)


def rms_backward(values, inverse, gain, grads):
    scaled = grads * gain
    normed = values * inverse
    gain_grad = jnp.sum((grads * normed).reshape(-1, values.shape[-1]), axis=0)
    inner = jnp.mean(scaled * normed, axis=-1, keepdims=True)
    return (inverse * (scaled - normed * inner), gain_grad)


def block_scores(queries, keys, query_pos, query_doc, key_pos, key_doc, score_scale):
    scores = (
        jnp.einsum("qjgd,kjd->jgqk", queries, keys, preferred_element_type=jnp.float32)
        * score_scale
    )
    visible = (key_doc[None, :] == query_doc[:, None]) & (key_pos[None, :] <= query_pos[:, None])
    return (scores, visible[None, None])


def block_grads(
    queries,
    out_grads,
    log_mass,
    deltas,
    keys,
    values,
    query_pos,
    query_doc,
    key_pos,
    key_doc,
    score_scale,
):
    scores, visible = block_scores(
        queries, keys, query_pos, query_doc, key_pos, key_doc, score_scale
    )
    probs_full = jnp.where(visible, jnp.exp(scores - log_mass[..., None]), 0.0)
    prob_grads = jnp.einsum("qjgd,kjd->jgqk", out_grads, values, preferred_element_type=jnp.float32)
    score_grads = (probs_full * (prob_grads - deltas[..., None])).astype(jnp.bfloat16)
    query_part = (
        jnp.einsum("jgqk,kjd->qjgd", score_grads, keys, preferred_element_type=jnp.float32)
        * score_scale
    )
    key_part = (
        jnp.einsum("jgqk,qjgd->kjd", score_grads, queries, preferred_element_type=jnp.float32)
        * score_scale
    )
    value_part = jnp.einsum(
        "jgqk,qjgd->kjd",
        probs_full.astype(jnp.bfloat16),
        out_grads,
        preferred_element_type=jnp.float32,
    )
    return (query_part, key_part, value_part)


def shards(
    hidden_in,
    doc_starts,
    norm1_gain,
    w_query,
    w_key,
    w_value,
    query_gain,
    key_gain,
    w_out,
    norm2_gain,
    w_gate,
    w_up,
    w_down,
    out_grad,
):
    tok_rows = hidden_in.shape[0]
    head_dim = query_gain.shape[0]
    local_heads = w_query.shape[1] // head_dim
    local_kv = w_key.shape[1] // head_dim
    group_size = local_heads // local_kv
    score_scale = head_dim ** (-0.5)
    key_block = 4 * tok_rows
    block_total = lax.axis_size("ctx") // 4
    stream_len = tok_rows * lax.axis_size("ctx")
    first_pos = lax.axis_index("ctx") * tok_rows
    query_pos = first_pos + jnp.arange(tok_rows, dtype=jnp.int32)
    stream_pos = jnp.arange(stream_len, dtype=jnp.int32)
    query_doc, query_begin = doc_info(query_pos, doc_starts)
    stream_doc = doc_info(stream_pos, doc_starts)[0]
    cosine, sine = rope_tables(query_pos - query_begin, head_dim)
    inputs = hidden_in.astype(jnp.float32)
    normed_one, inverse_one = rms_forward(inputs, norm1_gain)
    h_one = normed_one.astype(jnp.bfloat16)
    query_pre = jnp.dot(h_one, w_query, preferred_element_type=jnp.float32).reshape(
        tok_rows, local_heads, head_dim
    )
    key_pre = jnp.dot(h_one, w_key, preferred_element_type=jnp.float32).reshape(
        tok_rows, local_kv, head_dim
    )
    value_rows = jnp.dot(h_one, w_value, preferred_element_type=jnp.float32).astype(jnp.bfloat16)
    query_normed, query_inverse = rms_forward(query_pre, query_gain)
    key_normed, key_inverse = rms_forward(key_pre, key_gain)
    query_rows = rotate(query_normed, cosine, sine).astype(jnp.bfloat16)
    key_rows = (
        rotate(key_normed, cosine, sine).astype(jnp.bfloat16).reshape(tok_rows, local_kv * head_dim)
    )
    key_stream, value_stream = (
        lax.all_gather(key_rows, "ctx", axis=0, tiled=True),
        lax.all_gather(value_rows, "ctx", axis=0, tiled=True),
    )
    query_four = query_rows.reshape(tok_rows, local_kv, group_size, head_dim)

    def key_slices(block_start):
        keys = lax.dynamic_slice_in_dim(key_stream, block_start, key_block, 0).reshape(
            key_block, local_kv, head_dim
        )
        values = lax.dynamic_slice_in_dim(value_stream, block_start, key_block, 0).reshape(
            key_block, local_kv, head_dim
        )
        key_doc = lax.dynamic_slice_in_dim(stream_doc, block_start, key_block, 0)
        key_pos = block_start + jnp.arange(key_block, dtype=jnp.int32)
        return (keys, values, key_pos, key_doc)

    def seen_block(block_start):
        return (block_start <= query_pos[tok_rows - 1]) & (
            block_start + key_block - 1 >= query_begin[0]
        )

    def keep_state(running):
        return running

    def stats_step(step_index, running):
        block_start = step_index * key_block

        def stats_visit(running):
            row_peak, row_mass = running
            keys, values, key_pos, key_doc = key_slices(block_start)
            scores, visible = block_scores(
                query_four, keys, query_pos, query_doc, key_pos, key_doc, score_scale
            )
            fresh_peak = jnp.maximum(
                row_peak, jnp.max(jnp.where(visible, scores, masked_score), axis=-1)
            )
            fresh_mass = row_mass * jnp.exp(row_peak - fresh_peak) + jnp.sum(
                jnp.where(visible, jnp.exp(scores - fresh_peak[..., None]), 0.0), axis=-1
            )
            return (fresh_peak, fresh_mass)

        return lax.cond(seen_block(block_start), stats_visit, keep_state, running)

    stat_shape = (local_kv, group_size, tok_rows)
    row_peak, row_mass = lax.fori_loop(
        0,
        block_total,
        stats_step,
        (jnp.full(stat_shape, masked_score, jnp.float32), jnp.zeros(stat_shape, jnp.float32)),
    )
    log_mass = row_peak + jnp.log(row_mass)

    def value_step(step_index, running):
        block_start = step_index * key_block

        def value_visit(running):
            keys, values, key_pos, key_doc = key_slices(block_start)
            scores, visible = block_scores(
                query_four, keys, query_pos, query_doc, key_pos, key_doc, score_scale
            )
            attention_probs = jnp.where(visible, jnp.exp(scores - log_mass[..., None]), 0.0).astype(
                jnp.bfloat16
            )
            return running + jnp.einsum(
                "jgqk,kjd->qjgd", attention_probs, values, preferred_element_type=jnp.float32
            )

        return lax.cond(seen_block(block_start), value_visit, keep_state, running)

    attended = lax.fori_loop(
        0,
        block_total,
        value_step,
        jnp.zeros((tok_rows, local_kv, group_size, head_dim), jnp.float32),
    )
    attended_low = attended.reshape(tok_rows, local_heads * head_dim).astype(jnp.bfloat16)
    mixed = inputs + lax.psum(
        jnp.dot(attended_low, w_out, preferred_element_type=jnp.float32).astype(jnp.bfloat16), "tp"
    ).astype(jnp.float32)
    normed_two, inverse_two = rms_forward(mixed, norm2_gain)
    h_two = normed_two.astype(jnp.bfloat16)
    gate_rows = jnp.dot(h_two, w_gate, preferred_element_type=jnp.float32)
    up_rows = jnp.dot(h_two, w_up, preferred_element_type=jnp.float32)
    sigma = jax.nn.sigmoid(gate_rows)
    activation = (gate_rows * sigma * up_rows).astype(jnp.bfloat16)
    feed_out = lax.psum(
        jnp.dot(activation, w_down, preferred_element_type=jnp.float32).astype(jnp.bfloat16), "tp"
    ).astype(jnp.float32)
    layer_out = (mixed + feed_out).astype(jnp.bfloat16)
    down_grad = jnp.einsum("tf,td->fd", activation, out_grad, preferred_element_type=jnp.float32)
    act_grad = jnp.einsum("td,fd->tf", out_grad, w_down, preferred_element_type=jnp.float32)
    gate_grad = (act_grad * up_rows * sigma * (1.0 + gate_rows * (1.0 - sigma))).astype(
        jnp.bfloat16
    )
    up_grad = (act_grad * gate_rows * sigma).astype(jnp.bfloat16)
    gate_w_grad = jnp.einsum("td,tf->df", h_two, gate_grad, preferred_element_type=jnp.float32)
    up_w_grad = jnp.einsum("td,tf->df", h_two, up_grad, preferred_element_type=jnp.float32)
    two_partial = jnp.einsum(
        "tf,df->td", gate_grad, w_gate, preferred_element_type=jnp.float32
    ) + jnp.einsum("tf,df->td", up_grad, w_up, preferred_element_type=jnp.float32)
    h_two_grad = lax.psum(two_partial.astype(jnp.bfloat16), "tp").astype(jnp.float32)
    mixed_norm_grad, gain_two_grad = rms_backward(mixed, inverse_two, norm2_gain, h_two_grad)
    mixed_grad = out_grad.astype(jnp.float32) + mixed_norm_grad
    attn_grad = mixed_grad.astype(jnp.bfloat16)
    out_w_grad = jnp.einsum(
        "tf,td->fd", attended_low, attn_grad, preferred_element_type=jnp.float32
    )
    attended_grad = jnp.einsum(
        "td,fd->tf", attn_grad, w_out, preferred_element_type=jnp.float32
    ).astype(jnp.bfloat16)
    out_four = attended_grad.reshape(tok_rows, local_kv, group_size, head_dim)
    delta_rows = jnp.sum(out_four.astype(jnp.float32) * attended, axis=-1)
    deltas = jnp.transpose(delta_rows, (1, 2, 0))

    def grad_step(step_index, running):
        block_start = step_index * key_block

        def grad_visit(running):
            query_sum, stream_term = running
            keys, values, key_pos, key_doc = key_slices(block_start)
            query_part, key_part, value_part = block_grads(
                query_four,
                out_four,
                log_mass,
                deltas,
                keys,
                values,
                query_pos,
                query_doc,
                key_pos,
                key_doc,
                score_scale,
            )
            joined = jnp.concatenate(
                [
                    key_part.reshape(key_block, local_kv * head_dim),
                    value_part.reshape(key_block, local_kv * head_dim),
                ],
                axis=1,
            )
            return (
                query_sum + query_part,
                lax.dynamic_update_slice_in_dim(stream_term, joined, block_start, 0),
            )

        return lax.cond(seen_block(block_start), grad_visit, keep_state, running)

    start_state = (
        jnp.zeros((tok_rows, local_kv, group_size, head_dim), jnp.float32),
        jnp.zeros((stream_len, 2 * local_kv * head_dim), jnp.float32),
    )
    query_grad, stream_term = lax.fori_loop(0, block_total, grad_step, start_state)
    own_kv = lax.psum_scatter(stream_term, "ctx", scatter_dimension=0, tiled=True)
    key_grad = own_kv[:, : local_kv * head_dim].reshape(tok_rows, local_kv, head_dim)
    value_grad = own_kv[:, local_kv * head_dim :].reshape(tok_rows, local_kv, head_dim)
    query_low = (
        query_grad.reshape(tok_rows, local_heads, head_dim).astype(jnp.bfloat16).astype(jnp.float32)
    )
    key_low = key_grad.astype(jnp.bfloat16).astype(jnp.float32)
    value_low = value_grad.reshape(tok_rows, local_kv * head_dim).astype(jnp.bfloat16)
    query_pre_grad, query_gain_part = rms_backward(
        query_pre, query_inverse, query_gain, rotate_back(query_low, cosine, sine)
    )
    key_pre_grad, key_gain_part = rms_backward(
        key_pre, key_inverse, key_gain, rotate_back(key_low, cosine, sine)
    )
    query_pre_low = query_pre_grad.reshape(tok_rows, local_heads * head_dim).astype(jnp.bfloat16)
    key_pre_low = key_pre_grad.reshape(tok_rows, local_kv * head_dim).astype(jnp.bfloat16)
    query_w_grad = jnp.einsum("td,tf->df", h_one, query_pre_low, preferred_element_type=jnp.float32)
    key_w_grad = jnp.einsum("td,tf->df", h_one, key_pre_low, preferred_element_type=jnp.float32)
    value_w_grad = jnp.einsum("td,tf->df", h_one, value_low, preferred_element_type=jnp.float32)
    one_partial = jnp.einsum(
        "tf,df->td", query_pre_low, w_query, preferred_element_type=jnp.float32
    )
    one_partial = one_partial + jnp.einsum(
        "tf,df->td", key_pre_low, w_key, preferred_element_type=jnp.float32
    )
    one_partial = one_partial + jnp.einsum(
        "tf,df->td", value_low, w_value, preferred_element_type=jnp.float32
    )
    h_one_grad = lax.psum(one_partial.astype(jnp.bfloat16), "tp").astype(jnp.float32)
    input_norm_grad, gain_one_grad = rms_backward(inputs, inverse_one, norm1_gain, h_one_grad)
    input_grad = mixed_grad + input_norm_grad
    query_gain_grad, key_gain_grad = lax.psum((query_gain_part, key_gain_part), ("ctx", "tp"))
    summed_all = (
        lax.psum_scatter(gain_one_grad, "ctx", scatter_dimension=0, tiled=True),
        lax.psum_scatter(query_w_grad, "ctx", scatter_dimension=0, tiled=True),
        lax.psum_scatter(key_w_grad, "ctx", scatter_dimension=0, tiled=True),
        lax.psum_scatter(value_w_grad, "ctx", scatter_dimension=0, tiled=True),
        lax.psum_scatter(out_w_grad, "ctx", scatter_dimension=1, tiled=True),
        lax.psum_scatter(gain_two_grad, "ctx", scatter_dimension=0, tiled=True),
        lax.psum_scatter(gate_w_grad, "ctx", scatter_dimension=0, tiled=True),
        lax.psum_scatter(up_w_grad, "ctx", scatter_dimension=0, tiled=True),
        lax.psum_scatter(down_grad, "ctx", scatter_dimension=1, tiled=True),
    )
    (
        gain_one_sum,
        query_w_sum,
        key_w_sum,
        value_w_sum,
        out_w_sum,
        gain_two_sum,
        gate_w_sum,
        up_w_sum,
        down_w_sum,
    ) = summed_all
    return (
        layer_out,
        input_grad,
        gain_one_sum,
        query_w_sum,
        key_w_sum,
        value_w_sum,
        query_gain_grad,
        key_gain_grad,
        out_w_sum,
        gain_two_sum,
        gate_w_sum,
        up_w_sum,
        down_w_sum,
    )


def solution(mesh):
    in_specs = (
        P("ctx", None),
        P(),
        P(),
        P(None, "tp"),
        P(None, "tp"),
        P(None, "tp"),
        P(),
        P(),
        P("tp", None),
        P(),
        P(None, "tp"),
        P(None, "tp"),
        P("tp", None),
        P("ctx", None),
    )
    out_specs = (
        P("ctx", None),
        P("ctx", None),
        P("ctx"),
        P("ctx", "tp"),
        P("ctx", "tp"),
        P("ctx", "tp"),
        P(),
        P(),
        P("tp", "ctx"),
        P("ctx"),
        P("ctx", "tp"),
        P("ctx", "tp"),
        P("tp", "ctx"),
    )
    return jax.shard_map(shards, mesh=mesh, in_specs=in_specs, out_specs=out_specs, check_vma=False)
```

profile of v0, /device:TPU:0, one launch (start us, length us, event | category | flops | bytes accessed | tf_op | source)
XLA Modules:
  0.0 701.0 jit_solution(14257217911775646045)
XLA Ops:
  8.9 1.4 fusion.41
  10.3 1.6 convolution_convert_fusion.3
  12.0 13.1 %all_gather.6 = bf16[3072,128]{1,0:T(8,128)(2,1)} all-gather(bf16[384,128]{1,0:T(8,128)(2,1)S(1)} %convolution_convert_fusion.3), channel_id=1, replica_groups=mesh['ctx'=8,'tp'=4] {'ctx'}, dimensions={0}, use_global_device_ids=true | all-gather | bytes 884736 | tf_op jit(solution)/shard_map/all_gather | solution.py:151
  25.0 2.3 copy.145
  27.9 1.4 multiply_reduce_fusion.5
  33.2 1.6 subtract_convert_fusion
  35.5 11.3 %all_gather.7 = bf16[3072,128]{0,1:T(8,128)(2,1)S(1)} all-gather(bf16[384,128]{0,1:T(8,128)(2,1)S(1)} %bitcast.226), channel_id=1, replica_groups=mesh['ctx'=8,'tp'=4] {'ctx'}, dimensions={0}, use_global_device_ids=true | all-gather | bytes 884736 | tf_op jit(solution)/shard_map/all_gather | solution.py:150
  46.9 1.9 multiply_reduce_fusion.4
  49.6 9.9 %while.58 = (s32[]{:T(128)}, f32[2,2,384]{2,1,0:T(2,128)S(1)}, f32[2,2,384]{2,1,0:T(2,128)S(1)}, s32[384]{0:T(512)S(1)}, s32[384]{0:T(512)S(1)}, /*index=5*/s32[...) while((s32[]{:T(128)}, f32[2,2,384]{2,1,0:T(2,128)S(1)}, ...), condition=%wide.region_11.12_spmd, body=%wide.region_6.11_spmd.sunk | while | flops 320279040 | bytes 22134100 | solution.py:194
  52.0 5.0 conditional.6
  53.2 1.7 fusion
  55.0 2.0 fusion.3
  60.3 13.5 %while.59 = (s32[]{:T(128)}, f32[384,2,2,64]{0,3,2,1:T(8,128)}, s32[384]{0:T(512)S(1)}, s32[384]{0:T(512)S(1)}, bf16[3072,128]{0,1:T(8,128)(2,1)}, /*index=5*/s3...) while((s32[]{:T(128)}, f32[384,2,2,64]{0,3,2,1:T(8,128)}, ...), condition=%wide.region_15.16_spmd, body=%wide.region_12.15_spmd.sunk | while | flops 615286272 | bytes 4562245 | solution.py:219
  62.7 8.7 %conditional.7 = (f32[384,2,2,64]{0,3,2,1:T(8,128)}) conditional(s32[]{:T(128)} %convert_element_type.375, f32[384,2,2,64]{0,3,2,1:T(8,128)} %get-tuple-element.1676, (s32[]{:T(128)}, bf16[3072,128]{0,1:T(8,128)(2,1)}, s32[3072]{0:T(1024)S(1)}, s32[384]{0:T(512)S(1)}, s32[384]{0:T(512)S(1)}, /*index=5*/bf16[3072,128]{0,1:T(8,128)(2,1)S(1)}, ...), branch_computations={%region_13.13_spmd, %region_14.14_spmd} | conditional | flops 615286272 | bytes 4561974 | solution.py:217
  62.7 1.9 constant_dynamic-slice_fusion.1
  64.7 1.8 compare_and_fusion.1
  66.5 4.9 fusion.9
  75.5 2.3 convolution_convert_fusion.1
  78.2 57.5 %all-reduce.9.cloned.1.call-done = bf16[384,1024]{1,0:T(8,128)(2,1)} async-done(((bf16[384,1024]{1,0:T(8,128)(2,1)}), bf16[384,1024]{1,0:T(8,128)(2,1)}) %all-reduce.9.cloned.1.call-update) | async-done | bytes 786448 | tf_op jit(solution)/shard_map/psum | solution.py:226
  135.7 1.8 multiply_reduce_fusion
  137.9 1.3 copy-done.71
  142.4 2.6 multiply_convert_fusion
  146.2 2.1 add_convert_fusion.1
  148.7 42.8 %all-reduce.11.cloned.1.call-done = bf16[384,1024]{1,0:T(8,128)(2,1)} async-done(((bf16[384,1024]{1,0:T(8,128)(2,1)}), bf16[384,1024]{1,0:T(8,128)(2,1)}) %all-reduce.11.cloned.1.call-update) | async-done | bytes 786448 | tf_op jit(solution)/shard_map/psum | solution.py:250
  191.5 3.1 fusion.37
  194.6 2.9 multiply_reduce_fusion.3
  198.3 2.0 broadcast_in_dim.65
  200.3 19.4 %while.60 = (s32[]{:T(128)}, f32[384,2,2,64]{0,3,2,1:T(8,128)}, f32[3072,256]{0,1:T(8,128)}, s32[384]{0:T(512)S(1)}, s32[384]{0:T(512)S(1)}, /*index=5*/bf16[307...) while((s32[]{:T(128)}, f32[384,2,2,64]{0,3,2,1:T(8,128)}, ...), condition=%wide.region_25.26_spmd, body=%wide.region_22.0_spmd.sunk | while | flops 1536099840 | bytes 82431520 | solution.py:301
  202.7 14.6 %conditional.8 = ((f32[384,2,2,64]{0,3,2,1:T(8,128)}, f32[3072,256]{0,1:T(8,128)})) conditional(s32[]{:T(128)} %convert_element_type.376, (f32[384,2,2,64]{0,3,2,1:T(8,128)}, f32[3072,256]{0,1:T(8,128)}) %tuple.196, (s32[]{:T(128)}, bf16[3072,128]{0,1:T(8,128)(2,1)S(1)}, s32[3072]{0:T(1024)S(1)}, s32[384]{0:T(512)S(1)}, s32[384]{0:T(512)S(1)}, ...), branch_computations={%region_23.23_spmd, %region_24.24_spmd} | conditional | flops 1536099840 | bytes 82431184 | solution.py:295
  203.8 1.4 fusion.72
  206.4 3.4 fusion.13
  211.5 2.1 fusion.17
  213.6 1.5 fusion.20
  215.7 1.6 copy-done.10
  221.1 3.3 convolution_convert_fusion
  225.7 1.6 fusion.76
  227.3 52.8 %reduce-scatter.9.cloned.1.call-done = f32[384,256]{0,1:T(8,128)} async-done(((f32[3072,256]{0,1:T(8,128)}), f32[384,256]{0,1:T(8,128)}) %reduce-scatter.9.cloned.1.call-update) | async-done | bytes 393232 | tf_op jit(solution)/shard_map/reduce_scatter | solution.py:302
  283.7 1.6 multiply_add_fusion.1
  285.3 2.3 multiply_reduce_fusion.1
  291.7 1.3 fusion.77
  293.1 1.3 add_convert_fusion
  295.5 2.2 fusion.62
  297.8 3.6 fusion.48
  301.5 2.3 fusion.60
  303.8 2.0 fusion.54
  305.9 5.1 fusion.78
  311.1 5.1 fusion.79
  316.4 5.1 fusion.80
  321.5 2.0 copy.156
  325.9 2.1 reshape.410
  329.1 1.8 reshape.411
  330.9 1.2 dynamic-slice
  335.1 2.3 fusion.43
  337.7 40.2 %all-reduce.2 = (f32[64]{0:T(128)}, f32[64]{0:T(128)}) all-reduce(f32[64]{0:T(128)S(1)} %fusion.43, f32[64]{0:T(128)S(1)} %fusion.47), channel_id=1, replica_groups=mesh['ctx'=8,'tp'=4] {'ctx','tp'}, use_global_device_ids=true, to_apply=%region_37.38 | all-reduce | flops 128 | bytes 1024 | tf_op jit(solution)/shard_map/psum | solution.py:333
  377.9 1.8 fusion.40
  379.7 13.4 %all-reduce.3 = (f32[1024]{0:T(1024)S(1)}, f32[1024]{0:T(1024)S(1)}) all-reduce(f32[1024]{0:T(1024)S(1)} %get-tuple-element.1308, f32[1024]{0:T(1024)S(1)} %copy-done.63), channel_id=3, replica_groups=mesh['ctx'=8,'tp'=4] {'ctx'}, use_global_device_ids=true, to_apply=%region_32.33.clone | all-reduce | flops 2048 | bytes 16384
  394.2 4.6 fusion.33
  398.9 5.1 reduce-scatter.11.cloned.1.call-done
  403.9 40.0 %reduce-scatter.17.cloned.1.call-done = f32[256,128]{1,0:T(8,128)} async-done(((f32[256,1024]{1,0:T(8,128)}), f32[256,128]{1,0:T(8,128)}) %reduce-scatter.17.cloned.1.call-update) | async-done | bytes 131088 | tf_op jit(solution)/shard_map/reduce_scatter | solution.py:339
  443.9 38.1 %reduce-scatter.13.cloned.1.call-done = f32[128,128]{1,0:T(8,128)} async-done(((f32[1024,128]{1,0:T(8,128)}), f32[128,128]{1,0:T(8,128)}) %reduce-scatter.13.cloned.1.call-update) | async-done | bytes 65552 | tf_op jit(solution)/shard_map/reduce_scatter | solution.py:337
  482.0 37.8 %reduce-scatter.15.cloned.1.call-done = f32[128,128]{1,0:T(8,128)} async-done(((f32[1024,128]{1,0:T(8,128)}), f32[128,128]{1,0:T(8,128)}) %reduce-scatter.15.cloned.1.call-update) | async-done | bytes 65552 | tf_op jit(solution)/shard_map/reduce_scatter | solution.py:338
  519.8 58.4 %reduce-scatter.19.cloned.1.call-done = f32[128,1152]{1,0:T(8,128)} async-done(((f32[1024,1152]{1,0:T(8,128)}), f32[128,1152]{1,0:T(8,128)}) %reduce-scatter.19.cloned.1.call-update) | async-done | bytes 589840 | tf_op jit(solution)/shard_map/reduce_scatter | solution.py:341
  578.2 57.8 %reduce-scatter.21.cloned.1.call-done = f32[128,1152]{1,0:T(8,128)} async-done(((f32[1024,1152]{1,0:T(8,128)}), f32[128,1152]{1,0:T(8,128)}) %reduce-scatter.21.cloned.1.call-update) | async-done | bytes 589840 | tf_op jit(solution)/shard_map/reduce_scatter | solution.py:342
  636.0 58.3 %reduce-scatter.23.cloned.1.call-done = f32[1152,128]{1,0:T(8,128)} async-done(((f32[1152,1024]{1,0:T(8,128)}), f32[1152,128]{1,0:T(8,128)}) %reduce-scatter.23.cloned.1.call-update) | async-done | bytes 589840 | tf_op jit(solution)/shard_map/reduce_scatter | solution.py:343
  (260 shorter events, 47.4 us)
Async XLA Ops:
  7.2 135.2 %copy-start = (bf16[1152,1024]{1,0:T(8,128)(2,1)S(1)}, bf16[1152,1024]{1,0:T(8,128)(2,1)}, u32[]{:S(2)}) copy-start(bf16[1152,1024]{1,0:T(8,128)(2,1)} %param.38) | copy-start | bytes 7077892
  7.2 128.5 %all-reduce.9.cloned.1.call-start = ((), (), s32[]{:S(2)}) async-start(), calls=%async_computation.8 | async-start | bytes 1572864 | tf_op jit(solution)/shard_map/psum | solution.py:226
  8.9 21.3 %copy-start.66 = (s32[384]{0:T(512)}, s32[384]{0:T(512)S(1)}, u32[]{:S(2)}) copy-start(s32[384]{0:T(512)S(1)} %get-tuple-element.1705) | copy-start | bytes 4612
  10.3 17.6 %copy-start.56 = (f32[384]{0:T(512)}, f32[384]{0:T(512)S(1)}, u32[]{:S(2)}) copy-start(f32[384]{0:T(512)S(1)} %add_rsqrt_fusion.3) | copy-start | bytes 4612
  11.9 16.0 %copy-start.1 = (bf16[384,1024]{1,0:T(8,128)(2,1)S(1)}, bf16[384,1024]{1,0:T(8,128)(2,1)}, u32[]{:S(2)}) copy-start(bf16[384,1024]{1,0:T(8,128)(2,1)} %param.26) | copy-start | bytes 2359300
  12.0 16.0 %copy-start.52 = (f32[1024]{0:T(1024)S(1)}, f32[1024]{0:T(1024)}, u32[]{:S(2)}) copy-start(f32[1024]{0:T(1024)} %param.28) | copy-start | bytes 12292
  29.6 5.2 copy-start.16
  30.2 4.6 copy-start.24
  30.8 4.6 copy-start.32
  35.5 13.3 %copy-start.68 = (f32[64]{0:T(128)S(1)}, f32[64]{0:T(128)}, u32[]{:S(2)}) copy-start(f32[64]{0:T(128)} %param.32) | copy-start | bytes 772
  46.9 2.0 copy-start.41
  46.9 2.1 copy-start.44
  46.9 2.7 copy-start.46
  46.9 2.7 copy-start.67
  75.5 62.0 %copy-start.54 = (f32[1024]{0:T(1024)S(1)}, f32[1024]{0:T(1024)}, u32[]{:S(2)}) copy-start(f32[1024]{0:T(1024)} %param.35) | copy-start | bytes 12292
  77.9 113.6 %all-reduce.11.cloned.1.call-start = ((), (), s32[]{:S(2)}) async-start(), calls=%async_computation.9 | async-start | bytes 1572864 | tf_op jit(solution)/shard_map/psum | solution.py:250
  135.7 1.9 copy-start.2
  135.7 1.9 copy-start.11
  137.5 1.7 copy-start.71
  137.6 57.0 %copy-start.58 = (f32[384]{0:T(512)}, f32[384]{0:T(512)S(1)}, u32[]{:S(2)}) copy-start(f32[384]{0:T(512)S(1)} %add_rsqrt_fusion.2) | copy-start | bytes 4612
  139.2 1.9 copy-start.72
  148.4 131.7 %reduce-scatter.9.cloned.1.call-start = ((), (), s32[]{:S(2)}) async-start(), calls=%async_computation.10 | async-start | bytes 3538944 | tf_op jit(solution)/shard_map/reduce_scatter | solution.py:302
  191.5 3.1 copy-start.3
  191.5 3.1 copy-start.12
  191.5 3.1 copy-start.23
  194.6 3.0 copy-start.64
  203.8 2.6 copy-start.73
  206.4 3.4 copy-start.5
  213.6 1.9 copy-start.9
  215.7 1.6 copy-start.10
  219.8 158.1 %all-reduce.13.cloned.1.call-start = ((), (), s32[]{:S(2)}) async-start(), calls=%async_computation.18 | async-start | bytes 3145728 | tf_op jit(solution)/shard_map/psum | solution.py:235
  221.1 3.3 copy-start.7
  221.1 3.3 copy-start.42
  221.1 3.3 copy-start.45
  224.5 2.8 copy-start.28
  224.5 2.8 copy-start.30
  281.8 3.5 copy-start.17
  281.8 3.5 copy-start.25
  285.3 2.4 copy-start.20
  285.3 5.8 copy-start.18
  285.3 4.6 copy-start.61
  287.7 5.4 copy-start.38
  289.9 3.2 copy-start.13
  289.9 3.2 copy-start.49
  294.4 3.4 copy-start.55
  294.4 109.5 %reduce-scatter.11.cloned.1.call-start = ((), (), s32[]{:S(2)}) async-start(), calls=%async_computation.11 | async-start | bytes 1179648 | tf_op jit(solution)/shard_map/reduce_scatter | solution.py:336
  297.8 146.2 %reduce-scatter.17.cloned.1.call-start = ((), (), s32[]{:S(2)}) async-start(), calls=%async_computation.14 | async-start | bytes 1179648 | tf_op jit(solution)/shard_map/reduce_scatter | solution.py:339
  301.4 2.4 copy-start.39
  301.4 180.6 %reduce-scatter.13.cloned.1.call-start = ((), (), s32[]{:S(2)}) async-start(), calls=%async_computation.12 | async-start | bytes 589824 | tf_op jit(solution)/shard_map/reduce_scatter | solution.py:337
  303.8 216.0 %reduce-scatter.15.cloned.1.call-start = ((), (), s32[]{:S(2)}) async-start(), calls=%async_computation.13 | async-start | bytes 589824 | tf_op jit(solution)/shard_map/reduce_scatter | solution.py:338
  305.9 272.3 %reduce-scatter.19.cloned.1.call-start = ((), (), s32[]{:S(2)}) async-start(), calls=%async_computation.15 | async-start | bytes 5308416 | tf_op jit(solution)/shard_map/reduce_scatter | solution.py:341
  311.0 324.9 %reduce-scatter.21.cloned.1.call-start = ((), (), s32[]{:S(2)}) async-start(), calls=%async_computation.16 | async-start | bytes 5308416 | tf_op jit(solution)/shard_map/reduce_scatter | solution.py:342
  316.2 378.1 %reduce-scatter.23.cloned.1.call-start = ((), (), s32[]{:S(2)}) async-start(), calls=%async_computation.17 | async-start | bytes 5308416 | tf_op jit(solution)/shard_map/reduce_scatter | solution.py:343
  321.5 2.9 copy-start.27
  325.2 8.8 %copy-start.29 = (f32[384,4,32]{0,2,1:T(8,128)S(1)}, f32[384,4,32]{0,2,1:T(8,128)}, u32[]{:S(2)}) copy-start(f32[384,4,32]{0,2,1:T(8,128)} %copy-done.28) | copy-start | bytes 589828
  325.9 6.9 copy-start.31
  333.9 3.5 copy-start.62
  335.1 2.3 copy-start.19
  335.1 2.3 copy-start.21
  335.1 2.4 copy-start.33
  335.1 42.8 %copy-start.57 = (f32[384]{0:T(512)S(1)}, f32[384]{0:T(512)}, u32[]{:S(2)}) copy-start(f32[384]{0:T(512)} %copy-done.56) | copy-start | bytes 4612
  337.4 42.3 %copy-start.63 = (f32[1024]{0:T(1024)S(1)}, f32[1024]{0:T(1024)}, u32[]{:S(2)}) copy-start(f32[1024]{0:T(1024)} %get-tuple-element.1306) | copy-start | bytes 12292
  337.4 56.8 %copy-start.59 = (f32[384]{0:T(512)S(1)}, f32[384]{0:T(512)}, u32[]{:S(2)}) copy-start(f32[384]{0:T(512)} %copy-done.58) | copy-start | bytes 4612
  337.4 56.8 %copy-start.65 = (f32[384]{0:T(512)S(1)}, f32[384]{0:T(512)}, u32[]{:S(2)}) copy-start(f32[384]{0:T(512)} %copy-done.64) | copy-start | bytes 4612
  (21 other events, 18.6 us)
Sparse Core Ops, SparseCore 0:
  78.0 57.6 all-reduce.8
  148.5 42.9 all-reduce.10
  219.9 60.1 reduce-scatter.8
  294.5 70.1 all-reduce.12
  368.7 35.2 reduce-scatter.10
  407.9 36.0 reduce-scatter.16
  447.9 34.1 reduce-scatter.12
  485.7 34.0 reduce-scatter.14
  524.2 53.9 reduce-scatter.18
  582.1 53.8 reduce-scatter.20
  640.4 53.8 reduce-scatter.22
where the time goes:
time: 706 us; the launch traced here: 701 us
  waiting for transfers between devices  449 us (64%)
  blocking collectives  77.9 us (11%)
  matrix products  67.3 us (10%)
  local copies, waits for them, and re-layouts  46.6 us (7%)
  other arithmetic  35.1 us (5%)
  between operations  15.6 us (2%)
  loops' own time  8.21 us (1%)
    reduce_scatter x1, waiting for transfers between devices, shards(): lax.psum_scatter(gate_w_grad, 'ctx', scatter_dimension=0, tiled=True)  58.4 us
    reduce_scatter x1, waiting for transfers between devices, shards(): lax.psum_scatter(down_grad, 'ctx', scatter_dimension=1, tiled=True)  58.3 us
    reduce_scatter x1, waiting for transfers between devices, shards(): lax.psum_scatter(up_w_grad, 'ctx', scatter_dimension=0, tiled=True)  57.8 us
    psum x1, waiting for transfers between devices, shards(): lax.psum(jnp.dot(attended_low, w_out, preferred_element_type=jnp.float32)...  57.5 us
    reduce_scatter x1, waiting for transfers between devices, shards(): lax.psum_scatter(stream_term, 'ctx', scatter_dimension=0, tiled=True)  52.8 us
    psum x1, waiting for transfers between devices, shards(): lax.psum(two_partial.astype(jnp.bfloat16), 'tp').astype(jnp.float32)  42.8 us
    psum x1, blocking collectives, shards(): lax.psum((query_gain_part, key_gain_part), ('ctx', 'tp'))  40.2 us
    reduce_scatter x1, waiting for transfers between devices, shards(): lax.psum_scatter(out_w_grad, 'ctx', scatter_dimension=1, tiled=True)  40 us
  transfers between devices with their start and end apart: 11, of which 10 were waited for; matrix products, arithmetic and copies ran while one was open for 8% of the time, Pallas kernels for 0%

commit v1 on v0

v1 whole, which is shorter than its diff:
```python
import functools
import math

import jax
import jax.numpy as jnp
from jax import lax
from jax.experimental import pallas as pl
from jax.experimental.pallas import tpu as pltpu
from jax.sharding import PartitionSpec as P

norm_eps = 1e-05
rope_base = 1000000.0
f32 = jnp.float32
bf16 = jnp.bfloat16
NN = (((1,), (0,)), ((), ()))
NT = (((1,), (1,)), ((), ()))
TN = (((0,), (0,)), ((), ()))
VMEM = pl.BlockSpec(memory_space=pltpu.VMEM)
SMEM = pl.BlockSpec(memory_space=pltpu.SMEM)
vmem_limit = 56 * 1024 * 1024


def dot(left, right, dims=NN):
    return lax.dot_general(left, right, dims, preferred_element_type=f32)


def call(body, inputs, outs, scratch=(), flops=0, **kwargs):
    in_specs = kwargs.pop("in_specs", None)
    if in_specs is None:
        in_specs = [
            SMEM if (x.dtype == jnp.int32 and x.ndim == 1) else VMEM for x in inputs
        ]
    out_specs = kwargs.pop("out_specs", [VMEM] * len(outs))
    moved = sum(x.size * x.dtype.itemsize for x in inputs) + sum(
        math.prod(o.shape) * o.dtype.itemsize for o in outs
    )
    return pl.pallas_call(
        body,
        out_shape=outs,
        in_specs=in_specs,
        out_specs=out_specs,
        scratch_shapes=list(scratch),
        compiler_params=pltpu.CompilerParams(vmem_limit_bytes=vmem_limit),
        cost_estimate=pl.CostEstimate(flops=flops, bytes_accessed=moved, transcendentals=0),
        **kwargs,
    )(*inputs)


def shape(dims, dtype):
    return jax.ShapeDtypeStruct(dims, dtype)


def lanes(x):
    return lax.broadcasted_iota(jnp.int32, x.shape, 1)


def head_mean(x):
    first = lanes(x) < 64
    low = jnp.sum(jnp.where(first, x, 0.0), axis=1, keepdims=True)
    high = jnp.sum(jnp.where(first, 0.0, x), axis=1, keepdims=True)
    return jnp.where(first, low, high) * (1.0 / 64.0)


def swap_halves(x):
    return jnp.where(lanes(x) % 64 < 32, pltpu.roll(x, 96, 1), pltpu.roll(x, 32, 1))


def head_norm(pre, gain):
    inverse = lax.rsqrt(head_mean(pre * pre) + norm_eps)
    return pre * inverse * gain


def head_norm_back(pre, gain, grads):
    inverse = lax.rsqrt(head_mean(pre * pre) + norm_eps)
    normed = pre * inverse
    scaled = grads * gain
    inner = head_mean(scaled * normed)
    return inverse * (scaled - normed * inner), grads * normed


def row_norm(x):
    return lax.rsqrt(jnp.mean(x * x, axis=1, keepdims=True) + norm_eps)


def kv_kernel(x_ref, gain_ref, wk_ref, wv_ref, cos_ref, sin_ref, kgain_ref, h_ref, kv_ref, kpre_ref):
    x = x_ref[...].astype(f32)
    h = (x * row_norm(x) * gain_ref[...]).astype(bf16)
    h_ref[...] = h
    kpre = dot(h, wk_ref[...])
    kpre_ref[...] = kpre
    kn = head_norm(kpre, kgain_ref[...])
    key = kn * cos_ref[...] + swap_halves(kn) * sin_ref[...]
    kv_ref[:, :128] = key.astype(bf16)
    kv_ref[:, 128:] = dot(h, wv_ref[...]).astype(bf16)


def spread(x, half, out_ref, base, rows):
    rolled = pltpu.roll(x, 64, 1)
    keep = (lanes(x) < 64) if half == 0 else (lanes(x) >= 64)
    first, second = (x, rolled) if half == 0 else (rolled, x)
    out_ref[pl.ds(base, rows), :] = jnp.where(keep, first, 0.0).astype(bf16)
    return jnp.where(keep, second, 0.0).astype(bf16)


def q_kernel(h_ref, wq_ref, cos_ref, sin_ref, qgain_ref, qpad_ref, qpre_ref):
    rows = h_ref.shape[0]
    qpre = dot(h_ref[...], wq_ref[...])
    qpre_ref[...] = qpre
    for half in range(2):
        qn = head_norm(qpre[:, 128 * half : 128 * half + 128], qgain_ref[...])
        x = qn * cos_ref[...] + swap_halves(qn) * sin_ref[...]
        base = 2 * half * rows
        qpad_ref[pl.ds(base + rows, rows), :] = spread(x, half, qpad_ref, base, rows)


def block_id(index, parity, mine, relative):
    return jnp.bitwise_xor(mine, 2 * index + parity) if relative else index


def block_mask(scal_ref, begin_ref, block, rows):
    dims = (rows, 2 * rows)
    key_pos = lax.broadcasted_iota(jnp.int32, dims, 0) + block * rows
    across = lax.broadcasted_iota(jnp.int32, (1, 2 * rows), 1)
    query_pos = scal_ref[0] * rows + jnp.where(across < rows, across, across - rows)
    return (key_pos <= query_pos) & (key_pos >= begin_ref[...])


def attend_kernel(relative, scale, scal_ref, begin_ref, qpad_ref, *refs):
    count = 2 if relative else 1
    kv_refs = refs[:count]
    o_ref, o32_ref, lse_ref, acc_ref, mass_ref = refs[count:]
    rows = o_ref.shape[0]
    mine = scal_ref[0]
    acc_ref[...] = jnp.zeros_like(acc_ref)
    mass_ref[...] = jnp.zeros_like(mass_ref)
    factor = scale * math.log2(math.e)

    for parity, kv_ref in enumerate(kv_refs):

        def visit(index, masked, kv_ref=kv_ref, parity=parity):
            block = block_id(index, parity, mine, relative)
            at = pl.ds(pl.multiple_of(index * rows, rows), rows)
            keys = kv_ref[at, :128]
            values_t = kv_ref[at, 128:].T
            for j in range(2):
                s = dot(keys, qpad_ref[2 * rows * j : 2 * rows * (j + 1), :], NT)
                p = jnp.exp2(s * factor)
                if masked:
                    p = jnp.where(block_mask(scal_ref, begin_ref, block, rows), p, 0.0)
                mass_ref[j : j + 1, :] += jnp.sum(p, axis=0, keepdims=True)
                acc_ref[j] += dot(values_t, p.astype(bf16))

        def step(index, carry, visit=visit, parity=parity):
            block = block_id(index, parity, mine, relative)
            start = block * rows
            seen = (block <= mine) & (start + rows - 1 >= scal_ref[2])
            whole = (block < mine) & (start >= scal_ref[3])
            pl.when(seen & whole)(lambda: visit(index, False))
            pl.when(seen & jnp.logical_not(whole))(lambda: visit(index, True))
            return carry

        lax.fori_loop(0, kv_ref.shape[0] // rows, step, 0)

    mass = mass_ref[...]
    lse_ref[...] = jnp.log2(mass)
    parts = []
    for j in range(2):
        normed = acc_ref[j, 64 * j : 64 * j + 64, :] / mass[j : j + 1, :]
        parts += [normed[:, :rows], normed[:, rows:]]
    o32 = jnp.concatenate(parts, axis=0).T
    o32_ref[...] = o32
    o_ref[...] = o32.astype(bf16)


def attend_back_kernel(relative, scale, n_tp, scal_ref, begin_ref, qpad_ref, o32_ref, lse_ref, *refs):
    count = 2 if relative else 1
    kv_refs, refs = refs[:count], refs[count:]
    dout_refs, refs = refs[:n_tp], refs[n_tp:]
    dq_ref, refs = refs[0], refs[1:]
    dkv_refs, refs = refs[:count], refs[count:]
    dout_ref, dopad_ref, dqt_ref = refs
    rows = dq_ref.shape[0]
    own = rows // n_tp
    mine = scal_ref[0]
    factor = scale * math.log2(math.e)
    for k in range(n_tp):
        at = pl.multiple_of(jnp.bitwise_xor(scal_ref[1], k) * own, own)
        dout_ref[pl.ds(at, own), :] = dout_refs[k][...].astype(f32)
    dout = dout_ref[...]
    for half in range(2):
        x = dout[:, 128 * half : 128 * half + 128]
        base = 2 * half * rows
        dopad_ref[pl.ds(base + rows, rows), :] = spread(x, half, dopad_ref, base, rows)
    weighted = (dout * o32_ref[...]).T
    deltas = [jnp.sum(weighted[64 * h : 64 * h + 64], axis=0, keepdims=True) for h in range(4)]
    delta = [jnp.concatenate(deltas[2 * j : 2 * j + 2], axis=1) for j in range(2)]
    dqt_ref[...] = jnp.zeros_like(dqt_ref)

    for parity in range(count):
        kv_ref, dkv_ref = kv_refs[parity], dkv_refs[parity]

        def visit(index, masked, kv_ref=kv_ref, dkv_ref=dkv_ref, parity=parity):
            block = block_id(index, parity, mine, relative)
            at = pl.ds(pl.multiple_of(index * rows, rows), rows)
            keys = kv_ref[at, :128]
            values = kv_ref[at, 128:]
            keys_t = keys.T
            dk = jnp.zeros((rows, 128), f32)
            dv = jnp.zeros((rows, 128), f32)
            for j in range(2):
                qpad = qpad_ref[2 * rows * j : 2 * rows * (j + 1), :]
                dopad = dopad_ref[2 * rows * j : 2 * rows * (j + 1), :]
                p = jnp.exp2(dot(keys, qpad, NT) * factor - lse_ref[j : j + 1, :])
                if masked:
                    p = jnp.where(block_mask(scal_ref, begin_ref, block, rows), p, 0.0)
                ds = (p * (dot(values, dopad, NT) - delta[j])).astype(bf16)
                dv += dot(p.astype(bf16), dopad)
                dk += dot(ds, qpad)
                dqt_ref[j] += dot(keys_t, ds)
            dkv_ref[at, :128] = (dk * scale).astype(bf16)
            dkv_ref[at, 128:] = dv.astype(bf16)

        def skip(index, dkv_ref=dkv_ref):
            at = pl.ds(pl.multiple_of(index * rows, rows), rows)
            dkv_ref[at, :] = jnp.zeros((rows, 256), bf16)

        def step(index, carry, visit=visit, skip=skip, parity=parity):
            block = block_id(index, parity, mine, relative)
            start = block * rows
            seen = (block <= mine) & (start + rows - 1 >= scal_ref[2])
            whole = (block < mine) & (start >= scal_ref[3])
            pl.when(seen & whole)(lambda: visit(index, False))
            pl.when(seen & jnp.logical_not(whole))(lambda: visit(index, True))
            pl.when(jnp.logical_not(seen))(lambda: skip(index))
            return carry

        lax.fori_loop(0, kv_ref.shape[0] // rows, step, 0)

    parts = []
    for j in range(2):
        part = dqt_ref[j, 64 * j : 64 * j + 64, :]
        parts += [part[:, :rows], part[:, rows:]]
    dq_ref[...] = (jnp.concatenate(parts, axis=0).T * scale).astype(bf16)


def mix_kernel(n_tp, n_ctx, relative, scal_ref, x_ref, gain_ref, w0_ref, *refs):
    wm_ref, wp_ref = refs[:2]
    o_refs = refs[2 : 2 + n_tp]
    h_ref, hp_ref, y_ref, acc_ref = refs[2 + n_tp :]
    rows = x_ref.shape[0]
    own = rows // n_tp
    acc = x_ref[...].astype(f32) + dot(o_refs[0][...], w0_ref[...])
    core = scal_ref[4]
    half = o_refs[0].shape[1] // 2
    for k in range(1, n_tp):
        first = pl.multiple_of(core * half, half)
        second = pl.multiple_of((1 - core) * half, half)
        acc += dot(o_refs[k][:, pl.ds(first, half)], wm_ref[k - 1])
        acc += dot(o_refs[k][:, pl.ds(second, half)], wp_ref[k - 1])
    acc_ref[...] = acc
    y_ref[...] = acc_ref[pl.ds(pl.multiple_of(scal_ref[1] * own, own), own), :]
    h_ref[...] = (acc * row_norm(acc) * gain_ref[...]).astype(bf16)
    permute_columns(n_ctx, relative, scal_ref[0], h_ref, hp_ref)


def permute_columns(n_ctx, relative, mine, src_ref, dst_ref):
    if not relative:
        dst_ref[...] = src_ref[...]
        return
    width = src_ref.shape[1] // n_ctx
    for place, k in enumerate([*range(0, n_ctx, 2), *range(1, n_ctx, 2)]):
        at = pl.multiple_of(jnp.bitwise_xor(mine, k) * width, width)
        dst_ref[:, place * width : (place + 1) * width] = src_ref[:, pl.ds(at, width)]


def order_kernel(n_ctx, relative, scal_ref, a_ref, b_ref, ap_ref, bp_ref):
    permute_columns(n_ctx, relative, scal_ref[0], a_ref, ap_ref)
    permute_columns(n_ctx, relative, scal_ref[0], b_ref, bp_ref)


def feed_kernel(n_tp, scal_ref, h_ref, g_ref, wg_ref, wu_ref, wd_ref, act_ref, dg_ref, du_ref, dh_ref, acc_ref):
    step = pl.program_id(0)
    gate = dot(h_ref[...], wg_ref[...])
    up = dot(h_ref[...], wu_ref[...])
    dact = dot(g_ref[...], wd_ref[...], NT)
    sigma = jax.nn.sigmoid(gate)
    silu = gate * sigma
    act_ref[...] = (silu * up).astype(bf16)
    dgate = (dact * up * sigma * (1.0 + gate * (1.0 - sigma))).astype(bf16)
    dup = (dact * silu).astype(bf16)
    dg_ref[...] = dgate
    du_ref[...] = dup
    total = dot(dgate, wg_ref[...], NT) + dot(dup, wu_ref[...], NT)

    @pl.when(step == 0)
    def _():
        acc_ref[...] = total

    @pl.when(step > 0)
    def _():
        acc_ref[...] += total

    @pl.when(step == pl.num_programs(0) - 1)
    def _():
        own = acc_ref.shape[0] // n_tp
        for k in range(n_tp):
            at = pl.multiple_of(jnp.bitwise_xor(scal_ref[1], k) * own, own)
            dh_ref[k] = acc_ref[pl.ds(at, own), :].astype(bf16)


def mid_kernel(n_tp, n_ctx, relative, scal_ref, g_ref, y_ref, gain_ref, w0_ref, wm_ref, wp_ref, *refs):
    dh_refs = refs[:n_tp]
    dy_ref, dattn_ref, gaing_ref, dout_ref, low_ref = refs[n_tp:]
    own = y_ref.shape[0]
    dh = dh_refs[0][...].astype(f32)
    for k in range(1, n_tp):
        dh += dh_refs[k][...].astype(f32)
    y = y_ref[...]
    inverse = row_norm(y)
    z = y * inverse
    gaing_ref[...] = jnp.sum(dh * z, axis=0, keepdims=True)
    e = dh * gain_ref[...]
    inner = jnp.mean(e * z, axis=1, keepdims=True)
    at = pl.multiple_of(scal_ref[1] * own, own)
    dy = g_ref[pl.ds(at, own), :].astype(f32) + inverse * (e - z * inner)
    dy_ref[...] = dy
    low = dy.astype(bf16)
    low_ref[...] = low
    permute_columns(n_ctx, relative, scal_ref[0], low_ref, dattn_ref)
    dout_ref[0] = dot(low, w0_ref[...], NT).astype(bf16)
    core = scal_ref[4]
    half = w0_ref.shape[0] // 2
    for k in range(1, n_tp):
        first = pl.multiple_of(core * half, half)
        second = pl.multiple_of((1 - core) * half, half)
        dout_ref[k, :, pl.ds(first, half)] = dot(low, wm_ref[k - 1], NT).astype(bf16)
        dout_ref[k, :, pl.ds(second, half)] = dot(low, wp_ref[k - 1], NT).astype(bf16)


def q_back_kernel(dq_ref, qpre_ref, cos_ref, sin_ref, qgain_ref, wq_ref, low_ref, gaing_ref, dh_ref):
    total = jnp.zeros((1, 128), f32)
    for half in range(2):
        cut = slice(128 * half, 128 * half + 128)
        x = dq_ref[:, cut].astype(f32)
        dqn = x * cos_ref[...] - swap_halves(x) * sin_ref[...]
        dpre, weighted = head_norm_back(qpre_ref[:, cut], qgain_ref[...], dqn)
        low_ref[:, cut] = dpre.astype(bf16)
        total += jnp.sum(weighted, axis=0, keepdims=True)
    gaing_ref[...] = total + pltpu.roll(total, 64, 1)
    dh_ref[...] = dot(low_ref[...], wq_ref[...], NT)


def k_back_kernel(n_tp, n_parts, scal_ref, *refs):
    parts, refs = refs[:n_parts], refs[n_parts:]
    kpre_ref, cos_ref, sin_ref, kgain_ref, wk_ref, wv_ref, dhq_ref, x_ref = refs[:8]
    low_ref, gaing_ref, gain1_ref, dh_ref, acc_ref = refs[8:]
    total = parts[0][...].astype(f32)
    for part in parts[1:]:
        total += part[...].astype(f32)
    low = total.astype(bf16)
    x = low[:, :128].astype(f32)
    dkn = x * cos_ref[...] - swap_halves(x) * sin_ref[...]
    dpre, weighted = head_norm_back(kpre_ref[...], kgain_ref[...], dkn)
    gains = jnp.sum(weighted, axis=0, keepdims=True)
    gaing_ref[...] = gains + pltpu.roll(gains, 64, 1)
    dk = dpre.astype(bf16)
    dv = low[:, 128:]
    low_ref[:, :128] = dk
    low_ref[:, 128:] = dv
    dh = dhq_ref[...] + dot(dk, wk_ref[...], NT) + dot(dv, wv_ref[...], NT)
    acc_ref[...] = dh
    x_in = x_ref[...].astype(f32)
    gain1_ref[...] = jnp.sum(dh * (x_in * row_norm(x_in)), axis=0, keepdims=True)
    own = acc_ref.shape[0] // n_tp
    for k in range(n_tp):
        at = pl.multiple_of(jnp.bitwise_xor(scal_ref[1], k) * own, own)
        dh_ref[k] = acc_ref[pl.ds(at, own), :].astype(bf16)


def last_kernel(n_tp, scal_ref, x_ref, dy_ref, gain_ref, *refs):
    dh_refs, out_ref = refs[:n_tp], refs[n_tp]
    own = dy_ref.shape[0]
    dh = dh_refs[0][...].astype(f32)
    for k in range(1, n_tp):
        dh += dh_refs[k][...].astype(f32)
    x = x_ref[pl.ds(pl.multiple_of(scal_ref[1] * own, own), own), :].astype(f32)
    inverse = row_norm(x)
    z = x * inverse
    e = dh * gain_ref[...]
    inner = jnp.mean(e * z, axis=1, keepdims=True)
    out_ref[...] = (dy_ref[...] + inverse * (e - z * inner)).astype(bf16)


def join_kernel(n_tp, scal_ref, *refs):
    out_ref = refs[n_tp]
    own = refs[0].shape[0]
    for k in range(n_tp):
        at = pl.multiple_of(jnp.bitwise_xor(scal_ref[1], k) * own, own)
        out_ref[pl.ds(at, own), :] = refs[k][...].astype(out_ref.dtype)


def swap(x, axis, k):
    size = lax.axis_size(axis)
    return lax.ppermute(x, axis, [(i, i ^ k) for i in range(size)])


def shards(
    hidden_in,
    doc_starts,
    norm1_gain,
    w_query,
    w_key,
    w_value,
    query_gain,
    key_gain,
    w_out,
    norm2_gain,
    w_gate,
    w_up,
    w_down,
    out_grad,
):
    rows, width = hidden_in.shape
    n_ctx, n_tp = lax.axis_size("ctx"), lax.axis_size("tp")
    head_dim = query_gain.shape[0]
    scale = head_dim ** (-0.5)
    relative = n_ctx <= 8 and (width // n_ctx) % 128 == 0
    own = rows // n_tp
    hidden_units = w_gate.shape[1]
    others = range(1, n_tp)
    mine, place = lax.axis_index("ctx"), lax.axis_index("tp")

    positions = mine * rows + jnp.arange(rows, dtype=jnp.int32)
    inside = doc_starts[None, :] <= positions[:, None]
    begin = jnp.max(jnp.where(inside, doc_starts[None, :], 0), axis=1)
    frequency = rope_base ** (-2.0 * jnp.arange(head_dim // 2, dtype=f32) / head_dim)
    angles = (positions - begin).astype(f32)[:, None] * frequency[None, :]
    cosine, sine = jnp.cos(angles), jnp.sin(angles)
    cosine = jnp.concatenate([cosine] * 4, axis=1)
    sine = jnp.concatenate([-sine, sine, -sine, sine], axis=1)
    scal = jnp.stack([mine, place, begin[0], begin[rows - 1], mine % 2]).astype(jnp.int32)
    begin_row = jnp.concatenate([begin, begin])[None, :]
    gain_one, gain_two = norm1_gain[None, :], norm2_gain[None, :]
    q_gain = jnp.concatenate([query_gain, query_gain])[None, :]
    k_gain = jnp.concatenate([key_gain, key_gain])[None, :]

    h_one, kv, key_pre = call(
        kv_kernel,
        [hidden_in, gain_one, w_key, w_value, cosine, sine, k_gain],
        [shape((rows, width), bf16), shape((rows, 256), bf16), shape((rows, 128), f32)],
        flops=2 * rows * width * 256,
    )
    if relative:
        even = jnp.concatenate([kv] + [swap(kv, "ctx", k) for k in range(2, n_ctx, 2)], axis=0)
        kv_all = [even, swap(even, "ctx", 1)]
    else:
        kv_all = [lax.all_gather(kv, "ctx", axis=0, tiled=True)]
    half = w_out.shape[0] // 2
    w_half = lax.dynamic_slice_in_dim(w_out, (mine % 2) * half, half, 0)
    w_mine = jnp.stack([swap(w_half, "tp", k) for k in others])
    w_pair = swap(w_mine, "ctx", 1)

    qpad, query_pre = call(
        q_kernel,
        [h_one, w_query, cosine, sine, q_gain],
        [shape((4 * rows, 128), bf16), shape((rows, 256), f32)],
        flops=2 * rows * width * 256,
    )
    attend_flops = 2 * 2 * (2 * rows) * (rows * n_ctx) * 128 * 2
    attended, attended32, log_mass = call(
        functools.partial(attend_kernel, relative, scale),
        [scal, begin_row, qpad, *kv_all],
        [shape((rows, 256), bf16), shape((rows, 256), f32), shape((2, 2 * rows), f32)],
        [pltpu.VMEM((2, 128, 2 * rows), f32), pltpu.VMEM((2, 2 * rows), f32)],
        flops=attend_flops,
    )
    o_parts = [attended] + [swap(attended, "tp", k) for k in others]
    h_two, h_two_p, mixed_own = call(
        functools.partial(mix_kernel, n_tp, n_ctx, relative),
        [scal, hidden_in, gain_two, w_out, w_mine, w_pair, *o_parts],
        [shape((rows, width), bf16), shape((rows, width), bf16), shape((own, width), f32)],
        [pltpu.VMEM((rows, width), f32)],
        flops=2 * rows * width * width,
    )
    h_one_p, out_grad_p = call(
        functools.partial(order_kernel, n_ctx, relative),
        [scal, h_one, out_grad],
        [shape((rows, width), bf16)] * 2,
    )

    cut = 384 if hidden_units % 384 == 0 else 128
    whole = lambda *dims: pl.BlockSpec(dims, lambda i: (0,) * len(dims))
    down = pl.BlockSpec((width, cut), lambda i: (0, i))
    part = pl.BlockSpec((rows, cut), lambda i: (0, i))
    act, gate_grad, up_grad, two_parts = call(
        functools.partial(feed_kernel, n_tp),
        [scal, h_two, out_grad, w_gate, w_up, w_down],
        [shape((rows, hidden_units), bf16)] * 3 + [shape((n_tp, own, width), bf16)],
        [pltpu.VMEM((rows, width), f32)],
        flops=2 * rows * width * hidden_units * 5,
        grid=(hidden_units // cut,),
        in_specs=[
            SMEM,
            whole(rows, width),
            whole(rows, width),
            down,
            down,
            pl.BlockSpec((cut, width), lambda i: (i, 0)),
        ],
        out_specs=[part, part, part, whole(n_tp, own, width)],
    )
    two_got = [two_parts[0]] + [swap(two_parts[k], "tp", k) for k in others]
    mixed_grad, attn_grad_p, gain_two_part, out_parts = call(
        functools.partial(mid_kernel, n_tp, n_ctx, relative),
        [scal, out_grad, mixed_own, gain_two, w_out, w_mine, w_pair, *two_got],
        [
            shape((own, width), f32),
            shape((own, width), bf16),
            shape((1, width), f32),
            shape((n_tp, own, 256), bf16),
        ],
        [pltpu.VMEM((own, width), bf16)],
        flops=2 * own * width * width,
    )
    dout = [out_parts[0]] + [swap(out_parts[k], "tp", k) for k in others]

    got = call(
        functools.partial(attend_back_kernel, relative, scale, n_tp),
        [scal, begin_row, qpad, attended32, log_mass, *kv_all, *dout],
        [shape((rows, 256), bf16)] + [shape(x.shape, bf16) for x in kv_all],
        [
            pltpu.VMEM((rows, 256), f32),
            pltpu.VMEM((4 * rows, 128), bf16),
            pltpu.VMEM((2, 128, 2 * rows), f32),
        ],
        flops=attend_flops * 5 // 2,
    )
    query_low, dkv = got[0], got[1:]
    if relative:
        chip = dkv[0] + swap(dkv[1], "ctx", 1)
        pieces = [chip[i * rows : (i + 1) * rows] for i in range(n_ctx // 2)]
        kv_parts = [pieces[0]] + [swap(pieces[i], "ctx", 2 * i) for i in range(1, n_ctx // 2)]
    else:
        kv_parts = [lax.psum_scatter(dkv[0], "ctx", scatter_dimension=0, tiled=True)]
    query_pre_low, q_gain_part, one_query = call(
        q_back_kernel,
        [query_low, query_pre, cosine, sine, q_gain, w_query],
        [shape((rows, 256), bf16), shape((1, 128), f32), shape((rows, width), f32)],
        flops=2 * rows * width * 256,
    )
    kv_pre_low, k_gain_part, gain_one_part, one_parts = call(
        functools.partial(k_back_kernel, n_tp, len(kv_parts)),
        [scal, *kv_parts, key_pre, cosine, sine, k_gain, w_key, w_value, one_query, hidden_in],
        [
            shape((rows, 256), bf16),
            shape((1, 128), f32),
            shape((1, width), f32),
            shape((n_tp, own, width), bf16),
        ],
        [pltpu.VMEM((rows, width), f32)],
        flops=2 * rows * width * 256,
    )
    one_got = [one_parts[0]] + [swap(one_parts[k], "tp", k) for k in others]
    input_own = call(
        functools.partial(last_kernel, n_tp),
        [scal, hidden_in, mixed_grad, gain_one, *one_got],
        [shape((own, width), bf16)],
    )[0]
    input_parts = [input_own] + [swap(input_own, "tp", k) for k in others]
    input_grad = call(
        functools.partial(join_kernel, n_tp), [scal, *input_parts], [shape((rows, width), f32)]
    )[0]

    feed = dot(act, w_down).astype(bf16)
    feed_parts = [
        lax.dynamic_slice_in_dim(feed, jnp.bitwise_xor(place, k) * own, own, 0) for k in range(n_tp)
    ]
    feed_got = [feed_parts[0]] + [swap(feed_parts[k], "tp", k) for k in others]
    layer_own = (mixed_own + sum(x.astype(f32) for x in feed_got)).astype(bf16)
    layer_parts = [layer_own] + [swap(layer_own, "tp", k) for k in others]
    layer_out = call(
        functools.partial(join_kernel, n_tp), [scal, *layer_parts], [shape((rows, width), bf16)]
    )[0]

    def ctx_sum(grad):
        if not relative:
            return lax.psum_scatter(grad, "ctx", scatter_dimension=0, tiled=True).astype(f32)
        block = grad.shape[0] // n_ctx
        chip = grad[: width // 2] + swap(grad[width // 2 :], "ctx", 1)
        total = chip[:block].astype(f32)
        for i in range(1, n_ctx // 2):
            total += swap(chip[i * block : (i + 1) * block], "ctx", 2 * i).astype(f32)
        return total

    attn_grad_all = jnp.concatenate(
        [attn_grad_p] + [swap(attn_grad_p, "tp", k) for k in others], axis=0
    )
    attended_rel = jnp.concatenate(
        [
            lax.dynamic_slice_in_dim(attended, jnp.bitwise_xor(place, k) * own, own, 0)
            for k in range(n_tp)
        ],
        axis=0,
    )
    down_w = ctx_sum(dot(out_grad_p, act, TN).astype(bf16)).T
    gate_w = ctx_sum(dot(h_two_p, gate_grad, TN).astype(bf16))
    up_w = ctx_sum(dot(h_two_p, up_grad, TN).astype(bf16))
    out_w = ctx_sum(dot(attn_grad_all, attended_rel, TN).astype(bf16)).T
    query_w = ctx_sum(dot(h_one_p, query_pre_low, TN).astype(bf16))
    key_value_w = ctx_sum(dot(h_one_p, kv_pre_low, TN).astype(bf16))

    gains = jnp.concatenate(
        [
            gain_one_part.reshape(-1, 128),
            gain_two_part.reshape(-1, 128),
            jnp.concatenate([q_gain_part[:, :64], k_gain_part[:, :64]], axis=1),
        ],
        axis=0,
    )
    for axis, size in (("ctx", n_ctx), ("tp", n_tp)):
        k = 1
        while k < size:
            gains = gains + swap(gains, axis, k)
            k *= 2
    lots = width // 128
    block = width // n_ctx
    gain_one_sum = lax.dynamic_slice_in_dim(gains[:lots].reshape(width), mine * block, block, 0)
    gain_two_sum = lax.dynamic_slice_in_dim(
        gains[lots : 2 * lots].reshape(width), mine * block, block, 0
    )
    return (
        layer_out,
        input_grad,
        gain_one_sum,
        query_w,
        key_value_w[:, :128],
        key_value_w[:, 128:],
        gains[2 * lots, :64],
        gains[2 * lots, 64:],
        out_w,
        gain_two_sum,
        gate_w,
        up_w,
        down_w,
    )


def solution(mesh):
    in_specs = (
        P("ctx", None),
        P(),
        P(),
        P(None, "tp"),
        P(None, "tp"),
        P(None, "tp"),
        P(),
        P(),
        P("tp", None),
        P(),
        P(None, "tp"),
        P(None, "tp"),
        P("tp", None),
        P("ctx", None),
    )
    out_specs = (
        P("ctx", None),
        P("ctx", None),
        P("ctx"),
        P("ctx", "tp"),
        P("ctx", "tp"),
        P("ctx", "tp"),
        P(),
        P(),
        P("tp", "ctx"),
        P("ctx"),
        P("ctx", "tp"),
        P("ctx", "tp"),
        P("tp", "ctx"),
    )
    return jax.shard_map(shards, mesh=mesh, in_specs=in_specs, out_specs=out_specs, check_vma=False)
```

time: 706 us -> 314 us (0.44)
  waiting for transfers between devices: 449 us -> 99.2 us
  starting transfers between devices: 1.56 us -> 106 us
  blocking collectives: 77.9 us -> 0 us
  matrix products: 67.3 us -> 9.05 us
  Pallas kernels: 0 us -> 54.8 us
  local copies, waits for them, and re-layouts: 46.6 us -> 26.2 us
  other arithmetic: 35.1 us -> 16.6 us
  between operations: 15.6 us -> 1.3 us
  loops' own time: 8.21 us -> 0 us
    reduce_scatter x8 -> x0, waiting for transfers between devices: 348 us -> none  [the longest x1 58.4 us: shards(): lax.psum_scatter(gate_w_grad, 'ctx', scatter_dimension=0, tiled=True)]
    ppermute x0 -> x65, starting transfers between devices: none -> 106 us  [swap(): return lax.ppermute(x, axis, [(i, i ^ k) for i in range(size)])]
    psum x3 -> x0, waiting for transfers between devices: 100 us -> none  [the longest x1 57.5 us: shards(): lax.psum(jnp.dot(attended_low, w_out, preferred_element_type=jnp.float32)...]
    ppermute x0 -> x65, waiting for transfers between devices: none -> 99.2 us  [swap(): return lax.ppermute(x, axis, [(i, i ^ k) for i in range(size)])]
    dot_general x28 -> x7, matrix products: 67.3 us -> 9.05 us  [dot(): return lax.dot_general(left, right, dims, preferred_element_type=f32)]
    pallas_call x0 -> x13, Pallas kernels: none -> 54.8 us  [call(): pl.pallas_call(body, out_shape=outs, in_specs=in_specs, out_specs=out_spe...]
    psum x1 -> x0, blocking collectives: 40.2 us -> none  [shards(): lax.psum((query_gain_part, key_gain_part), ('ctx', 'tp'))]
    all_gather x2 -> x0, blocking collectives: 24.4 us -> none  [the longest x1 13.1 us: shards(): lax.all_gather(value_rows, 'ctx', axis=0, tiled=True)]
  transfers between devices with their start and end apart: 11 -> 65, of which waited for: 10 -> 26; matrix products, arithmetic and copies ran while one was open for 8% -> 13% of each run, Pallas kernels for 0% -> 10%
where the time goes in v1:
time: 314 us; the launch traced here: 313 us
  starting transfers between devices  106 us (34%)
  waiting for transfers between devices  99.2 us (32%)
  Pallas kernels  54.8 us (17%)
  local copies, waits for them, and re-layouts  26.2 us (8%)
  other arithmetic  16.6 us (5%)
  matrix products  9.05 us (3%)
    ppermute x65, starting transfers between devices, swap(): return lax.ppermute(x, axis, [(i, i ^ k) for i in range(size)])  106 us
    ppermute x65, waiting for transfers between devices, swap(): return lax.ppermute(x, axis, [(i, i ^ k) for i in range(size)])  99.2 us
    pallas_call x13, Pallas kernels, call(): pl.pallas_call(body, out_shape=outs, in_specs=in_specs, out_specs=out_spe...  54.8 us
    dot_general x7, matrix products, dot(): return lax.dot_general(left, right, dims, preferred_element_type=f32)  9.05 us
    unnamed x121, local copies, waits for them, and re-layouts  8.84 us
  transfers between devices with their start and end apart: 65, of which 26 were waited for; matrix products, arithmetic and copies ran while one was open for 13% of the time, Pallas kernels for 10%

profile of v1, /device:TPU:0, one launch (start us, length us, event | category | flops | bytes accessed | tf_op | source)
XLA Modules:
  0.0 313.4 jit_solution(4096805564602142449)
XLA Ops:
  4.7 3.2 %shard_map.237 = (bf16[384,1024]{1,0:T(8,128)(2,1)}, bf16[384,256]{1,0:T(8,128)(2,1)}, f32[384,128]{1,0:T(8,128)}) custom-call(bf16[384,1024]{1,0:T(8,128)(2,1)} %x_ref.5, f32[1,1024]{1,0:T(1,128)} %bitcast.69, bf16[1024,128]{1,0:T(8,128)(2,1)} %refs_8_.1, bf16[1024,128]{1,0:T(8,128)(2,1)} %refs_9_.1, f32[384,128]{1,0:T(8,128)} %get-tuple-element.166.cos_ref.refs_5_, ...), custom_call_target="tpu_custom_call" | custom-call | flops 201326592 | bytes 2888192 | tf_op jit(solution)/shard_map/pallas_call | solution.py:37
  8.0 2.9 collective-permute-start.4
  13.4 3.4 %collective-permute-done.4 = bf16[384,256]{1,0:T(8,128)(2,1)S(1)} collective-permute-done((bf16[384,256]{1,0:T(8,128)(2,1)}, bf16[384,256]{1,0:T(8,128)(2,1)S(1)}, u32[]{:S(2)}, u32[]{:S(2)}) %collective-permute-start.4) | collective-permute-done | bytes 196640 | tf_op jit(solution)/shard_map/ppermute | solution.py:404
  16.9 6.0 %collective-permute-done.5 = bf16[384,256]{1,0:T(8,128)(2,1)S(1)} collective-permute-done((bf16[384,256]{1,0:T(8,128)(2,1)}, bf16[384,256]{1,0:T(8,128)(2,1)S(1)}, u32[]{:S(2)}, u32[]{:S(2)}) %collective-permute-start.5) | collective-permute-done | bytes 196640 | tf_op jit(solution)/shard_map/ppermute | solution.py:404
  23.1 3.7 %collective-permute-start.2 = (bf16[128,1024]{1,0:T(8,128)(2,1)S(1)}, bf16[128,1024]{1,0:T(8,128)(2,1)S(1)}, u32[]{:S(2)}, u32[]{:S(2)}) collective-permute-start(bf16[128,1024]{1,0:T(8,128)(2,1)S(1)} %constant_dynamic-slice_fusion.7), channel_id=1, source_target_pairs={{0,3},{1,2},{2,1},{3,0},{4,7},{5,6},{6,5},{7,4},{8,11},{9,10},{10,... | collective-permute-start | bytes 786440 | tf_op jit(solution)/shard_map/ppermute | solution.py:404
  27.5 6.7 %collective-permute-done.2 = bf16[128,1024]{1,0:T(8,128)(2,1)S(1)} collective-permute-done((bf16[128,1024]{1,0:T(8,128)(2,1)S(1)}, bf16[128,1024]{1,0:T(8,128)(2,1)S(1)}, u32[]{:S(2)}, u32[]{:S(2)}) %collective-permute-start.2) | collective-permute-done | bytes 262176 | tf_op jit(solution)/shard_map/ppermute | solution.py:404
  34.2 15.5 %collective-permute-done.1 = bf16[128,1024]{1,0:T(8,128)(2,1)S(1)} collective-permute-done((bf16[128,1024]{1,0:T(8,128)(2,1)S(1)}, bf16[128,1024]{1,0:T(8,128)(2,1)S(1)}, u32[]{:S(2)}, u32[]{:S(2)}) %collective-permute-start.1) | collective-permute-done | bytes 262176 | tf_op jit(solution)/shard_map/ppermute | solution.py:404
  51.2 1.9 stack.27.scal_ref
  53.7 3.1 shard_map.238
  57.6 3.8 %shard_map.239 = (bf16[384,256]{1,0:T(8,128)(2,1)}, f32[384,256]{1,0:T(8,128)}, f32[2,768]{1,0:T(2,128)}) custom-call(s32[5]{0:T(128)} %stack.27.scal_ref, s32[1,768]{1,0:T(1,128)} %broadcast_in_dim.32.begin_ref, bf16[1536,128]{1,0:T(8,128)(2,1)} %get-tuple-element.45.qpad_ref, bf16[1536,256]{1,0:T(8,128)(2,1)} %copy-done.32, bf16[1536,256]{1,0:T(8,128)(2,1)} %copy-done.40), custom_call_target="tpu_custom_call" | custom-call | flops 2415919104 | bytes 2565140 | tf_op jit(solution)/shard_map/pallas_call | solution.py:37
  61.4 2.5 collective-permute-start.10
  63.9 1.9 collective-permute-start.8
  65.9 3.0 shard_map.249
  69.5 1.5 collective-permute-done.10.refs_5_
  71.0 9.7 %collective-permute-done.9.refs_4_ = bf16[384,256]{1,0:T(8,128)(2,1)S(1)} collective-permute-done((bf16[384,256]{1,0:T(8,128)(2,1)}, bf16[384,256]{1,0:T(8,128)(2,1)S(1)}, u32[]{:S(2)}, u32[]{:S(2)}) %collective-permute-start.9) | collective-permute-done | bytes 196640 | tf_op jit(solution)/shard_map/ppermute | solution.py:404
  81.5 5.1 %shard_map.240 = (bf16[384,1024]{1,0:T(8,128)(2,1)}, bf16[384,1024]{1,0:T(8,128)(2,1)}, f32[96,1024]{1,0:T(8,128)}) custom-call(s32[5]{0:T(128)} %stack.27.scal_ref, bf16[384,1024]{1,0:T(8,128)(2,1)} %x_ref.5, f32[1,1024]{1,0:T(1,128)} %bitcast.67, bf16[256,1024]{1,0:T(8,128)(2,1)} %w0_ref.3, bf16[3,128,1024]{2,1,0:T(8,128)(2,1)} %copy-done, ...), custom_call_target="tpu_custom_call" | custom-call | flops 805306368 | bytes 5640212 | tf_op jit(solution)/shard_map/pallas_call | solution.py:37
  86.6 11.3 %shard_map.241 = (bf16[384,1152]{1,0:T(8,128)(2,1)}, bf16[384,1152]{1,0:T(8,128)(2,1)}, bf16[384,1152]{1,0:T(8,128)(2,1)}, bf16[4,96,1024]{2,1,0:T(8,128)(2,1)}) custom-call(s32[5]{0:T(128)} %stack.27.scal_ref, bf16[384,1024]{1,0:T(8,128)(2,1)} %get-tuple-element.49.h_ref, bf16[384,1024]{1,0:T(8,128)(2,1)} %b_ref.1, bf16[1024,1152]{1,0:T(8,128)(2,1)} %wg_ref.1, ...), custom_call_target="tpu_custom_call" | custom-call | flops 4529848320 | bytes 12091412 | tf_op jit(solution)/shard_map/pallas_call | solution.py:37
  97.9 2.0 slice_bitcast_fusion.4
  99.9 1.6 collective-permute-start.19
  101.5 2.8 collective-permute-start.17
  105.6 1.6 collective-permute-start.13
  108.8 1.5 convolution_convert_fusion.2
  110.3 5.3 %collective-permute-start.12 = (bf16[96,1024]{1,0:T(8,128)(2,1)S(1)}, bf16[96,1024]{1,0:T(8,128)(2,1)S(1)}, u32[]{:S(2)}, u32[]{:S(2)}) collective-permute-start(bf16[96,1024]{1,0:T(8,128)(2,1)S(1)} %get-tuple-element.137), channel_id=1, source_target_pairs={{0,2},{1,3},{2,0},{3,1},{4,6},{5,7},{6,4},{7,5},{8,10},{9,11},{10,... | collective-permute-start | bytes 589832 | tf_op jit(solution)/shard_map/ppermute | solution.py:404
  115.7 3.3 %collective-permute-done.18.refs_2_ = bf16[96,1024]{1,0:T(8,128)(2,1)S(1)} collective-permute-done((bf16[96,1024]{1,0:T(8,128)(2,1)S(1)}, bf16[96,1024]{1,0:T(8,128)(2,1)S(1)}, u32[]{:S(2)}, u32[]{:S(2)}) %collective-permute-start.18) | collective-permute-done | bytes 196640 | tf_op jit(solution)/shard_map/ppermute | solution.py:404
  119.7 3.9 %shard_map.243 = (f32[96,1024]{1,0:T(8,128)}, bf16[96,1024]{1,0:T(8,128)(2,1)}, f32[1,1024]{1,0:T(1,128)}, bf16[4,96,256]{2,1,0:T(8,128)(2,1)}) custom-call(s32[5]{0:T(128)} %stack.27.scal_ref, bf16[384,1024]{1,0:T(8,128)(2,1)} %b_ref.1, f32[96,1024]{1,0:T(8,128)} %get-tuple-element.48.y_ref, f32[1,1024]{1,0:T(1,128)} %bitcast.68, bf16[256,1024]{1,0:T(8,128)(2,1)} %w0_ref.3, ...), custom_call_target="tpu_custom_call" | custom-call | flops 201326592 | bytes 4857876 | tf_op jit(solution)/shard_map/pallas_call | solution.py:37
  123.6 1.9 collective-permute-start.48
  127.0 2.0 collective-permute-start.22
  128.9 13.1 %collective-permute-start.21 = (bf16[96,256]{1,0:T(8,128)(2,1)S(1)}, bf16[96,256]{1,0:T(8,128)(2,1)S(1)}, u32[]{:S(2)}, u32[]{:S(2)}) collective-permute-start(bf16[96,256]{1,0:T(8,128)(2,1)S(1)} %get-tuple-element.152), channel_id=1, source_target_pairs={{0,2},{1,3},{2,0},{3,1},{4,6},{5,7},{6,4},{7,5},{8,10},{9,11},{10,... | collective-permute-start | bytes 147464 | tf_op jit(solution)/shard_map/ppermute | solution.py:404
  142.0 4.3 %collective-permute-done.12 = bf16[96,1024]{1,0:T(8,128)(2,1)S(1)} collective-permute-done((bf16[96,1024]{1,0:T(8,128)(2,1)S(1)}, bf16[96,1024]{1,0:T(8,128)(2,1)S(1)}, u32[]{:S(2)}, u32[]{:S(2)}) %collective-permute-start.12) | collective-permute-done | bytes 196640 | tf_op jit(solution)/shard_map/ppermute | solution.py:404
  147.2 9.1 %collective-permute-start.46 = (bf16[96,1024]{1,0:T(8,128)(2,1)S(1)}, bf16[96,1024]{1,0:T(8,128)(2,1)}, u32[]{:S(2)}, u32[]{:S(2)}) collective-permute-start(bf16[96,1024]{1,0:T(8,128)(2,1)S(1)} %copy-done.44), channel_id=1, source_target_pairs={{0,1},{1,0},{2,3},{3,2},{4,5},{5,4},{6,7},{7,6},{8,9},{9,8},{10,11... | collective-permute-start | bytes 589832 | tf_op jit(solution)/shard_map/ppermute | solution.py:404
  156.3 2.2 collective-permute-start.16
  159.1 5.4 %shard_map.244 = (bf16[384,256]{1,0:T(8,128)(2,1)}, bf16[1536,256]{1,0:T(8,128)(2,1)}, bf16[1536,256]{1,0:T(8,128)(2,1)}) custom-call(s32[5]{0:T(128)} %stack.27.scal_ref, s32[1,768]{1,0:T(1,128)} %broadcast_in_dim.32.begin_ref, bf16[1536,128]{1,0:T(8,128)(2,1)} %get-tuple-element.45.qpad_ref, f32[384,256]{1,0:T(8,128)} %get-tuple-element.53.o32_ref, ...), custom_call_target="tpu_custom_call" | custom-call | flops 6039797760 | bytes 4334612 | tf_op jit(solution)/shard_map/pallas_call | solution.py:37
  164.5 4.1 %shard_map.245 = (bf16[384,256]{1,0:T(8,128)(2,1)}, f32[1,128]{1,0:T(1,128)}, f32[384,1024]{1,0:T(8,128)}) custom-call(bf16[384,256]{1,0:T(8,128)(2,1)} %get-tuple-element.59.dq_ref, f32[384,256]{1,0:T(8,128)} %get-tuple-element.60.qpre_ref, f32[384,128]{1,0:T(8,128)} %get-tuple-element.166.cos_ref.refs_5_, f32[384,128]{1,0:T(8,128)} %get-tuple-element.167.sin_ref.refs_6_, ...), custom_call_target="tpu_custom_call" | custom-call | flops 201326592 | bytes 3277824 | tf_op jit(solution)/shard_map/pallas_call | solution.py:37
  170.9 1.6 collective-permute-start.14
  173.2 1.5 convolution_convert_fusion.1
  180.7 2.2 shard_map.242
  183.9 7.1 %collective-permute-start.39 = (bf16[128,256]{1,0:T(8,128)(2,1)S(1)}, bf16[128,256]{1,0:T(8,128)(2,1)S(1)}, u32[]{:S(2)}, u32[]{:S(2)}) collective-permute-start(bf16[128,256]{1,0:T(8,128)(2,1)S(1)} %get-tuple-element.144), channel_id=1, source_target_pairs={{0,8},{4,12},{8,0},{12,4},{16,24},{20,28},{24,16},{28,20},{1,9},{5... | collective-permute-start | bytes 196616 | tf_op jit(solution)/shard_map/ppermute | solution.py:404
  191.0 11.8 %collective-permute-start.41 = (bf16[128,256]{1,0:T(8,128)(2,1)S(1)}, bf16[128,256]{1,0:T(8,128)(2,1)S(1)}, u32[]{:S(2)}, u32[]{:S(2)}) collective-permute-start(bf16[128,256]{1,0:T(8,128)(2,1)S(1)} %get-tuple-element.145), channel_id=1, source_target_pairs={{0,24},{4,28},{8,16},{12,20},{16,8},{20,12},{24,0},{28,4},{1,25},{... | collective-permute-start | bytes 196616 | tf_op jit(solution)/shard_map/ppermute | solution.py:404
  203.4 1.5 collective-permute-start.50
  205.0 1.9 collective-permute-done.41
  208.2 1.9 collective-permute-start.51
  213.6 1.7 copy.32
  215.3 1.7 add.155
  219.0 2.0 collective-permute-start.25
  221.5 1.9 collective-permute-start.62
  224.7 1.7 collective-permute-done.26.refs_3_
  227.8 1.6 collective-permute-done.25.refs_2_
  229.4 2.0 collective-permute-start.63
  232.1 4.8 %shard_map.246 = (bf16[384,256]{1,0:T(8,128)(2,1)}, f32[1,128]{1,0:T(1,128)}, f32[1,1024]{1,0:T(1,128)}, bf16[4,96,1024]{2,1,0:T(8,128)(2,1)}) custom-call(s32[5]{0:T(128)} %stack.27.scal_ref, bf16[384,256]{1,0:T(8,128)(2,1)} %get-tuple-element.130.refs_0_, bf16[384,256]{1,0:T(8,128)(2,1)} %copy-done.20, bf16[384,256]{1,0:T(8,128)(2,1)} %copy-done.18, ...), custom_call_target="tpu_custom_call" | custom-call | flops 201326592 | bytes 5248020 | tf_op jit(solution)/shard_map/pallas_call | solution.py:37
  240.1 2.9 collective-permute-done.34
  243.2 3.6 %collective-permute-done.35 = f32[17,128]{1,0:T(8,128)S(1)} collective-permute-done((f32[17,128]{1,0:T(8,128)S(1)}, f32[17,128]{1,0:T(8,128)S(1)}, u32[]{:S(2)}, u32[]{:S(2)}) %collective-permute-start.35) | collective-permute-done | bytes 8736 | tf_op jit(solution)/shard_map/ppermute | solution.py:404
  247.8 2.0 collective-permute-start.29
  252.7 6.2 %collective-permute-done.37 = f32[17,128]{1,0:T(8,128)S(1)} collective-permute-done((f32[17,128]{1,0:T(8,128)S(1)}, f32[17,128]{1,0:T(8,128)S(1)}, u32[]{:S(2)}, u32[]{:S(2)}) %collective-permute-start.37) | collective-permute-done | bytes 8736 | tf_op jit(solution)/shard_map/ppermute | solution.py:404
  260.1 2.2 collective-permute-start.27
  262.9 5.7 %collective-permute-done.28.refs_2_ = bf16[96,1024]{1,0:T(8,128)(2,1)S(1)} collective-permute-done((bf16[96,1024]{1,0:T(8,128)(2,1)S(1)}, bf16[96,1024]{1,0:T(8,128)(2,1)S(1)}, u32[]{:S(2)}, u32[]{:S(2)}) %collective-permute-start.28) | collective-permute-done | bytes 196640 | tf_op jit(solution)/shard_map/ppermute | solution.py:404
  271.2 2.5 shard_map.247.refs_0_
  279.5 5.8 %collective-permute-done.56 = bf16[128,1152]{1,0:T(8,128)(2,1)} collective-permute-done((bf16[128,1152]{1,0:T(8,128)(2,1)S(1)}, bf16[128,1152]{1,0:T(8,128)(2,1)}, u32[]{:S(2)}, u32[]{:S(2)}) %collective-permute-start.56) | collective-permute-done | bytes 294944 | tf_op jit(solution)/shard_map/ppermute | solution.py:404
  285.3 4.8 %collective-permute-done.55 = bf16[128,1152]{1,0:T(8,128)(2,1)S(1)} collective-permute-done((bf16[128,1152]{1,0:T(8,128)(2,1)S(1)}, bf16[128,1152]{1,0:T(8,128)(2,1)S(1)}, u32[]{:S(2)}, u32[]{:S(2)}) %collective-permute-start.55) | collective-permute-done | bytes 294944 | tf_op jit(solution)/shard_map/ppermute | solution.py:404
  290.1 2.2 collective-permute-start.32
  292.3 2.0 convert_add_fusion.1
  295.6 2.0 collective-permute-done.60
  298.9 2.5 collective-permute-done.59
  306.3 3.9 %collective-permute-done.30.refs_1_ = bf16[96,1024]{1,0:T(8,128)(2,1)S(1)} collective-permute-done((bf16[96,1024]{1,0:T(8,128)(2,1)S(1)}, bf16[96,1024]{1,0:T(8,128)(2,1)S(1)}, u32[]{:S(2)}, u32[]{:S(2)}) %collective-permute-start.30) | collective-permute-done | bytes 196640 | tf_op jit(solution)/shard_map/ppermute | solution.py:404
  311.0 2.5 shard_map.248
  (265 shorter events, 65.1 us)
Async XLA Ops:
  8.0 8.9 %collective-permute-start.4 = (bf16[384,256]{1,0:T(8,128)(2,1)}, bf16[384,256]{1,0:T(8,128)(2,1)S(1)}, u32[]{:S(2)}, u32[]{:S(2)}) collective-permute-start(bf16[384,256]{1,0:T(8,128)(2,1)} %get-tuple-element.46), channel_id=1, source_target_pairs={{0,8},{4,12},{8,0},{12,4},{16,24},{20,28},{24,16},{28,20},{1,9},{5... | collective-permute-start | bytes 589832 | tf_op jit(solution)/shard_map/ppermute | solution.py:404
  10.9 12.0 %collective-permute-start.6 = (bf16[384,256]{1,0:T(8,128)(2,1)}, bf16[384,256]{1,0:T(8,128)(2,1)S(1)}, u32[]{:S(2)}, u32[]{:S(2)}) collective-permute-start(bf16[384,256]{1,0:T(8,128)(2,1)} %get-tuple-element.46), channel_id=1, source_target_pairs={{0,24},{4,28},{8,16},{12,20},{16,8},{20,12},{24,0},{28,4},{1,25},{... | collective-permute-start | bytes 589832 | tf_op jit(solution)/shard_map/ppermute | solution.py:404
  12.4 10.5 %collective-permute-start.5 = (bf16[384,256]{1,0:T(8,128)(2,1)}, bf16[384,256]{1,0:T(8,128)(2,1)S(1)}, u32[]{:S(2)}, u32[]{:S(2)}) collective-permute-start(bf16[384,256]{1,0:T(8,128)(2,1)} %get-tuple-element.46), channel_id=1, source_target_pairs={{0,16},{4,20},{8,24},{12,28},{16,0},{20,4},{24,8},{28,12},{1,17},{... | collective-permute-start | bytes 589832 | tf_op jit(solution)/shard_map/ppermute | solution.py:404
  23.0 33.8 %collective-permute-start.7 = (bf16[1536,256]{1,0:T(8,128)(2,1)S(1)}, bf16[1536,256]{1,0:T(8,128)(2,1)S(1)}, u32[]{:S(2)}, u32[]{:S(2)}) collective-permute-start(bf16[1536,256]{1,0:T(8,128)(2,1)S(1)} %constant_dynamic-update-slice_fusion.refs_0_), channel_id=1, source_target_pairs={{0,4},{4,0},{8,12},{12,8},{16,20},{20,16},{24,28},{28,24},{1,5},{5... | collective-permute-start | bytes 2359304 | tf_op jit(solution)/shard_map/ppermute | solution.py:404
  23.1 11.1 %collective-permute-start.2 = (bf16[128,1024]{1,0:T(8,128)(2,1)S(1)}, bf16[128,1024]{1,0:T(8,128)(2,1)S(1)}, u32[]{:S(2)}, u32[]{:S(2)}) collective-permute-start(bf16[128,1024]{1,0:T(8,128)(2,1)S(1)} %constant_dynamic-slice_fusion.7), channel_id=1, source_target_pairs={{0,3},{1,2},{2,1},{3,0},{4,7},{5,6},{6,5},{7,4},{8,11},{9,10},{10,... | collective-permute-start | bytes 786440 | tf_op jit(solution)/shard_map/ppermute | solution.py:404
  26.7 23.0 %collective-permute-start.1 = (bf16[128,1024]{1,0:T(8,128)(2,1)S(1)}, bf16[128,1024]{1,0:T(8,128)(2,1)S(1)}, u32[]{:S(2)}, u32[]{:S(2)}) collective-permute-start(bf16[128,1024]{1,0:T(8,128)(2,1)S(1)} %constant_dynamic-slice_fusion.7), channel_id=1, source_target_pairs={{0,2},{1,3},{2,0},{3,1},{4,6},{5,7},{6,4},{7,5},{8,10},{9,11},{10,... | collective-permute-start | bytes 786440 | tf_op jit(solution)/shard_map/ppermute | solution.py:404
  26.8 23.0 %collective-permute-start = (bf16[128,1024]{1,0:T(8,128)(2,1)S(1)}, bf16[128,1024]{1,0:T(8,128)(2,1)S(1)}, u32[]{:S(2)}, u32[]{:S(2)}) collective-permute-start(bf16[128,1024]{1,0:T(8,128)(2,1)S(1)} %constant_dynamic-slice_fusion.7), channel_id=1, source_target_pairs={{0,1},{1,0},{2,3},{3,2},{4,5},{5,4},{6,7},{7,6},{8,9},{9,8},{10,11... | collective-permute-start | bytes 786440 | tf_op jit(solution)/shard_map/ppermute | solution.py:404
  49.8 19.7 %collective-permute-start.3 = (bf16[3,128,1024]{2,1,0:T(8,128)(2,1)S(1)}, bf16[3,128,1024]{2,1,0:T(8,128)(2,1)S(1)}, u32[]{:S(2)}, u32[]{:S(2)}) collective-permute-start(bf16[3,128,1024]{2,1,0:T(8,128)(2,1)S(1)} %pad_maximum_fusion.refs_0_.wm_ref), channel_id=1, source_target_pairs={{0,4},{4,0},{8,12},{12,8},{16,20},{20,16},{24,28},{28,24},{1,5},{5... | collective-permute-start | bytes 2359304 | tf_op jit(solution)/shard_map/ppermute | solution.py:404
  61.4 9.6 %collective-permute-start.10 = (bf16[384,256]{1,0:T(8,128)(2,1)}, bf16[384,256]{1,0:T(8,128)(2,1)S(1)}, u32[]{:S(2)}, u32[]{:S(2)}) collective-permute-start(bf16[384,256]{1,0:T(8,128)(2,1)} %get-tuple-element.47.refs_2_), channel_id=1, source_target_pairs={{0,3},{1,2},{2,1},{3,0},{4,7},{5,6},{6,5},{7,4},{8,11},{9,10},{10,... | collective-permute-start | bytes 589832 | tf_op jit(solution)/shard_map/ppermute | solution.py:404
  63.9 16.8 %collective-permute-start.9 = (bf16[384,256]{1,0:T(8,128)(2,1)}, bf16[384,256]{1,0:T(8,128)(2,1)S(1)}, u32[]{:S(2)}, u32[]{:S(2)}) collective-permute-start(bf16[384,256]{1,0:T(8,128)(2,1)} %get-tuple-element.47.refs_2_), channel_id=1, source_target_pairs={{0,2},{1,3},{2,0},{3,1},{4,6},{5,7},{6,4},{7,5},{8,10},{9,11},{10,... | collective-permute-start | bytes 589832 | tf_op jit(solution)/shard_map/ppermute | solution.py:404
  63.9 16.8 %collective-permute-start.8 = (bf16[384,256]{1,0:T(8,128)(2,1)}, bf16[384,256]{1,0:T(8,128)(2,1)S(1)}, u32[]{:S(2)}, u32[]{:S(2)}) collective-permute-start(bf16[384,256]{1,0:T(8,128)(2,1)} %get-tuple-element.47.refs_2_), channel_id=1, source_target_pairs={{0,1},{1,0},{2,3},{3,2},{4,5},{5,4},{6,7},{7,6},{8,9},{9,8},{10,11... | collective-permute-start | bytes 589832 | tf_op jit(solution)/shard_map/ppermute | solution.py:404
  99.9 10.4 %collective-permute-start.19 = (bf16[96,1024]{1,0:T(8,128)(2,1)S(1)}, bf16[96,1024]{1,0:T(8,128)(2,1)S(1)}, u32[]{:S(2)}, u32[]{:S(2)}) collective-permute-start(bf16[96,1024]{1,0:T(8,128)(2,1)S(1)} %get-tuple-element.131), channel_id=1, source_target_pairs={{0,3},{1,2},{2,1},{3,0},{4,7},{5,6},{6,5},{7,4},{8,11},{9,10},{10,... | collective-permute-start | bytes 589832 | tf_op jit(solution)/shard_map/ppermute | solution.py:404
  101.5 17.5 %collective-permute-start.18 = (bf16[96,1024]{1,0:T(8,128)(2,1)S(1)}, bf16[96,1024]{1,0:T(8,128)(2,1)S(1)}, u32[]{:S(2)}, u32[]{:S(2)}) collective-permute-start(bf16[96,1024]{1,0:T(8,128)(2,1)S(1)} %get-tuple-element.132), channel_id=1, source_target_pairs={{0,2},{1,3},{2,0},{3,1},{4,6},{5,7},{6,4},{7,5},{8,10},{9,11},{10,... | collective-permute-start | bytes 589832 | tf_op jit(solution)/shard_map/ppermute | solution.py:404
  101.5 17.5 %collective-permute-start.17 = (bf16[96,1024]{1,0:T(8,128)(2,1)S(1)}, bf16[96,1024]{1,0:T(8,128)(2,1)S(1)}, u32[]{:S(2)}, u32[]{:S(2)}) collective-permute-start(bf16[96,1024]{1,0:T(8,128)(2,1)S(1)} %get-tuple-element.133), channel_id=1, source_target_pairs={{0,1},{1,0},{2,3},{3,2},{4,5},{5,4},{6,7},{7,6},{8,9},{9,8},{10,11... | collective-permute-start | bytes 589832 | tf_op jit(solution)/shard_map/ppermute | solution.py:404
  105.5 21.4 %collective-permute-start.11 = (bf16[96,1024]{1,0:T(8,128)(2,1)S(1)}, bf16[96,1024]{1,0:T(8,128)(2,1)S(1)}, u32[]{:S(2)}, u32[]{:S(2)}) collective-permute-start(bf16[96,1024]{1,0:T(8,128)(2,1)S(1)} %get-tuple-element.135), channel_id=1, source_target_pairs={{0,1},{1,0},{2,3},{3,2},{4,5},{5,4},{6,7},{7,6},{8,9},{9,8},{10,11... | collective-permute-start | bytes 589832 | tf_op jit(solution)/shard_map/ppermute | solution.py:404
  105.6 23.3 %collective-permute-start.13 = (bf16[96,1024]{1,0:T(8,128)(2,1)S(1)}, bf16[96,1024]{1,0:T(8,128)(2,1)S(1)}, u32[]{:S(2)}, u32[]{:S(2)}) collective-permute-start(bf16[96,1024]{1,0:T(8,128)(2,1)S(1)} %get-tuple-element.136), channel_id=1, source_target_pairs={{0,3},{1,2},{2,1},{3,0},{4,7},{5,6},{6,5},{7,4},{8,11},{9,10},{10,... | collective-permute-start | bytes 589832 | tf_op jit(solution)/shard_map/ppermute | solution.py:404
  110.3 36.0 %collective-permute-start.12 = (bf16[96,1024]{1,0:T(8,128)(2,1)S(1)}, bf16[96,1024]{1,0:T(8,128)(2,1)S(1)}, u32[]{:S(2)}, u32[]{:S(2)}) collective-permute-start(bf16[96,1024]{1,0:T(8,128)(2,1)S(1)} %get-tuple-element.137), channel_id=1, source_target_pairs={{0,2},{1,3},{2,0},{3,1},{4,6},{5,7},{6,4},{7,5},{8,10},{9,11},{10,... | collective-permute-start | bytes 589832 | tf_op jit(solution)/shard_map/ppermute | solution.py:404
  123.6 47.3 %collective-permute-start.48 = (bf16[96,1024]{1,0:T(8,128)(2,1)}, bf16[96,1024]{1,0:T(8,128)(2,1)S(1)}, u32[]{:S(2)}, u32[]{:S(2)}) collective-permute-start(bf16[96,1024]{1,0:T(8,128)(2,1)} %get-tuple-element.70), channel_id=1, source_target_pairs={{0,3},{1,2},{2,1},{3,0},{4,7},{5,6},{6,5},{7,4},{8,11},{9,10},{10,... | collective-permute-start | bytes 589832 | tf_op jit(solution)/shard_map/ppermute | solution.py:404
  125.4 47.1 %collective-permute-start.47 = (bf16[96,1024]{1,0:T(8,128)(2,1)}, bf16[96,1024]{1,0:T(8,128)(2,1)S(1)}, u32[]{:S(2)}, u32[]{:S(2)}) collective-permute-start(bf16[96,1024]{1,0:T(8,128)(2,1)} %get-tuple-element.70), channel_id=1, source_target_pairs={{0,2},{1,3},{2,0},{3,1},{4,6},{5,7},{6,4},{7,5},{8,10},{9,11},{10,... | collective-permute-start | bytes 589832 | tf_op jit(solution)/shard_map/ppermute | solution.py:404
  127.0 20.2 %collective-permute-start.22 = (bf16[96,256]{1,0:T(8,128)(2,1)S(1)}, bf16[96,256]{1,0:T(8,128)(2,1)S(1)}, u32[]{:S(2)}, u32[]{:S(2)}) collective-permute-start(bf16[96,256]{1,0:T(8,128)(2,1)S(1)} %get-tuple-element.151), channel_id=1, source_target_pairs={{0,3},{1,2},{2,1},{3,0},{4,7},{5,6},{6,5},{7,4},{8,11},{9,10},{10,... | collective-permute-start | bytes 147464 | tf_op jit(solution)/shard_map/ppermute | solution.py:404
  128.9 27.4 %collective-permute-start.21 = (bf16[96,256]{1,0:T(8,128)(2,1)S(1)}, bf16[96,256]{1,0:T(8,128)(2,1)S(1)}, u32[]{:S(2)}, u32[]{:S(2)}) collective-permute-start(bf16[96,256]{1,0:T(8,128)(2,1)S(1)} %get-tuple-element.152), channel_id=1, source_target_pairs={{0,2},{1,3},{2,0},{3,1},{4,6},{5,7},{6,4},{7,5},{8,10},{9,11},{10,... | collective-permute-start | bytes 147464 | tf_op jit(solution)/shard_map/ppermute | solution.py:404
  146.3 12.1 %collective-permute-start.20 = (bf16[96,256]{1,0:T(8,128)(2,1)S(1)}, bf16[96,256]{1,0:T(8,128)(2,1)S(1)}, u32[]{:S(2)}, u32[]{:S(2)}) collective-permute-start(bf16[96,256]{1,0:T(8,128)(2,1)S(1)} %get-tuple-element.153), channel_id=1, source_target_pairs={{0,1},{1,0},{2,3},{3,2},{4,5},{5,4},{6,7},{7,6},{8,9},{9,8},{10,11... | collective-permute-start | bytes 147464 | tf_op jit(solution)/shard_map/ppermute | solution.py:404
  147.2 31.2 %collective-permute-start.46 = (bf16[96,1024]{1,0:T(8,128)(2,1)S(1)}, bf16[96,1024]{1,0:T(8,128)(2,1)}, u32[]{:S(2)}, u32[]{:S(2)}) collective-permute-start(bf16[96,1024]{1,0:T(8,128)(2,1)S(1)} %copy-done.44), channel_id=1, source_target_pairs={{0,1},{1,0},{2,3},{3,2},{4,5},{5,4},{6,7},{7,6},{8,9},{9,8},{10,11... | collective-permute-start | bytes 589832 | tf_op jit(solution)/shard_map/ppermute | solution.py:404
  156.3 23.8 %collective-permute-start.16 = (bf16[96,1024]{1,0:T(8,128)(2,1)}, bf16[96,1024]{1,0:T(8,128)(2,1)}, u32[]{:S(2)}, u32[]{:S(2)}) collective-permute-start(bf16[96,1024]{1,0:T(8,128)(2,1)} %add_convert_fusion.refs_0_), channel_id=1, source_target_pairs={{0,3},{1,2},{2,1},{3,0},{4,7},{5,6},{6,5},{7,4},{8,11},{9,10},{10,... | collective-permute-start | bytes 589832 | tf_op jit(solution)/shard_map/ppermute | solution.py:404
  158.5 21.9 %collective-permute-start.15 = (bf16[96,1024]{1,0:T(8,128)(2,1)}, bf16[96,1024]{1,0:T(8,128)(2,1)}, u32[]{:S(2)}, u32[]{:S(2)}) collective-permute-start(bf16[96,1024]{1,0:T(8,128)(2,1)} %add_convert_fusion.refs_0_), channel_id=1, source_target_pairs={{0,2},{1,3},{2,0},{3,1},{4,6},{5,7},{6,4},{7,5},{8,10},{9,11},{10,... | collective-permute-start | bytes 589832 | tf_op jit(solution)/shard_map/ppermute | solution.py:404
  170.9 9.9 %collective-permute-start.14 = (bf16[96,1024]{1,0:T(8,128)(2,1)}, bf16[96,1024]{1,0:T(8,128)(2,1)}, u32[]{:S(2)}, u32[]{:S(2)}) collective-permute-start(bf16[96,1024]{1,0:T(8,128)(2,1)} %add_convert_fusion.refs_0_), channel_id=1, source_target_pairs={{0,1},{1,0},{2,3},{3,2},{4,5},{5,4},{6,7},{7,6},{8,9},{9,8},{10,11... | collective-permute-start | bytes 589832 | tf_op jit(solution)/shard_map/ppermute | solution.py:404
  172.5 10.4 %collective-permute-start.38 = (bf16[512,256]{1,0:T(8,128)(2,1)}, bf16[512,256]{1,0:T(8,128)(2,1)}, u32[]{:S(2)}, u32[]{:S(2)}) collective-permute-start(bf16[512,256]{1,0:T(8,128)(2,1)} %slice.254), channel_id=1, source_target_pairs={{0,4},{4,0},{8,12},{12,8},{16,20},{20,16},{24,28},{28,24},{1,5},{5... | collective-permute-start | bytes 786440 | tf_op jit(solution)/shard_map/ppermute | solution.py:404
  178.3 42.7 %collective-permute-start.61 = (bf16[512,1152]{1,0:T(8,128)(2,1)}, bf16[512,1152]{1,0:T(8,128)(2,1)S(1)}, u32[]{:S(2)}, u32[]{:S(2)}) collective-permute-start(bf16[512,1152]{1,0:T(8,128)(2,1)} %slice.289), channel_id=1, source_target_pairs={{0,4},{4,0},{8,12},{12,8},{16,20},{20,16},{24,28},{28,24},{1,5},{5... | collective-permute-start | bytes 3538952 | tf_op jit(solution)/shard_map/ppermute | solution.py:404
  180.2 35.1 %collective-permute-start.23 = (bf16[1536,256]{1,0:T(8,128)(2,1)}, bf16[1536,256]{1,0:T(8,128)(2,1)}, u32[]{:S(2)}, u32[]{:S(2)}) collective-permute-start(bf16[1536,256]{1,0:T(8,128)(2,1)} %get-tuple-element.57), channel_id=1, source_target_pairs={{0,4},{4,0},{8,12},{12,8},{16,20},{20,16},{24,28},{28,24},{1,5},{5... | collective-permute-start | bytes 2359304 | tf_op jit(solution)/shard_map/ppermute | solution.py:404
  180.4 22.5 %collective-permute-start.49 = (bf16[512,256]{1,0:T(8,128)(2,1)S(1)}, bf16[512,256]{1,0:T(8,128)(2,1)S(1)}, u32[]{:S(2)}, u32[]{:S(2)}) collective-permute-start(bf16[512,256]{1,0:T(8,128)(2,1)S(1)} %slice.270), channel_id=1, source_target_pairs={{0,4},{4,0},{8,12},{12,8},{16,20},{20,16},{24,28},{28,24},{1,5},{5... | collective-permute-start | bytes 786440 | tf_op jit(solution)/shard_map/ppermute | solution.py:404
  183.9 19.5 %collective-permute-start.39 = (bf16[128,256]{1,0:T(8,128)(2,1)S(1)}, bf16[128,256]{1,0:T(8,128)(2,1)S(1)}, u32[]{:S(2)}, u32[]{:S(2)}) collective-permute-start(bf16[128,256]{1,0:T(8,128)(2,1)S(1)} %get-tuple-element.144), channel_id=1, source_target_pairs={{0,8},{4,12},{8,0},{12,4},{16,24},{20,28},{24,16},{28,20},{1,9},{5... | collective-permute-start | bytes 196616 | tf_op jit(solution)/shard_map/ppermute | solution.py:404
  191.0 15.9 %collective-permute-start.41 = (bf16[128,256]{1,0:T(8,128)(2,1)S(1)}, bf16[128,256]{1,0:T(8,128)(2,1)S(1)}, u32[]{:S(2)}, u32[]{:S(2)}) collective-permute-start(bf16[128,256]{1,0:T(8,128)(2,1)S(1)} %get-tuple-element.145), channel_id=1, source_target_pairs={{0,24},{4,28},{8,16},{12,20},{16,8},{20,12},{24,0},{28,4},{1,25},{... | collective-permute-start | bytes 196616 | tf_op jit(solution)/shard_map/ppermute | solution.py:404
  202.9 5.3 %collective-permute-start.40 = (bf16[128,256]{1,0:T(8,128)(2,1)S(1)}, bf16[128,256]{1,0:T(8,128)(2,1)S(1)}, u32[]{:S(2)}, u32[]{:S(2)}) collective-permute-start(bf16[128,256]{1,0:T(8,128)(2,1)S(1)} %get-tuple-element.146), channel_id=1, source_target_pairs={{0,16},{4,20},{8,24},{12,28},{16,0},{20,4},{24,8},{28,12},{1,17},{... | collective-permute-start | bytes 196616 | tf_op jit(solution)/shard_map/ppermute | solution.py:404
  203.4 7.4 %collective-permute-start.50 = (bf16[128,256]{1,0:T(8,128)(2,1)S(1)}, bf16[128,256]{1,0:T(8,128)(2,1)S(1)}, u32[]{:S(2)}, u32[]{:S(2)}) collective-permute-start(bf16[128,256]{1,0:T(8,128)(2,1)S(1)} %get-tuple-element.138), channel_id=1, source_target_pairs={{0,8},{4,12},{8,0},{12,4},{16,24},{20,28},{24,16},{28,20},{1,9},{5... | collective-permute-start | bytes 196616 | tf_op jit(solution)/shard_map/ppermute | solution.py:404
  206.9 5.3 %collective-permute-start.52 = (bf16[128,256]{1,0:T(8,128)(2,1)S(1)}, bf16[128,256]{1,0:T(8,128)(2,1)S(1)}, u32[]{:S(2)}, u32[]{:S(2)}) collective-permute-start(bf16[128,256]{1,0:T(8,128)(2,1)S(1)} %get-tuple-element.139), channel_id=1, source_target_pairs={{0,24},{4,28},{8,16},{12,20},{16,8},{20,12},{24,0},{28,4},{1,25},{... | collective-permute-start | bytes 196616 | tf_op jit(solution)/shard_map/ppermute | solution.py:404
  208.2 4.7 %collective-permute-start.51 = (bf16[128,256]{1,0:T(8,128)(2,1)S(1)}, bf16[128,256]{1,0:T(8,128)(2,1)S(1)}, u32[]{:S(2)}, u32[]{:S(2)}) collective-permute-start(bf16[128,256]{1,0:T(8,128)(2,1)S(1)} %get-tuple-element.140), channel_id=1, source_target_pairs={{0,16},{4,20},{8,24},{12,28},{16,0},{20,4},{24,8},{28,12},{1,17},{... | collective-permute-start | bytes 196616 | tf_op jit(solution)/shard_map/ppermute | solution.py:404
  210.8 10.7 %collective-permute-start.53 = (bf16[512,1152]{1,0:T(8,128)(2,1)}, bf16[512,1152]{1,0:T(8,128)(2,1)}, u32[]{:S(2)}, u32[]{:S(2)}) collective-permute-start(bf16[512,1152]{1,0:T(8,128)(2,1)} %slice.277), channel_id=1, source_target_pairs={{0,4},{4,0},{8,12},{12,8},{16,20},{20,16},{24,28},{28,24},{1,5},{5... | collective-permute-start | bytes 3538952 | tf_op jit(solution)/shard_map/ppermute | solution.py:404
  212.2 25.6 %collective-permute-start.57 = (bf16[512,1152]{1,0:T(8,128)(2,1)}, bf16[512,1152]{1,0:T(8,128)(2,1)}, u32[]{:S(2)}, u32[]{:S(2)}) collective-permute-start(bf16[512,1152]{1,0:T(8,128)(2,1)} %slice.283), channel_id=1, source_target_pairs={{0,4},{4,0},{8,12},{12,8},{16,20},{20,16},{24,28},{28,24},{1,5},{5... | collective-permute-start | bytes 3538952 | tf_op jit(solution)/shard_map/ppermute | solution.py:404
  217.7 8.7 %collective-permute-start.26 = (bf16[384,256]{1,0:T(8,128)(2,1)S(1)}, bf16[384,256]{1,0:T(8,128)(2,1)S(1)}, u32[]{:S(2)}, u32[]{:S(2)}) collective-permute-start(bf16[384,256]{1,0:T(8,128)(2,1)S(1)} %get-tuple-element.127), channel_id=1, source_target_pairs={{0,24},{4,28},{8,16},{12,20},{16,8},{20,12},{24,0},{28,4},{1,25},{... | collective-permute-start | bytes 589832 | tf_op jit(solution)/shard_map/ppermute | solution.py:404
  219.0 10.4 %collective-permute-start.25 = (bf16[384,256]{1,0:T(8,128)(2,1)S(1)}, bf16[384,256]{1,0:T(8,128)(2,1)S(1)}, u32[]{:S(2)}, u32[]{:S(2)}) collective-permute-start(bf16[384,256]{1,0:T(8,128)(2,1)S(1)} %get-tuple-element.128), channel_id=1, source_target_pairs={{0,16},{4,20},{8,24},{12,28},{16,0},{20,4},{24,8},{28,12},{1,17},{... | collective-permute-start | bytes 589832 | tf_op jit(solution)/shard_map/ppermute | solution.py:404
  221.0 10.4 %collective-permute-start.24 = (bf16[384,256]{1,0:T(8,128)(2,1)S(1)}, bf16[384,256]{1,0:T(8,128)(2,1)S(1)}, u32[]{:S(2)}, u32[]{:S(2)}) collective-permute-start(bf16[384,256]{1,0:T(8,128)(2,1)S(1)} %get-tuple-element.129), channel_id=1, source_target_pairs={{0,8},{4,12},{8,0},{12,4},{16,24},{20,28},{24,16},{28,20},{1,9},{5... | collective-permute-start | bytes 589832 | tf_op jit(solution)/shard_map/ppermute | solution.py:404
  221.5 52.3 %collective-permute-start.62 = (bf16[128,1152]{1,0:T(8,128)(2,1)S(1)}, bf16[128,1152]{1,0:T(8,128)(2,1)S(1)}, u32[]{:S(2)}, u32[]{:S(2)}) collective-permute-start(bf16[128,1152]{1,0:T(8,128)(2,1)S(1)} %get-tuple-element.114), channel_id=1, source_target_pairs={{0,8},{4,12},{8,0},{12,4},{16,24},{20,28},{24,16},{28,20},{1,9},{5... | collective-permute-start | bytes 884744 | tf_op jit(solution)/shard_map/ppermute | solution.py:404
  226.5 48.2 %collective-permute-start.64 = (bf16[128,1152]{1,0:T(8,128)(2,1)S(1)}, bf16[128,1152]{1,0:T(8,128)(2,1)S(1)}, u32[]{:S(2)}, u32[]{:S(2)}) collective-permute-start(bf16[128,1152]{1,0:T(8,128)(2,1)S(1)} %get-tuple-element.115), channel_id=1, source_target_pairs={{0,24},{4,28},{8,16},{12,20},{16,8},{20,12},{24,0},{28,4},{1,25},{... | collective-permute-start | bytes 884744 | tf_op jit(solution)/shard_map/ppermute | solution.py:404
  229.4 46.7 %collective-permute-start.63 = (bf16[128,1152]{1,0:T(8,128)(2,1)S(1)}, bf16[128,1152]{1,0:T(8,128)(2,1)S(1)}, u32[]{:S(2)}, u32[]{:S(2)}) collective-permute-start(bf16[128,1152]{1,0:T(8,128)(2,1)S(1)} %get-tuple-element.116), channel_id=1, source_target_pairs={{0,16},{4,20},{8,24},{12,28},{16,0},{20,4},{24,8},{28,12},{1,17},{... | collective-permute-start | bytes 884744 | tf_op jit(solution)/shard_map/ppermute | solution.py:404
  239.3 3.7 %collective-permute-start.34 = (f32[17,128]{1,0:T(8,128)S(1)}, f32[17,128]{1,0:T(8,128)S(1)}, u32[]{:S(2)}, u32[]{:S(2)}) collective-permute-start(f32[17,128]{1,0:T(8,128)S(1)} %fusion.16), channel_id=1, source_target_pairs={{0,8},{4,12},{8,0},{12,4},{16,24},{20,28},{24,16},{28,20},{1,9},{5... | collective-permute-start | bytes 26120 | tf_op jit(solution)/shard_map/ppermute | solution.py:404
  243.0 3.8 %collective-permute-start.35 = (f32[17,128]{1,0:T(8,128)S(1)}, f32[17,128]{1,0:T(8,128)S(1)}, u32[]{:S(2)}, u32[]{:S(2)}) collective-permute-start(f32[17,128]{1,0:T(8,128)S(1)} %add.157), channel_id=1, source_target_pairs={{0,16},{4,20},{8,24},{12,28},{16,0},{20,4},{24,8},{28,12},{1,17},{... | collective-permute-start | bytes 26120 | tf_op jit(solution)/shard_map/ppermute | solution.py:404
  246.8 3.7 %collective-permute-start.36 = (f32[17,128]{1,0:T(8,128)S(1)}, f32[17,128]{1,0:T(8,128)S(1)}, u32[]{:S(2)}, u32[]{:S(2)}) collective-permute-start(f32[17,128]{1,0:T(8,128)S(1)} %add.158), channel_id=1, source_target_pairs={{0,1},{1,0},{2,3},{3,2},{4,5},{5,4},{6,7},{7,6},{8,9},{9,8},{10,11... | collective-permute-start | bytes 26120 | tf_op jit(solution)/shard_map/ppermute | solution.py:404
  247.8 12.2 %collective-permute-start.29 = (bf16[96,1024]{1,0:T(8,128)(2,1)S(1)}, bf16[96,1024]{1,0:T(8,128)(2,1)S(1)}, u32[]{:S(2)}, u32[]{:S(2)}) collective-permute-start(bf16[96,1024]{1,0:T(8,128)(2,1)S(1)} %get-tuple-element.123), channel_id=1, source_target_pairs={{0,3},{1,2},{2,1},{3,0},{4,7},{5,6},{6,5},{7,4},{8,11},{9,10},{10,... | collective-permute-start | bytes 589832 | tf_op jit(solution)/shard_map/ppermute | solution.py:404
  250.5 8.4 %collective-permute-start.37 = (f32[17,128]{1,0:T(8,128)S(1)}, f32[17,128]{1,0:T(8,128)S(1)}, u32[]{:S(2)}, u32[]{:S(2)}) collective-permute-start(f32[17,128]{1,0:T(8,128)S(1)} %add.159), channel_id=1, source_target_pairs={{0,2},{1,3},{2,0},{3,1},{4,6},{5,7},{6,4},{7,5},{8,10},{9,11},{10,... | collective-permute-start | bytes 26120 | tf_op jit(solution)/shard_map/ppermute | solution.py:404
  258.9 9.7 %collective-permute-start.28 = (bf16[96,1024]{1,0:T(8,128)(2,1)S(1)}, bf16[96,1024]{1,0:T(8,128)(2,1)S(1)}, u32[]{:S(2)}, u32[]{:S(2)}) collective-permute-start(bf16[96,1024]{1,0:T(8,128)(2,1)S(1)} %get-tuple-element.124), channel_id=1, source_target_pairs={{0,2},{1,3},{2,0},{3,1},{4,6},{5,7},{6,4},{7,5},{8,10},{9,11},{10,... | collective-permute-start | bytes 589832 | tf_op jit(solution)/shard_map/ppermute | solution.py:404
  260.1 10.0 %collective-permute-start.27 = (bf16[96,1024]{1,0:T(8,128)(2,1)S(1)}, bf16[96,1024]{1,0:T(8,128)(2,1)S(1)}, u32[]{:S(2)}, u32[]{:S(2)}) collective-permute-start(bf16[96,1024]{1,0:T(8,128)(2,1)S(1)} %get-tuple-element.125), channel_id=1, source_target_pairs={{0,1},{1,0},{2,3},{3,2},{4,5},{5,4},{6,7},{7,6},{8,9},{9,8},{10,11... | collective-permute-start | bytes 589832 | tf_op jit(solution)/shard_map/ppermute | solution.py:404
  268.6 10.2 %collective-permute-start.54 = (bf16[128,1152]{1,0:T(8,128)(2,1)}, bf16[128,1152]{1,0:T(8,128)(2,1)}, u32[]{:S(2)}, u32[]{:S(2)}) collective-permute-start(bf16[128,1152]{1,0:T(8,128)(2,1)} %get-tuple-element.120), channel_id=1, source_target_pairs={{0,8},{4,12},{8,0},{12,4},{16,24},{20,28},{24,16},{28,20},{1,9},{5... | collective-permute-start | bytes 884744 | tf_op jit(solution)/shard_map/ppermute | solution.py:404
  270.0 15.3 %collective-permute-start.56 = (bf16[128,1152]{1,0:T(8,128)(2,1)S(1)}, bf16[128,1152]{1,0:T(8,128)(2,1)}, u32[]{:S(2)}, u32[]{:S(2)}) collective-permute-start(bf16[128,1152]{1,0:T(8,128)(2,1)S(1)} %get-tuple-element.121), channel_id=1, source_target_pairs={{0,24},{4,28},{8,16},{12,20},{16,8},{20,12},{24,0},{28,4},{1,25},{... | collective-permute-start | bytes 884744 | tf_op jit(solution)/shard_map/ppermute | solution.py:404
  273.7 16.3 %collective-permute-start.55 = (bf16[128,1152]{1,0:T(8,128)(2,1)S(1)}, bf16[128,1152]{1,0:T(8,128)(2,1)S(1)}, u32[]{:S(2)}, u32[]{:S(2)}) collective-permute-start(bf16[128,1152]{1,0:T(8,128)(2,1)S(1)} %get-tuple-element.122), channel_id=1, source_target_pairs={{0,16},{4,20},{8,24},{12,28},{16,0},{20,4},{24,8},{28,12},{1,17},{... | collective-permute-start | bytes 884744 | tf_op jit(solution)/shard_map/ppermute | solution.py:404
  274.7 19.7 %collective-permute-start.58 = (bf16[128,1152]{1,0:T(8,128)(2,1)S(1)}, bf16[128,1152]{1,0:T(8,128)(2,1)S(1)}, u32[]{:S(2)}, u32[]{:S(2)}) collective-permute-start(bf16[128,1152]{1,0:T(8,128)(2,1)S(1)} %get-tuple-element.117), channel_id=1, source_target_pairs={{0,8},{4,12},{8,0},{12,4},{16,24},{20,28},{24,16},{28,20},{1,9},{5... | collective-permute-start | bytes 884744 | tf_op jit(solution)/shard_map/ppermute | solution.py:404
  276.1 21.5 %collective-permute-start.60 = (bf16[128,1152]{1,0:T(8,128)(2,1)S(1)}, bf16[128,1152]{1,0:T(8,128)(2,1)S(1)}, u32[]{:S(2)}, u32[]{:S(2)}) collective-permute-start(bf16[128,1152]{1,0:T(8,128)(2,1)S(1)} %get-tuple-element.118), channel_id=1, source_target_pairs={{0,24},{4,28},{8,16},{12,20},{16,8},{20,12},{24,0},{28,4},{1,25},{... | collective-permute-start | bytes 884744 | tf_op jit(solution)/shard_map/ppermute | solution.py:404
  278.7 22.6 %collective-permute-start.59 = (bf16[128,1152]{1,0:T(8,128)(2,1)S(1)}, bf16[128,1152]{1,0:T(8,128)(2,1)S(1)}, u32[]{:S(2)}, u32[]{:S(2)}) collective-permute-start(bf16[128,1152]{1,0:T(8,128)(2,1)S(1)} %get-tuple-element.119), channel_id=1, source_target_pairs={{0,16},{4,20},{8,24},{12,28},{16,0},{20,4},{24,8},{28,12},{1,17},{... | collective-permute-start | bytes 884744 | tf_op jit(solution)/shard_map/ppermute | solution.py:404
  285.3 9.0 %collective-permute-start.42 = (bf16[512,256]{1,0:T(8,128)(2,1)S(1)}, bf16[512,256]{1,0:T(8,128)(2,1)S(1)}, u32[]{:S(2)}, u32[]{:S(2)}) collective-permute-start(bf16[512,256]{1,0:T(8,128)(2,1)S(1)} %copy-done.13), channel_id=1, source_target_pairs={{0,4},{4,0},{8,12},{12,8},{16,20},{20,16},{24,28},{28,24},{1,5},{5... | collective-permute-start | bytes 786440 | tf_op jit(solution)/shard_map/ppermute | solution.py:404
  290.1 16.2 %collective-permute-start.32 = (bf16[96,1024]{1,0:T(8,128)(2,1)S(1)}, bf16[96,1024]{1,0:T(8,128)(2,1)S(1)}, u32[]{:S(2)}, u32[]{:S(2)}) collective-permute-start(bf16[96,1024]{1,0:T(8,128)(2,1)S(1)} %copy-done.9), channel_id=1, source_target_pairs={{0,3},{1,2},{2,1},{3,0},{4,7},{5,6},{6,5},{7,4},{8,11},{9,10},{10,... | collective-permute-start | bytes 589832 | tf_op jit(solution)/shard_map/ppermute | solution.py:404
  294.3 12.0 %collective-permute-start.31 = (bf16[96,1024]{1,0:T(8,128)(2,1)S(1)}, bf16[96,1024]{1,0:T(8,128)(2,1)S(1)}, u32[]{:S(2)}, u32[]{:S(2)}) collective-permute-start(bf16[96,1024]{1,0:T(8,128)(2,1)S(1)} %copy-done.9), channel_id=1, source_target_pairs={{0,2},{1,3},{2,0},{3,1},{4,6},{5,7},{6,4},{7,5},{8,10},{9,11},{10,... | collective-permute-start | bytes 589832 | tf_op jit(solution)/shard_map/ppermute | solution.py:404
  294.4 10.2 %collective-permute-start.43 = (bf16[128,256]{1,0:T(8,128)(2,1)S(1)}, bf16[128,256]{1,0:T(8,128)(2,1)S(1)}, u32[]{:S(2)}, u32[]{:S(2)}) collective-permute-start(bf16[128,256]{1,0:T(8,128)(2,1)S(1)} %get-tuple-element.141), channel_id=1, source_target_pairs={{0,8},{4,12},{8,0},{12,4},{16,24},{20,28},{24,16},{28,20},{1,9},{5... | collective-permute-start | bytes 196616 | tf_op jit(solution)/shard_map/ppermute | solution.py:404
  297.6 7.0 %collective-permute-start.45 = (bf16[128,256]{1,0:T(8,128)(2,1)S(1)}, bf16[128,256]{1,0:T(8,128)(2,1)S(1)}, u32[]{:S(2)}, u32[]{:S(2)}) collective-permute-start(bf16[128,256]{1,0:T(8,128)(2,1)S(1)} %get-tuple-element.142), channel_id=1, source_target_pairs={{0,24},{4,28},{8,16},{12,20},{16,8},{20,12},{24,0},{28,4},{1,25},{... | collective-permute-start | bytes 196616 | tf_op jit(solution)/shard_map/ppermute | solution.py:404
  301.3 4.3 %collective-permute-start.44 = (bf16[128,256]{1,0:T(8,128)(2,1)S(1)}, bf16[128,256]{1,0:T(8,128)(2,1)S(1)}, u32[]{:S(2)}, u32[]{:S(2)}) collective-permute-start(bf16[128,256]{1,0:T(8,128)(2,1)S(1)} %get-tuple-element.143), channel_id=1, source_target_pairs={{0,16},{4,20},{8,24},{12,28},{16,0},{20,4},{24,8},{28,12},{1,17},{... | collective-permute-start | bytes 196616 | tf_op jit(solution)/shard_map/ppermute | solution.py:404
  304.6 5.7 %collective-permute-start.30 = (bf16[96,1024]{1,0:T(8,128)(2,1)S(1)}, bf16[96,1024]{1,0:T(8,128)(2,1)S(1)}, u32[]{:S(2)}, u32[]{:S(2)}) collective-permute-start(bf16[96,1024]{1,0:T(8,128)(2,1)S(1)} %copy-done.9), channel_id=1, source_target_pairs={{0,1},{1,0},{2,3},{3,2},{4,5},{5,4},{6,7},{7,6},{8,9},{9,8},{10,11... | collective-permute-start | bytes 589832 | tf_op jit(solution)/shard_map/ppermute | solution.py:404
  (59 other events, 456.1 us)

commit v2 on v1

v2 whole, which is shorter than its diff:
```python
import functools
import math

import jax
import jax.numpy as jnp
from jax import lax
from jax.experimental import pallas as pl
from jax.experimental.pallas import tpu as pltpu
from jax.sharding import PartitionSpec as P

norm_eps = 1e-05
rope_base = 1000000.0
f32 = jnp.float32
bf16 = jnp.bfloat16
NN = (((1,), (0,)), ((), ()))
NT = (((1,), (1,)), ((), ()))
TN = (((0,), (0,)), ((), ()))
VMEM = pl.BlockSpec(memory_space=pltpu.VMEM)
SMEM = pl.BlockSpec(memory_space=pltpu.SMEM)
vmem_limit = 56 * 1024 * 1024
work = 5 * 10**10


def dot(left, right, dims=NN):
    return lax.dot_general(left, right, dims, preferred_element_type=f32)


def call(body, inputs, outs, scratch=(), work=work, **kwargs):
    in_specs = kwargs.pop("in_specs", None)
    if in_specs is None:
        in_specs = [
            SMEM if (x.dtype == jnp.int32 and x.ndim == 1) else VMEM for x in inputs
        ]
    out_specs = kwargs.pop("out_specs", [VMEM] * len(outs))
    moved = sum(x.size * x.dtype.itemsize for x in inputs) + sum(
        math.prod(o.shape) * o.dtype.itemsize for o in outs
    )
    return pl.pallas_call(
        body,
        out_shape=outs,
        in_specs=in_specs,
        out_specs=out_specs,
        scratch_shapes=list(scratch),
        compiler_params=pltpu.CompilerParams(vmem_limit_bytes=vmem_limit),
        cost_estimate=pl.CostEstimate(flops=work, bytes_accessed=moved, transcendentals=0),
        **kwargs,
    )(*inputs)


def shape(dims, dtype):
    return jax.ShapeDtypeStruct(dims, dtype)


def lanes(x):
    return lax.broadcasted_iota(jnp.int32, x.shape, 1)


def head_mean(x):
    first = lanes(x) < 64
    low = jnp.sum(jnp.where(first, x, 0.0), axis=1, keepdims=True)
    high = jnp.sum(jnp.where(first, 0.0, x), axis=1, keepdims=True)
    return jnp.where(first, low, high) * (1.0 / 64.0)


def swap_halves(x):
    return jnp.where(lanes(x) % 64 < 32, pltpu.roll(x, 96, 1), pltpu.roll(x, 32, 1))


def head_norm(pre, gain):
    inverse = lax.rsqrt(head_mean(pre * pre) + norm_eps)
    return pre * inverse * gain


def head_norm_back(pre, gain, grads):
    inverse = lax.rsqrt(head_mean(pre * pre) + norm_eps)
    normed = pre * inverse
    scaled = grads * gain
    inner = head_mean(scaled * normed)
    return inverse * (scaled - normed * inner), grads * normed


def doc_begin(positions, starts_ref):
    begin = jnp.zeros_like(positions)
    for i in range(starts_ref.shape[0]):
        begin = jnp.where(starts_ref[i] <= positions, starts_ref[i], begin)
    return begin


def twice(gain_ref):
    return jnp.concatenate([gain_ref[...], gain_ref[...]], axis=1)


def quarter(partner, size):
    place = jnp.bitwise_xor(lax.axis_index("tp"), partner)
    return pl.ds(pl.multiple_of(place * size, size), size)


def row_norm(x):
    return lax.rsqrt(jnp.mean(x * x, axis=1, keepdims=True) + norm_eps)


def kv_kernel(
    starts_ref, x_ref, gain_ref, wk_ref, wv_ref, freq_ref, kgain_ref, h_ref, kv_ref, kpre_ref, cos_ref, sin_ref
):
    rows = x_ref.shape[0]
    positions = lax.axis_index("ctx") * rows + lax.broadcasted_iota(jnp.int32, (rows, 128), 0)
    angles = (positions - doc_begin(positions, starts_ref)).astype(f32) * freq_ref[...]
    cosine, sine = jnp.cos(angles), jnp.sin(angles)
    sine = jnp.where(lanes(sine) % 64 < 32, -sine, sine)
    cos_ref[...] = cosine
    sin_ref[...] = sine
    x = x_ref[...].astype(f32)
    h = (x * row_norm(x) * gain_ref[...]).astype(bf16)
    h_ref[...] = h
    kpre = dot(h, wk_ref[...])
    kpre_ref[...] = kpre
    kn = head_norm(kpre, twice(kgain_ref))
    key = kn * cosine + swap_halves(kn) * sine
    kv_ref[:, :128] = key.astype(bf16)
    kv_ref[:, 128:] = dot(h, wv_ref[...]).astype(bf16)


def spread(x, half, out_ref, base, rows):
    rolled = pltpu.roll(x, 64, 1)
    keep = (lanes(x) < 64) if half == 0 else (lanes(x) >= 64)
    first, second = (x, rolled) if half == 0 else (rolled, x)
    out_ref[pl.ds(base, rows), :] = jnp.where(keep, first, 0.0).astype(bf16)
    out_ref[pl.ds(base + rows, rows), :] = jnp.where(keep, second, 0.0).astype(bf16)


def q_kernel(h_ref, wq_ref, cos_ref, sin_ref, qgain_ref, qpad_ref, qpre_ref):
    rows = h_ref.shape[0]
    qpre = dot(h_ref[...], wq_ref[...])
    qpre_ref[...] = qpre
    for half in range(2):
        qn = head_norm(qpre[:, 128 * half : 128 * half + 128], twice(qgain_ref))
        x = qn * cos_ref[...] + swap_halves(qn) * sin_ref[...]
        spread(x, half, qpad_ref, 2 * half * rows, rows)


def visit_blocks(near, rows, starts_ref, count, lists, visit, skip=None):
    mine = lax.axis_index("ctx")
    first, last = mine * rows, mine * rows + rows - 1
    first_begin, last_begin = doc_begin(first, starts_ref), doc_begin(last, starts_ref)
    for which in range(lists):

        def step(index, carry, which=which):
            block = jnp.bitwise_xor(mine, 2 * index + which) if near else index
            start = block * rows
            seen = (block <= mine) & (start + rows - 1 >= first_begin)
            whole = (block < mine) & (start >= last_begin)

            def mask():
                dims = (rows, 2 * rows)
                key_pos = lax.broadcasted_iota(jnp.int32, dims, 0) + start
                across = lax.broadcasted_iota(jnp.int32, (1, 2 * rows), 1)
                query_pos = first + jnp.where(across < rows, across, across - rows)
                return (key_pos <= query_pos) & (key_pos >= doc_begin(query_pos, starts_ref))

            pl.when(seen & whole)(lambda: visit(which, index, None))
            pl.when(seen & jnp.logical_not(whole))(lambda: visit(which, index, mask))
            if skip is not None:
                pl.when(jnp.logical_not(seen))(lambda: skip(which, index))
            return carry

        lax.fori_loop(0, count, step, 0)


def attend_kernel(near, scale, starts_ref, qpad_ref, *refs):
    lists = 2 if near else 1
    kv_refs = refs[:lists]
    o_ref, o32_ref, lse_ref, acc_ref, mass_ref = refs[lists:]
    rows = o_ref.shape[0]
    acc_ref[...] = jnp.zeros_like(acc_ref)
    mass_ref[...] = jnp.zeros_like(mass_ref)
    factor = scale * math.log2(math.e)

    def visit(which, index, mask):
        at = pl.ds(pl.multiple_of(index * rows, rows), rows)
        keys = kv_refs[which][at, :128]
        values_t = kv_refs[which][at, 128:].T
        for j in range(2):
            p = jnp.exp2(dot(keys, qpad_ref[2 * rows * j : 2 * rows * (j + 1), :], NT) * factor)
            if mask is not None:
                p = jnp.where(mask(), p, 0.0)
            mass_ref[j : j + 1, :] += jnp.sum(p, axis=0, keepdims=True)
            acc_ref[j] += dot(values_t, p.astype(bf16))

    visit_blocks(near, rows, starts_ref, kv_refs[0].shape[0] // rows, lists, visit)
    mass = mass_ref[...]
    lse_ref[...] = jnp.log2(mass)
    parts = []
    for j in range(2):
        normed = acc_ref[j, 64 * j : 64 * j + 64, :] / mass[j : j + 1, :]
        parts += [normed[:, :rows], normed[:, rows:]]
    o32 = jnp.concatenate(parts, axis=0).T
    o32_ref[...] = o32
    o_ref[...] = o32.astype(bf16)


def attend_back_kernel(near, scale, n_tp, starts_ref, qpad_ref, o32_ref, lse_ref, *refs):
    lists = 2 if near else 1
    kv_refs, refs = refs[:lists], refs[lists:]
    dout_refs, refs = refs[:n_tp], refs[n_tp:]
    dq_ref, refs = refs[0], refs[1:]
    dkv_refs, refs = refs[:lists], refs[lists:]
    dout_ref, dopad_ref, dqt_ref = refs
    rows = dq_ref.shape[0]
    factor = scale * math.log2(math.e)
    for k in range(n_tp):
        dout_ref[quarter(k, rows // n_tp), :] = dout_refs[k][...].astype(f32)
    dout = dout_ref[...]
    for half in range(2):
        spread(dout[:, 128 * half : 128 * half + 128], half, dopad_ref, 2 * half * rows, rows)
    weighted = (dout * o32_ref[...]).T
    deltas = [jnp.sum(weighted[64 * h : 64 * h + 64], axis=0, keepdims=True) for h in range(4)]
    delta = [jnp.concatenate(deltas[2 * j : 2 * j + 2], axis=1) for j in range(2)]
    dqt_ref[...] = jnp.zeros_like(dqt_ref)

    def visit(which, index, mask):
        at = pl.ds(pl.multiple_of(index * rows, rows), rows)
        keys = kv_refs[which][at, :128]
        values = kv_refs[which][at, 128:]
        keys_t = keys.T
        dk = jnp.zeros((rows, 128), f32)
        dv = jnp.zeros((rows, 128), f32)
        for j in range(2):
            qpad = qpad_ref[2 * rows * j : 2 * rows * (j + 1), :]
            dopad = dopad_ref[2 * rows * j : 2 * rows * (j + 1), :]
            p = jnp.exp2(dot(keys, qpad, NT) * factor - lse_ref[j : j + 1, :])
            if mask is not None:
                p = jnp.where(mask(), p, 0.0)
            ds = (p * (dot(values, dopad, NT) - delta[j])).astype(bf16)
            dv += dot(p.astype(bf16), dopad)
            dk += dot(ds, qpad)
            dqt_ref[j] += dot(keys_t, ds)
        dkv_refs[which][at, :128] = (dk * scale).astype(bf16)
        dkv_refs[which][at, 128:] = dv.astype(bf16)

    def skip(which, index):
        at = pl.ds(pl.multiple_of(index * rows, rows), rows)
        dkv_refs[which][at, :] = jnp.zeros((rows, 256), bf16)

    visit_blocks(near, rows, starts_ref, kv_refs[0].shape[0] // rows, lists, visit, skip)
    parts = []
    for j in range(2):
        part = dqt_ref[j, 64 * j : 64 * j + 64, :]
        parts += [part[:, :rows], part[:, rows:]]
    dq_ref[...] = (jnp.concatenate(parts, axis=0).T * scale).astype(bf16)


def core_halves(size):
    core = lax.axis_index("ctx") % 2
    return (
        pl.ds(pl.multiple_of(core * size, size), size),
        pl.ds(pl.multiple_of((1 - core) * size, size), size),
    )


def mix_kernel(n_tp, x_ref, gain_ref, w0_ref, *refs):
    wm_refs, wp_refs, o_refs = refs[: n_tp - 1], refs[n_tp - 1 : 2 * n_tp - 2], refs[2 * n_tp - 2 : 3 * n_tp - 2]
    h_ref, y_ref, acc_ref = refs[3 * n_tp - 2 :]
    acc = x_ref[...].astype(f32) + dot(o_refs[0][...], w0_ref[...])
    first, second = core_halves(w0_ref.shape[0] // 2)
    for k in range(1, n_tp):
        acc += dot(o_refs[k][:, first], wm_refs[k - 1][...])
        acc += dot(o_refs[k][:, second], wp_refs[k - 1][...])
    acc_ref[...] = acc
    y_ref[...] = acc_ref[quarter(0, y_ref.shape[0]), :]
    h_ref[...] = (acc * row_norm(acc) * gain_ref[...]).astype(bf16)


def feed_kernel(n_tp, h_ref, g_ref, wg_ref, wu_ref, wd_ref, act_ref, dg_ref, du_ref, *refs):
    dh_refs, acc_ref = refs[:n_tp], refs[n_tp]
    step = pl.program_id(0)
    gate = dot(h_ref[...], wg_ref[...])
    up = dot(h_ref[...], wu_ref[...])
    dact = dot(g_ref[...], wd_ref[...], NT)
    sigma = jax.nn.sigmoid(gate)
    silu = gate * sigma
    act_ref[...] = (silu * up).astype(bf16)
    dgate = (dact * up * sigma * (1.0 + gate * (1.0 - sigma))).astype(bf16)
    dup = (dact * silu).astype(bf16)
    dg_ref[...] = dgate
    du_ref[...] = dup
    total = dot(dgate, wg_ref[...], NT) + dot(dup, wu_ref[...], NT)

    @pl.when(step == 0)
    def _():
        acc_ref[...] = total

    @pl.when(step > 0)
    def _():
        acc_ref[...] += total

    @pl.when(step == pl.num_programs(0) - 1)
    def _():
        for k in range(n_tp):
            dh_refs[k][...] = acc_ref[quarter(k, dh_refs[k].shape[0]), :].astype(bf16)


def mid_kernel(n_tp, g_ref, y_ref, gain_ref, w0_ref, *refs):
    wm_refs, wp_refs, refs = refs[: n_tp - 1], refs[n_tp - 1 : 2 * n_tp - 2], refs[2 * n_tp - 2 :]
    dh_refs, refs = refs[:n_tp], refs[n_tp:]
    dy_ref, dattn_ref, gaing_ref = refs[:3]
    dout_refs = refs[3:]
    dh = dh_refs[0][...].astype(f32)
    for k in range(1, n_tp):
        dh += dh_refs[k][...].astype(f32)
    y = y_ref[...]
    inverse = row_norm(y)
    z = y * inverse
    gaing_ref[...] = jnp.sum(dh * z, axis=0, keepdims=True)
    e = dh * gain_ref[...]
    inner = jnp.mean(e * z, axis=1, keepdims=True)
    dy = g_ref[quarter(0, y_ref.shape[0]), :].astype(f32) + inverse * (e - z * inner)
    dy_ref[...] = dy
    low = dy.astype(bf16)
    dattn_ref[...] = low
    dout_refs[0][...] = dot(low, w0_ref[...], NT).astype(bf16)
    first, second = core_halves(w0_ref.shape[0] // 2)
    for k in range(1, n_tp):
        dout_refs[k][:, first] = dot(low, wm_refs[k - 1][...], NT).astype(bf16)
        dout_refs[k][:, second] = dot(low, wp_refs[k - 1][...], NT).astype(bf16)


def down_kernel(n_tp, act_ref, wd_ref, dattn_ref, *refs):
    out_refs, acc_ref = refs[:n_tp], refs[n_tp]
    own, width = dattn_ref.shape
    acc_ref[...] = dot(act_ref[...], wd_ref[...])
    for k in range(n_tp):
        out_refs[k][:, :width] = acc_ref[quarter(k, own), :].astype(bf16)
        out_refs[k][:, width:] = dattn_ref[:, quarter(k, width // n_tp)]


def layer_kernel(n_tp, y_ref, *refs):
    own, width = y_ref.shape
    out_ref, cut_ref = refs[n_tp:]
    total = y_ref[...]
    for k in range(n_tp):
        total += refs[k][:, :width].astype(f32)
        cut_ref[quarter(k, own), :] = refs[k][:, width:]
    out_ref[...] = total.astype(bf16)


def q_back_kernel(near, n_tp, dq_ref, qpre_ref, cos_ref, sin_ref, qgain_ref, wq_ref, h_ref, *refs):
    if near:
        dattn_ref, o_refs, refs = refs[0], refs[1 : 1 + n_tp], refs[1 + n_tp :]
        odd_ref, even_ref, hp_ref, oall_ref = refs[3:]
    low_ref, gaing_ref, dh_ref = refs[:3]
    total = jnp.zeros((1, 128), f32)
    for half in range(2):
        cut = slice(128 * half, 128 * half + 128)
        x = dq_ref[:, cut].astype(f32)
        dqn = x * cos_ref[...] - swap_halves(x) * sin_ref[...]
        dpre, weighted = head_norm_back(qpre_ref[:, cut], twice(qgain_ref), dqn)
        low_ref[:, cut] = dpre.astype(bf16)
        total += jnp.sum(weighted, axis=0, keepdims=True)
    gaing_ref[...] = total + pltpu.roll(total, 64, 1)
    dh_ref[...] = dot(low_ref[...], wq_ref[...], NT)
    if near:
        mine, place = lax.axis_index("ctx"), lax.axis_index("tp")
        for k in range(n_tp):
            oall_ref[k] = o_refs[k][...]
        for parity, out_ref in ((1, odd_ref), (0, even_ref)):
            gather_columns(parity, h_ref, hp_ref)
            out_ref[:, :256] = dot(hp_ref[...], low_ref[...], TN).astype(bf16)
            left = columns(dattn_ref, jnp.bitwise_xor(mine % 2, parity)).T
            for at, chip in enumerate(block_order(parity)):
                heads = jnp.bitwise_xor(jnp.bitwise_xor(mine // 2, chip), place)
                out_ref[128 * at : 128 * at + 128, 256:] = dot(left, oall_ref[heads]).astype(bf16)


def k_back_kernel(near, n_tp, n_parts, *refs):
    parts, refs = refs[:n_parts], refs[n_parts:]
    kpre_ref, cos_ref, sin_ref, kgain_ref, wk_ref, wv_ref, dhq_ref, x_ref, gain2_ref, qg_ref, h_ref = refs[:11]
    low_ref, gains_ref = refs[11:13]
    dh_refs, refs = refs[13 : 13 + n_tp], refs[13 + n_tp :]
    acc_ref = refs[-1]
    total = parts[0][...].astype(f32)
    for part in parts[1:]:
        total += part[...].astype(f32)
    low = total.astype(bf16)
    x = low[:, :128].astype(f32)
    dkn = x * cos_ref[...] - swap_halves(x) * sin_ref[...]
    dpre, weighted = head_norm_back(kpre_ref[...], twice(kgain_ref), dkn)
    dk = dpre.astype(bf16)
    dv = low[:, 128:]
    low_ref[:, :128] = dk
    low_ref[:, 128:] = dv
    dh = dhq_ref[...] + dot(dk, wk_ref[...], NT) + dot(dv, wv_ref[...], NT)
    acc_ref[...] = dh
    for k in range(n_tp):
        dh_refs[k][...] = acc_ref[quarter(k, dh_refs[k].shape[0]), :].astype(bf16)
    x_in = x_ref[...].astype(f32)
    width = x_in.shape[1]
    lots = width // 128
    gain_one = jnp.sum(dh * (x_in * row_norm(x_in)), axis=0, keepdims=True)
    for i in range(lots):
        gains_ref[i : i + 1, :] = gain_one[:, 128 * i : 128 * i + 128]
        gains_ref[lots + i : lots + i + 1, :] = gain2_ref[:, 128 * i : 128 * i + 128]
    gains = jnp.sum(weighted, axis=0, keepdims=True)
    gains_ref[2 * lots : 2 * lots + 1, :] = qg_ref[...]
    gains_ref[2 * lots + 1 : 2 * lots + 2, :] = gains + pltpu.roll(gains, 64, 1)
    gains_ref[2 * lots + 2 :, :] = jnp.zeros((gains_ref.shape[0] - 2 * lots - 2, 128), f32)
    if near:
        odd_ref, even_ref, hp_ref = refs[:3]
        mine = lax.axis_index("ctx")
        for parity, out_ref in ((1, odd_ref), (0, even_ref)):
            gather_columns(parity, h_ref, hp_ref)
            out_ref[:, :256] = dot(hp_ref[...], low_ref[...], TN).astype(bf16)
            for at, chip in enumerate(block_order(parity)):
                block = jnp.bitwise_xor(mine, 2 * chip + parity)
                out_ref[128 * at : 128 * at + 128, 256:] = parted(gain_columns(gains_ref, block, lots))


def last_kernel(n_tp, x_ref, dy_ref, gain_ref, *refs):
    dh_refs, out_ref = refs[:n_tp], refs[n_tp]
    dh = dh_refs[0][...].astype(f32)
    for k in range(1, n_tp):
        dh += dh_refs[k][...].astype(f32)
    x = x_ref[quarter(0, dy_ref.shape[0]), :].astype(f32)
    inverse = row_norm(x)
    z = x * inverse
    e = dh * gain_ref[...]
    inner = jnp.mean(e * z, axis=1, keepdims=True)
    out_ref[...] = (dy_ref[...] + inverse * (e - z * inner)).astype(bf16)


def join_kernel(n_tp, *refs):
    out_ref = refs[n_tp]
    for k in range(n_tp):
        out_ref[quarter(k, refs[k].shape[0]), :] = refs[k][...].astype(out_ref.dtype)


def block_order(parity):
    core = lax.axis_index("ctx") % 2
    first, second = 1 + core, 2 - core
    return (0, first, second, 3) if parity else (0, second, first, 3)


def columns(src_ref, block):
    return src_ref[:, pl.ds(pl.multiple_of(block * 128, 128), 128)]


def gather_columns(parity, src_ref, dst_ref):
    mine = lax.axis_index("ctx")
    for place, chip in enumerate(block_order(parity)):
        dst_ref[:, 128 * place : 128 * place + 128] = columns(src_ref, jnp.bitwise_xor(mine, 2 * chip + parity))


def feed_grad_kernel(h_ref, g_ref, act_ref, dg_ref, du_ref, odd_ref, even_ref, hp_ref, gp_ref):
    units = act_ref.shape[1]
    for parity, out_ref in ((1, odd_ref), (0, even_ref)):
        gather_columns(parity, h_ref, hp_ref)
        gather_columns(parity, g_ref, gp_ref)
        for i, (left_ref, right_ref) in enumerate(((hp_ref, dg_ref), (hp_ref, du_ref), (gp_ref, act_ref))):
            out_ref[:, units * i : units * (i + 1)] = dot(left_ref[...], right_ref[...], TN).astype(bf16)


def feed_grad_sum_kernel(keep_ref, got_ref, gate_ref, up_ref, down_ref):
    units = gate_ref.shape[1]
    for i, out_ref in enumerate((gate_ref, up_ref, down_ref)):
        cut = slice(units * i, units * (i + 1))
        total = keep_ref[:, cut].astype(f32) + got_ref[:, cut].astype(f32)
        out_ref[...] = total.T if i == 2 else total


def joined(x):
    x = x.astype(f32)
    return x + pltpu.roll(x, 64, 1)


def parted(x):
    high = x.astype(bf16).astype(f32)
    return jnp.where(lanes(x) < 64, high, x - high).astype(bf16)


def gain_columns(gains_ref, block, lots):
    row = lambda i: gains_ref[pl.ds(i, 1), :]
    heads = jnp.where(lanes(row(0)) < 64, row(2 * lots), row(2 * lots + 1))
    rows = jnp.concatenate([row(block), row(lots + block), heads, jnp.zeros((125, 128), f32)], axis=0)
    total = rows.T
    return total + pltpu.roll(total, 64, 1)


def attn_grad_chip_kernel(q_ref, q_got_ref, kv_ref, kv_got_ref, here_ref, send_ref):
    half = here_ref.shape[0]
    for i, out_ref in enumerate((here_ref, send_ref)):
        row = slice(half * i, half * (i + 1))
        out_ref[:, :512] = (q_ref[row, :].astype(f32) + q_got_ref[row, :].astype(f32)).astype(bf16)
        out_ref[:, 512:768] = (kv_ref[row, :256].astype(f32) + kv_got_ref[row, :256].astype(f32)).astype(bf16)
        out_ref[:, 768:] = parted(joined(kv_ref[row, 256:]) + joined(kv_got_ref[row, 256:]))


def attn_grad_pass_kernel(keep_ref, got_ref, here_ref, send_ref):
    half = here_ref.shape[0]
    for i, out_ref in enumerate((here_ref, send_ref)):
        row = slice(half * i, half * (i + 1))
        out_ref[:, :768] = (keep_ref[row, :768].astype(f32) + got_ref[row, :768].astype(f32)).astype(bf16)
        out_ref[:, 768:] = parted(joined(keep_ref[row, 768:]) + joined(got_ref[row, 768:]))


def attn_grad_sum_kernel(keep_ref, got_ref, q_ref, k_ref, v_ref, o_ref, gains_ref):
    total = keep_ref[:, :768].astype(f32) + got_ref[:, :768].astype(f32)
    q_ref[...] = total[:, :256]
    o_ref[...] = total[:, 256:512].T.astype(bf16)
    k_ref[...] = total[:, 512:640]
    v_ref[...] = total[:, 640:]
    gains_ref[...] = (joined(keep_ref[:, 768:]) + joined(got_ref[:, 768:])).T[:8]


def gain_kernel(block, a_ref, b_ref, w_ref, one_ref, two_ref, q_ref, k_ref, out_ref):
    out_ref[...] = w_ref[...].astype(f32)
    total = a_ref[...] + b_ref[...]
    one_ref[...] = total[0:1, :block]
    two_ref[...] = total[1:2, :block]
    q_ref[...] = total[2:3, :64]
    k_ref[...] = total[2:3, 64:]


def swap(x, axis, k):
    size = lax.axis_size(axis)
    return lax.ppermute(x, axis, [(i, i ^ k) for i in range(size)])


def swap_across(x, step):
    size = lax.axis_size("ctx")
    return lax.ppermute(x, "ctx", [(i, i ^ (2 << ((i + step) % 2))) for i in range(size)])


def after(x, *first):
    return lax.optimization_barrier((x, *first))[0]


def shards(
    hidden_in,
    doc_starts,
    norm1_gain,
    w_query,
    w_key,
    w_value,
    query_gain,
    key_gain,
    w_out,
    norm2_gain,
    w_gate,
    w_up,
    w_down,
    out_grad,
):
    rows, width = hidden_in.shape
    n_ctx, n_tp = lax.axis_size("ctx"), lax.axis_size("tp")
    head_dim = query_gain.shape[0]
    scale = head_dim ** (-0.5)
    near = n_ctx == 2 * n_tp and width == 128 * n_ctx
    own = rows // n_tp
    units = w_gate.shape[1]
    others = range(1, n_tp)
    chips = range(1, n_ctx // 2)
    mine, place = lax.axis_index("ctx"), lax.axis_index("tp")
    gain_one, gain_two = norm1_gain[None, :], norm2_gain[None, :]
    q_gain, k_gain = query_gain[None, :], key_gain[None, :]
    frequency = rope_base ** (-2.0 * jnp.arange(head_dim // 2, dtype=f32) / head_dim)
    frequency = jnp.concatenate([frequency] * 4)[None, :]

    def exchange(parts):
        return [parts[0]] + [swap(parts[k], "tp", k) for k in others]

    h_one, kv, key_pre, cosine, sine = call(
        kv_kernel,
        [doc_starts, hidden_in, gain_one, w_key, w_value, frequency, k_gain],
        [
            shape((rows, width), bf16),
            shape((rows, 256), bf16),
            shape((rows, 128), f32),
            shape((rows, 128), f32),
            shape((rows, 128), f32),
        ],
    )
    if near:
        kv_got = [swap(kv, "ctx", 2 * i) for i in chips]
    else:
        kv_all = [lax.all_gather(kv, "ctx", axis=0, tiled=True)]
    half = w_out.shape[0] // 2
    w_half = lax.dynamic_slice_in_dim(w_out, (mine % 2) * half, half, 0)
    w_two = swap(w_half, "tp", 2)
    qpad, query_pre = call(
        q_kernel,
        [h_one, w_query, cosine, sine, q_gain],
        [shape((4 * rows, 128), bf16), shape((rows, 256), f32)],
        work=1,
    )
    w_rest = swap(jnp.stack([w_half, w_two]), "tp", 1)
    if near:
        even = jnp.concatenate([after(kv, qpad, w_two), *kv_got], axis=0)
        kv_all = [even, swap(even, "ctx", 1)]
    attended, attended32, log_mass = call(
        functools.partial(attend_kernel, near, scale),
        [doc_starts, qpad, *kv_all],
        [shape((rows, 256), bf16), shape((rows, 256), f32), shape((2, 2 * rows), f32)],
        [pltpu.VMEM((2, 128, 2 * rows), f32), pltpu.VMEM((2, 2 * rows), f32)],
    )
    o_parts = exchange([attended] * n_tp)
    w_two, w_rest = lax.optimization_barrier((w_two, w_rest, attended))[:2]
    w_two_pair, w_rest_pair = swap(w_two, "ctx", 1), swap(w_rest, "ctx", 1)
    w_all = [w_rest[0], w_two, w_rest[1], w_rest_pair[0], w_two_pair, w_rest_pair[1]]
    h_two, mixed_own = call(
        functools.partial(mix_kernel, n_tp),
        [hidden_in, gain_two, w_out, *w_all, *o_parts],
        [shape((rows, width), bf16), shape((own, width), f32)],
        [pltpu.VMEM((rows, width), f32)],
    )

    cut = 384 if units % 384 == 0 else 128
    whole = lambda *dims: pl.BlockSpec(dims, lambda i: (0,) * len(dims))
    across = pl.BlockSpec((width, cut), lambda i: (0, i))
    part = pl.BlockSpec((rows, cut), lambda i: (0, i))
    got = call(
        functools.partial(feed_kernel, n_tp),
        [h_two, out_grad, w_gate, w_up, w_down],
        [shape((rows, units), bf16)] * 3 + [shape((own, width), bf16)] * n_tp,
        [pltpu.VMEM((rows, width), f32)],
        grid=(units // cut,),
        in_specs=[
            whole(rows, width),
            whole(rows, width),
            across,
            across,
            pl.BlockSpec((cut, width), lambda i: (i, 0)),
        ],
        out_specs=[part, part, part] + [whole(own, width)] * n_tp,
    )
    act, gate_grad, up_grad = got[:3]
    two_got = exchange(got[3:])
    block = width // n_ctx
    if near:
        ordered = pltpu.VMEM((rows, 4 * block), bf16)
        feed_odd, feed_even = call(
            feed_grad_kernel,
            [h_two, out_grad, act, gate_grad, up_grad],
            [shape((4 * block, 3 * units), bf16)] * 2,
            [ordered, ordered],
        )
        mixed_own = after(mixed_own, feed_even)
    got = call(
        functools.partial(mid_kernel, n_tp),
        [out_grad, mixed_own, gain_two, w_out, *w_all, *two_got],
        [shape((own, width), f32), shape((own, width), bf16), shape((1, width), f32)]
        + [shape((own, 256), bf16)] * n_tp,
    )
    mixed_grad, attn_grad, gain_two_part = got[:3]
    dout = exchange(got[3:])

    down = call(
        functools.partial(down_kernel, n_tp),
        [act, w_down, attn_grad],
        [shape((own, width + width // n_tp), bf16)] * n_tp,
        [pltpu.VMEM((rows, width), f32)],
    )
    if near:
        half = 2 * block
        feed_other = swap(feed_odd, "ctx", 1)
        feed_send = feed_even[half:] + feed_other[half:]
        feed_got = swap_across(feed_send, 0)
        qpad = after(qpad, feed_send)
    down_got = exchange(list(lax.optimization_barrier((*down, *dout[1:]))[:n_tp]))

    got = call(
        functools.partial(attend_back_kernel, near, scale, n_tp),
        [doc_starts, qpad, attended32, log_mass, *kv_all, *dout],
        [shape((rows, 256), bf16)] + [shape(x.shape, bf16) for x in kv_all],
        [
            pltpu.VMEM((rows, 256), f32),
            pltpu.VMEM((4 * rows, 128), bf16),
            pltpu.VMEM((2, 128, 2 * rows), f32),
        ],
    )
    query_low, dkv = got[0], got[1:]
    if near:
        other = swap(dkv[1], "ctx", 1)
        pieces = [
            dkv[0][i * rows : (i + 1) * rows] + other[i * rows : (i + 1) * rows] for i in range(n_ctx // 2)
        ]
        kv_parts = [pieces[0]] + [swap(pieces[i], "ctx", 2 * i) for i in chips]
    else:
        kv_parts = [lax.psum_scatter(dkv[0], "ctx", scatter_dimension=0, tiled=True)]
    down_got = list(lax.optimization_barrier((*down_got, query_low))[:n_tp])
    layer_own, attn_grad_cut = call(
        functools.partial(layer_kernel, n_tp),
        [mixed_own, *down_got],
        [shape((own, width), bf16), shape((rows, width // n_tp), bf16)],
    )
    layer_two = swap(layer_own, "tp", 2)

    if near:
        feed_parts = lax.optimization_barrier((feed_even, feed_other, feed_got, query_low))[:3]
        feed_here = sum(x[:half].astype(f32) for x in feed_parts).astype(bf16)
        query_low = after(query_low, *pieces)
    more = [attn_grad_cut, *o_parts] if near else []
    got = call(
        functools.partial(q_back_kernel, near, n_tp),
        [query_low, query_pre, cosine, sine, q_gain, w_query, h_one, *more],
        [shape((rows, 256), bf16), shape((1, 128), f32), shape((rows, width), f32)]
        + ([shape((4 * block, 512), bf16)] * 2 if near else []),
        [ordered, pltpu.VMEM((n_tp, rows, 256), bf16)] if near else [],
    )
    query_pre_low, q_gain_part, one_query = got[:3]
    layer_pair = jnp.stack([layer_own, after(layer_two, one_query)])
    layer_rest = swap(layer_pair, "tp", 1)
    done = [layer_pair, feed_here] if near else [layer_pair]
    if near:
        q_odd, q_even = got[3:]
        q_other = swap(q_odd, "ctx", 1)
        done.append(q_other)
    lots = width // 128
    gain_rows = 2 * lots + 8
    got = call(
        functools.partial(k_back_kernel, near, n_tp, len(kv_parts)),
        [
            *kv_parts,
            after(key_pre, *done),
            cosine,
            sine,
            k_gain,
            w_key,
            w_value,
            one_query,
            hidden_in,
            gain_two_part,
            q_gain_part,
            h_one,
        ],
        [shape((rows, 256), bf16), shape((gain_rows, 128), f32)]
        + [shape((own, width), bf16)] * n_tp
        + ([shape((4 * block, 384), bf16)] * 2 if near else []),
        ([ordered] if near else []) + [pltpu.VMEM((rows, width), f32)],
    )
    kv_pre_low, gains = got[:2]
    one_parts = got[2 : 2 + n_tp]
    one_got = exchange(one_parts)
    if near:
        kv_odd, kv_even = got[2 + n_tp :]
        attn_here, attn_send = call(
            attn_grad_chip_kernel,
            [q_even, q_other, kv_even, swap(kv_odd, "ctx", 1)],
            [shape((2 * block, 896), bf16)] * 2,
        )
        attn_here, attn_send = call(
            attn_grad_pass_kernel,
            [attn_here, swap_across(attn_send, 0)],
            [shape((block, 896), bf16)] * 2,
            work=1,
        )
        mixed_grad = after(mixed_grad, attn_here)
    input_own = call(
        functools.partial(last_kernel, n_tp),
        [hidden_in, mixed_grad, gain_one, *one_got],
        [shape((own, width), bf16)],
    )[0]
    input_parts = exchange([input_own] * n_tp)
    layer_rest = after(layer_rest, input_own)
    layer_out = call(
        functools.partial(join_kernel, n_tp),
        [layer_own, layer_rest[0], layer_two, layer_rest[1]],
        [shape((rows, width), bf16)],
        work=1,
    )[0]
    if near:
        feed_send = after(feed_here[block:], one_parts[0])
        feed_here = feed_here[:block]
        gate_w, up_w, down_w = call(
            feed_grad_sum_kernel,
            [after(feed_here, input_own), swap_across(feed_send, 1)],
            [shape((block, units), f32), shape((block, units), f32), shape((units, block), f32)],
            work=1,
        )
        query_w, key_w, value_w, out_w, gains = call(
            attn_grad_sum_kernel,
            [after(attn_here, input_own), swap_across(attn_send, 1)],
            [
                shape((block, 256), f32),
                shape((block, 128), f32),
                shape((block, 128), f32),
                shape((256, block), bf16),
                shape((8, 128), f32),
            ],
            work=1,
        )
        out_w, gains = lax.optimization_barrier((out_w, gains, input_parts[1]))[:2]
        turn = []
        for a in range(n_tp):
            for b in range(2):
                for t in range(n_tp):
                    turn.append(((2 * a + b) * n_tp + t, (2 * t + b) * n_tp + a))
        out_w = lax.ppermute(out_w, ("ctx", "tp"), turn)
    else:

        def scatter(left, right, dim=0):
            grad = dot(left, right, TN).astype(bf16)
            return lax.psum_scatter(grad, "ctx", scatter_dimension=dim, tiled=True).astype(f32)

        attn_grad_all = lax.all_gather(attn_grad, "tp", axis=0, tiled=True)
        down_w = scatter(act, out_grad, 1)
        gate_w = scatter(h_two, gate_grad)
        up_w = scatter(h_two, up_grad)
        out_w = scatter(attended, attn_grad_all, 1)
        query_w = scatter(h_one, query_pre_low)
        kv_w = scatter(h_one, kv_pre_low)
        key_w, value_w = kv_w[:, :128], kv_w[:, 128:]

    if not near:
        gains = lax.psum(gains, "ctx")
        cut = lambda row: lax.dynamic_slice_in_dim(
            gains[row : row + lots].reshape(width), mine * block, block, 0
        )
        heads = jnp.concatenate([gains[2 * lots, :64], gains[2 * lots + 1, :64]])
        gains = jnp.stack([jnp.pad(cut(0), (0, 128 - block)), jnp.pad(cut(lots), (0, 128 - block)), heads])
        gains = jnp.pad(gains, ((0, 5), (0, 0)))
    gains = gains + swap(gains, "tp", 1)
    gain_one_sum, gain_two_sum, q_gain_sum, k_gain_sum, out_w = call(
        functools.partial(gain_kernel, block),
        [gains, swap(gains, "tp", 2), out_w],
        [shape((1, block), f32)] * 2 + [shape((1, 64), f32)] * 2 + [shape(out_w.shape, f32)],
        work=1,
    )
    input_parts[0] = after(input_parts[0], gate_w, layer_out, out_w)
    input_grad = call(
        functools.partial(join_kernel, n_tp), input_parts, [shape((rows, width), f32)]
    )[0]

    return (
        layer_out,
        input_grad,
        gain_one_sum[0],
        query_w,
        key_w,
        value_w,
        q_gain_sum[0],
        k_gain_sum[0],
        out_w,
        gain_two_sum[0],
        gate_w,
        up_w,
        down_w,
    )


def solution(mesh):
    in_specs = (
        P("ctx", None),
        P(),
        P(),
        P(None, "tp"),
        P(None, "tp"),
        P(None, "tp"),
        P(),
        P(),
        P("tp", None),
        P(),
        P(None, "tp"),
        P(None, "tp"),
        P("tp", None),
        P("ctx", None),
    )
    out_specs = (
        P("ctx", None),
        P("ctx", None),
        P("ctx"),
        P("ctx", "tp"),
        P("ctx", "tp"),
        P("ctx", "tp"),
        P(),
        P(),
        P("tp", "ctx"),
        P("ctx"),
        P("ctx", "tp"),
        P("ctx", "tp"),
        P("tp", "ctx"),
    )
    return jax.shard_map(shards, mesh=mesh, in_specs=in_specs, out_specs=out_specs, check_vma=False)
```

time: 314 us -> 220 us (0.70)
  starting transfers between devices: 106 us -> 56.5 us
  waiting for transfers between devices: 99.2 us -> 58.9 us
  Pallas kernels: 54.8 us -> 79.5 us
  other arithmetic: 16.6 us -> 6.31 us
  local copies, waits for them, and re-layouts: 26.2 us -> 16.6 us
  matrix products: 9.05 us -> 0 us
    ppermute x65 -> x37, starting transfers between devices: 106 us -> 49.2 us  [swap(): return lax.ppermute(x, axis, [(i, i ^ k) for i in range(size)])]
    ppermute x65 -> x37, waiting for transfers between devices: 99.2 us -> 48.6 us  [swap(): return lax.ppermute(x, axis, [(i, i ^ k) for i in range(size)])]
    pallas_call x13 -> x20, Pallas kernels: 54.8 us -> 79.5 us  [call(): pl.pallas_call(body, out_shape=outs, in_specs=in_specs, out_specs=out_spe...]
    ppermute x0 -> x5, waiting for transfers between devices: none -> 10.3 us  [the longest x4 10.3 us: swap_across(): lax.ppermute(x, 'ctx', [(i, i ^ 2 << (i + step) % 2) for i in range(size)])]
    dot_general x7 -> x0, matrix products: 9.05 us -> none  [dot(): return lax.dot_general(left, right, dims, preferred_element_type=f32)]
    ppermute x0 -> x5, starting transfers between devices: none -> 7.33 us  [the longest x4 5.84 us: swap_across(): lax.ppermute(x, 'ctx', [(i, i ^ 2 << (i + step) % 2) for i in range(size)])]
    slice x15 -> x1, local copies, waits for them, and re-layouts: 8.01 us -> 1.03 us  [shards(): feed_send = after(feed_here[block:], one_parts[0])]
    add x17 -> x3, other arithmetic: 9.46 us -> 2.97 us  [the longest x1 1.53 us: shards(): feed_send = feed_even[half:] + feed_other[half:]]
  transfers between devices with their start and end apart: 65 -> 42, of which waited for: 26 -> 12; matrix products, arithmetic and copies ran while one was open for 13% -> 5% of each run, Pallas kernels for 10% -> 25%
where the time goes in v2:
time: 220 us; the launch traced here: 219 us
  Pallas kernels  79.5 us (36%)
  waiting for transfers between devices  58.9 us (27%)
  starting transfers between devices  56.5 us (26%)
  local copies, waits for them, and re-layouts  16.6 us (8%)
  other arithmetic  6.31 us (3%)
    pallas_call x20, Pallas kernels, call(): pl.pallas_call(body, out_shape=outs, in_specs=in_specs, out_specs=out_spe...  79.5 us
    ppermute x37, starting transfers between devices, swap(): return lax.ppermute(x, axis, [(i, i ^ k) for i in range(size)])  49.2 us
    ppermute x37, waiting for transfers between devices, swap(): return lax.ppermute(x, axis, [(i, i ^ k) for i in range(size)])  48.6 us
    unnamed x83, local copies, waits for them, and re-layouts  12.1 us
    ppermute x4, waiting for transfers between devices, swap_across(): lax.ppermute(x, 'ctx', [(i, i ^ 2 << (i + step) % 2) for i in range(size)])  10.3 us
    ppermute x4, starting transfers between devices, swap_across(): lax.ppermute(x, 'ctx', [(i, i ^ 2 << (i + step) % 2) for i in range(size)])  5.84 us
  transfers between devices with their start and end apart: 42, of which 12 were waited for; matrix products, arithmetic and copies ran while one was open for 5% of the time, Pallas kernels for 25%

profile of v2, /device:TPU:0, one launch (start us, length us, event | category | flops | bytes accessed | tf_op | source)
XLA Modules:
  0.0 218.9 jit_solution(15005356572323879910)
XLA Ops:
  0.7 1.0 constant_dynamic-slice_fusion
  1.6 4.1 %collective-permute-start = (bf16[128,1024]{1,0:T(8,128)(2,1)S(1)}, bf16[128,1024]{1,0:T(8,128)(2,1)S(1)}, u32[]{:S(2)}, u32[]{:S(2)}) collective-permute-start(bf16[128,1024]{1,0:T(8,128)(2,1)S(1)} %constant_dynamic-slice_fusion), channel_id=1, source_target_pairs={{0,2},{1,3},{2,0},{3,1},{4,6},{5,7},{6,4},{7,5},{8,10},{9,11},{10,... | collective-permute-start | bytes 786440 | tf_op jit(solution)/shard_map/ppermute | solution.py:524
  6.3 3.8 %shard_map.237 = (bf16[384,1024]{1,0:T(8,128)(2,1)}, bf16[384,256]{1,0:T(8,128)(2,1)}, f32[384,128]{1,0:T(8,128)}, f32[384,128]{1,0:T(8,128)}, f32[384,128]{1,0:T(8,128)}) custom-call(s32[8]{0:T(128)} %starts_ref.5, bf16[384,1024]{1,0:T(8,128)(2,1)} %x_ref.5, f32[1,1024]{1,0:T(1,128)} %bitcast.34, bf16[1024,128]{1,0:T(8,128)(2,1)} %refs_8_.1, ...), custom_call_target="tpu_custom_call" | custom-call | flops 49999998976 | bytes 2888480 | tf_op jit(solution)/shard_map/pallas_call | solution.py:38
  10.2 1.5 collective-permute-start.2
  11.6 1.5 collective-permute-start.4
  13.6 3.1 %shard_map.238 = (bf16[1536,128]{1,0:T(8,128)(2,1)}, f32[384,256]{1,0:T(8,128)}) custom-call(bf16[384,1024]{1,0:T(8,128)(2,1)} %get-tuple-element.104.h_ref.refs_14_, bf16[1024,256]{1,0:T(8,128)(2,1)} %wq_ref.3, f32[384,128]{1,0:T(8,128)} %get-tuple-element.105.cos_ref.refs_5_, f32[384,128]{1,0:T(8,128)} %get-tuple-element.106.sin_ref.refs_6_, f32[1,64]{1,0:T(1,128)} %bitcast.30), custom_call_target="tpu_custom_call" | custom-call | flops 1 | bytes 2490624 | tf_op jit(solution)/shard_map/pallas_call | solution.py:38
  16.7 1.0 collective-permute-done.refs_1_
  17.7 1.0 constant_dynamic-update-slice_fusion.3
  18.7 4.6 %collective-permute-done.3 = bf16[384,256]{1,0:T(8,128)(2,1)S(1)} collective-permute-done((bf16[384,256]{1,0:T(8,128)(2,1)}, bf16[384,256]{1,0:T(8,128)(2,1)S(1)}, u32[]{:S(2)}, u32[]{:S(2)}) %collective-permute-start.3) | collective-permute-done | bytes 196640 | tf_op jit(solution)/shard_map/ppermute | solution.py:524
  23.6 1.6 collective-permute-start.1
  25.8 0.9 copy-done.15
  26.7 3.8 %shard_map.239 = (bf16[384,256]{1,0:T(8,128)(2,1)}, f32[384,256]{1,0:T(8,128)}, f32[2,768]{1,0:T(2,128)}) custom-call(s32[8]{0:T(128)} %starts_ref.5, bf16[1536,128]{1,0:T(8,128)(2,1)} %get-tuple-element.137.qpad_ref, bf16[1536,256]{1,0:T(8,128)(2,1)} %copy-done.12, bf16[1536,256]{1,0:T(8,128)(2,1)} %copy-done.15), custom_call_target="tpu_custom_call" | custom-call | flops 49999998976 | bytes 2562080 | tf_op jit(solution)/shard_map/pallas_call | solution.py:38
  30.5 7.4 %collective-permute-done.1 = bf16[2,128,1024]{2,1,0:T(8,128)(2,1)S(1)} collective-permute-done((bf16[2,128,1024]{2,1,0:T(8,128)(2,1)S(1)}, bf16[2,128,1024]{2,1,0:T(8,128)(2,1)S(1)}, u32[]{:S(2)}, u32[]{:S(2)}) %collective-permute-start.1) | collective-permute-done | bytes 524320 | tf_op jit(solution)/shard_map/ppermute | solution.py:524
  38.0 1.3 collective-permute-start.10
  39.3 1.7 collective-permute-start.9
  41.0 1.3 collective-permute-start.8
  44.0 3.8 %collective-permute-done.10.refs_9_.refs_4_ = bf16[384,256]{1,0:T(8,128)(2,1)S(1)} collective-permute-done((bf16[384,256]{1,0:T(8,128)(2,1)}, bf16[384,256]{1,0:T(8,128)(2,1)S(1)}, u32[]{:S(2)}, u32[]{:S(2)}) %collective-permute-start.10) | collective-permute-done | bytes 196640 | tf_op jit(solution)/shard_map/ppermute | solution.py:524
  47.8 11.3 %collective-permute-done.9.refs_8_.refs_3_ = bf16[384,256]{1,0:T(8,128)(2,1)S(1)} collective-permute-done((bf16[384,256]{1,0:T(8,128)(2,1)}, bf16[384,256]{1,0:T(8,128)(2,1)S(1)}, u32[]{:S(2)}, u32[]{:S(2)}) %collective-permute-start.9) | collective-permute-done | bytes 196640 | tf_op jit(solution)/shard_map/ppermute | solution.py:524
  60.0 4.7 %shard_map.240 = (bf16[384,1024]{1,0:T(8,128)(2,1)}, f32[96,1024]{1,0:T(8,128)}) custom-call(bf16[384,1024]{1,0:T(8,128)(2,1)} %x_ref.5, f32[1,1024]{1,0:T(1,128)} %bitcast.32, bf16[256,1024]{1,0:T(8,128)(2,1)} %w0_ref.3, bf16[128,1024]{1,0:T(8,128)(2,1)} %get-tuple-element.204.refs_0_, bf16[128,1024]{1,0:T(8,128)(2,1)} %copy-done.9, ...), custom_call_target="tpu_custom_call" | custom-call | flops 49999998976 | bytes 4853760 | tf_op jit(solution)/shard_map/pallas_call | solution.py:38
  64.8 11.2 %shard_map.241 = (bf16[384,1152]{1,0:T(8,128)(2,1)}, bf16[384,1152]{1,0:T(8,128)(2,1)}, bf16[384,1152]{1,0:T(8,128)(2,1)}, bf16[96,1024]{1,0:T(8,128)(2,1)}, bf1...) custom-call(bf16[384,1024]{1,0:T(8,128)(2,1)} %get-tuple-element.114.h_ref, ...), custom_call_target="tpu_custom_call" | custom-call | flops 49999998976 | bytes 12091392 | tf_op jit(solution)/shard_map/pallas_call | solution.py:38
  76.0 1.7 collective-permute-start.12
  77.8 2.6 %collective-permute-start.13 = (bf16[96,1024]{1,0:T(8,128)(2,1)}, bf16[96,1024]{1,0:T(8,128)(2,1)S(1)}, u32[]{:S(2)}, u32[]{:S(2)}) collective-permute-start(bf16[96,1024]{1,0:T(8,128)(2,1)} %get-tuple-element.123), channel_id=1, source_target_pairs={{0,3},{1,2},{2,1},{3,0},{4,7},{5,6},{6,5},{7,4},{8,11},{9,10},{10,... | collective-permute-start | bytes 589832 | tf_op jit(solution)/shard_map/ppermute | solution.py:524
  80.4 8.3 %shard_map.242 = (bf16[512,3456]{1,0:T(8,128)(2,1)}, bf16[512,3456]{1,0:T(8,128)(2,1)}) custom-call(bf16[384,1024]{1,0:T(8,128)(2,1)} %get-tuple-element.114.h_ref, bf16[384,1024]{1,0:T(8,128)(2,1)} %g_ref.5, bf16[384,1152]{1,0:T(8,128)(2,1)} %get-tuple-element.115.act_ref, bf16[384,1152]{1,0:T(8,128)(2,1)} %get-tuple-element.116.dg_ref, ...), custom_call_target="tpu_custom_call" | custom-call | flops 49999998976 | bytes 11304960 | tf_op jit(solution)/shard_map/pallas_call | solution.py:38
  88.7 4.7 %collective-permute-done.12.refs_8_ = bf16[96,1024]{1,0:T(8,128)(2,1)S(1)} collective-permute-done((bf16[96,1024]{1,0:T(8,128)(2,1)}, bf16[96,1024]{1,0:T(8,128)(2,1)S(1)}, u32[]{:S(2)}, u32[]{:S(2)}) %collective-permute-start.12) | collective-permute-done | bytes 196640 | tf_op jit(solution)/shard_map/ppermute | solution.py:524
  94.2 3.7 %shard_map.243 = (f32[96,1024]{1,0:T(8,128)}, bf16[96,1024]{1,0:T(8,128)(2,1)}, f32[1,1024]{1,0:T(1,128)}, bf16[96,256]{1,0:T(8,128)(2,1)}, bf16[96,256]{1,0:T(8...) custom-call(bf16[384,1024]{1,0:T(8,128)(2,1)} %g_ref.5, f32[96,1024]{1,0:T(8,128)} %get-tuple-element.119.y_ref, ...), custom_call_target="tpu_custom_call" | custom-call | flops 49999998976 | bytes 4857856 | tf_op jit(solution)/shard_map/pallas_call | solution.py:38
  97.9 3.5 %collective-permute-start.14 = (bf16[96,256]{1,0:T(8,128)(2,1)}, bf16[96,256]{1,0:T(8,128)(2,1)S(1)}, u32[]{:S(2)}, u32[]{:S(2)}) collective-permute-start(bf16[96,256]{1,0:T(8,128)(2,1)} %get-tuple-element.129), channel_id=1, source_target_pairs={{0,1},{1,0},{2,3},{3,2},{4,5},{5,4},{6,7},{7,6},{8,9},{9,8},{10,11... | collective-permute-start | bytes 147464 | tf_op jit(solution)/shard_map/ppermute | solution.py:524
  101.3 2.4 %collective-permute-start.16 = (bf16[96,256]{1,0:T(8,128)(2,1)}, bf16[96,256]{1,0:T(8,128)(2,1)S(1)}, u32[]{:S(2)}, u32[]{:S(2)}) collective-permute-start(bf16[96,256]{1,0:T(8,128)(2,1)} %get-tuple-element.131), channel_id=1, source_target_pairs={{0,3},{1,2},{2,1},{3,0},{4,7},{5,6},{6,5},{7,4},{8,11},{9,10},{10,... | collective-permute-start | bytes 147464 | tf_op jit(solution)/shard_map/ppermute | solution.py:524
  103.8 4.3 %shard_map.244 = (bf16[96,1280]{1,0:T(8,128)(2,1)}, bf16[96,1280]{1,0:T(8,128)(2,1)}, bf16[96,1280]{1,0:T(8,128)(2,1)}, bf16[96,1280]{1,0:T(8,128)(2,1)}) custom-call(bf16[384,1152]{1,0:T(8,128)(2,1)} %get-tuple-element.115.act_ref, bf16[1152,1024]{1,0:T(8,128)(2,1)} %wd_ref.3, bf16[96,1024]{1,0:T(8,128)(2,1)} %get-tuple-element.124.dattn_ref), custom_call_target="tpu_custom_call" | custom-call | flops 49999998976 | bytes 4423680 | tf_op jit(solution)/shard_map/pallas_call | solution.py:38
  108.1 1.1 collective-permute-start.17
  109.2 1.3 collective-permute-start.18
  110.5 2.1 collective-permute-start.19
  112.6 1.5 slice_add_fusion
  115.0 1.5 collective-permute-start.28
  116.5 5.6 %shard_map.245 = (bf16[384,256]{1,0:T(8,128)(2,1)}, bf16[1536,256]{1,0:T(8,128)(2,1)}, bf16[1536,256]{1,0:T(8,128)(2,1)}) custom-call(s32[8]{0:T(128)} %starts_ref.5, bf16[1536,128]{1,0:T(8,128)(2,1)} %get-tuple-element.137.qpad_ref, f32[384,256]{1,0:T(8,128)} %get-tuple-element.138.o32_ref, f32[2,768]{1,0:T(2,128)} %get-tuple-element.139.lse_ref, ...), custom_call_target="tpu_custom_call" | custom-call | flops 49999998976 | bytes 4331552 | tf_op jit(solution)/shard_map/pallas_call | solution.py:38
  122.1 6.6 %collective-permute-done.18.refs_2_ = bf16[96,1280]{1,0:T(8,128)(2,1)S(1)} collective-permute-done((bf16[96,1280]{1,0:T(8,128)(2,1)}, bf16[96,1280]{1,0:T(8,128)(2,1)S(1)}, u32[]{:S(2)}, u32[]{:S(2)}) %collective-permute-start.18) | collective-permute-done | bytes 245792 | tf_op jit(solution)/shard_map/ppermute | solution.py:524
  129.5 2.2 shard_map.246
  131.7 3.5 %collective-permute-start.21 = (bf16[96,1024]{1,0:T(8,128)(2,1)}, bf16[96,1024]{1,0:T(8,128)(2,1)S(1)}, u32[]{:S(2)}, u32[]{:S(2)}) collective-permute-start(bf16[96,1024]{1,0:T(8,128)(2,1)} %get-tuple-element.146.refs_0_), channel_id=1, source_target_pairs={{0,2},{1,3},{2,0},{3,1},{4,6},{5,7},{6,4},{7,5},{8,10},{9,11},{10,... | collective-permute-start | bytes 589832 | tf_op jit(solution)/shard_map/ppermute | solution.py:524
  136.0 1.4 collective-permute-start.27
  137.3 1.6 collective-permute-start.26
  139.5 5.3 %shard_map.247 = (bf16[384,256]{1,0:T(8,128)(2,1)}, f32[1,128]{1,0:T(1,128)}, f32[384,1024]{1,0:T(8,128)}, bf16[512,512]{1,0:T(8,128)(2,1)}, bf16[512,512]{1,0:T(8,128)(2,1)}) custom-call(bf16[384,256]{1,0:T(8,128)(2,1)} %get-tuple-element.149.dq_ref, f32[384,256]{1,0:T(8,128)} %get-tuple-element.150.qpre_ref, ...), custom_call_target="tpu_custom_call" | custom-call | flops 49999998976 | bytes 6095616 | tf_op jit(solution)/shard_map/pallas_call | solution.py:38
  145.4 2.6 %add_convert_fusion = bf16[256,3456]{1,0:T(8,128)(2,1)S(1)} fusion(bf16[256,3456]{1,0:T(8,128)(2,1)} %collective-permute-done.28, bf16[512,3456]{1,0:T(8,128)(2,1)} %copy-done.2, bf16[512,3456]{1,0:T(8,128)(2,1)S(1)} %copy-done.1), kind=kLoop, calls=%fused_computation | loop fusion | flops 5308416 | bytes 7077888 | tf_op jit(solution)/shard_map/convert_element_type | solution.py:698
  149.0 5.3 %shard_map.248 = (bf16[384,256]{1,0:T(8,128)(2,1)}, f32[24,128]{1,0:T(8,128)}, bf16[96,1024]{1,0:T(8,128)(2,1)}, bf16[96,1024]{1,0:T(8,128)(2,1)}, bf16[96,1024]...) custom-call(bf16[384,256]{1,0:T(8,128)(2,1)} %get-tuple-element.200.refs_0_, ...), custom_call_target="tpu_custom_call" | custom-call | flops 49999998976 | bytes 6832896 | tf_op jit(solution)/shard_map/pallas_call | solution.py:38
  155.3 1.2 collective-permute-start.31
  156.5 1.8 collective-permute-start.32
  158.3 1.4 collective-permute-start.33
  160.4 2.7 %shard_map.249 = (bf16[256,896]{1,0:T(8,128)(2,1)}, bf16[256,896]{1,0:T(8,128)(2,1)}) custom-call(bf16[512,512]{1,0:T(8,128)(2,1)} %get-tuple-element.155.q_ref, bf16[512,512]{1,0:T(8,128)(2,1)} %copy-done.16, bf16[512,384]{1,0:T(8,128)(2,1)} %get-tuple-element.164.kv_ref, bf16[512,384]{1,0:T(8,128)(2,1)} %copy-done.17), custom_call_target="tpu_custom_call" | custom-call | flops 49999998976 | bytes 2752512 | tf_op jit(solution)/shard_map/pallas_call | solution.py:38
  163.1 1.8 collective-permute-start.30
  164.8 1.0 fusion
  165.9 5.9 %collective-permute-done.30.got_ref = bf16[256,896]{1,0:T(8,128)(2,1)S(1)} collective-permute-done((bf16[256,896]{1,0:T(8,128)(2,1)}, bf16[256,896]{1,0:T(8,128)(2,1)S(1)}, u32[]{:S(2)}, u32[]{:S(2)}) %collective-permute-start.30) | collective-permute-done | bytes 458784 | tf_op jit(solution)/shard_map/ppermute | solution.py:529
  171.8 1.8 collective-permute-start.34
  173.6 2.1 shard_map.250
  176.5 3.3 %collective-permute-done.33.refs_3_ = bf16[96,1024]{1,0:T(8,128)(2,1)S(1)} collective-permute-done((bf16[96,1024]{1,0:T(8,128)(2,1)}, bf16[96,1024]{1,0:T(8,128)(2,1)S(1)}, u32[]{:S(2)}, u32[]{:S(2)}) %collective-permute-start.33) | collective-permute-done | bytes 196640 | tf_op jit(solution)/shard_map/ppermute | solution.py:524
  180.5 2.5 %shard_map.251.refs_0_ = bf16[96,1024]{1,0:T(8,128)(2,1)} custom-call(bf16[384,1024]{1,0:T(8,128)(2,1)} %x_ref.5, f32[96,1024]{1,0:T(8,128)} %get-tuple-element.169.dy_ref, f32[1,1024]{1,0:T(1,128)} %bitcast.35, bf16[96,1024]{1,0:T(8,128)(2,1)} %get-tuple-element.170.refs_0_, bf16[96,1024]{1,0:T(8,128)(2,1)} %copy-done.31, bf16[96,1024]{1,0:T(8,128)(2,1)} %copy-done.32, ...), custom_call_target="tpu_custom_call" | custom-call | flops 49999998976 | bytes 2166784 | tf_op jit(solution)/shard_map/pallas_call | solution.py:38
  182.9 4.3 %collective-permute-done.35.got_ref = bf16[128,896]{1,0:T(8,128)(2,1)S(1)} collective-permute-done((bf16[128,896]{1,0:T(8,128)(2,1)}, bf16[128,896]{1,0:T(8,128)(2,1)S(1)}, u32[]{:S(2)}, u32[]{:S(2)}) %collective-permute-start.35) | collective-permute-done | bytes 229408 | tf_op jit(solution)/shard_map/ppermute | solution.py:529
  188.0 1.9 shard_map.254
  189.9 0.9 collective-permute-start.37
  190.8 1.9 collective-permute-start.41
  193.4 1.5 collective-permute-start.39
  195.6 4.6 %collective-permute-start.38 = (f32[8,128]{1,0:T(8,128)S(1)}, f32[8,128]{1,0:T(8,128)S(1)}, u32[]{:S(2)}, u32[]{:S(2)}) collective-permute-start(f32[8,128]{1,0:T(8,128)S(1)} %add.40.a_ref), channel_id=1, source_target_pairs={{0,2},{1,3},{2,0},{3,1},{4,6},{5,7},{6,4},{7,5},{8,10},{9,11},{10,... | collective-permute-start | bytes 12296 | tf_op jit(solution)/shard_map/ppermute | solution.py:524
  201.0 2.2 shard_map.252
  204.0 2.9 %shard_map.253 = (f32[128,1152]{1,0:T(8,128)}, f32[128,1152]{1,0:T(8,128)}, f32[1152,128]{1,0:T(8,128)}) custom-call(bf16[128,3456]{1,0:T(8,128)(2,1)} %get-tuple-element.175.keep_ref, bf16[128,3456]{1,0:T(8,128)(2,1)} %copy-done.3), custom_call_target="tpu_custom_call" | custom-call | flops 1 | bytes 3538944 | tf_op jit(solution)/shard_map/pallas_call | solution.py:38
  206.9 5.3 %collective-permute-done.38.b_ref = f32[8,128]{1,0:T(8,128)S(1)} collective-permute-done((f32[8,128]{1,0:T(8,128)S(1)}, f32[8,128]{1,0:T(8,128)S(1)}, u32[]{:S(2)}, u32[]{:S(2)}) %collective-permute-start.38) | collective-permute-done | bytes 4128 | tf_op jit(solution)/shard_map/ppermute | solution.py:524
  213.4 1.6 shard_map.255
  216.4 2.5 %shard_map.256 = f32[384,1024]{1,0:T(8,128)} custom-call(bf16[96,1024]{1,0:T(8,128)(2,1)} %shard_map.251.refs_0_, bf16[96,1024]{1,0:T(8,128)(2,1)} %copy-done.25, bf16[96,1024]{1,0:T(8,128)(2,1)} %copy-done.30, bf16[96,1024]{1,0:T(8,128)(2,1)} %copy-done.28), custom_call_target="tpu_custom_call" | custom-call | flops 49999998976 | bytes 2359296 | tf_op jit(solution)/shard_map/pallas_call | solution.py:38
  (138 shorter events, 19.2 us)
Async XLA Ops:
  1.6 16.0 %collective-permute-start = (bf16[128,1024]{1,0:T(8,128)(2,1)S(1)}, bf16[128,1024]{1,0:T(8,128)(2,1)S(1)}, u32[]{:S(2)}, u32[]{:S(2)}) collective-permute-start(bf16[128,1024]{1,0:T(8,128)(2,1)S(1)} %constant_dynamic-slice_fusion), channel_id=1, source_target_pairs={{0,2},{1,3},{2,0},{3,1},{4,6},{5,7},{6,4},{7,5},{8,10},{9,11},{10,... | collective-permute-start | bytes 786440 | tf_op jit(solution)/shard_map/ppermute | solution.py:524
  10.2 13.4 %copy-start.7 = (bf16[256,1024]{1,0:T(8,128)(2,1)S(1)}, bf16[256,1024]{1,0:T(8,128)(2,1)}, u32[]{:S(2)}) copy-start(bf16[256,1024]{1,0:T(8,128)(2,1)} %w0_ref.3) | copy-start | bytes 1572868
  10.2 8.6 %collective-permute-start.2 = (bf16[384,256]{1,0:T(8,128)(2,1)}, bf16[384,256]{1,0:T(8,128)(2,1)S(1)}, u32[]{:S(2)}, u32[]{:S(2)}) collective-permute-start(bf16[384,256]{1,0:T(8,128)(2,1)} %get-tuple-element.109), channel_id=1, source_target_pairs={{0,8},{4,12},{8,0},{12,4},{16,24},{20,28},{24,16},{28,20},{1,9},{5... | collective-permute-start | bytes 589832 | tf_op jit(solution)/shard_map/ppermute | solution.py:524
  11.6 11.7 %collective-permute-start.4 = (bf16[384,256]{1,0:T(8,128)(2,1)}, bf16[384,256]{1,0:T(8,128)(2,1)S(1)}, u32[]{:S(2)}, u32[]{:S(2)}) collective-permute-start(bf16[384,256]{1,0:T(8,128)(2,1)} %get-tuple-element.109), channel_id=1, source_target_pairs={{0,24},{4,28},{8,16},{12,20},{16,8},{20,12},{24,0},{28,4},{1,25},{... | collective-permute-start | bytes 589832 | tf_op jit(solution)/shard_map/ppermute | solution.py:524
  13.1 10.2 %collective-permute-start.3 = (bf16[384,256]{1,0:T(8,128)(2,1)}, bf16[384,256]{1,0:T(8,128)(2,1)S(1)}, u32[]{:S(2)}, u32[]{:S(2)}) collective-permute-start(bf16[384,256]{1,0:T(8,128)(2,1)} %get-tuple-element.109), channel_id=1, source_target_pairs={{0,16},{4,20},{8,24},{12,28},{16,0},{20,4},{24,8},{28,12},{1,17},{... | collective-permute-start | bytes 589832 | tf_op jit(solution)/shard_map/ppermute | solution.py:524
  17.7 24.7 %copy-start.9 = (bf16[128,1024]{1,0:T(8,128)(2,1)}, bf16[128,1024]{1,0:T(8,128)(2,1)S(1)}, u32[]{:S(2)}) copy-start(bf16[128,1024]{1,0:T(8,128)(2,1)S(1)} %collective-permute-done.refs_1_) | copy-start | bytes 786436
  23.4 2.4 %copy-start.12 = (bf16[1536,256]{1,0:T(8,128)(2,1)}, bf16[1536,256]{1,0:T(8,128)(2,1)S(1)}, u32[]{:S(2)}) copy-start(bf16[1536,256]{1,0:T(8,128)(2,1)S(1)} %constant_dynamic-update-slice_fusion.refs_0_) | copy-start | bytes 2359300
  23.4 2.4 %collective-permute-start.5 = (bf16[1536,256]{1,0:T(8,128)(2,1)S(1)}, bf16[1536,256]{1,0:T(8,128)(2,1)S(1)}, u32[]{:S(2)}, u32[]{:S(2)}) collective-permute-start(bf16[1536,256]{1,0:T(8,128)(2,1)S(1)} %constant_dynamic-update-slice_fusion.refs_0_), channel_id=1, source_target_pairs={{0,4},{4,0},{8,12},{12,8},{16,20},{20,16},{24,28},{28,24},{1,5},{5... | collective-permute-start | bytes 2359304 | tf_op jit(solution)/shard_map/ppermute | solution.py:524
  23.6 14.4 %collective-permute-start.1 = (bf16[2,128,1024]{2,1,0:T(8,128)(2,1)S(1)}, bf16[2,128,1024]{2,1,0:T(8,128)(2,1)S(1)}, u32[]{:S(2)}, u32[]{:S(2)}) collective-permute-start(bf16[2,128,1024]{2,1,0:T(8,128)(2,1)S(1)} %pad_maximum_fusion), channel_id=1, source_target_pairs={{0,1},{1,0},{2,3},{3,2},{4,5},{5,4},{6,7},{7,6},{8,9},{9,8},{10,11... | collective-permute-start | bytes 1572872 | tf_op jit(solution)/shard_map/ppermute | solution.py:524
  25.8 0.9 copy-start.15
  38.0 5.2 %collective-permute-start.6 = (bf16[2,128,1024]{2,1,0:T(8,128)(2,1)S(1)}, bf16[2,128,1024]{2,1,0:T(8,128)(2,1)S(1)}, u32[]{:S(2)}, u32[]{:S(2)}) collective-permute-start(bf16[2,128,1024]{2,1,0:T(8,128)(2,1)S(1)} %collective-permute-done.1), channel_id=1, source_target_pairs={{0,4},{4,0},{8,12},{12,8},{16,20},{20,16},{24,28},{28,24},{1,5},{5... | collective-permute-start | bytes 1572872 | tf_op jit(solution)/shard_map/ppermute | solution.py:524
  38.0 9.8 %collective-permute-start.10 = (bf16[384,256]{1,0:T(8,128)(2,1)}, bf16[384,256]{1,0:T(8,128)(2,1)S(1)}, u32[]{:S(2)}, u32[]{:S(2)}) collective-permute-start(bf16[384,256]{1,0:T(8,128)(2,1)} %get-tuple-element.110.refs_6_.refs_1_), channel_id=1, source_target_pairs={{0,3},{1,2},{2,1},{3,0},{4,7},{5,6},{6,5},{7,4},{8,11},{9,10},{10,... | collective-permute-start | bytes 589832 | tf_op jit(solution)/shard_map/ppermute | solution.py:524
  39.3 19.8 %collective-permute-start.9 = (bf16[384,256]{1,0:T(8,128)(2,1)}, bf16[384,256]{1,0:T(8,128)(2,1)S(1)}, u32[]{:S(2)}, u32[]{:S(2)}) collective-permute-start(bf16[384,256]{1,0:T(8,128)(2,1)} %get-tuple-element.110.refs_6_.refs_1_), channel_id=1, source_target_pairs={{0,2},{1,3},{2,0},{3,1},{4,6},{5,7},{6,4},{7,5},{8,10},{9,11},{10,... | collective-permute-start | bytes 589832 | tf_op jit(solution)/shard_map/ppermute | solution.py:524
  41.0 18.1 %collective-permute-start.8 = (bf16[384,256]{1,0:T(8,128)(2,1)}, bf16[384,256]{1,0:T(8,128)(2,1)S(1)}, u32[]{:S(2)}, u32[]{:S(2)}) collective-permute-start(bf16[384,256]{1,0:T(8,128)(2,1)} %get-tuple-element.110.refs_6_.refs_1_), channel_id=1, source_target_pairs={{0,1},{1,0},{2,3},{3,2},{4,5},{5,4},{6,7},{7,6},{8,9},{9,8},{10,11... | collective-permute-start | bytes 589832 | tf_op jit(solution)/shard_map/ppermute | solution.py:524
  42.4 16.8 %collective-permute-start.7 = (bf16[128,1024]{1,0:T(8,128)(2,1)S(1)}, bf16[128,1024]{1,0:T(8,128)(2,1)S(1)}, u32[]{:S(2)}, u32[]{:S(2)}) collective-permute-start(bf16[128,1024]{1,0:T(8,128)(2,1)S(1)} %collective-permute-done.refs_1_), channel_id=1, source_target_pairs={{0,4},{4,0},{8,12},{12,8},{16,20},{20,16},{24,28},{28,24},{1,5},{5... | collective-permute-start | bytes 786440 | tf_op jit(solution)/shard_map/ppermute | solution.py:524
  47.8 11.4 %copy-start.22 = (bf16[384,256]{1,0:T(8,128)(2,1)}, bf16[384,256]{1,0:T(8,128)(2,1)S(1)}, u32[]{:S(2)}) copy-start(bf16[384,256]{1,0:T(8,128)(2,1)S(1)} %collective-permute-done.10.refs_9_.refs_4_) | copy-start | bytes 589828
  75.9 12.8 %collective-permute-start.11 = (bf16[96,1024]{1,0:T(8,128)(2,1)}, bf16[96,1024]{1,0:T(8,128)(2,1)S(1)}, u32[]{:S(2)}, u32[]{:S(2)}) collective-permute-start(bf16[96,1024]{1,0:T(8,128)(2,1)} %get-tuple-element.121), channel_id=1, source_target_pairs={{0,1},{1,0},{2,3},{3,2},{4,5},{5,4},{6,7},{7,6},{8,9},{9,8},{10,11... | collective-permute-start | bytes 589832 | tf_op jit(solution)/shard_map/ppermute | solution.py:524
  76.0 17.4 %collective-permute-start.12 = (bf16[96,1024]{1,0:T(8,128)(2,1)}, bf16[96,1024]{1,0:T(8,128)(2,1)S(1)}, u32[]{:S(2)}, u32[]{:S(2)}) collective-permute-start(bf16[96,1024]{1,0:T(8,128)(2,1)} %get-tuple-element.122), channel_id=1, source_target_pairs={{0,2},{1,3},{2,0},{3,1},{4,6},{5,7},{6,4},{7,5},{8,10},{9,11},{10,... | collective-permute-start | bytes 589832 | tf_op jit(solution)/shard_map/ppermute | solution.py:524
  77.8 15.7 %collective-permute-start.13 = (bf16[96,1024]{1,0:T(8,128)(2,1)}, bf16[96,1024]{1,0:T(8,128)(2,1)S(1)}, u32[]{:S(2)}, u32[]{:S(2)}) collective-permute-start(bf16[96,1024]{1,0:T(8,128)(2,1)} %get-tuple-element.123), channel_id=1, source_target_pairs={{0,3},{1,2},{2,1},{3,0},{4,7},{5,6},{6,5},{7,4},{8,11},{9,10},{10,... | collective-permute-start | bytes 589832 | tf_op jit(solution)/shard_map/ppermute | solution.py:524
  88.7 23.9 %collective-permute-start.20 = (bf16[512,3456]{1,0:T(8,128)(2,1)}, bf16[512,3456]{1,0:T(8,128)(2,1)S(1)}, u32[]{:S(2)}, u32[]{:S(2)}) collective-permute-start(bf16[512,3456]{1,0:T(8,128)(2,1)} %get-tuple-element.136), channel_id=1, source_target_pairs={{0,4},{4,0},{8,12},{12,8},{16,20},{20,16},{24,28},{28,24},{1,5},{5... | collective-permute-start | bytes 10616840 | tf_op jit(solution)/shard_map/ppermute | solution.py:524
  88.7 4.7 %copy-start.34 = (bf16[96,1024]{1,0:T(8,128)(2,1)}, bf16[96,1024]{1,0:T(8,128)(2,1)S(1)}, u32[]{:S(2)}) copy-start(bf16[96,1024]{1,0:T(8,128)(2,1)S(1)} %collective-permute-done.11.refs_7_) | copy-start | bytes 589828
  97.9 10.2 %collective-permute-start.14 = (bf16[96,256]{1,0:T(8,128)(2,1)}, bf16[96,256]{1,0:T(8,128)(2,1)S(1)}, u32[]{:S(2)}, u32[]{:S(2)}) collective-permute-start(bf16[96,256]{1,0:T(8,128)(2,1)} %get-tuple-element.129), channel_id=1, source_target_pairs={{0,1},{1,0},{2,3},{3,2},{4,5},{5,4},{6,7},{7,6},{8,9},{9,8},{10,11... | collective-permute-start | bytes 147464 | tf_op jit(solution)/shard_map/ppermute | solution.py:524
  101.3 6.8 %collective-permute-start.15 = (bf16[96,256]{1,0:T(8,128)(2,1)}, bf16[96,256]{1,0:T(8,128)(2,1)S(1)}, u32[]{:S(2)}, u32[]{:S(2)}) collective-permute-start(bf16[96,256]{1,0:T(8,128)(2,1)} %get-tuple-element.130), channel_id=1, source_target_pairs={{0,2},{1,3},{2,0},{3,1},{4,6},{5,7},{6,4},{7,5},{8,10},{9,11},{10,... | collective-permute-start | bytes 147464 | tf_op jit(solution)/shard_map/ppermute | solution.py:524
  101.3 6.8 %collective-permute-start.16 = (bf16[96,256]{1,0:T(8,128)(2,1)}, bf16[96,256]{1,0:T(8,128)(2,1)S(1)}, u32[]{:S(2)}, u32[]{:S(2)}) collective-permute-start(bf16[96,256]{1,0:T(8,128)(2,1)} %get-tuple-element.131), channel_id=1, source_target_pairs={{0,3},{1,2},{2,1},{3,0},{4,7},{5,6},{6,5},{7,4},{8,11},{9,10},{10,... | collective-permute-start | bytes 147464 | tf_op jit(solution)/shard_map/ppermute | solution.py:524
  103.8 8.8 %copy-start = (bf16[512,3456]{1,0:T(8,128)(2,1)S(1)}, bf16[512,3456]{1,0:T(8,128)(2,1)}, u32[]{:S(2)}) copy-start(bf16[512,3456]{1,0:T(8,128)(2,1)} %get-tuple-element.158) | copy-start | bytes 10616836
  108.1 6.0 %copy-start.37 = (bf16[96,256]{1,0:T(8,128)(2,1)}, bf16[96,256]{1,0:T(8,128)(2,1)S(1)}, u32[]{:S(2)}) copy-start(bf16[96,256]{1,0:T(8,128)(2,1)S(1)} %collective-permute-done.14.refs_3_) | copy-start | bytes 147460
  108.1 6.0 %copy-start.38 = (bf16[96,256]{1,0:T(8,128)(2,1)}, bf16[96,256]{1,0:T(8,128)(2,1)S(1)}, u32[]{:S(2)}) copy-start(bf16[96,256]{1,0:T(8,128)(2,1)S(1)} %collective-permute-done.15.refs_4_) | copy-start | bytes 147460
  108.1 6.0 %copy-start.39 = (bf16[96,256]{1,0:T(8,128)(2,1)}, bf16[96,256]{1,0:T(8,128)(2,1)S(1)}, u32[]{:S(2)}) copy-start(bf16[96,256]{1,0:T(8,128)(2,1)S(1)} %collective-permute-done.16.refs_5_) | copy-start | bytes 147460
  108.1 13.9 %collective-permute-start.17 = (bf16[96,1280]{1,0:T(8,128)(2,1)}, bf16[96,1280]{1,0:T(8,128)(2,1)S(1)}, u32[]{:S(2)}, u32[]{:S(2)}) collective-permute-start(bf16[96,1280]{1,0:T(8,128)(2,1)} %get-tuple-element.133), channel_id=1, source_target_pairs={{0,1},{1,0},{2,3},{3,2},{4,5},{5,4},{6,7},{7,6},{8,9},{9,8},{10,11... | collective-permute-start | bytes 737288 | tf_op jit(solution)/shard_map/ppermute | solution.py:524
  109.2 19.4 %collective-permute-start.18 = (bf16[96,1280]{1,0:T(8,128)(2,1)}, bf16[96,1280]{1,0:T(8,128)(2,1)S(1)}, u32[]{:S(2)}, u32[]{:S(2)}) collective-permute-start(bf16[96,1280]{1,0:T(8,128)(2,1)} %get-tuple-element.134), channel_id=1, source_target_pairs={{0,2},{1,3},{2,0},{3,1},{4,6},{5,7},{6,4},{7,5},{8,10},{9,11},{10,... | collective-permute-start | bytes 737288 | tf_op jit(solution)/shard_map/ppermute | solution.py:524
  110.5 18.2 %collective-permute-start.19 = (bf16[96,1280]{1,0:T(8,128)(2,1)}, bf16[96,1280]{1,0:T(8,128)(2,1)S(1)}, u32[]{:S(2)}, u32[]{:S(2)}) collective-permute-start(bf16[96,1280]{1,0:T(8,128)(2,1)} %get-tuple-element.135), channel_id=1, source_target_pairs={{0,3},{1,2},{2,1},{3,0},{4,7},{5,6},{6,5},{7,4},{8,11},{9,10},{10,... | collective-permute-start | bytes 737288 | tf_op jit(solution)/shard_map/ppermute | solution.py:524
  112.6 2.4 %copy-start.2 = (bf16[512,3456]{1,0:T(8,128)(2,1)}, bf16[512,3456]{1,0:T(8,128)(2,1)S(1)}, u32[]{:S(2)}) copy-start(bf16[512,3456]{1,0:T(8,128)(2,1)S(1)} %collective-permute-done.20) | copy-start | bytes 10616836
  115.0 30.4 %collective-permute-start.28 = (bf16[256,3456]{1,0:T(8,128)(2,1)}, bf16[256,3456]{1,0:T(8,128)(2,1)}, u32[]{:S(2)}, u32[]{:S(2)}) collective-permute-start(bf16[256,3456]{1,0:T(8,128)(2,1)} %slice_add_fusion), channel_id=1, source_target_pairs={{0,8},{4,20},{8,0},{12,28},{16,24},{20,4},{24,16},{28,12},{1,9},{5... | collective-permute-start | bytes 5308424 | tf_op jit(solution)/shard_map/ppermute | solution.py:529
  122.0 6.7 %copy-start.19 = (bf16[96,1280]{1,0:T(8,128)(2,1)}, bf16[96,1280]{1,0:T(8,128)(2,1)S(1)}, u32[]{:S(2)}) copy-start(bf16[96,1280]{1,0:T(8,128)(2,1)S(1)} %collective-permute-done.17.refs_1_) | copy-start | bytes 737284
  128.7 6.5 %copy-start.6 = (bf16[1536,256]{1,0:T(8,128)(2,1)S(1)}, bf16[1536,256]{1,0:T(8,128)(2,1)}, u32[]{:S(2)}) copy-start(bf16[1536,256]{1,0:T(8,128)(2,1)} %get-tuple-element.147) | copy-start | bytes 2359300
  128.7 6.5 %collective-permute-start.22 = (bf16[1536,256]{1,0:T(8,128)(2,1)}, bf16[1536,256]{1,0:T(8,128)(2,1)S(1)}, u32[]{:S(2)}, u32[]{:S(2)}) collective-permute-start(bf16[1536,256]{1,0:T(8,128)(2,1)} %get-tuple-element.148), channel_id=1, source_target_pairs={{0,4},{4,0},{8,12},{12,8},{16,20},{20,16},{24,28},{28,24},{1,5},{5... | collective-permute-start | bytes 2359304 | tf_op jit(solution)/shard_map/ppermute | solution.py:524
  131.7 13.1 %collective-permute-start.21 = (bf16[96,1024]{1,0:T(8,128)(2,1)}, bf16[96,1024]{1,0:T(8,128)(2,1)S(1)}, u32[]{:S(2)}, u32[]{:S(2)}) collective-permute-start(bf16[96,1024]{1,0:T(8,128)(2,1)} %get-tuple-element.146.refs_0_), channel_id=1, source_target_pairs={{0,2},{1,3},{2,0},{3,1},{4,6},{5,7},{6,4},{7,5},{8,10},{9,11},{10,... | collective-permute-start | bytes 589832 | tf_op jit(solution)/shard_map/ppermute | solution.py:524
  136.0 12.1 %collective-permute-start.27 = (bf16[384,256]{1,0:T(8,128)(2,1)S(1)}, bf16[384,256]{1,0:T(8,128)(2,1)S(1)}, u32[]{:S(2)}, u32[]{:S(2)}) collective-permute-start(bf16[384,256]{1,0:T(8,128)(2,1)S(1)} %get-tuple-element.197), channel_id=1, source_target_pairs={{0,24},{4,28},{8,16},{12,20},{16,8},{20,12},{24,0},{28,4},{1,25},{... | collective-permute-start | bytes 589832 | tf_op jit(solution)/shard_map/ppermute | solution.py:524
  137.3 10.7 %collective-permute-start.26 = (bf16[384,256]{1,0:T(8,128)(2,1)S(1)}, bf16[384,256]{1,0:T(8,128)(2,1)S(1)}, u32[]{:S(2)}, u32[]{:S(2)}) collective-permute-start(bf16[384,256]{1,0:T(8,128)(2,1)S(1)} %get-tuple-element.198), channel_id=1, source_target_pairs={{0,16},{4,20},{8,24},{12,28},{16,0},{20,4},{24,8},{28,12},{1,17},{... | collective-permute-start | bytes 589832 | tf_op jit(solution)/shard_map/ppermute | solution.py:524
  138.9 9.2 %collective-permute-start.25 = (bf16[384,256]{1,0:T(8,128)(2,1)S(1)}, bf16[384,256]{1,0:T(8,128)(2,1)S(1)}, u32[]{:S(2)}, u32[]{:S(2)}) collective-permute-start(bf16[384,256]{1,0:T(8,128)(2,1)S(1)} %get-tuple-element.199), channel_id=1, source_target_pairs={{0,8},{4,12},{8,0},{12,4},{16,24},{20,28},{24,16},{28,20},{1,9},{5... | collective-permute-start | bytes 589832 | tf_op jit(solution)/shard_map/ppermute | solution.py:524
  139.5 5.3 %copy-start.4 = (bf16[96,1024]{1,0:T(8,128)(2,1)S(1)}, bf16[96,1024]{1,0:T(8,128)(2,1)}, u32[]{:S(2)}) copy-start(bf16[96,1024]{1,0:T(8,128)(2,1)} %get-tuple-element.146.refs_0_) | copy-start | bytes 589828
  139.5 5.9 %copy-start.1 = (bf16[512,3456]{1,0:T(8,128)(2,1)S(1)}, bf16[512,3456]{1,0:T(8,128)(2,1)}, u32[]{:S(2)}) copy-start(bf16[512,3456]{1,0:T(8,128)(2,1)} %get-tuple-element.158) | copy-start | bytes 10616836
  144.7 3.3 %collective-permute-start.24 = (bf16[512,512]{1,0:T(8,128)(2,1)}, bf16[512,512]{1,0:T(8,128)(2,1)S(1)}, u32[]{:S(2)}, u32[]{:S(2)}) collective-permute-start(bf16[512,512]{1,0:T(8,128)(2,1)} %get-tuple-element.156), channel_id=1, source_target_pairs={{0,4},{4,0},{8,12},{12,8},{16,20},{20,16},{24,28},{28,24},{1,5},{5... | collective-permute-start | bytes 1572872 | tf_op jit(solution)/shard_map/ppermute | solution.py:524
  148.1 6.2 %copy-start.16 = (bf16[512,512]{1,0:T(8,128)(2,1)}, bf16[512,512]{1,0:T(8,128)(2,1)S(1)}, u32[]{:S(2)}) copy-start(bf16[512,512]{1,0:T(8,128)(2,1)S(1)} %collective-permute-done.24.q_got_ref) | copy-start | bytes 1572868
  154.3 5.4 %collective-permute-start.29 = (bf16[512,384]{1,0:T(8,128)(2,1)}, bf16[512,384]{1,0:T(8,128)(2,1)S(1)}, u32[]{:S(2)}, u32[]{:S(2)}) collective-permute-start(bf16[512,384]{1,0:T(8,128)(2,1)} %get-tuple-element.165), channel_id=1, source_target_pairs={{0,4},{4,0},{8,12},{12,8},{16,20},{20,16},{24,28},{28,24},{1,5},{5... | collective-permute-start | bytes 1179656 | tf_op jit(solution)/shard_map/ppermute | solution.py:524
  154.4 39.0 %collective-permute-start.23 = (bf16[2,96,1024]{2,1,0:T(8,128)(2,1)S(1)}, bf16[2,96,1024]{2,1,0:T(8,128)(2,1)S(1)}, u32[]{:S(2)}, u32[]{:S(2)}) collective-permute-start(bf16[2,96,1024]{2,1,0:T(8,128)(2,1)S(1)} %pad_maximum_fusion.1), channel_id=1, source_target_pairs={{0,1},{1,0},{2,3},{3,2},{4,5},{5,4},{6,7},{7,6},{8,9},{9,8},{10,11... | collective-permute-start | bytes 1179656 | tf_op jit(solution)/shard_map/ppermute | solution.py:524
  155.3 20.4 %collective-permute-start.31 = (bf16[96,1024]{1,0:T(8,128)(2,1)}, bf16[96,1024]{1,0:T(8,128)(2,1)S(1)}, u32[]{:S(2)}, u32[]{:S(2)}) collective-permute-start(bf16[96,1024]{1,0:T(8,128)(2,1)} %get-tuple-element.171), channel_id=1, source_target_pairs={{0,1},{1,0},{2,3},{3,2},{4,5},{5,4},{6,7},{7,6},{8,9},{9,8},{10,11... | collective-permute-start | bytes 589832 | tf_op jit(solution)/shard_map/ppermute | solution.py:524
  156.5 20.0 %collective-permute-start.32 = (bf16[96,1024]{1,0:T(8,128)(2,1)}, bf16[96,1024]{1,0:T(8,128)(2,1)S(1)}, u32[]{:S(2)}, u32[]{:S(2)}) collective-permute-start(bf16[96,1024]{1,0:T(8,128)(2,1)} %get-tuple-element.172), channel_id=1, source_target_pairs={{0,2},{1,3},{2,0},{3,1},{4,6},{5,7},{6,4},{7,5},{8,10},{9,11},{10,... | collective-permute-start | bytes 589832 | tf_op jit(solution)/shard_map/ppermute | solution.py:524
  158.3 21.5 %collective-permute-start.33 = (bf16[96,1024]{1,0:T(8,128)(2,1)}, bf16[96,1024]{1,0:T(8,128)(2,1)S(1)}, u32[]{:S(2)}, u32[]{:S(2)}) collective-permute-start(bf16[96,1024]{1,0:T(8,128)(2,1)} %get-tuple-element.173), channel_id=1, source_target_pairs={{0,3},{1,2},{2,1},{3,0},{4,7},{5,6},{6,5},{7,4},{8,11},{9,10},{10,... | collective-permute-start | bytes 589832 | tf_op jit(solution)/shard_map/ppermute | solution.py:524
  163.1 8.7 %collective-permute-start.30 = (bf16[256,896]{1,0:T(8,128)(2,1)}, bf16[256,896]{1,0:T(8,128)(2,1)S(1)}, u32[]{:S(2)}, u32[]{:S(2)}) collective-permute-start(bf16[256,896]{1,0:T(8,128)(2,1)} %get-tuple-element.167), channel_id=1, source_target_pairs={{0,8},{4,20},{8,0},{12,28},{16,24},{20,4},{24,16},{28,12},{1,9},{5... | collective-permute-start | bytes 1376264 | tf_op jit(solution)/shard_map/ppermute | solution.py:529
  171.8 1.8 copy-start.8
  171.8 31.3 %collective-permute-start.34 = (bf16[128,3456]{1,0:T(8,128)(2,1)S(1)}, bf16[128,3456]{1,0:T(8,128)(2,1)S(1)}, u32[]{:S(2)}, u32[]{:S(2)}) collective-permute-start(bf16[128,3456]{1,0:T(8,128)(2,1)S(1)} %get-tuple-element.176), channel_id=1, source_target_pairs={{0,16},{4,12},{8,24},{12,4},{16,0},{20,28},{24,8},{28,20},{1,17},{... | collective-permute-start | bytes 2654216 | tf_op jit(solution)/shard_map/ppermute | solution.py:529
  175.7 4.1 %copy-start.31 = (bf16[96,1024]{1,0:T(8,128)(2,1)}, bf16[96,1024]{1,0:T(8,128)(2,1)S(1)}, u32[]{:S(2)}) copy-start(bf16[96,1024]{1,0:T(8,128)(2,1)S(1)} %collective-permute-done.31.refs_1_) | copy-start | bytes 589828
  175.7 11.6 %collective-permute-start.35 = (bf16[128,896]{1,0:T(8,128)(2,1)}, bf16[128,896]{1,0:T(8,128)(2,1)S(1)}, u32[]{:S(2)}, u32[]{:S(2)}) collective-permute-start(bf16[128,896]{1,0:T(8,128)(2,1)} %get-tuple-element.179), channel_id=1, source_target_pairs={{0,16},{4,12},{8,24},{12,4},{16,0},{20,28},{24,8},{28,20},{1,17},{... | collective-permute-start | bytes 688136 | tf_op jit(solution)/shard_map/ppermute | solution.py:529
  176.5 3.3 %copy-start.32 = (bf16[96,1024]{1,0:T(8,128)(2,1)}, bf16[96,1024]{1,0:T(8,128)(2,1)S(1)}, u32[]{:S(2)}) copy-start(bf16[96,1024]{1,0:T(8,128)(2,1)S(1)} %collective-permute-done.32.refs_2_) | copy-start | bytes 589828
  182.9 6.9 %collective-permute-start.36 = (bf16[96,1024]{1,0:T(8,128)(2,1)}, bf16[96,1024]{1,0:T(8,128)(2,1)S(1)}, u32[]{:S(2)}, u32[]{:S(2)}) collective-permute-start(bf16[96,1024]{1,0:T(8,128)(2,1)} %shard_map.251.refs_0_), channel_id=1, source_target_pairs={{0,1},{1,0},{2,3},{3,2},{4,5},{5,4},{6,7},{7,6},{8,9},{9,8},{10,11... | collective-permute-start | bytes 589832 | tf_op jit(solution)/shard_map/ppermute | solution.py:524
  189.9 25.2 %copy-start.25 = (bf16[96,1024]{1,0:T(8,128)(2,1)}, bf16[96,1024]{1,0:T(8,128)(2,1)S(1)}, u32[]{:S(2)}) copy-start(bf16[96,1024]{1,0:T(8,128)(2,1)S(1)} %collective-permute-done.36.refs_1_) | copy-start | bytes 589828
  189.9 5.0 %collective-permute-start.37 = (f32[8,128]{1,0:T(8,128)}, f32[8,128]{1,0:T(8,128)S(1)}, u32[]{:S(2)}, u32[]{:S(2)}) collective-permute-start(f32[8,128]{1,0:T(8,128)} %get-tuple-element.182), channel_id=1, source_target_pairs={{0,1},{1,0},{2,3},{3,2},{4,5},{5,4},{6,7},{7,6},{8,9},{9,8},{10,11... | collective-permute-start | bytes 12296 | tf_op jit(solution)/shard_map/ppermute | solution.py:524
  190.8 24.2 %collective-permute-start.41 = (bf16[96,1024]{1,0:T(8,128)(2,1)}, bf16[96,1024]{1,0:T(8,128)(2,1)S(1)}, u32[]{:S(2)}, u32[]{:S(2)}) collective-permute-start(bf16[96,1024]{1,0:T(8,128)(2,1)} %shard_map.251.refs_0_), channel_id=1, source_target_pairs={{0,3},{1,2},{2,1},{3,0},{4,7},{5,6},{6,5},{7,4},{8,11},{9,10},{10,... | collective-permute-start | bytes 589832 | tf_op jit(solution)/shard_map/ppermute | solution.py:524
  192.6 22.4 %collective-permute-start.40 = (bf16[96,1024]{1,0:T(8,128)(2,1)}, bf16[96,1024]{1,0:T(8,128)(2,1)S(1)}, u32[]{:S(2)}, u32[]{:S(2)}) collective-permute-start(bf16[96,1024]{1,0:T(8,128)(2,1)} %shard_map.251.refs_0_), channel_id=1, source_target_pairs={{0,2},{1,3},{2,0},{3,1},{4,6},{5,7},{6,4},{7,5},{8,10},{9,11},{10,... | collective-permute-start | bytes 589832 | tf_op jit(solution)/shard_map/ppermute | solution.py:524
  193.4 18.8 %collective-permute-start.39 = (bf16[256,128]{1,0:T(8,128)(2,1)}, bf16[256,128]{1,0:T(8,128)(2,1)S(1)}, u32[]{:S(2)}, u32[]{:S(2)}) collective-permute-start(bf16[256,128]{1,0:T(8,128)(2,1)} %get-tuple-element.183), channel_id=1, source_target_pairs={{0,0},{1,8},{2,16},{3,24},{4,4},{5,12},{6,20},{7,28},{8,1},{9,9},{... | collective-permute-start | bytes 196616 | tf_op jit(solution)/shard_map/ppermute | solution.py:796
  195.6 16.6 %copy-start.13 = (f32[8,128]{1,0:T(8,128)}, f32[8,128]{1,0:T(8,128)S(1)}, u32[]{:S(2)}) copy-start(f32[8,128]{1,0:T(8,128)S(1)} %add.40.a_ref) | copy-start | bytes 12292
  195.6 16.6 %collective-permute-start.38 = (f32[8,128]{1,0:T(8,128)S(1)}, f32[8,128]{1,0:T(8,128)S(1)}, u32[]{:S(2)}, u32[]{:S(2)}) collective-permute-start(f32[8,128]{1,0:T(8,128)S(1)} %add.40.a_ref), channel_id=1, source_target_pairs={{0,2},{1,3},{2,0},{3,1},{4,6},{5,7},{6,4},{7,5},{8,10},{9,11},{10,... | collective-permute-start | bytes 12296 | tf_op jit(solution)/shard_map/ppermute | solution.py:524
  203.1 0.9 copy-start.3
  (18 other events, 12.9 us)

commit v3 on v2

--- a/solution.py
+++ b/solution.py
@@ -17,7 +17,7 @@
 TN = (((0,), (0,)), ((), ()))
 VMEM = pl.BlockSpec(memory_space=pltpu.VMEM)
 SMEM = pl.BlockSpec(memory_space=pltpu.SMEM)
-vmem_limit = 56 * 1024 * 1024
+megabyte = 1024 * 1024
 work = 5 * 10**10
 
 
@@ -25,7 +25,7 @@
     return lax.dot_general(left, right, dims, preferred_element_type=f32)
 
 
-def call(body, inputs, outs, scratch=(), work=work, **kwargs):
+def call(body, inputs, outs, scratch=(), work=work, limit=18, **kwargs):
     in_specs = kwargs.pop("in_specs", None)
     if in_specs is None:
         in_specs = [
@@ -41,7 +41,7 @@
         in_specs=in_specs,
         out_specs=out_specs,
         scratch_shapes=list(scratch),
-        compiler_params=pltpu.CompilerParams(vmem_limit_bytes=vmem_limit),
+        compiler_params=pltpu.CompilerParams(vmem_limit_bytes=limit * megabyte),
         cost_estimate=pl.CostEstimate(flops=work, bytes_accessed=moved, transcendentals=0),
         **kwargs,
     )(*inputs)
@@ -93,6 +93,26 @@
 def quarter(partner, size):
     place = jnp.bitwise_xor(lax.axis_index("tp"), partner)
     return pl.ds(pl.multiple_of(place * size, size), size)
+
+
+def around(refs):
+    return [
+        refs[0][...],
+        refs[1][...],
+        jnp.concatenate([refs[2][...], refs[3][...]], axis=0),
+        refs[4][...],
+    ]
+
+
+def store_around(acc_ref, refs):
+    own = refs[0].shape[0]
+    half = own // 2
+    refs[0][...] = acc_ref[quarter(0, own), :].astype(bf16)
+    refs[1][...] = acc_ref[quarter(1, own), :].astype(bf16)
+    far = acc_ref[quarter(2, own), :].astype(bf16)
+    refs[2][...] = far[:half]
+    refs[3][...] = far[half:]
+    refs[4][...] = acc_ref[quarter(3, own), :].astype(bf16)
 
 
 def row_norm(x):
@@ -257,22 +277,23 @@
     )
 
 
-def mix_kernel(n_tp, x_ref, gain_ref, w0_ref, *refs):
-    wm_refs, wp_refs, o_refs = refs[: n_tp - 1], refs[n_tp - 1 : 2 * n_tp - 2], refs[2 * n_tp - 2 : 3 * n_tp - 2]
-    h_ref, y_ref, acc_ref = refs[3 * n_tp - 2 :]
-    acc = x_ref[...].astype(f32) + dot(o_refs[0][...], w0_ref[...])
-    first, second = core_halves(w0_ref.shape[0] // 2)
-    for k in range(1, n_tp):
-        acc += dot(o_refs[k][:, first], wm_refs[k - 1][...])
-        acc += dot(o_refs[k][:, second], wp_refs[k - 1][...])
+def mix_kernel(x_ref, gain_ref, w0_ref, wm_ref, wp_ref, *refs):
+    parts = around(refs[:5])
+    h_ref, y_ref, acc_ref = refs[5:]
+    acc = x_ref[...].astype(f32) + dot(parts[0], w0_ref[...])
+    core = lax.axis_index("ctx") % 2
+    half = w0_ref.shape[0] // 2
+    for k in range(1, 4):
+        low, high = parts[k][:, :half], parts[k][:, half:]
+        acc += dot(jnp.where(core == 0, low, high), wm_ref[k - 1])
+        acc += dot(jnp.where(core == 0, high, low), wp_ref[k - 1])
     acc_ref[...] = acc
     y_ref[...] = acc_ref[quarter(0, y_ref.shape[0]), :]
     h_ref[...] = (acc * row_norm(acc) * gain_ref[...]).astype(bf16)
 
 
-def feed_kernel(n_tp, h_ref, g_ref, wg_ref, wu_ref, wd_ref, act_ref, dg_ref, du_ref, *refs):
-    dh_refs, acc_ref = refs[:n_tp], refs[n_tp]
-    step = pl.program_id(0)
+def feed_kernel(h_ref, g_ref, wg_ref, wu_ref, wd_ref, act_ref, dg_ref, du_ref, *refs):
+    dh_refs, acc_ref = refs[:5], refs[5]
     gate = dot(h_ref[...], wg_ref[...])
     up = dot(h_ref[...], wu_ref[...])
     dact = dot(g_ref[...], wd_ref[...], NT)
@@ -283,30 +304,23 @@
     dup = (dact * silu).astype(bf16)
     dg_ref[...] = dgate
     du_ref[...] = dup
-    total = dot(dgate, wg_ref[...], NT) + dot(dup, wu_ref[...], NT)
-
-    @pl.when(step == 0)
-    def _():
-        acc_ref[...] = total
-
-    @pl.when(step > 0)
-    def _():
-        acc_ref[...] += total
-
-    @pl.when(step == pl.num_programs(0) - 1)
-    def _():
-        for k in range(n_tp):
-            dh_refs[k][...] = acc_ref[quarter(k, dh_refs[k].shape[0]), :].astype(bf16)
-
-
-def mid_kernel(n_tp, g_ref, y_ref, gain_ref, w0_ref, *refs):
-    wm_refs, wp_refs, refs = refs[: n_tp - 1], refs[n_tp - 1 : 2 * n_tp - 2], refs[2 * n_tp - 2 :]
-    dh_refs, refs = refs[:n_tp], refs[n_tp:]
+    acc_ref[...] = dot(dgate, wg_ref[...], NT) + dot(dup, wu_ref[...], NT)
+    store_around(acc_ref, dh_refs)
+
+
+def reduce_kernel(one_ref, three_ref, got_one_ref, got_three_ref, to_one_ref, to_three_ref):
+    half = got_one_ref.shape[0]
+    to_one_ref[:half, :] = one_ref[:half, :]
+    to_one_ref[half:, :] = (one_ref[half:, :].astype(f32) + got_three_ref[...].astype(f32)).astype(bf16)
+    to_three_ref[:half, :] = (three_ref[:half, :].astype(f32) + got_one_ref[...].astype(f32)).astype(bf16)
+    to_three_ref[half:, :] = three_ref[half:, :]
+
+
+def mid_kernel(g_ref, y_ref, gain_ref, w0_ref, wm_ref, wp_ref, *refs):
+    dh_refs, refs = refs[:3], refs[3:]
     dy_ref, dattn_ref, gaing_ref = refs[:3]
     dout_refs = refs[3:]
-    dh = dh_refs[0][...].astype(f32)
-    for k in range(1, n_tp):
-        dh += dh_refs[k][...].astype(f32)
+    dh = sum(ref[...].astype(f32) for ref in dh_refs)
     y = y_ref[...]
     inverse = row_norm(y)
     z = y * inverse
@@ -319,9 +333,9 @@
     dattn_ref[...] = low
     dout_refs[0][...] = dot(low, w0_ref[...], NT).astype(bf16)
     first, second = core_halves(w0_ref.shape[0] // 2)
-    for k in range(1, n_tp):
-        dout_refs[k][:, first] = dot(low, wm_refs[k - 1][...], NT).astype(bf16)
-        dout_refs[k][:, second] = dot(low, wp_refs[k - 1][...], NT).astype(bf16)
+    for k in range(1, 4):
+        dout_refs[k][:, first] = dot(low, wm_ref[k - 1], NT).astype(bf16)
+        dout_refs[k][:, second] = dot(low, wp_ref[k - 1], NT).astype(bf16)
 
 
 def down_kernel(n_tp, act_ref, wd_ref, dattn_ref, *refs):
@@ -343,9 +357,9 @@
     out_ref[...] = total.astype(bf16)
 
 
-def q_back_kernel(near, n_tp, dq_ref, qpre_ref, cos_ref, sin_ref, qgain_ref, wq_ref, h_ref, *refs):
-    if near:
-        dattn_ref, o_refs, refs = refs[0], refs[1 : 1 + n_tp], refs[1 + n_tp :]
+def q_back_kernel(near, dq_ref, qpre_ref, cos_ref, sin_ref, qgain_ref, wq_ref, h_ref, *refs):
+    if near:
+        dattn_ref, parts, refs = refs[0], around(refs[1:6]), refs[6:]
         odd_ref, even_ref, hp_ref, oall_ref = refs[3:]
     low_ref, gaing_ref, dh_ref = refs[:3]
     total = jnp.zeros((1, 128), f32)
@@ -360,8 +374,8 @@
     dh_ref[...] = dot(low_ref[...], wq_ref[...], NT)
     if near:
         mine, place = lax.axis_index("ctx"), lax.axis_index("tp")
-        for k in range(n_tp):
-            oall_ref[k] = o_refs[k][...]
+        for k, part in enumerate(parts):
+            oall_ref[k] = part
         for parity, out_ref in ((1, odd_ref), (0, even_ref)):
             gather_columns(parity, h_ref, hp_ref)
             out_ref[:, :256] = dot(hp_ref[...], low_ref[...], TN).astype(bf16)
@@ -371,11 +385,11 @@
                 out_ref[128 * at : 128 * at + 128, 256:] = dot(left, oall_ref[heads]).astype(bf16)
 
 
-def k_back_kernel(near, n_tp, n_parts, *refs):
+def k_back_kernel(near, n_parts, *refs):
     parts, refs = refs[:n_parts], refs[n_parts:]
     kpre_ref, cos_ref, sin_ref, kgain_ref, wk_ref, wv_ref, dhq_ref, x_ref, gain2_ref, qg_ref, h_ref = refs[:11]
     low_ref, gains_ref = refs[11:13]
-    dh_refs, refs = refs[13 : 13 + n_tp], refs[13 + n_tp :]
+    dh_refs, refs = refs[13:18], refs[18:]
     acc_ref = refs[-1]
     total = parts[0][...].astype(f32)
     for part in parts[1:]:
@@ -390,8 +404,7 @@
     low_ref[:, 128:] = dv
     dh = dhq_ref[...] + dot(dk, wk_ref[...], NT) + dot(dv, wv_ref[...], NT)
     acc_ref[...] = dh
-    for k in range(n_tp):
-        dh_refs[k][...] = acc_ref[quarter(k, dh_refs[k].shape[0]), :].astype(bf16)
+    store_around(acc_ref, dh_refs)
     x_in = x_ref[...].astype(f32)
     width = x_in.shape[1]
     lots = width // 128
@@ -414,11 +427,9 @@
                 out_ref[128 * at : 128 * at + 128, 256:] = parted(gain_columns(gains_ref, block, lots))
 
 
-def last_kernel(n_tp, x_ref, dy_ref, gain_ref, *refs):
-    dh_refs, out_ref = refs[:n_tp], refs[n_tp]
-    dh = dh_refs[0][...].astype(f32)
-    for k in range(1, n_tp):
-        dh += dh_refs[k][...].astype(f32)
+def last_kernel(x_ref, dy_ref, gain_ref, *refs):
+    dh_refs, out_ref = refs[:3], refs[3]
+    dh = sum(ref[...].astype(f32) for ref in dh_refs)
     x = x_ref[quarter(0, dy_ref.shape[0]), :].astype(f32)
     inverse = row_norm(x)
     z = x * inverse
@@ -427,10 +438,10 @@
     out_ref[...] = (dy_ref[...] + inverse * (e - z * inner)).astype(bf16)
 
 
-def join_kernel(n_tp, *refs):
-    out_ref = refs[n_tp]
-    for k in range(n_tp):
-        out_ref[quarter(k, refs[k].shape[0]), :] = refs[k][...].astype(out_ref.dtype)
+def join_kernel(*refs):
+    out_ref = refs[5]
+    for k, part in enumerate(around(refs[:5])):
+        out_ref[quarter(k, part.shape[0]), :] = part.astype(out_ref.dtype)
 
 
 def block_order(parity):
@@ -567,6 +578,27 @@
     def exchange(parts):
         return [parts[0]] + [swap(parts[k], "tp", k) for k in others]
 
+    def gather(x, *first):
+        one, three = swap(x, "tp", 1), swap(x, "tp", 3)
+        half = x.shape[0] // 2
+        near_one, near_three = lax.optimization_barrier((one, three, *first))[:2] if first else (one, three)
+        return [x, one, swap(near_three[:half], "tp", 1), swap(near_one[half:], "tp", 3), three]
+
+    def reduce(parts, *first):
+        here, one, far_low, far_high, three = parts
+        got_one, got_three = swap(far_low, "tp", 1), swap(far_high, "tp", 3)
+        if first:
+            one = after(one, *first)
+        to_one, to_three = call(
+            reduce_kernel,
+            [one, three, got_one, got_three],
+            [shape(one.shape, bf16)] * 2,
+            work=1,
+        )
+        return [here, swap(to_one, "tp", 1), swap(to_three, "tp", 3)], to_one
+
+    quarters = [shape((own, width), bf16)] * 2 + [shape((own // 2, width), bf16)] * 2 + [shape((own, width), bf16)]
+
     h_one, kv, key_pre, cosine, sine = call(
         kv_kernel,
         [doc_starts, hidden_in, gain_one, w_key, w_value, frequency, k_gain],
@@ -577,6 +609,7 @@
             shape((rows, 128), f32),
             shape((rows, 128), f32),
         ],
+        limit=56,
     )
     if near:
         kv_got = [swap(kv, "ctx", 2 * i) for i in chips]
@@ -584,16 +617,14 @@
         kv_all = [lax.all_gather(kv, "ctx", axis=0, tiled=True)]
     half = w_out.shape[0] // 2
     w_half = lax.dynamic_slice_in_dim(w_out, (mine % 2) * half, half, 0)
-    w_two = swap(w_half, "tp", 2)
+    w_around = gather(w_half)
     qpad, query_pre = call(
         q_kernel,
         [h_one, w_query, cosine, sine, q_gain],
         [shape((4 * rows, 128), bf16), shape((rows, 256), f32)],
-        work=1,
-    )
-    w_rest = swap(jnp.stack([w_half, w_two]), "tp", 1)
-    if near:
-        even = jnp.concatenate([after(kv, qpad, w_two), *kv_got], axis=0)
+    )
+    if near:
+        even = jnp.concatenate([after(kv, qpad, w_around[1], w_around[4]), *kv_got], axis=0)
         kv_all = [even, swap(even, "ctx", 1)]
     attended, attended32, log_mass = call(
         functools.partial(attend_kernel, near, scale),
@@ -601,38 +632,26 @@
         [shape((rows, 256), bf16), shape((rows, 256), f32), shape((2, 2 * rows), f32)],
         [pltpu.VMEM((2, 128, 2 * rows), f32), pltpu.VMEM((2, 2 * rows), f32)],
     )
-    o_parts = exchange([attended] * n_tp)
-    w_two, w_rest = lax.optimization_barrier((w_two, w_rest, attended))[:2]
-    w_two_pair, w_rest_pair = swap(w_two, "ctx", 1), swap(w_rest, "ctx", 1)
-    w_all = [w_rest[0], w_two, w_rest[1], w_rest_pair[0], w_two_pair, w_rest_pair[1]]
+    o_parts = gather(attended)
+    w_around = lax.optimization_barrier((*w_around, attended))[:5]
+    w_mine = jnp.stack([w_around[1], jnp.concatenate(w_around[2:4], axis=0), w_around[4]])
+    w_all = [w_mine, swap(w_mine, "ctx", 1)]
     h_two, mixed_own = call(
-        functools.partial(mix_kernel, n_tp),
+        mix_kernel,
         [hidden_in, gain_two, w_out, *w_all, *o_parts],
         [shape((rows, width), bf16), shape((own, width), f32)],
         [pltpu.VMEM((rows, width), f32)],
     )
 
-    cut = 384 if units % 384 == 0 else 128
-    whole = lambda *dims: pl.BlockSpec(dims, lambda i: (0,) * len(dims))
-    across = pl.BlockSpec((width, cut), lambda i: (0, i))
-    part = pl.BlockSpec((rows, cut), lambda i: (0, i))
     got = call(
-        functools.partial(feed_kernel, n_tp),
+        feed_kernel,
         [h_two, out_grad, w_gate, w_up, w_down],
-        [shape((rows, units), bf16)] * 3 + [shape((own, width), bf16)] * n_tp,
+        [shape((rows, units), bf16)] * 3 + quarters,
         [pltpu.VMEM((rows, width), f32)],
-        grid=(units // cut,),
-        in_specs=[
-            whole(rows, width),
-            whole(rows, width),
-            across,
-            across,
-            pl.BlockSpec((cut, width), lambda i: (i, 0)),
-        ],
-        out_specs=[part, part, part] + [whole(own, width)] * n_tp,
+        limit=24,
     )
     act, gate_grad, up_grad = got[:3]
-    two_got = exchange(got[3:])
+    two_parts = got[3:]
     block = width // n_ctx
     if near:
         ordered = pltpu.VMEM((rows, 4 * block), bf16)
@@ -642,9 +661,9 @@
             [shape((4 * block, 3 * units), bf16)] * 2,
             [ordered, ordered],
         )
-        mixed_own = after(mixed_own, feed_even)
+    two_got, _ = reduce(two_parts, *([feed_even] if near else []))
     got = call(
-        functools.partial(mid_kernel, n_tp),
+        mid_kernel,
         [out_grad, mixed_own, gain_two, w_out, *w_all, *two_got],
         [shape((own, width), f32), shape((own, width), bf16), shape((1, width), f32)]
         + [shape((own, 256), bf16)] * n_tp,
@@ -663,7 +682,7 @@
         feed_other = swap(feed_odd, "ctx", 1)
         feed_send = feed_even[half:] + feed_other[half:]
         feed_got = swap_across(feed_send, 0)
-        qpad = after(qpad, feed_send)
+        qpad = after(qpad, feed_send, down[1])
     down_got = exchange(list(lax.optimization_barrier((*down, *dout[1:]))[:n_tp]))
 
     got = call(
@@ -678,7 +697,7 @@
     )
     query_low, dkv = got[0], got[1:]
     if near:
-        other = swap(dkv[1], "ctx", 1)
+        other = swap(after(dkv[1], *down_got[1:]), "ctx", 1)
         pieces = [
             dkv[0][i * rows : (i + 1) * rows] + other[i * rows : (i + 1) * rows] for i in range(n_ctx // 2)
         ]
@@ -690,8 +709,9 @@
         functools.partial(layer_kernel, n_tp),
         [mixed_own, *down_got],
         [shape((own, width), bf16), shape((rows, width // n_tp), bf16)],
-    )
-    layer_two = swap(layer_own, "tp", 2)
+        work=1,
+    )
+    layer_one, layer_three = swap(layer_own, "tp", 1), swap(layer_own, "tp", 3)
 
     if near:
         feed_parts = lax.optimization_barrier((feed_even, feed_other, feed_got, query_low))[:3]
@@ -699,16 +719,15 @@
         query_low = after(query_low, *pieces)
     more = [attn_grad_cut, *o_parts] if near else []
     got = call(
-        functools.partial(q_back_kernel, near, n_tp),
+        functools.partial(q_back_kernel, near),
         [query_low, query_pre, cosine, sine, q_gain, w_query, h_one, *more],
         [shape((rows, 256), bf16), shape((1, 128), f32), shape((rows, width), f32)]
         + ([shape((4 * block, 512), bf16)] * 2 if near else []),
         [ordered, pltpu.VMEM((n_tp, rows, 256), bf16)] if near else [],
+        work=1,
     )
     query_pre_low, q_gain_part, one_query = got[:3]
-    layer_pair = jnp.stack([layer_own, after(layer_two, one_query)])
-    layer_rest = swap(layer_pair, "tp", 1)
-    done = [layer_pair, feed_here] if near else [layer_pair]
+    done = [layer_one, layer_three, feed_here] if near else [layer_one, layer_three]
     if near:
         q_odd, q_even = got[3:]
         q_other = swap(q_odd, "ctx", 1)
@@ -716,7 +735,7 @@
     lots = width // 128
     gain_rows = 2 * lots + 8
     got = call(
-        functools.partial(k_back_kernel, near, n_tp, len(kv_parts)),
+        functools.partial(k_back_kernel, near, len(kv_parts)),
         [
             *kv_parts,
             after(key_pre, *done),
@@ -732,19 +751,21 @@
             h_one,
         ],
         [shape((rows, 256), bf16), shape((gain_rows, 128), f32)]
-        + [shape((own, width), bf16)] * n_tp
+        + quarters
         + ([shape((4 * block, 384), bf16)] * 2 if near else []),
         ([ordered] if near else []) + [pltpu.VMEM((rows, width), f32)],
     )
     kv_pre_low, gains = got[:2]
-    one_parts = got[2 : 2 + n_tp]
-    one_got = exchange(one_parts)
-    if near:
-        kv_odd, kv_even = got[2 + n_tp :]
+    one_parts = got[2:7]
+    one_got, token = reduce(one_parts)
+    if near:
+        kv_odd, kv_even = got[7:]
+        kv_odd = after(kv_odd, token)
         attn_here, attn_send = call(
             attn_grad_chip_kernel,
             [q_even, q_other, kv_even, swap(kv_odd, "ctx", 1)],
             [shape((2 * block, 896), bf16)] * 2,
+            work=1,
         )
         attn_here, attn_send = call(
             attn_grad_pass_kernel,
@@ -753,16 +774,26 @@
             work=1,
         )
         mixed_grad = after(mixed_grad, attn_here)
+    far_one, far_three, _ = lax.optimization_barrier((layer_one, layer_three, token))
+    half = own // 2
+    layer_parts = [
+        layer_own,
+        layer_one,
+        swap(far_three[:half], "tp", 1),
+        swap(far_one[half:], "tp", 3),
+        layer_three,
+    ]
+    mixed_grad = after(mixed_grad, *layer_parts[2:4])
     input_own = call(
-        functools.partial(last_kernel, n_tp),
+        last_kernel,
         [hidden_in, mixed_grad, gain_one, *one_got],
         [shape((own, width), bf16)],
     )[0]
-    input_parts = exchange([input_own] * n_tp)
-    layer_rest = after(layer_rest, input_own)
+    input_parts = gather(input_own)
+    layer_parts[4] = after(layer_parts[4], input_own)
     layer_out = call(
-        functools.partial(join_kernel, n_tp),
-        [layer_own, layer_rest[0], layer_two, layer_rest[1]],
+        join_kernel,
+        layer_parts,
         [shape((rows, width), bf16)],
         work=1,
     )[0]
@@ -777,7 +808,7 @@
         )
         query_w, key_w, value_w, out_w, gains = call(
             attn_grad_sum_kernel,
-            [after(attn_here, input_own), swap_across(attn_send, 1)],
+            [after(attn_here, input_parts[1]), swap_across(attn_send, 1)],
             [
                 shape((block, 256), f32),
                 shape((block, 128), f32),
@@ -787,7 +818,6 @@
             ],
             work=1,
         )
-        out_w, gains = lax.optimization_barrier((out_w, gains, input_parts[1]))[:2]
         turn = []
         for a in range(n_tp):
             for b in range(2):
@@ -820,13 +850,13 @@
     gains = gains + swap(gains, "tp", 1)
     gain_one_sum, gain_two_sum, q_gain_sum, k_gain_sum, out_w = call(
         functools.partial(gain_kernel, block),
-        [gains, swap(gains, "tp", 2), out_w],
+        [gains, swap(gains, "tp", 3), out_w],
         [shape((1, block), f32)] * 2 + [shape((1, 64), f32)] * 2 + [shape(out_w.shape, f32)],
         work=1,
     )
     input_parts[0] = after(input_parts[0], gate_w, layer_out, out_w)
     input_grad = call(
-        functools.partial(join_kernel, n_tp), input_parts, [shape((rows, width), f32)]
+        join_kernel, input_parts, [shape((rows, width), f32)]
     )[0]
 
     return (

time: 220 us -> 185 us (0.84)
  Pallas kernels: 79.5 us -> 35.8 us
  starting transfers between devices: 56.5 us -> 69.1 us
  waiting for transfers between devices: 58.9 us -> 70.7 us
  local copies, waits for them, and re-layouts: 16.6 us -> 6.52 us
  other arithmetic: 6.31 us -> 1.67 us
    pallas_call x20 -> x22, Pallas kernels: 79.5 us -> 35.8 us  [call(): pl.pallas_call(body, out_shape=outs, in_specs=in_specs, out_specs=out_spe...]
    ppermute x37 -> x44, waiting for transfers between devices: 48.6 us -> 63.4 us  [swap(): return lax.ppermute(x, axis, [(i, i ^ k) for i in range(size)])]
    ppermute x37 -> x44, starting transfers between devices: 49.2 us -> 63.7 us  [swap(): return lax.ppermute(x, axis, [(i, i ^ k) for i in range(size)])]
    unnamed x83, local copies, waits for them, and re-layouts: 12.1 us -> 5.34 us
    ppermute x4, waiting for transfers between devices: 10.3 us -> 7.29 us  [swap_across(): lax.ppermute(x, 'ctx', [(i, i ^ 2 << (i + step) % 2) for i in range(size)])]
    squeeze x3 -> x0, local copies, waits for them, and re-layouts: 2.41 us -> none  [the longest x1 0.83 us: shards(): w_rest[1]]
  transfers between devices with their start and end apart: 42 -> 49, of which waited for: 12 -> 25; matrix products, arithmetic and copies ran while one was open for 5% -> 1% of each run, Pallas kernels for 25% -> 13%
where the time goes in v3:
time: 185 us
  waiting for transfers between devices  70.7 us (38%)
  starting transfers between devices  69.1 us (37%)
  Pallas kernels  35.8 us (19%)
  local copies, waits for them, and re-layouts  6.52 us (4%)
    ppermute x44, starting transfers between devices, swap(): return lax.ppermute(x, axis, [(i, i ^ k) for i in range(size)])  63.7 us
    ppermute x44, waiting for transfers between devices, swap(): return lax.ppermute(x, axis, [(i, i ^ k) for i in range(size)])  63.4 us
    pallas_call x22, Pallas kernels, call(): pl.pallas_call(body, out_shape=outs, in_specs=in_specs, out_specs=out_spe...  35.8 us
    ppermute x4, waiting for transfers between devices, swap_across(): lax.ppermute(x, 'ctx', [(i, i ^ 2 << (i + step) % 2) for i in range(size)])  7.29 us
    unnamed x83, local copies, waits for them, and re-layouts  5.34 us
    ppermute x4, starting transfers between devices, swap_across(): lax.ppermute(x, 'ctx', [(i, i ^ 2 << (i + step) % 2) for i in range(size)])  4.79 us
  transfers between devices with their start and end apart: 49, of which 25 were waited for; matrix products, arithmetic and copies ran while one was open for 1% of the time, Pallas kernels for 13%

profile of v3, /device:TPU:0, one launch (start us, length us, event | category | flops | bytes accessed | tf_op | source)
XLA Modules:
  0.0 185.2 jit_solution(12938421583377936569)
XLA Ops:
  0.7 1.0 constant_dynamic-slice_fusion
  1.6 5.1 %collective-permute-start.1 = (bf16[128,1024]{1,0:T(8,128)(2,1)S(1)}, bf16[128,1024]{1,0:T(8,128)(2,1)S(1)}, u32[]{:S(2)}, u32[]{:S(2)}) collective-permute-start(bf16[128,1024]{1,0:T(8,128)(2,1)S(1)} %constant_dynamic-slice_fusion), channel_id=1, source_target_pairs={{0,3},{1,2},{2,1},{3,0},{4,7},{5,6},{6,5},{7,4},{8,11},{9,10},{10,... | collective-permute-start | bytes 786440 | tf_op jit(solution)/shard_map/ppermute | solution.py:535
  7.4 3.9 %shard_map.237 = (bf16[384,1024]{1,0:T(8,128)(2,1)}, bf16[384,256]{1,0:T(8,128)(2,1)}, f32[384,128]{1,0:T(8,128)}, f32[384,128]{1,0:T(8,128)}, f32[384,128]{1,0:T(8,128)}) custom-call(s32[8]{0:T(128)} %starts_ref.5, bf16[384,1024]{1,0:T(8,128)(2,1)} %x_ref.5, f32[1,1024]{1,0:T(1,128)} %bitcast.18, bf16[1024,128]{1,0:T(8,128)(2,1)} %refs_8_.1, ...), custom_call_target="tpu_custom_call" | custom-call | flops 49999998976 | bytes 2888480 | tf_op jit(solution)/shard_map/pallas_call | solution.py:38
  11.2 2.5 %collective-permute-start.6 = (bf16[384,256]{1,0:T(8,128)(2,1)}, bf16[384,256]{1,0:T(8,128)(2,1)S(1)}, u32[]{:S(2)}, u32[]{:S(2)}) collective-permute-start(bf16[384,256]{1,0:T(8,128)(2,1)} %get-tuple-element.119), channel_id=1, source_target_pairs={{0,24},{4,28},{8,16},{12,20},{16,8},{20,12},{24,0},{28,4},{1,25},{... | collective-permute-start | bytes 589832 | tf_op jit(solution)/shard_map/ppermute | solution.py:535
  14.7 1.1 copy-done
  15.9 0.9 copy-done.7
  16.8 0.9 copy-done.9
  17.7 0.9 shard_map.238
  18.8 4.2 %collective-permute-done.4 = bf16[384,256]{1,0:T(8,128)(2,1)S(1)} collective-permute-done((bf16[384,256]{1,0:T(8,128)(2,1)}, bf16[384,256]{1,0:T(8,128)(2,1)S(1)}, u32[]{:S(2)}, u32[]{:S(2)}) %collective-permute-start.4) | collective-permute-done | bytes 196640 | tf_op jit(solution)/shard_map/ppermute | solution.py:535
  23.2 1.8 collective-permute-start.2
  25.5 2.2 %shard_map.239 = (bf16[384,256]{1,0:T(8,128)(2,1)S(1)}, f32[384,256]{1,0:T(8,128)S(1)}, f32[2,768]{1,0:T(2,128)S(1)}) custom-call(s32[8]{0:T(128)S(1)} %copy-done.33, bf16[1536,128]{1,0:T(8,128)(2,1)S(1)} %get-tuple-element.152.qpad_ref, bf16[1536,256]{1,0:T(8,128)(2,1)S(1)} %constant_dynamic-update-slice_fusion.refs_0_, ...), custom_call_target="tpu_custom_call" | custom-call | flops 49999998976 | bytes 2562080 | tf_op jit(solution)/shard_map/pallas_call | solution.py:38
  29.2 3.4 %collective-permute-done.3 = bf16[64,1024]{1,0:T(8,128)(2,1)S(1)} collective-permute-done((bf16[64,1024]{1,0:T(8,128)(2,1)S(1)}, bf16[64,1024]{1,0:T(8,128)(2,1)S(1)}, u32[]{:S(2)}, u32[]{:S(2)}) %collective-permute-start.3) | collective-permute-done | bytes 131104 | tf_op jit(solution)/shard_map/ppermute | solution.py:535
  32.8 3.0 %collective-permute-start.10 = (bf16[384,256]{1,0:T(8,128)(2,1)S(1)}, bf16[384,256]{1,0:T(8,128)(2,1)S(1)}, u32[]{:S(2)}, u32[]{:S(2)}) collective-permute-start(bf16[384,256]{1,0:T(8,128)(2,1)S(1)} %get-tuple-element.120.refs_0_.refs_1_), channel_id=1, source_target_pairs={{0,3},{1,2},{2,1},{3,0},{4,7},{5,6},{6,5},{7,4},{8,11},{9,10},{10,... | collective-permute-start | bytes 589832 | tf_op jit(solution)/shard_map/ppermute | solution.py:535
  35.8 6.7 %collective-permute-done.10.refs_4_.refs_5_ = bf16[384,256]{1,0:T(8,128)(2,1)S(1)} collective-permute-done((bf16[384,256]{1,0:T(8,128)(2,1)S(1)}, bf16[384,256]{1,0:T(8,128)(2,1)S(1)}, u32[]{:S(2)}, u32[]{:S(2)}) %collective-permute-start.10) | collective-permute-done | bytes 196640 | tf_op jit(solution)/shard_map/ppermute | solution.py:535
  42.5 3.1 %collective-permute-start.11 = (bf16[192,256]{1,0:T(8,128)(2,1)S(1)}, bf16[192,256]{1,0:T(8,128)(2,1)S(1)}, u32[]{:S(2)}, u32[]{:S(2)}) collective-permute-start(bf16[192,256]{1,0:T(8,128)(2,1)S(1)} %slice.90), channel_id=1, source_target_pairs={{0,1},{1,0},{2,3},{3,2},{4,5},{5,4},{6,7},{7,6},{8,9},{9,8},{10,11... | collective-permute-start | bytes 294920 | tf_op jit(solution)/shard_map/ppermute | solution.py:535
  46.3 2.0 %collective-permute-start.12 = (bf16[192,256]{1,0:T(8,128)(2,1)S(1)}, bf16[192,256]{1,0:T(8,128)(2,1)S(1)}, u32[]{:S(2)}, u32[]{:S(2)}) collective-permute-start(bf16[192,256]{1,0:T(8,128)(2,1)S(1)} %slice.91), channel_id=1, source_target_pairs={{0,3},{1,2},{2,1},{3,0},{4,7},{5,6},{6,5},{7,4},{8,11},{9,10},{10,... | collective-permute-start | bytes 294920 | tf_op jit(solution)/shard_map/ppermute | solution.py:535
  48.4 4.6 %collective-permute-done.12.refs_3_.refs_4_ = bf16[192,256]{1,0:T(8,128)(2,1)S(1)} collective-permute-done((bf16[192,256]{1,0:T(8,128)(2,1)S(1)}, bf16[192,256]{1,0:T(8,128)(2,1)S(1)}, u32[]{:S(2)}, u32[]{:S(2)}) %collective-permute-start.12) | collective-permute-done | bytes 98336 | tf_op jit(solution)/shard_map/ppermute | solution.py:535
  53.1 1.8 shard_map.240
  56.3 5.8 %shard_map.241 = (bf16[384,1152]{1,0:T(8,128)(2,1)S(1)}, bf16[384,1152]{1,0:T(8,128)(2,1)S(1)}, bf16[384,1152]{1,0:T(8,128)(2,1)S(1)}, bf16[96,1024]{1,0:T(8,128...) custom-call(bf16[384,1024]{1,0:T(8,128)(2,1)S(1)} %get-tuple-element, ...), custom_call_target="tpu_custom_call" | custom-call | flops 49999998976 | bytes 12091392 | tf_op jit(solution)/shard_map/pallas_call | solution.py:38
  62.1 1.2 collective-permute-start.13
  63.9 4.4 %shard_map.242 = (bf16[512,3456]{1,0:T(8,128)(2,1)S(1)}, bf16[512,3456]{1,0:T(8,128)(2,1)S(1)}) custom-call(bf16[384,1024]{1,0:T(8,128)(2,1)S(1)} %get-tuple-element.126.h_ref, bf16[384,1024]{1,0:T(8,128)(2,1)S(1)} %copy-done.24, bf16[384,1152]{1,0:T(8,128)(2,1)S(1)} %get-tuple-element.127.act_ref, bf16[384,1152]{1,0:T(8,128)(2,1)S(1)} %get-tuple-element.130.dg_ref, ...), custom_call_target="tpu_custom_call" | custom-call | flops 49999998976 | bytes 11304960 | tf_op jit(solution)/shard_map/pallas_call | solution.py:38
  68.3 1.3 collective-permute-done.14.got_three_ref
  69.8 1.9 %collective-permute-start.16 = (bf16[96,1024]{1,0:T(8,128)(2,1)S(1)}, bf16[96,1024]{1,0:T(8,128)(2,1)S(1)}, u32[]{:S(2)}, u32[]{:S(2)}) collective-permute-start(bf16[96,1024]{1,0:T(8,128)(2,1)S(1)} %get-tuple-element.138), channel_id=1, source_target_pairs={{0,3},{1,2},{2,1},{3,0},{4,7},{5,6},{6,5},{7,4},{8,11},{9,10},{10,... | collective-permute-start | bytes 589832 | tf_op jit(solution)/shard_map/ppermute | solution.py:535
  71.7 5.4 %collective-permute-done.15.refs_1_ = bf16[96,1024]{1,0:T(8,128)(2,1)S(1)} collective-permute-done((bf16[96,1024]{1,0:T(8,128)(2,1)S(1)}, bf16[96,1024]{1,0:T(8,128)(2,1)S(1)}, u32[]{:S(2)}, u32[]{:S(2)}) %collective-permute-start.15) | collective-permute-done | bytes 196640 | tf_op jit(solution)/shard_map/ppermute | solution.py:535
  77.1 2.1 %collective-permute-done.16.refs_2_ = bf16[96,1024]{1,0:T(8,128)(2,1)S(1)} collective-permute-done((bf16[96,1024]{1,0:T(8,128)(2,1)S(1)}, bf16[96,1024]{1,0:T(8,128)(2,1)S(1)}, u32[]{:S(2)}, u32[]{:S(2)}) %collective-permute-start.16) | collective-permute-done | bytes 196640 | tf_op jit(solution)/shard_map/ppermute | solution.py:535
  79.2 0.9 shard_map.244
  80.1 1.3 collective-permute-start.17
  81.4 0.9 collective-permute-start.18
  82.3 2.2 %collective-permute-start.19 = (bf16[96,256]{1,0:T(8,128)(2,1)S(1)}, bf16[96,256]{1,0:T(8,128)(2,1)S(1)}, u32[]{:S(2)}, u32[]{:S(2)}) collective-permute-start(bf16[96,256]{1,0:T(8,128)(2,1)S(1)} %get-tuple-element.146), channel_id=1, source_target_pairs={{0,3},{1,2},{2,1},{3,0},{4,7},{5,6},{6,5},{7,4},{8,11},{9,10},{10,... | collective-permute-start | bytes 147464 | tf_op jit(solution)/shard_map/ppermute | solution.py:535
  84.6 1.6 shard_map.245
  87.0 1.7 collective-permute-done.19.refs_5_
  88.9 2.9 %collective-permute-start.21 = (bf16[96,1280]{1,0:T(8,128)(2,1)S(1)}, bf16[96,1280]{1,0:T(8,128)(2,1)S(1)}, u32[]{:S(2)}, u32[]{:S(2)}) collective-permute-start(bf16[96,1280]{1,0:T(8,128)(2,1)S(1)} %get-tuple-element.149), channel_id=1, source_target_pairs={{0,2},{1,3},{2,0},{3,1},{4,6},{5,7},{6,4},{7,5},{8,10},{9,11},{10,... | collective-permute-start | bytes 737288 | tf_op jit(solution)/shard_map/ppermute | solution.py:535
  91.8 1.5 collective-permute-start.22
  93.4 1.6 collective-permute-start.30
  95.0 3.5 %shard_map.246 = (bf16[384,256]{1,0:T(8,128)(2,1)S(1)}, bf16[1536,256]{1,0:T(8,128)(2,1)S(1)}, bf16[1536,256]{1,0:T(8,128)(2,1)S(1)}) custom-call(s32[8]{0:T(128)S(1)} %copy-done.34, bf16[1536,128]{1,0:T(8,128)(2,1)S(1)} %copy-done.37, f32[384,256]{1,0:T(8,128)S(1)} %get-tuple-element.153.o32_ref, f32[2,768]{1,0:T(2,128)S(1)} %get-tuple-element.154.lse_ref, ...), custom_call_target="tpu_custom_call" | custom-call | flops 49999998976 | bytes 4331552 | tf_op jit(solution)/shard_map/pallas_call | solution.py:38
  99.2 7.1 %collective-permute-done.21.refs_2_ = bf16[96,1280]{1,0:T(8,128)(2,1)S(1)} collective-permute-done((bf16[96,1280]{1,0:T(8,128)(2,1)S(1)}, bf16[96,1280]{1,0:T(8,128)(2,1)S(1)}, u32[]{:S(2)}, u32[]{:S(2)}) %collective-permute-start.21) | collective-permute-done | bytes 245792 | tf_op jit(solution)/shard_map/ppermute | solution.py:535
  106.4 1.8 collective-permute-start.25
  108.2 3.0 %collective-permute-start.24 = (bf16[96,1024]{1,0:T(8,128)(2,1)S(1)}, bf16[96,1024]{1,0:T(8,128)(2,1)S(1)}, u32[]{:S(2)}, u32[]{:S(2)}) collective-permute-start(bf16[96,1024]{1,0:T(8,128)(2,1)S(1)} %get-tuple-element.161.refs_0_), channel_id=1, source_target_pairs={{0,1},{1,0},{2,3},{3,2},{4,5},{5,4},{6,7},{7,6},{8,9},{9,8},{10,11... | collective-permute-start | bytes 589832 | tf_op jit(solution)/shard_map/ppermute | solution.py:535
  111.3 5.1 %collective-permute-start.29 = (bf16[384,256]{1,0:T(8,128)(2,1)S(1)}, bf16[384,256]{1,0:T(8,128)(2,1)S(1)}, u32[]{:S(2)}, u32[]{:S(2)}) collective-permute-start(bf16[384,256]{1,0:T(8,128)(2,1)S(1)} %get-tuple-element.217), channel_id=1, source_target_pairs={{0,24},{4,28},{8,16},{12,20},{16,8},{20,12},{24,0},{28,4},{1,25},{... | collective-permute-start | bytes 589832 | tf_op jit(solution)/shard_map/ppermute | solution.py:535
  116.4 2.3 %shard_map.248 = (bf16[384,256]{1,0:T(8,128)(2,1)}, f32[1,128]{1,0:T(1,128)S(1)}, f32[384,1024]{1,0:T(8,128)S(1)}, bf16[512,512]{1,0:T(8,128)(2,1)S(1)}, bf16[512,512]{1,0:T(8,128)(2,1)S(1)}) custom-call(bf16[384,256]{1,0:T(8,128)(2,1)S(1)} %get-tuple-element.169.dq_ref, f32[384,256]{1,0:T(8,128)S(1)} %get-tuple-element.170.qpre_ref, ...), custom_call_target="tpu_custom_call" | custom-call | flops 1 | bytes 6095616 | tf_op jit(solution)/shard_map/pallas_call | solution.py:38
  120.2 1.2 collective-permute-done.31.q_got_ref
  121.4 3.8 %collective-permute-done.29.refs_3_ = bf16[384,256]{1,0:T(8,128)(2,1)S(1)} collective-permute-done((bf16[384,256]{1,0:T(8,128)(2,1)S(1)}, bf16[384,256]{1,0:T(8,128)(2,1)S(1)}, u32[]{:S(2)}, u32[]{:S(2)}) %collective-permute-start.29) | collective-permute-done | bytes 196640 | tf_op jit(solution)/shard_map/ppermute | solution.py:535
  125.2 1.1 collective-permute-done.28.refs_2_
  126.4 2.1 %shard_map.249 = (bf16[384,256]{1,0:T(8,128)(2,1)}, f32[24,128]{1,0:T(8,128)}, bf16[96,1024]{1,0:T(8,128)(2,1)S(1)}, bf16[96,1024]{1,0:T(8,128)(2,1)S(1)}, bf16[...) custom-call(bf16[384,256]{1,0:T(8,128)(2,1)S(1)} %get-tuple-element., ...), custom_call_target="tpu_custom_call" | custom-call | flops 49999998976 | bytes 6832896 | tf_op jit(solution)/shard_map/pallas_call | solution.py:38
  129.3 2.1 %collective-permute-start.33 = (bf16[48,1024]{1,0:T(8,128)(2,1)S(1)}, bf16[48,1024]{1,0:T(8,128)(2,1)S(1)}, u32[]{:S(2)}, u32[]{:S(2)}) collective-permute-start(bf16[48,1024]{1,0:T(8,128)(2,1)S(1)} %get-tuple-element.180), channel_id=1, source_target_pairs={{0,3},{1,2},{2,1},{3,0},{4,7},{5,6},{6,5},{7,4},{8,11},{9,10},{10,... | collective-permute-start | bytes 294920 | tf_op jit(solution)/shard_map/ppermute | solution.py:535
  131.4 1.8 collective-permute-done.32.got_one_ref
  133.2 3.1 %collective-permute-done.33.got_three_ref = bf16[48,1024]{1,0:T(8,128)(2,1)S(1)} collective-permute-done((bf16[48,1024]{1,0:T(8,128)(2,1)S(1)}, bf16[48,1024]{1,0:T(8,128)(2,1)S(1)}, u32[]{:S(2)}, u32[]{:S(2)}) %collective-permute-start.33) | collective-permute-done | bytes 98336 | tf_op jit(solution)/shard_map/ppermute | solution.py:535
  136.4 1.0 collective-permute-start.38
  137.4 2.1 %collective-permute-start.35 = (bf16[48,1024]{1,0:T(8,128)(2,1)S(1)}, bf16[48,1024]{1,0:T(8,128)(2,1)S(1)}, u32[]{:S(2)}, u32[]{:S(2)}) collective-permute-start(bf16[48,1024]{1,0:T(8,128)(2,1)S(1)} %slice.83), channel_id=1, source_target_pairs={{0,3},{1,2},{2,1},{3,0},{4,7},{5,6},{6,5},{7,4},{8,11},{9,10},{10,... | collective-permute-start | bytes 294920 | tf_op jit(solution)/shard_map/ppermute | solution.py:535
  139.5 2.0 %collective-permute-start.39 = (bf16[96,1024]{1,0:T(8,128)(2,1)S(1)}, bf16[96,1024]{1,0:T(8,128)(2,1)S(1)}, u32[]{:S(2)}, u32[]{:S(2)}) collective-permute-start(bf16[96,1024]{1,0:T(8,128)(2,1)S(1)} %get-tuple-element.195), channel_id=1, source_target_pairs={{0,3},{1,2},{2,1},{3,0},{4,7},{5,6},{6,5},{7,4},{8,11},{9,10},{10,... | collective-permute-start | bytes 589832 | tf_op jit(solution)/shard_map/ppermute | solution.py:535
  142.0 1.1 collective-permute-start.37
  143.3 7.3 %collective-permute-done.37.got_ref = bf16[256,896]{1,0:T(8,128)(2,1)S(1)} collective-permute-done((bf16[256,896]{1,0:T(8,128)(2,1)S(1)}, bf16[256,896]{1,0:T(8,128)(2,1)S(1)}, u32[]{:S(2)}, u32[]{:S(2)}) %collective-permute-start.37) | collective-permute-done | bytes 458784 | tf_op jit(solution)/shard_map/ppermute | solution.py:540
  150.6 1.4 collective-permute-start.40
  153.5 1.9 %collective-permute-start.46 = (bf16[96,1024]{1,0:T(8,128)(2,1)S(1)}, bf16[96,1024]{1,0:T(8,128)(2,1)S(1)}, u32[]{:S(2)}, u32[]{:S(2)}) collective-permute-start(bf16[96,1024]{1,0:T(8,128)(2,1)S(1)} %shard_map.253.refs_0_), channel_id=1, source_target_pairs={{0,3},{1,2},{2,1},{3,0},{4,7},{5,6},{6,5},{7,4},{8,11},{9,10},{10,... | collective-permute-start | bytes 589832 | tf_op jit(solution)/shard_map/ppermute | solution.py:535
  155.5 7.7 %collective-permute-done.46.refs_4_ = bf16[96,1024]{1,0:T(8,128)(2,1)S(1)} collective-permute-done((bf16[96,1024]{1,0:T(8,128)(2,1)S(1)}, bf16[96,1024]{1,0:T(8,128)(2,1)S(1)}, u32[]{:S(2)}, u32[]{:S(2)}) %collective-permute-start.46) | collective-permute-done | bytes 196640 | tf_op jit(solution)/shard_map/ppermute | solution.py:535
  163.3 1.3 collective-permute-start.47
  164.5 1.7 collective-permute-done.41.refs_1_
  166.2 1.8 collective-permute-start.48
  169.5 3.8 %collective-permute-start.43 = (f32[8,128]{1,0:T(8,128)S(1)}, f32[8,128]{1,0:T(8,128)S(1)}, u32[]{:S(2)}, u32[]{:S(2)}) collective-permute-start(f32[8,128]{1,0:T(8,128)S(1)} %get-tuple-element.202), channel_id=1, source_target_pairs={{0,1},{1,0},{2,3},{3,2},{4,5},{5,4},{6,7},{7,6},{8,9},{9,8},{10,11... | collective-permute-start | bytes 12296 | tf_op jit(solution)/shard_map/ppermute | solution.py:535
  173.3 2.9 %collective-permute-done.43 = f32[8,128]{1,0:T(8,128)S(1)} collective-permute-done((f32[8,128]{1,0:T(8,128)S(1)}, f32[8,128]{1,0:T(8,128)S(1)}, u32[]{:S(2)}, u32[]{:S(2)}) %collective-permute-start.43) | collective-permute-done | bytes 4128 | tf_op jit(solution)/shard_map/ppermute | solution.py:535
  176.2 4.6 %collective-permute-start.44 = (f32[8,128]{1,0:T(8,128)S(1)}, f32[8,128]{1,0:T(8,128)S(1)}, u32[]{:S(2)}, u32[]{:S(2)}) collective-permute-start(f32[8,128]{1,0:T(8,128)S(1)} %add.40.a_ref), channel_id=1, source_target_pairs={{0,3},{1,2},{2,1},{3,0},{4,7},{5,6},{6,5},{7,4},{8,11},{9,10},{10,... | collective-permute-start | bytes 12296 | tf_op jit(solution)/shard_map/ppermute | solution.py:535
  180.8 0.9 shard_map.254
  181.7 1.5 shard_map.255
  183.9 1.3 shard_map.258
  (158 shorter events, 15.8 us)
Async XLA Ops:
  1.6 17.0 %collective-permute-start.1 = (bf16[128,1024]{1,0:T(8,128)(2,1)S(1)}, bf16[128,1024]{1,0:T(8,128)(2,1)S(1)}, u32[]{:S(2)}, u32[]{:S(2)}) collective-permute-start(bf16[128,1024]{1,0:T(8,128)(2,1)S(1)} %constant_dynamic-slice_fusion), channel_id=1, source_target_pairs={{0,3},{1,2},{2,1},{3,0},{4,7},{5,6},{6,5},{7,4},{8,11},{9,10},{10,... | collective-permute-start | bytes 786440 | tf_op jit(solution)/shard_map/ppermute | solution.py:535
  6.7 12.0 %collective-permute-start = (bf16[128,1024]{1,0:T(8,128)(2,1)S(1)}, bf16[128,1024]{1,0:T(8,128)(2,1)S(1)}, u32[]{:S(2)}, u32[]{:S(2)}) collective-permute-start(bf16[128,1024]{1,0:T(8,128)(2,1)S(1)} %constant_dynamic-slice_fusion), channel_id=1, source_target_pairs={{0,1},{1,0},{2,3},{3,2},{4,5},{5,4},{6,7},{7,6},{8,9},{9,8},{10,11... | collective-permute-start | bytes 786440 | tf_op jit(solution)/shard_map/ppermute | solution.py:535
  11.2 11.8 %collective-permute-start.6 = (bf16[384,256]{1,0:T(8,128)(2,1)}, bf16[384,256]{1,0:T(8,128)(2,1)S(1)}, u32[]{:S(2)}, u32[]{:S(2)}) collective-permute-start(bf16[384,256]{1,0:T(8,128)(2,1)} %get-tuple-element.119), channel_id=1, source_target_pairs={{0,24},{4,28},{8,16},{12,20},{16,8},{20,12},{24,0},{28,4},{1,25},{... | collective-permute-start | bytes 589832 | tf_op jit(solution)/shard_map/ppermute | solution.py:535
  13.7 9.4 %collective-permute-start.5 = (bf16[384,256]{1,0:T(8,128)(2,1)}, bf16[384,256]{1,0:T(8,128)(2,1)S(1)}, u32[]{:S(2)}, u32[]{:S(2)}) collective-permute-start(bf16[384,256]{1,0:T(8,128)(2,1)} %get-tuple-element.119), channel_id=1, source_target_pairs={{0,16},{4,20},{8,24},{12,28},{16,0},{20,4},{24,8},{28,12},{1,17},{... | collective-permute-start | bytes 589832 | tf_op jit(solution)/shard_map/ppermute | solution.py:535
  14.2 8.8 %collective-permute-start.4 = (bf16[384,256]{1,0:T(8,128)(2,1)}, bf16[384,256]{1,0:T(8,128)(2,1)S(1)}, u32[]{:S(2)}, u32[]{:S(2)}) collective-permute-start(bf16[384,256]{1,0:T(8,128)(2,1)} %get-tuple-element.119), channel_id=1, source_target_pairs={{0,8},{4,12},{8,0},{12,4},{16,24},{20,28},{24,16},{28,20},{1,9},{5... | collective-permute-start | bytes 589832 | tf_op jit(solution)/shard_map/ppermute | solution.py:535
  18.7 9.1 %copy-start.36 = (bf16[1536,128]{1,0:T(8,128)(2,1)}, bf16[1536,128]{1,0:T(8,128)(2,1)S(1)}, u32[]{:S(2)}) copy-start(bf16[1536,128]{1,0:T(8,128)(2,1)S(1)} %get-tuple-element.152.qpad_ref) | copy-start | bytes 1179652
  23.1 2.4 %collective-permute-start.7 = (bf16[1536,256]{1,0:T(8,128)(2,1)S(1)}, bf16[1536,256]{1,0:T(8,128)(2,1)S(1)}, u32[]{:S(2)}, u32[]{:S(2)}) collective-permute-start(bf16[1536,256]{1,0:T(8,128)(2,1)S(1)} %constant_dynamic-update-slice_fusion.refs_0_), channel_id=1, source_target_pairs={{0,4},{4,0},{8,12},{12,8},{16,20},{20,16},{24,28},{28,24},{1,5},{5... | collective-permute-start | bytes 2359304 | tf_op jit(solution)/shard_map/ppermute | solution.py:535
  23.2 6.0 %collective-permute-start.2 = (bf16[64,1024]{1,0:T(8,128)(2,1)S(1)}, bf16[64,1024]{1,0:T(8,128)(2,1)S(1)}, u32[]{:S(2)}, u32[]{:S(2)}) collective-permute-start(bf16[64,1024]{1,0:T(8,128)(2,1)S(1)} %slice.88), channel_id=1, source_target_pairs={{0,1},{1,0},{2,3},{3,2},{4,5},{5,4},{6,7},{7,6},{8,9},{9,8},{10,11... | collective-permute-start | bytes 393224 | tf_op jit(solution)/shard_map/ppermute | solution.py:535
  25.0 7.6 %collective-permute-start.3 = (bf16[64,1024]{1,0:T(8,128)(2,1)S(1)}, bf16[64,1024]{1,0:T(8,128)(2,1)S(1)}, u32[]{:S(2)}, u32[]{:S(2)}) collective-permute-start(bf16[64,1024]{1,0:T(8,128)(2,1)S(1)} %slice.89), channel_id=1, source_target_pairs={{0,3},{1,2},{2,1},{3,0},{4,7},{5,6},{6,5},{7,4},{8,11},{9,10},{10,... | collective-permute-start | bytes 393224 | tf_op jit(solution)/shard_map/ppermute | solution.py:535
  28.6 26.3 %copy-start.11 = (bf16[384,256]{1,0:T(8,128)(2,1)}, bf16[384,256]{1,0:T(8,128)(2,1)S(1)}, u32[]{:S(2)}) copy-start(bf16[384,256]{1,0:T(8,128)(2,1)S(1)} %get-tuple-element.120.refs_0_.refs_1_) | copy-start | bytes 589828
  28.6 24.4 %copy-start.13 = (bf16[256,1024]{1,0:T(8,128)(2,1)S(1)}, bf16[256,1024]{1,0:T(8,128)(2,1)}, u32[]{:S(2)}) copy-start(bf16[256,1024]{1,0:T(8,128)(2,1)} %w0_ref.3) | copy-start | bytes 1572868
  28.6 24.4 %copy-start.25 = (bf16[384,1024]{1,0:T(8,128)(2,1)S(1)}, bf16[384,1024]{1,0:T(8,128)(2,1)}, u32[]{:S(2)}) copy-start(bf16[384,1024]{1,0:T(8,128)(2,1)} %x_ref.5) | copy-start | bytes 2359300
  28.6 24.4 %copy-start.31 = (f32[1024]{0:T(1024)S(1)}, f32[1024]{0:T(1024)}, u32[]{:S(2)}) copy-start(f32[1024]{0:T(1024)} %param.23) | copy-start | bytes 12292
  32.7 20.2 %collective-permute-start.8 = (bf16[3,128,1024]{2,1,0:T(8,128)(2,1)S(1)}, bf16[3,128,1024]{2,1,0:T(8,128)(2,1)S(1)}, u32[]{:S(2)}, u32[]{:S(2)}) collective-permute-start(bf16[3,128,1024]{2,1,0:T(8,128)(2,1)S(1)} %pad_maximum_fusion.wm_ref), channel_id=1, source_target_pairs={{0,4},{4,0},{8,12},{12,8},{16,20},{20,16},{24,28},{28,24},{1,5},{5... | collective-permute-start | bytes 2359304 | tf_op jit(solution)/shard_map/ppermute | solution.py:535
  32.8 9.7 %collective-permute-start.10 = (bf16[384,256]{1,0:T(8,128)(2,1)S(1)}, bf16[384,256]{1,0:T(8,128)(2,1)S(1)}, u32[]{:S(2)}, u32[]{:S(2)}) collective-permute-start(bf16[384,256]{1,0:T(8,128)(2,1)S(1)} %get-tuple-element.120.refs_0_.refs_1_), channel_id=1, source_target_pairs={{0,3},{1,2},{2,1},{3,0},{4,7},{5,6},{6,5},{7,4},{8,11},{9,10},{10,... | collective-permute-start | bytes 589832 | tf_op jit(solution)/shard_map/ppermute | solution.py:535
  35.8 10.5 %collective-permute-start.9 = (bf16[384,256]{1,0:T(8,128)(2,1)S(1)}, bf16[384,256]{1,0:T(8,128)(2,1)S(1)}, u32[]{:S(2)}, u32[]{:S(2)}) collective-permute-start(bf16[384,256]{1,0:T(8,128)(2,1)S(1)} %get-tuple-element.120.refs_0_.refs_1_), channel_id=1, source_target_pairs={{0,1},{1,0},{2,3},{3,2},{4,5},{5,4},{6,7},{7,6},{8,9},{9,8},{10,11... | collective-permute-start | bytes 589832 | tf_op jit(solution)/shard_map/ppermute | solution.py:535
  42.5 12.4 %copy-start.3 = (bf16[384,256]{1,0:T(8,128)(2,1)}, bf16[384,256]{1,0:T(8,128)(2,1)S(1)}, u32[]{:S(2)}) copy-start(bf16[384,256]{1,0:T(8,128)(2,1)S(1)} %collective-permute-done.10.refs_4_.refs_5_) | copy-start | bytes 589828
  42.5 5.9 %collective-permute-start.11 = (bf16[192,256]{1,0:T(8,128)(2,1)S(1)}, bf16[192,256]{1,0:T(8,128)(2,1)S(1)}, u32[]{:S(2)}, u32[]{:S(2)}) collective-permute-start(bf16[192,256]{1,0:T(8,128)(2,1)S(1)} %slice.90), channel_id=1, source_target_pairs={{0,1},{1,0},{2,3},{3,2},{4,5},{5,4},{6,7},{7,6},{8,9},{9,8},{10,11... | collective-permute-start | bytes 294920 | tf_op jit(solution)/shard_map/ppermute | solution.py:535
  46.3 6.6 %collective-permute-start.12 = (bf16[192,256]{1,0:T(8,128)(2,1)S(1)}, bf16[192,256]{1,0:T(8,128)(2,1)S(1)}, u32[]{:S(2)}, u32[]{:S(2)}) collective-permute-start(bf16[192,256]{1,0:T(8,128)(2,1)S(1)} %slice.91), channel_id=1, source_target_pairs={{0,3},{1,2},{2,1},{3,0},{4,7},{5,6},{6,5},{7,4},{8,11},{9,10},{10,... | collective-permute-start | bytes 294920 | tf_op jit(solution)/shard_map/ppermute | solution.py:535
  62.1 6.3 %collective-permute-start.13 = (bf16[48,1024]{1,0:T(8,128)(2,1)S(1)}, bf16[48,1024]{1,0:T(8,128)(2,1)S(1)}, u32[]{:S(2)}, u32[]{:S(2)}) collective-permute-start(bf16[48,1024]{1,0:T(8,128)(2,1)S(1)} %get-tuple-element.135), channel_id=1, source_target_pairs={{0,1},{1,0},{2,3},{3,2},{4,5},{5,4},{6,7},{7,6},{8,9},{9,8},{10,11... | collective-permute-start | bytes 294920 | tf_op jit(solution)/shard_map/ppermute | solution.py:535
  63.2 6.4 %collective-permute-start.14 = (bf16[48,1024]{1,0:T(8,128)(2,1)S(1)}, bf16[48,1024]{1,0:T(8,128)(2,1)S(1)}, u32[]{:S(2)}, u32[]{:S(2)}) collective-permute-start(bf16[48,1024]{1,0:T(8,128)(2,1)S(1)} %get-tuple-element.136), channel_id=1, source_target_pairs={{0,3},{1,2},{2,1},{3,0},{4,7},{5,6},{6,5},{7,4},{8,11},{9,10},{10,... | collective-permute-start | bytes 294920 | tf_op jit(solution)/shard_map/ppermute | solution.py:535
  69.7 7.4 %collective-permute-start.15 = (bf16[96,1024]{1,0:T(8,128)(2,1)S(1)}, bf16[96,1024]{1,0:T(8,128)(2,1)S(1)}, u32[]{:S(2)}, u32[]{:S(2)}) collective-permute-start(bf16[96,1024]{1,0:T(8,128)(2,1)S(1)} %get-tuple-element.137), channel_id=1, source_target_pairs={{0,1},{1,0},{2,3},{3,2},{4,5},{5,4},{6,7},{7,6},{8,9},{9,8},{10,11... | collective-permute-start | bytes 589832 | tf_op jit(solution)/shard_map/ppermute | solution.py:535
  69.8 9.4 %collective-permute-start.16 = (bf16[96,1024]{1,0:T(8,128)(2,1)S(1)}, bf16[96,1024]{1,0:T(8,128)(2,1)S(1)}, u32[]{:S(2)}, u32[]{:S(2)}) collective-permute-start(bf16[96,1024]{1,0:T(8,128)(2,1)S(1)} %get-tuple-element.138), channel_id=1, source_target_pairs={{0,3},{1,2},{2,1},{3,0},{4,7},{5,6},{6,5},{7,4},{8,11},{9,10},{10,... | collective-permute-start | bytes 589832 | tf_op jit(solution)/shard_map/ppermute | solution.py:535
  71.7 21.6 %collective-permute-start.23 = (bf16[512,3456]{1,0:T(8,128)(2,1)S(1)}, bf16[512,3456]{1,0:T(8,128)(2,1)S(1)}, u32[]{:S(2)}, u32[]{:S(2)}) collective-permute-start(bf16[512,3456]{1,0:T(8,128)(2,1)S(1)} %get-tuple-element.151), channel_id=1, source_target_pairs={{0,4},{4,0},{8,12},{12,8},{16,20},{20,16},{24,28},{28,24},{1,5},{5... | collective-permute-start | bytes 10616840 | tf_op jit(solution)/shard_map/ppermute | solution.py:535
  80.1 6.0 %collective-permute-start.17 = (bf16[96,256]{1,0:T(8,128)(2,1)S(1)}, bf16[96,256]{1,0:T(8,128)(2,1)S(1)}, u32[]{:S(2)}, u32[]{:S(2)}) collective-permute-start(bf16[96,256]{1,0:T(8,128)(2,1)S(1)} %get-tuple-element.144), channel_id=1, source_target_pairs={{0,1},{1,0},{2,3},{3,2},{4,5},{5,4},{6,7},{7,6},{8,9},{9,8},{10,11... | collective-permute-start | bytes 147464 | tf_op jit(solution)/shard_map/ppermute | solution.py:535
  81.4 5.6 %collective-permute-start.18 = (bf16[96,256]{1,0:T(8,128)(2,1)S(1)}, bf16[96,256]{1,0:T(8,128)(2,1)S(1)}, u32[]{:S(2)}, u32[]{:S(2)}) collective-permute-start(bf16[96,256]{1,0:T(8,128)(2,1)S(1)} %get-tuple-element.145), channel_id=1, source_target_pairs={{0,2},{1,3},{2,0},{3,1},{4,6},{5,7},{6,4},{7,5},{8,10},{9,11},{10,... | collective-permute-start | bytes 147464 | tf_op jit(solution)/shard_map/ppermute | solution.py:535
  82.3 6.4 %collective-permute-start.19 = (bf16[96,256]{1,0:T(8,128)(2,1)S(1)}, bf16[96,256]{1,0:T(8,128)(2,1)S(1)}, u32[]{:S(2)}, u32[]{:S(2)}) collective-permute-start(bf16[96,256]{1,0:T(8,128)(2,1)S(1)} %get-tuple-element.146), channel_id=1, source_target_pairs={{0,3},{1,2},{2,1},{3,0},{4,7},{5,6},{6,5},{7,4},{8,11},{9,10},{10,... | collective-permute-start | bytes 147464 | tf_op jit(solution)/shard_map/ppermute | solution.py:535
  88.8 10.5 %collective-permute-start.20 = (bf16[96,1280]{1,0:T(8,128)(2,1)S(1)}, bf16[96,1280]{1,0:T(8,128)(2,1)S(1)}, u32[]{:S(2)}, u32[]{:S(2)}) collective-permute-start(bf16[96,1280]{1,0:T(8,128)(2,1)S(1)} %get-tuple-element.148), channel_id=1, source_target_pairs={{0,1},{1,0},{2,3},{3,2},{4,5},{5,4},{6,7},{7,6},{8,9},{9,8},{10,11... | collective-permute-start | bytes 737288 | tf_op jit(solution)/shard_map/ppermute | solution.py:535
  88.9 17.5 %collective-permute-start.21 = (bf16[96,1280]{1,0:T(8,128)(2,1)S(1)}, bf16[96,1280]{1,0:T(8,128)(2,1)S(1)}, u32[]{:S(2)}, u32[]{:S(2)}) collective-permute-start(bf16[96,1280]{1,0:T(8,128)(2,1)S(1)} %get-tuple-element.149), channel_id=1, source_target_pairs={{0,2},{1,3},{2,0},{3,1},{4,6},{5,7},{6,4},{7,5},{8,10},{9,11},{10,... | collective-permute-start | bytes 737288 | tf_op jit(solution)/shard_map/ppermute | solution.py:535
  91.8 14.6 %collective-permute-start.22 = (bf16[96,1280]{1,0:T(8,128)(2,1)S(1)}, bf16[96,1280]{1,0:T(8,128)(2,1)S(1)}, u32[]{:S(2)}, u32[]{:S(2)}) collective-permute-start(bf16[96,1280]{1,0:T(8,128)(2,1)S(1)} %get-tuple-element.150), channel_id=1, source_target_pairs={{0,3},{1,2},{2,1},{3,0},{4,7},{5,6},{6,5},{7,4},{8,11},{9,10},{10,... | collective-permute-start | bytes 737288 | tf_op jit(solution)/shard_map/ppermute | solution.py:535
  93.4 25.3 %collective-permute-start.30 = (bf16[256,3456]{1,0:T(8,128)(2,1)S(1)}, bf16[256,3456]{1,0:T(8,128)(2,1)S(1)}, u32[]{:S(2)}, u32[]{:S(2)}) collective-permute-start(bf16[256,3456]{1,0:T(8,128)(2,1)S(1)} %slice_add_fusion), channel_id=1, source_target_pairs={{0,8},{4,20},{8,0},{12,28},{16,24},{20,4},{24,16},{28,12},{1,9},{5... | collective-permute-start | bytes 5308424 | tf_op jit(solution)/shard_map/ppermute | solution.py:540
  98.5 17.9 %copy-start.1 = (bf16[384,1024]{1,0:T(8,128)(2,1)S(1)}, bf16[384,1024]{1,0:T(8,128)(2,1)}, u32[]{:S(2)}) copy-start(bf16[384,1024]{1,0:T(8,128)(2,1)} %get-tuple-element.114.h_ref.refs_14_) | copy-start | bytes 2359300
  98.5 17.9 %copy-start.4 = (bf16[384,256]{1,0:T(8,128)(2,1)S(1)}, bf16[384,256]{1,0:T(8,128)(2,1)}, u32[]{:S(2)}) copy-start(bf16[384,256]{1,0:T(8,128)(2,1)} %copy-done.3) | copy-start | bytes 589828
  98.5 17.9 %copy-start.6 = (bf16[384,256]{1,0:T(8,128)(2,1)S(1)}, bf16[384,256]{1,0:T(8,128)(2,1)}, u32[]{:S(2)}) copy-start(bf16[384,256]{1,0:T(8,128)(2,1)} %copy-done.5) | copy-start | bytes 589828
  98.5 17.9 %copy-start.8 = (f32[384,128]{1,0:T(8,128)S(1)}, f32[384,128]{1,0:T(8,128)}, u32[]{:S(2)}) copy-start(f32[384,128]{1,0:T(8,128)} %get-tuple-element.115.cos_ref.refs_5_) | copy-start | bytes 589828
  98.5 17.9 %copy-start.10 = (f32[384,128]{1,0:T(8,128)S(1)}, f32[384,128]{1,0:T(8,128)}, u32[]{:S(2)}) copy-start(f32[384,128]{1,0:T(8,128)} %get-tuple-element.116.sin_ref.refs_6_) | copy-start | bytes 589828
  98.5 17.9 %copy-start.12 = (bf16[384,256]{1,0:T(8,128)(2,1)S(1)}, bf16[384,256]{1,0:T(8,128)(2,1)}, u32[]{:S(2)}) copy-start(bf16[384,256]{1,0:T(8,128)(2,1)} %copy-done.11) | copy-start | bytes 589828
  98.5 17.9 %copy-start.15 = (bf16[192,256]{1,0:T(8,128)(2,1)S(1)}, bf16[192,256]{1,0:T(8,128)(2,1)}, u32[]{:S(2)}) copy-start(bf16[192,256]{1,0:T(8,128)(2,1)} %copy-done.14) | copy-start | bytes 294916
  98.5 17.9 %copy-start.17 = (bf16[192,256]{1,0:T(8,128)(2,1)S(1)}, bf16[192,256]{1,0:T(8,128)(2,1)}, u32[]{:S(2)}) copy-start(bf16[192,256]{1,0:T(8,128)(2,1)} %copy-done.16) | copy-start | bytes 294916
  106.3 4.9 %collective-permute-start.26 = (bf16[1536,256]{1,0:T(8,128)(2,1)S(1)}, bf16[1536,256]{1,0:T(8,128)(2,1)S(1)}, u32[]{:S(2)}, u32[]{:S(2)}) collective-permute-start(bf16[1536,256]{1,0:T(8,128)(2,1)S(1)} %get-tuple-element.164), channel_id=1, source_target_pairs={{0,4},{4,0},{8,12},{12,8},{16,20},{20,16},{24,28},{28,24},{1,5},{5... | collective-permute-start | bytes 2359304 | tf_op jit(solution)/shard_map/ppermute | solution.py:535
  106.4 12.9 %collective-permute-start.25 = (bf16[96,1024]{1,0:T(8,128)(2,1)S(1)}, bf16[96,1024]{1,0:T(8,128)(2,1)S(1)}, u32[]{:S(2)}, u32[]{:S(2)}) collective-permute-start(bf16[96,1024]{1,0:T(8,128)(2,1)S(1)} %get-tuple-element.161.refs_0_), channel_id=1, source_target_pairs={{0,3},{1,2},{2,1},{3,0},{4,7},{5,6},{6,5},{7,4},{8,11},{9,10},{10,... | collective-permute-start | bytes 589832 | tf_op jit(solution)/shard_map/ppermute | solution.py:535
  108.2 11.9 %collective-permute-start.24 = (bf16[96,1024]{1,0:T(8,128)(2,1)S(1)}, bf16[96,1024]{1,0:T(8,128)(2,1)S(1)}, u32[]{:S(2)}, u32[]{:S(2)}) collective-permute-start(bf16[96,1024]{1,0:T(8,128)(2,1)S(1)} %get-tuple-element.161.refs_0_), channel_id=1, source_target_pairs={{0,1},{1,0},{2,3},{3,2},{4,5},{5,4},{6,7},{7,6},{8,9},{9,8},{10,11... | collective-permute-start | bytes 589832 | tf_op jit(solution)/shard_map/ppermute | solution.py:535
  111.3 13.9 %collective-permute-start.29 = (bf16[384,256]{1,0:T(8,128)(2,1)S(1)}, bf16[384,256]{1,0:T(8,128)(2,1)S(1)}, u32[]{:S(2)}, u32[]{:S(2)}) collective-permute-start(bf16[384,256]{1,0:T(8,128)(2,1)S(1)} %get-tuple-element.217), channel_id=1, source_target_pairs={{0,24},{4,28},{8,16},{12,20},{16,8},{20,12},{24,0},{28,4},{1,25},{... | collective-permute-start | bytes 589832 | tf_op jit(solution)/shard_map/ppermute | solution.py:535
  116.4 10.0 %collective-permute-start.28 = (bf16[384,256]{1,0:T(8,128)(2,1)S(1)}, bf16[384,256]{1,0:T(8,128)(2,1)S(1)}, u32[]{:S(2)}, u32[]{:S(2)}) collective-permute-start(bf16[384,256]{1,0:T(8,128)(2,1)S(1)} %get-tuple-element.218), channel_id=1, source_target_pairs={{0,16},{4,20},{8,24},{12,28},{16,0},{20,4},{24,8},{28,12},{1,17},{... | collective-permute-start | bytes 589832 | tf_op jit(solution)/shard_map/ppermute | solution.py:535
  118.8 7.6 %collective-permute-start.27 = (bf16[384,256]{1,0:T(8,128)(2,1)S(1)}, bf16[384,256]{1,0:T(8,128)(2,1)S(1)}, u32[]{:S(2)}, u32[]{:S(2)}) collective-permute-start(bf16[384,256]{1,0:T(8,128)(2,1)S(1)} %get-tuple-element.219), channel_id=1, source_target_pairs={{0,8},{4,12},{8,0},{12,4},{16,24},{20,28},{24,16},{28,20},{1,9},{5... | collective-permute-start | bytes 589832 | tf_op jit(solution)/shard_map/ppermute | solution.py:535
  119.4 2.0 %collective-permute-start.31 = (bf16[512,512]{1,0:T(8,128)(2,1)S(1)}, bf16[512,512]{1,0:T(8,128)(2,1)S(1)}, u32[]{:S(2)}, u32[]{:S(2)}) collective-permute-start(bf16[512,512]{1,0:T(8,128)(2,1)S(1)} %get-tuple-element.172), channel_id=1, source_target_pairs={{0,4},{4,0},{8,12},{12,8},{16,20},{20,16},{24,28},{28,24},{1,5},{5... | collective-permute-start | bytes 1572872 | tf_op jit(solution)/shard_map/ppermute | solution.py:535
  128.5 4.6 %collective-permute-start.32 = (bf16[48,1024]{1,0:T(8,128)(2,1)S(1)}, bf16[48,1024]{1,0:T(8,128)(2,1)S(1)}, u32[]{:S(2)}, u32[]{:S(2)}) collective-permute-start(bf16[48,1024]{1,0:T(8,128)(2,1)S(1)} %get-tuple-element.179), channel_id=1, source_target_pairs={{0,1},{1,0},{2,3},{3,2},{4,5},{5,4},{6,7},{7,6},{8,9},{9,8},{10,11... | collective-permute-start | bytes 294920 | tf_op jit(solution)/shard_map/ppermute | solution.py:535
  129.3 7.0 %collective-permute-start.33 = (bf16[48,1024]{1,0:T(8,128)(2,1)S(1)}, bf16[48,1024]{1,0:T(8,128)(2,1)S(1)}, u32[]{:S(2)}, u32[]{:S(2)}) collective-permute-start(bf16[48,1024]{1,0:T(8,128)(2,1)S(1)} %get-tuple-element.180), channel_id=1, source_target_pairs={{0,3},{1,2},{2,1},{3,0},{4,7},{5,6},{6,5},{7,4},{8,11},{9,10},{10,... | collective-permute-start | bytes 294920 | tf_op jit(solution)/shard_map/ppermute | solution.py:535
  136.4 5.2 %collective-permute-start.36 = (bf16[512,384]{1,0:T(8,128)(2,1)S(1)}, bf16[512,384]{1,0:T(8,128)(2,1)S(1)}, u32[]{:S(2)}, u32[]{:S(2)}) collective-permute-start(bf16[512,384]{1,0:T(8,128)(2,1)S(1)} %get-tuple-element.188), channel_id=1, source_target_pairs={{0,4},{4,0},{8,12},{12,8},{16,20},{20,16},{24,28},{28,24},{1,5},{5... | collective-permute-start | bytes 1179656 | tf_op jit(solution)/shard_map/ppermute | solution.py:535
  136.4 16.8 %collective-permute-start.38 = (bf16[96,1024]{1,0:T(8,128)(2,1)S(1)}, bf16[96,1024]{1,0:T(8,128)(2,1)S(1)}, u32[]{:S(2)}, u32[]{:S(2)}) collective-permute-start(bf16[96,1024]{1,0:T(8,128)(2,1)S(1)} %get-tuple-element.181), channel_id=1, source_target_pairs={{0,1},{1,0},{2,3},{3,2},{4,5},{5,4},{6,7},{7,6},{8,9},{9,8},{10,11... | collective-permute-start | bytes 589832 | tf_op jit(solution)/shard_map/ppermute | solution.py:535
  137.4 14.8 %collective-permute-start.35 = (bf16[48,1024]{1,0:T(8,128)(2,1)S(1)}, bf16[48,1024]{1,0:T(8,128)(2,1)S(1)}, u32[]{:S(2)}, u32[]{:S(2)}) collective-permute-start(bf16[48,1024]{1,0:T(8,128)(2,1)S(1)} %slice.83), channel_id=1, source_target_pairs={{0,3},{1,2},{2,1},{3,0},{4,7},{5,6},{6,5},{7,4},{8,11},{9,10},{10,... | collective-permute-start | bytes 294920 | tf_op jit(solution)/shard_map/ppermute | solution.py:535
  139.5 12.7 %collective-permute-start.34 = (bf16[48,1024]{1,0:T(8,128)(2,1)S(1)}, bf16[48,1024]{1,0:T(8,128)(2,1)S(1)}, u32[]{:S(2)}, u32[]{:S(2)}) collective-permute-start(bf16[48,1024]{1,0:T(8,128)(2,1)S(1)} %slice.82), channel_id=1, source_target_pairs={{0,1},{1,0},{2,3},{3,2},{4,5},{5,4},{6,7},{7,6},{8,9},{9,8},{10,11... | collective-permute-start | bytes 294920 | tf_op jit(solution)/shard_map/ppermute | solution.py:535
  139.5 13.7 %collective-permute-start.39 = (bf16[96,1024]{1,0:T(8,128)(2,1)S(1)}, bf16[96,1024]{1,0:T(8,128)(2,1)S(1)}, u32[]{:S(2)}, u32[]{:S(2)}) collective-permute-start(bf16[96,1024]{1,0:T(8,128)(2,1)S(1)} %get-tuple-element.195), channel_id=1, source_target_pairs={{0,3},{1,2},{2,1},{3,0},{4,7},{5,6},{6,5},{7,4},{8,11},{9,10},{10,... | collective-permute-start | bytes 589832 | tf_op jit(solution)/shard_map/ppermute | solution.py:535
  142.0 11.2 %copy-start.32 = (f32[1024]{0:T(1024)S(1)}, f32[1024]{0:T(1024)}, u32[]{:S(2)}) copy-start(f32[1024]{0:T(1024)} %param.16) | copy-start | bytes 12292
  142.0 8.5 %collective-permute-start.37 = (bf16[256,896]{1,0:T(8,128)(2,1)S(1)}, bf16[256,896]{1,0:T(8,128)(2,1)S(1)}, u32[]{:S(2)}, u32[]{:S(2)}) collective-permute-start(bf16[256,896]{1,0:T(8,128)(2,1)S(1)} %get-tuple-element.190), channel_id=1, source_target_pairs={{0,8},{4,20},{8,0},{12,28},{16,24},{20,4},{24,16},{28,12},{1,9},{5... | collective-permute-start | bytes 1376264 | tf_op jit(solution)/shard_map/ppermute | solution.py:540
  150.6 31.1 %collective-permute-start.40 = (bf16[128,3456]{1,0:T(8,128)(2,1)S(1)}, bf16[128,3456]{1,0:T(8,128)(2,1)S(1)}, u32[]{:S(2)}, u32[]{:S(2)}) collective-permute-start(bf16[128,3456]{1,0:T(8,128)(2,1)S(1)} %get-tuple-element.198), channel_id=1, source_target_pairs={{0,16},{4,12},{8,24},{12,4},{16,0},{20,28},{24,8},{28,20},{1,17},{... | collective-permute-start | bytes 2654216 | tf_op jit(solution)/shard_map/ppermute | solution.py:540
  152.2 15.8 %collective-permute-start.42 = (bf16[128,896]{1,0:T(8,128)(2,1)S(1)}, bf16[128,896]{1,0:T(8,128)(2,1)S(1)}, u32[]{:S(2)}, u32[]{:S(2)}) collective-permute-start(bf16[128,896]{1,0:T(8,128)(2,1)S(1)} %get-tuple-element.201), channel_id=1, source_target_pairs={{0,16},{4,12},{8,24},{12,4},{16,0},{20,28},{24,8},{28,20},{1,17},{... | collective-permute-start | bytes 688136 | tf_op jit(solution)/shard_map/ppermute | solution.py:540
  153.5 9.7 %collective-permute-start.46 = (bf16[96,1024]{1,0:T(8,128)(2,1)S(1)}, bf16[96,1024]{1,0:T(8,128)(2,1)S(1)}, u32[]{:S(2)}, u32[]{:S(2)}) collective-permute-start(bf16[96,1024]{1,0:T(8,128)(2,1)S(1)} %shard_map.253.refs_0_), channel_id=1, source_target_pairs={{0,3},{1,2},{2,1},{3,0},{4,7},{5,6},{6,5},{7,4},{8,11},{9,10},{10,... | collective-permute-start | bytes 589832 | tf_op jit(solution)/shard_map/ppermute | solution.py:535
  155.4 10.8 %collective-permute-start.41 = (bf16[96,1024]{1,0:T(8,128)(2,1)S(1)}, bf16[96,1024]{1,0:T(8,128)(2,1)S(1)}, u32[]{:S(2)}, u32[]{:S(2)}) collective-permute-start(bf16[96,1024]{1,0:T(8,128)(2,1)S(1)} %shard_map.253.refs_0_), channel_id=1, source_target_pairs={{0,1},{1,0},{2,3},{3,2},{4,5},{5,4},{6,7},{7,6},{8,9},{9,8},{10,11... | collective-permute-start | bytes 589832 | tf_op jit(solution)/shard_map/ppermute | solution.py:535
  163.3 20.7 %collective-permute-start.47 = (bf16[48,1024]{1,0:T(8,128)(2,1)S(1)}, bf16[48,1024]{1,0:T(8,128)(2,1)S(1)}, u32[]{:S(2)}, u32[]{:S(2)}) collective-permute-start(bf16[48,1024]{1,0:T(8,128)(2,1)S(1)} %slice.99), channel_id=1, source_target_pairs={{0,1},{1,0},{2,3},{3,2},{4,5},{5,4},{6,7},{7,6},{8,9},{9,8},{10,11... | collective-permute-start | bytes 294920 | tf_op jit(solution)/shard_map/ppermute | solution.py:535
  166.2 17.7 %collective-permute-start.48 = (bf16[48,1024]{1,0:T(8,128)(2,1)S(1)}, bf16[48,1024]{1,0:T(8,128)(2,1)S(1)}, u32[]{:S(2)}, u32[]{:S(2)}) collective-permute-start(bf16[48,1024]{1,0:T(8,128)(2,1)S(1)} %slice.100), channel_id=1, source_target_pairs={{0,3},{1,2},{2,1},{3,0},{4,7},{5,6},{6,5},{7,4},{8,11},{9,10},{10,... | collective-permute-start | bytes 294920 | tf_op jit(solution)/shard_map/ppermute | solution.py:535
  168.8 14.4 %collective-permute-start.45 = (bf16[256,128]{1,0:T(8,128)(2,1)S(1)}, bf16[256,128]{1,0:T(8,128)(2,1)S(1)}, u32[]{:S(2)}, u32[]{:S(2)}) collective-permute-start(bf16[256,128]{1,0:T(8,128)(2,1)S(1)} %get-tuple-element.203), channel_id=1, source_target_pairs={{0,0},{1,8},{2,16},{3,24},{4,4},{5,12},{6,20},{7,28},{8,1},{9,9},{... | collective-permute-start | bytes 196616 | tf_op jit(solution)/shard_map/ppermute | solution.py:826
  169.5 6.7 %collective-permute-start.43 = (f32[8,128]{1,0:T(8,128)S(1)}, f32[8,128]{1,0:T(8,128)S(1)}, u32[]{:S(2)}, u32[]{:S(2)}) collective-permute-start(f32[8,128]{1,0:T(8,128)S(1)} %get-tuple-element.202), channel_id=1, source_target_pairs={{0,1},{1,0},{2,3},{3,2},{4,5},{5,4},{6,7},{7,6},{8,9},{9,8},{10,11... | collective-permute-start | bytes 12296 | tf_op jit(solution)/shard_map/ppermute | solution.py:535
  176.2 7.0 %collective-permute-start.44 = (f32[8,128]{1,0:T(8,128)S(1)}, f32[8,128]{1,0:T(8,128)S(1)}, u32[]{:S(2)}, u32[]{:S(2)}) collective-permute-start(f32[8,128]{1,0:T(8,128)S(1)} %add.40.a_ref), channel_id=1, source_target_pairs={{0,3},{1,2},{2,1},{3,0},{4,7},{5,6},{6,5},{7,4},{8,11},{9,10},{10,... | collective-permute-start | bytes 12296 | tf_op jit(solution)/shard_map/ppermute | solution.py:535
  (25 other events, 119.6 us)

commit v4 on v3

--- a/solution.py
+++ b/solution.py
@@ -3,6 +3,7 @@
 
 import jax
 import jax.numpy as jnp
+import numpy as np
 from jax import lax
 from jax.experimental import pallas as pl
 from jax.experimental.pallas import tpu as pltpu
@@ -99,20 +100,19 @@
     return [
         refs[0][...],
         refs[1][...],
-        jnp.concatenate([refs[2][...], refs[3][...]], axis=0),
-        refs[4][...],
+        refs[2][...],
+        jnp.concatenate([refs[3][...], refs[4][...]], axis=0),
     ]
 
 
 def store_around(acc_ref, refs):
     own = refs[0].shape[0]
     half = own // 2
-    refs[0][...] = acc_ref[quarter(0, own), :].astype(bf16)
-    refs[1][...] = acc_ref[quarter(1, own), :].astype(bf16)
-    far = acc_ref[quarter(2, own), :].astype(bf16)
-    refs[2][...] = far[:half]
-    refs[3][...] = far[half:]
-    refs[4][...] = acc_ref[quarter(3, own), :].astype(bf16)
+    for k in range(3):
+        refs[k][...] = acc_ref[quarter(k, own), :].astype(bf16)
+    far = acc_ref[quarter(3, own), :].astype(bf16)
+    refs[3][...] = far[:half]
+    refs[4][...] = far[half:]
 
 
 def row_norm(x):
@@ -204,14 +204,14 @@
             if mask is not None:
                 p = jnp.where(mask(), p, 0.0)
             mass_ref[j : j + 1, :] += jnp.sum(p, axis=0, keepdims=True)
-            acc_ref[j] += dot(values_t, p.astype(bf16))
+            acc_ref[j] += dot(values_t[64 * j : 64 * j + 64, :], p.astype(bf16))
 
     visit_blocks(near, rows, starts_ref, kv_refs[0].shape[0] // rows, lists, visit)
     mass = mass_ref[...]
     lse_ref[...] = jnp.log2(mass)
     parts = []
     for j in range(2):
-        normed = acc_ref[j, 64 * j : 64 * j + 64, :] / mass[j : j + 1, :]
+        normed = acc_ref[j] / mass[j : j + 1, :]
         parts += [normed[:, :rows], normed[:, rows:]]
     o32 = jnp.concatenate(parts, axis=0).T
     o32_ref[...] = o32
@@ -253,7 +253,7 @@
             ds = (p * (dot(values, dopad, NT) - delta[j])).astype(bf16)
             dv += dot(p.astype(bf16), dopad)
             dk += dot(ds, qpad)
-            dqt_ref[j] += dot(keys_t, ds)
+            dqt_ref[j] += dot(keys_t[64 * j : 64 * j + 64, :], ds)
         dkv_refs[which][at, :128] = (dk * scale).astype(bf16)
         dkv_refs[which][at, 128:] = dv.astype(bf16)
 
@@ -264,7 +264,7 @@
     visit_blocks(near, rows, starts_ref, kv_refs[0].shape[0] // rows, lists, visit, skip)
     parts = []
     for j in range(2):
-        part = dqt_ref[j, 64 * j : 64 * j + 64, :]
+        part = dqt_ref[j]
         parts += [part[:, :rows], part[:, rows:]]
     dq_ref[...] = (jnp.concatenate(parts, axis=0).T * scale).astype(bf16)
 
@@ -308,12 +308,12 @@
     store_around(acc_ref, dh_refs)
 
 
-def reduce_kernel(one_ref, three_ref, got_one_ref, got_three_ref, to_one_ref, to_three_ref):
+def reduce_kernel(one_ref, two_ref, got_one_ref, got_two_ref, to_one_ref, to_two_ref):
     half = got_one_ref.shape[0]
     to_one_ref[:half, :] = one_ref[:half, :]
-    to_one_ref[half:, :] = (one_ref[half:, :].astype(f32) + got_three_ref[...].astype(f32)).astype(bf16)
-    to_three_ref[:half, :] = (three_ref[:half, :].astype(f32) + got_one_ref[...].astype(f32)).astype(bf16)
-    to_three_ref[half:, :] = three_ref[half:, :]
+    to_one_ref[half:, :] = (one_ref[half:, :].astype(f32) + got_two_ref[...].astype(f32)).astype(bf16)
+    to_two_ref[:half, :] = (two_ref[:half, :].astype(f32) + got_one_ref[...].astype(f32)).astype(bf16)
+    to_two_ref[half:, :] = two_ref[half:, :]
 
 
 def mid_kernel(g_ref, y_ref, gain_ref, w0_ref, wm_ref, wp_ref, *refs):
@@ -572,32 +572,32 @@
     mine, place = lax.axis_index("ctx"), lax.axis_index("tp")
     gain_one, gain_two = norm1_gain[None, :], norm2_gain[None, :]
     q_gain, k_gain = query_gain[None, :], key_gain[None, :]
-    frequency = rope_base ** (-2.0 * jnp.arange(head_dim // 2, dtype=f32) / head_dim)
-    frequency = jnp.concatenate([frequency] * 4)[None, :]
+    frequency = rope_base ** (-2.0 * np.arange(head_dim // 2) / head_dim)
+    frequency = jnp.asarray(np.tile(frequency, 4)[None, :], f32)
 
     def exchange(parts):
         return [parts[0]] + [swap(parts[k], "tp", k) for k in others]
 
     def gather(x, *first):
-        one, three = swap(x, "tp", 1), swap(x, "tp", 3)
+        one, two = swap(x, "tp", 1), swap(x, "tp", 2)
         half = x.shape[0] // 2
-        near_one, near_three = lax.optimization_barrier((one, three, *first))[:2] if first else (one, three)
-        return [x, one, swap(near_three[:half], "tp", 1), swap(near_one[half:], "tp", 3), three]
+        from_one, from_two = lax.optimization_barrier((one, two, *first))[:2] if first else (one, two)
+        return [x, one, two, swap(from_two[:half], "tp", 1), swap(from_one[half:], "tp", 2)]
 
     def reduce(parts, *first):
-        here, one, far_low, far_high, three = parts
-        got_one, got_three = swap(far_low, "tp", 1), swap(far_high, "tp", 3)
+        here, one, two, far_low, far_high = parts
+        got_one, got_two = swap(far_low, "tp", 1), swap(far_high, "tp", 2)
         if first:
             one = after(one, *first)
-        to_one, to_three = call(
+        to_one, to_two = call(
             reduce_kernel,
-            [one, three, got_one, got_three],
+            [one, two, got_one, got_two],
             [shape(one.shape, bf16)] * 2,
             work=1,
         )
-        return [here, swap(to_one, "tp", 1), swap(to_three, "tp", 3)], to_one
-
-    quarters = [shape((own, width), bf16)] * 2 + [shape((own // 2, width), bf16)] * 2 + [shape((own, width), bf16)]
+        return [here, swap(to_one, "tp", 1), swap(to_two, "tp", 2)], to_one
+
+    quarters = [shape((own, width), bf16)] * 3 + [shape((own // 2, width), bf16)] * 2
 
     h_one, kv, key_pre, cosine, sine = call(
         kv_kernel,
@@ -624,17 +624,17 @@
         [shape((4 * rows, 128), bf16), shape((rows, 256), f32)],
     )
     if near:
-        even = jnp.concatenate([after(kv, qpad, w_around[1], w_around[4]), *kv_got], axis=0)
+        even = jnp.concatenate([after(kv, qpad, *w_around[1:3]), *kv_got], axis=0)
         kv_all = [even, swap(even, "ctx", 1)]
     attended, attended32, log_mass = call(
         functools.partial(attend_kernel, near, scale),
         [doc_starts, qpad, *kv_all],
         [shape((rows, 256), bf16), shape((rows, 256), f32), shape((2, 2 * rows), f32)],
-        [pltpu.VMEM((2, 128, 2 * rows), f32), pltpu.VMEM((2, 2 * rows), f32)],
+        [pltpu.VMEM((2, 64, 2 * rows), f32), pltpu.VMEM((2, 2 * rows), f32)],
     )
     o_parts = gather(attended)
     w_around = lax.optimization_barrier((*w_around, attended))[:5]
-    w_mine = jnp.stack([w_around[1], jnp.concatenate(w_around[2:4], axis=0), w_around[4]])
+    w_mine = jnp.stack([*w_around[1:3], jnp.concatenate(w_around[3:], axis=0)])
     w_all = [w_mine, swap(w_mine, "ctx", 1)]
     h_two, mixed_own = call(
         mix_kernel,
@@ -683,7 +683,7 @@
         feed_send = feed_even[half:] + feed_other[half:]
         feed_got = swap_across(feed_send, 0)
         qpad = after(qpad, feed_send, down[1])
-    down_got = exchange(list(lax.optimization_barrier((*down, *dout[1:]))[:n_tp]))
+    down_got = exchange(down)
 
     got = call(
         functools.partial(attend_back_kernel, near, scale, n_tp),
@@ -692,7 +692,7 @@
         [
             pltpu.VMEM((rows, 256), f32),
             pltpu.VMEM((4 * rows, 128), bf16),
-            pltpu.VMEM((2, 128, 2 * rows), f32),
+            pltpu.VMEM((2, 64, 2 * rows), f32),
         ],
     )
     query_low, dkv = got[0], got[1:]
@@ -711,7 +711,7 @@
         [shape((own, width), bf16), shape((rows, width // n_tp), bf16)],
         work=1,
     )
-    layer_one, layer_three = swap(layer_own, "tp", 1), swap(layer_own, "tp", 3)
+    layer_one, layer_two = swap(layer_own, "tp", 1), swap(layer_own, "tp", 2)
 
     if near:
         feed_parts = lax.optimization_barrier((feed_even, feed_other, feed_got, query_low))[:3]
@@ -727,7 +727,7 @@
         work=1,
     )
     query_pre_low, q_gain_part, one_query = got[:3]
-    done = [layer_one, layer_three, feed_here] if near else [layer_one, layer_three]
+    done = [layer_one, layer_two, feed_here] if near else [layer_one, layer_two]
     if near:
         q_odd, q_even = got[3:]
         q_other = swap(q_odd, "ctx", 1)
@@ -774,16 +774,16 @@
             work=1,
         )
         mixed_grad = after(mixed_grad, attn_here)
-    far_one, far_three, _ = lax.optimization_barrier((layer_one, layer_three, token))
+    far_one, far_two, _ = lax.optimization_barrier((layer_one, layer_two, token))
     half = own // 2
     layer_parts = [
         layer_own,
         layer_one,
-        swap(far_three[:half], "tp", 1),
-        swap(far_one[half:], "tp", 3),
-        layer_three,
+        layer_two,
+        swap(far_two[:half], "tp", 1),
+        swap(far_one[half:], "tp", 2),
     ]
-    mixed_grad = after(mixed_grad, *layer_parts[2:4])
+    mixed_grad = after(mixed_grad, *layer_parts[3:])
     input_own = call(
         last_kernel,
         [hidden_in, mixed_grad, gain_one, *one_got],
@@ -850,11 +850,11 @@
     gains = gains + swap(gains, "tp", 1)
     gain_one_sum, gain_two_sum, q_gain_sum, k_gain_sum, out_w = call(
         functools.partial(gain_kernel, block),
-        [gains, swap(gains, "tp", 3), out_w],
+        [gains, swap(gains, "tp", 2), out_w],
         [shape((1, block), f32)] * 2 + [shape((1, 64), f32)] * 2 + [shape(out_w.shape, f32)],
         work=1,
     )
-    input_parts[0] = after(input_parts[0], gate_w, layer_out, out_w)
+    input_parts[0] = after(input_parts[0], gate_w, layer_out)
     input_grad = call(
         join_kernel, input_parts, [shape((rows, width), f32)]
     )[0]

time: 185 us -> 181 us (0.978)
  starting transfers between devices: 69.1 us -> 62.1 us
  waiting for transfers between devices: 70.7 us -> 73.5 us
    ppermute x44, starting transfers between devices: 63.7 us -> 56.9 us  [swap(): return lax.ppermute(x, axis, [(i, i ^ k) for i in range(size)])]
    ppermute x44, waiting for transfers between devices: 63.4 us -> 66.1 us  [swap(): return lax.ppermute(x, axis, [(i, i ^ k) for i in range(size)])]
  transfers between devices with their start and end apart: 49 -> 49, of which waited for: 25 -> 22; matrix products, arithmetic and copies ran while one was open for 1% -> 1% of each run, Pallas kernels for 13% -> 14%
where the time goes in v4:
time: 181 us; the launch traced here: 180 us
  waiting for transfers between devices  73.5 us (41%)
  starting transfers between devices  62.1 us (34%)
  Pallas kernels  35.7 us (20%)
  local copies, waits for them, and re-layouts  6.52 us (4%)
    ppermute x44, waiting for transfers between devices, swap(): return lax.ppermute(x, axis, [(i, i ^ k) for i in range(size)])  66.1 us
    ppermute x44, starting transfers between devices, swap(): return lax.ppermute(x, axis, [(i, i ^ k) for i in range(size)])  56.9 us
    pallas_call x22, Pallas kernels, call(): pl.pallas_call(body, out_shape=outs, in_specs=in_specs, out_specs=out_spe...  35.7 us
    ppermute x4, waiting for transfers between devices, swap_across(): lax.ppermute(x, 'ctx', [(i, i ^ 2 << (i + step) % 2) for i in range(size)])  7.46 us
    unnamed x83, local copies, waits for them, and re-layouts  5.35 us
    ppermute x4, starting transfers between devices, swap_across(): lax.ppermute(x, 'ctx', [(i, i ^ 2 << (i + step) % 2) for i in range(size)])  4.56 us
  transfers between devices with their start and end apart: 49, of which 22 were waited for; matrix products, arithmetic and copies ran while one was open for 1% of the time, Pallas kernels for 14%

profile of v4, /device:TPU:0, one launch (start us, length us, event | category | flops | bytes accessed | tf_op | source)
XLA Modules:
  0.0 180.3 jit_solution(12754219193789441500)
XLA Ops:
  0.7 1.0 constant_dynamic-slice_fusion
  1.6 4.1 %collective-permute-start.1 = (bf16[128,1024]{1,0:T(8,128)(2,1)S(1)}, bf16[128,1024]{1,0:T(8,128)(2,1)S(1)}, u32[]{:S(2)}, u32[]{:S(2)}) collective-permute-start(bf16[128,1024]{1,0:T(8,128)(2,1)S(1)} %constant_dynamic-slice_fusion), channel_id=1, source_target_pairs={{0,2},{1,3},{2,0},{3,1},{4,6},{5,7},{6,4},{7,5},{8,10},{9,11},{10,... | collective-permute-start | bytes 786440 | tf_op jit(solution)/shard_map/ppermute | solution.py:535
  5.7 1.6 collective-permute-start
  7.3 3.9 %shard_map.246 = (bf16[384,1024]{1,0:T(8,128)(2,1)}, bf16[384,256]{1,0:T(8,128)(2,1)}, f32[384,128]{1,0:T(8,128)}, f32[384,128]{1,0:T(8,128)}, f32[384,128]{1,0:T(8,128)}) custom-call(s32[8]{0:T(128)} %starts_ref.5, bf16[384,1024]{1,0:T(8,128)(2,1)} %x_ref.5, f32[1,1024]{1,0:T(1,128)} %bitcast.16, bf16[1024,128]{1,0:T(8,128)(2,1)} %refs_8_.1, ...), custom_call_target="tpu_custom_call" | custom-call | flops 49999998976 | bytes 2888480 | tf_op jit(solution)/shard_map/pallas_call | solution.py:39
  11.2 2.4 %collective-permute-start.6 = (bf16[384,256]{1,0:T(8,128)(2,1)}, bf16[384,256]{1,0:T(8,128)(2,1)S(1)}, u32[]{:S(2)}, u32[]{:S(2)}) collective-permute-start(bf16[384,256]{1,0:T(8,128)(2,1)} %get-tuple-element.115), channel_id=1, source_target_pairs={{0,24},{4,28},{8,16},{12,20},{16,8},{20,12},{24,0},{28,4},{1,25},{... | collective-permute-start | bytes 589832 | tf_op jit(solution)/shard_map/ppermute | solution.py:535
  14.7 1.1 copy-done
  15.8 0.9 copy-done.7
  16.8 0.9 copy-done.9
  17.7 0.9 shard_map.247
  18.7 4.0 %collective-permute-done.4 = bf16[384,256]{1,0:T(8,128)(2,1)S(1)} collective-permute-done((bf16[384,256]{1,0:T(8,128)(2,1)}, bf16[384,256]{1,0:T(8,128)(2,1)S(1)}, u32[]{:S(2)}, u32[]{:S(2)}) %collective-permute-start.4) | collective-permute-done | bytes 196640 | tf_op jit(solution)/shard_map/ppermute | solution.py:535
  23.8 1.3 collective-permute-done.7.refs_1_
  25.2 2.2 %shard_map.248 = (bf16[384,256]{1,0:T(8,128)(2,1)S(1)}, f32[384,256]{1,0:T(8,128)S(1)}, f32[2,768]{1,0:T(2,128)S(1)}) custom-call(s32[8]{0:T(128)S(1)} %copy-done.33, bf16[1536,128]{1,0:T(8,128)(2,1)S(1)} %get-tuple-element.141.qpad_ref, bf16[1536,256]{1,0:T(8,128)(2,1)S(1)} %constant_dynamic-update-slice_fusion.refs_0_, ...), custom_call_target="tpu_custom_call" | custom-call | flops 49999998976 | bytes 2562080 | tf_op jit(solution)/shard_map/pallas_call | solution.py:39
  27.4 0.9 copy-done.27
  28.2 2.1 %collective-permute-done.2 = bf16[64,1024]{1,0:T(8,128)(2,1)S(1)} collective-permute-done((bf16[64,1024]{1,0:T(8,128)(2,1)S(1)}, bf16[64,1024]{1,0:T(8,128)(2,1)S(1)}, u32[]{:S(2)}, u32[]{:S(2)}) %collective-permute-start.2) | collective-permute-done | bytes 131104 | tf_op jit(solution)/shard_map/ppermute | solution.py:535
  30.4 2.5 %collective-permute-done.3 = bf16[64,1024]{1,0:T(8,128)(2,1)S(1)} collective-permute-done((bf16[64,1024]{1,0:T(8,128)(2,1)S(1)}, bf16[64,1024]{1,0:T(8,128)(2,1)S(1)}, u32[]{:S(2)}, u32[]{:S(2)}) %collective-permute-start.3) | collective-permute-done | bytes 131104 | tf_op jit(solution)/shard_map/ppermute | solution.py:535
  33.4 1.7 collective-permute-start.9
  35.1 9.3 %collective-permute-done.10.refs_2_.refs_3_ = bf16[384,256]{1,0:T(8,128)(2,1)S(1)} collective-permute-done((bf16[384,256]{1,0:T(8,128)(2,1)S(1)}, bf16[384,256]{1,0:T(8,128)(2,1)S(1)}, u32[]{:S(2)}, u32[]{:S(2)}) %collective-permute-start.10) | collective-permute-done | bytes 196640 | tf_op jit(solution)/shard_map/ppermute | solution.py:535
  44.6 2.9 %collective-permute-start.12 = (bf16[192,256]{1,0:T(8,128)(2,1)S(1)}, bf16[192,256]{1,0:T(8,128)(2,1)S(1)}, u32[]{:S(2)}, u32[]{:S(2)}) collective-permute-start(bf16[192,256]{1,0:T(8,128)(2,1)S(1)} %slice.91), channel_id=1, source_target_pairs={{0,2},{1,3},{2,0},{3,1},{4,6},{5,7},{6,4},{7,5},{8,10},{9,11},{10,... | collective-permute-start | bytes 294920 | tf_op jit(solution)/shard_map/ppermute | solution.py:535
  47.5 3.4 %collective-permute-done.11.refs_3_.refs_4_ = bf16[192,256]{1,0:T(8,128)(2,1)S(1)} collective-permute-done((bf16[192,256]{1,0:T(8,128)(2,1)S(1)}, bf16[192,256]{1,0:T(8,128)(2,1)S(1)}, u32[]{:S(2)}, u32[]{:S(2)}) %collective-permute-start.11) | collective-permute-done | bytes 98336 | tf_op jit(solution)/shard_map/ppermute | solution.py:535
  50.9 1.4 collective-permute-done.12.refs_4_.refs_5_
  52.4 1.8 %shard_map.249 = (bf16[384,1024]{1,0:T(8,128)(2,1)S(1)}, f32[96,1024]{1,0:T(8,128)S(1)}) custom-call(bf16[384,1024]{1,0:T(8,128)(2,1)S(1)} %copy-done.25, f32[1,1024]{1,0:T(1,128)S(1)} %bitcast.14, bf16[256,1024]{1,0:T(8,128)(2,1)S(1)} %copy-done.13, bf16[3,128,1024]{2,1,0:T(8,128)(2,1)S(1)} %pad_maximum_fusion.wm_ref, ...), custom_call_target="tpu_custom_call" | custom-call | flops 49999998976 | bytes 4853760 | tf_op jit(solution)/shard_map/pallas_call | solution.py:39
  54.8 0.7 copy-done.23
  55.6 5.8 %shard_map.250 = (bf16[384,1152]{1,0:T(8,128)(2,1)S(1)}, bf16[384,1152]{1,0:T(8,128)(2,1)S(1)}, bf16[384,1152]{1,0:T(8,128)(2,1)S(1)}, bf16[96,1024]{1,0:T(8,128...) custom-call(bf16[384,1024]{1,0:T(8,128)(2,1)S(1)} %get-tuple-element, ...), custom_call_target="tpu_custom_call" | custom-call | flops 49999998976 | bytes 12091392 | tf_op jit(solution)/shard_map/pallas_call | solution.py:39
  61.7 2.7 %collective-permute-start.14 = (bf16[48,1024]{1,0:T(8,128)(2,1)S(1)}, bf16[48,1024]{1,0:T(8,128)(2,1)S(1)}, u32[]{:S(2)}, u32[]{:S(2)}) collective-permute-start(bf16[48,1024]{1,0:T(8,128)(2,1)S(1)} %get-tuple-element.132), channel_id=1, source_target_pairs={{0,2},{1,3},{2,0},{3,1},{4,6},{5,7},{6,4},{7,5},{8,10},{9,11},{10,... | collective-permute-start | bytes 294920 | tf_op jit(solution)/shard_map/ppermute | solution.py:535
  64.4 4.4 %shard_map.251 = (bf16[512,3456]{1,0:T(8,128)(2,1)S(1)}, bf16[512,3456]{1,0:T(8,128)(2,1)S(1)}) custom-call(bf16[384,1024]{1,0:T(8,128)(2,1)S(1)} %get-tuple-element.122.h_ref, bf16[384,1024]{1,0:T(8,128)(2,1)S(1)} %copy-done.24, bf16[384,1152]{1,0:T(8,128)(2,1)S(1)} %get-tuple-element.123.act_ref, bf16[384,1152]{1,0:T(8,128)(2,1)S(1)} %get-tuple-element.126.dg_ref, ...), custom_call_target="tpu_custom_call" | custom-call | flops 49999998976 | bytes 11304960 | tf_op jit(solution)/shard_map/pallas_call | solution.py:39
  69.1 1.8 %collective-permute-start.16 = (bf16[96,1024]{1,0:T(8,128)(2,1)S(1)}, bf16[96,1024]{1,0:T(8,128)(2,1)S(1)}, u32[]{:S(2)}, u32[]{:S(2)}) collective-permute-start(bf16[96,1024]{1,0:T(8,128)(2,1)S(1)} %get-tuple-element.134), channel_id=1, source_target_pairs={{0,2},{1,3},{2,0},{3,1},{4,6},{5,7},{6,4},{7,5},{8,10},{9,11},{10,... | collective-permute-start | bytes 589832 | tf_op jit(solution)/shard_map/ppermute | solution.py:535
  71.0 6.1 %collective-permute-done.15.refs_1_ = bf16[96,1024]{1,0:T(8,128)(2,1)S(1)} collective-permute-done((bf16[96,1024]{1,0:T(8,128)(2,1)S(1)}, bf16[96,1024]{1,0:T(8,128)(2,1)S(1)}, u32[]{:S(2)}, u32[]{:S(2)}) %collective-permute-start.15) | collective-permute-done | bytes 196640 | tf_op jit(solution)/shard_map/ppermute | solution.py:535
  77.1 1.6 collective-permute-done.16.refs_2_
  78.7 0.9 shard_map.253
  80.1 2.6 %collective-permute-start.22 = (bf16[96,256]{1,0:T(8,128)(2,1)S(1)}, bf16[96,256]{1,0:T(8,128)(2,1)S(1)}, u32[]{:S(2)}, u32[]{:S(2)}) collective-permute-start(bf16[96,256]{1,0:T(8,128)(2,1)S(1)} %get-tuple-element.146), channel_id=1, source_target_pairs={{0,2},{1,3},{2,0},{3,1},{4,6},{5,7},{6,4},{7,5},{8,10},{9,11},{10,... | collective-permute-start | bytes 147464 | tf_op jit(solution)/shard_map/ppermute | solution.py:535
  82.7 1.4 collective-permute-start.23
  84.1 1.6 shard_map.254
  85.9 2.9 %collective-permute-start.17 = (bf16[96,1280]{1,0:T(8,128)(2,1)S(1)}, bf16[96,1280]{1,0:T(8,128)(2,1)S(1)}, u32[]{:S(2)}, u32[]{:S(2)}) collective-permute-start(bf16[96,1280]{1,0:T(8,128)(2,1)S(1)} %get-tuple-element.137), channel_id=1, source_target_pairs={{0,1},{1,0},{2,3},{3,2},{4,5},{5,4},{6,7},{7,6},{8,9},{9,8},{10,11... | collective-permute-start | bytes 737288 | tf_op jit(solution)/shard_map/ppermute | solution.py:535
  89.0 1.5 collective-permute-start.19
  90.5 1.5 collective-permute-start.30
  92.0 3.4 %shard_map.255 = (bf16[384,256]{1,0:T(8,128)(2,1)S(1)}, bf16[1536,256]{1,0:T(8,128)(2,1)S(1)}, bf16[1536,256]{1,0:T(8,128)(2,1)S(1)}) custom-call(s32[8]{0:T(128)S(1)} %copy-done.34, bf16[1536,128]{1,0:T(8,128)(2,1)S(1)} %copy-done.37, f32[384,256]{1,0:T(8,128)S(1)} %get-tuple-element.142.o32_ref, f32[2,768]{1,0:T(2,128)S(1)} %get-tuple-element.143.lse_ref, ...), custom_call_target="tpu_custom_call" | custom-call | flops 49999998976 | bytes 4331552 | tf_op jit(solution)/shard_map/pallas_call | solution.py:39
  95.5 8.0 %collective-permute-done.18.refs_2_ = bf16[96,1280]{1,0:T(8,128)(2,1)S(1)} collective-permute-done((bf16[96,1280]{1,0:T(8,128)(2,1)S(1)}, bf16[96,1280]{1,0:T(8,128)(2,1)S(1)}, u32[]{:S(2)}, u32[]{:S(2)}) %collective-permute-start.18) | collective-permute-done | bytes 245792 | tf_op jit(solution)/shard_map/ppermute | solution.py:535
  103.6 5.0 %collective-permute-start.25 = (bf16[96,1024]{1,0:T(8,128)(2,1)S(1)}, bf16[96,1024]{1,0:T(8,128)(2,1)S(1)}, u32[]{:S(2)}, u32[]{:S(2)}) collective-permute-start(bf16[96,1024]{1,0:T(8,128)(2,1)S(1)} %get-tuple-element.153.refs_0_), channel_id=1, source_target_pairs={{0,2},{1,3},{2,0},{3,1},{4,6},{5,7},{6,4},{7,5},{8,10},{9,11},{10,... | collective-permute-start | bytes 589832 | tf_op jit(solution)/shard_map/ppermute | solution.py:535
  108.8 4.6 %collective-permute-start.29 = (bf16[384,256]{1,0:T(8,128)(2,1)S(1)}, bf16[384,256]{1,0:T(8,128)(2,1)S(1)}, u32[]{:S(2)}, u32[]{:S(2)}) collective-permute-start(bf16[384,256]{1,0:T(8,128)(2,1)S(1)} %get-tuple-element.209), channel_id=1, source_target_pairs={{0,24},{4,28},{8,16},{12,20},{16,8},{20,12},{24,0},{28,4},{1,25},{... | collective-permute-start | bytes 589832 | tf_op jit(solution)/shard_map/ppermute | solution.py:535
  113.4 2.3 %shard_map.257 = (bf16[384,256]{1,0:T(8,128)(2,1)}, f32[1,128]{1,0:T(1,128)S(1)}, f32[384,1024]{1,0:T(8,128)S(1)}, bf16[512,512]{1,0:T(8,128)(2,1)S(1)}, bf16[512,512]{1,0:T(8,128)(2,1)S(1)}) custom-call(bf16[384,256]{1,0:T(8,128)(2,1)S(1)} %get-tuple-element.161.dq_ref, f32[384,256]{1,0:T(8,128)S(1)} %get-tuple-element.162.qpre_ref, ...), custom_call_target="tpu_custom_call" | custom-call | flops 1 | bytes 6095616 | tf_op jit(solution)/shard_map/pallas_call | solution.py:39
  116.4 2.1 %collective-permute-done.25.refs_2_ = bf16[96,1024]{1,0:T(8,128)(2,1)S(1)} collective-permute-done((bf16[96,1024]{1,0:T(8,128)(2,1)S(1)}, bf16[96,1024]{1,0:T(8,128)(2,1)S(1)}, u32[]{:S(2)}, u32[]{:S(2)}) %collective-permute-start.25) | collective-permute-done | bytes 196640 | tf_op jit(solution)/shard_map/ppermute | solution.py:535
  119.3 1.2 collective-permute-done.31.q_got_ref
  120.7 3.0 %collective-permute-done.28.refs_2_ = bf16[384,256]{1,0:T(8,128)(2,1)S(1)} collective-permute-done((bf16[384,256]{1,0:T(8,128)(2,1)S(1)}, bf16[384,256]{1,0:T(8,128)(2,1)S(1)}, u32[]{:S(2)}, u32[]{:S(2)}) %collective-permute-start.28) | collective-permute-done | bytes 196640 | tf_op jit(solution)/shard_map/ppermute | solution.py:535
  123.7 2.1 %shard_map.258 = (bf16[384,256]{1,0:T(8,128)(2,1)}, f32[24,128]{1,0:T(8,128)}, bf16[96,1024]{1,0:T(8,128)(2,1)S(1)}, bf16[96,1024]{1,0:T(8,128)(2,1)S(1)}, bf16[...) custom-call(bf16[384,256]{1,0:T(8,128)(2,1)S(1)} %get-tuple-element., ...), custom_call_target="tpu_custom_call" | custom-call | flops 49999998976 | bytes 6832896 | tf_op jit(solution)/shard_map/pallas_call | solution.py:39
  125.8 1.0 collective-permute-start.32
  126.8 1.1 collective-permute-start.33
  127.9 3.1 %collective-permute-done.32.got_one_ref = bf16[48,1024]{1,0:T(8,128)(2,1)S(1)} collective-permute-done((bf16[48,1024]{1,0:T(8,128)(2,1)S(1)}, bf16[48,1024]{1,0:T(8,128)(2,1)S(1)}, u32[]{:S(2)}, u32[]{:S(2)}) %collective-permute-start.32) | collective-permute-done | bytes 98336 | tf_op jit(solution)/shard_map/ppermute | solution.py:535
  131.1 3.2 %collective-permute-done.33.got_two_ref = bf16[48,1024]{1,0:T(8,128)(2,1)S(1)} collective-permute-done((bf16[48,1024]{1,0:T(8,128)(2,1)S(1)}, bf16[48,1024]{1,0:T(8,128)(2,1)S(1)}, u32[]{:S(2)}, u32[]{:S(2)}) %collective-permute-start.33) | collective-permute-done | bytes 98336 | tf_op jit(solution)/shard_map/ppermute | solution.py:535
  134.5 2.3 %collective-permute-start.35 = (bf16[48,1024]{1,0:T(8,128)(2,1)S(1)}, bf16[48,1024]{1,0:T(8,128)(2,1)S(1)}, u32[]{:S(2)}, u32[]{:S(2)}) collective-permute-start(bf16[48,1024]{1,0:T(8,128)(2,1)S(1)} %slice.83), channel_id=1, source_target_pairs={{0,2},{1,3},{2,0},{3,1},{4,6},{5,7},{6,4},{7,5},{8,10},{9,11},{10,... | collective-permute-start | bytes 294920 | tf_op jit(solution)/shard_map/ppermute | solution.py:535
  137.0 2.5 %collective-permute-start.39 = (bf16[96,1024]{1,0:T(8,128)(2,1)S(1)}, bf16[96,1024]{1,0:T(8,128)(2,1)S(1)}, u32[]{:S(2)}, u32[]{:S(2)}) collective-permute-start(bf16[96,1024]{1,0:T(8,128)(2,1)S(1)} %get-tuple-element.187), channel_id=1, source_target_pairs={{0,2},{1,3},{2,0},{3,1},{4,6},{5,7},{6,4},{7,5},{8,10},{9,11},{10,... | collective-permute-start | bytes 589832 | tf_op jit(solution)/shard_map/ppermute | solution.py:535
  140.0 1.0 collective-permute-start.37
  141.1 7.5 %collective-permute-done.37.got_ref = bf16[256,896]{1,0:T(8,128)(2,1)S(1)} collective-permute-done((bf16[256,896]{1,0:T(8,128)(2,1)S(1)}, bf16[256,896]{1,0:T(8,128)(2,1)S(1)}, u32[]{:S(2)}, u32[]{:S(2)}) %collective-permute-start.37) | collective-permute-done | bytes 458784 | tf_op jit(solution)/shard_map/ppermute | solution.py:540
  149.3 1.6 collective-permute-start.45
  151.8 2.0 %collective-permute-start.41 = (bf16[96,1024]{1,0:T(8,128)(2,1)S(1)}, bf16[96,1024]{1,0:T(8,128)(2,1)S(1)}, u32[]{:S(2)}, u32[]{:S(2)}) collective-permute-start(bf16[96,1024]{1,0:T(8,128)(2,1)S(1)} %shard_map.262.refs_0_), channel_id=1, source_target_pairs={{0,1},{1,0},{2,3},{3,2},{4,5},{5,4},{6,7},{7,6},{8,9},{9,8},{10,11... | collective-permute-start | bytes 589832 | tf_op jit(solution)/shard_map/ppermute | solution.py:535
  153.8 8.5 %collective-permute-done.42.refs_2_ = bf16[96,1024]{1,0:T(8,128)(2,1)S(1)} collective-permute-done((bf16[96,1024]{1,0:T(8,128)(2,1)S(1)}, bf16[96,1024]{1,0:T(8,128)(2,1)S(1)}, u32[]{:S(2)}, u32[]{:S(2)}) %collective-permute-start.42) | collective-permute-done | bytes 196640 | tf_op jit(solution)/shard_map/ppermute | solution.py:535
  162.4 2.1 %collective-permute-start.44 = (bf16[48,1024]{1,0:T(8,128)(2,1)S(1)}, bf16[48,1024]{1,0:T(8,128)(2,1)S(1)}, u32[]{:S(2)}, u32[]{:S(2)}) collective-permute-start(bf16[48,1024]{1,0:T(8,128)(2,1)S(1)} %slice.100), channel_id=1, source_target_pairs={{0,2},{1,3},{2,0},{3,1},{4,6},{5,7},{6,4},{7,5},{8,10},{9,11},{10,... | collective-permute-start | bytes 294920 | tf_op jit(solution)/shard_map/ppermute | solution.py:535
  164.5 0.8 shard_map.266
  166.0 3.9 %collective-permute-start.46 = (f32[8,128]{1,0:T(8,128)S(1)}, f32[8,128]{1,0:T(8,128)S(1)}, u32[]{:S(2)}, u32[]{:S(2)}) collective-permute-start(f32[8,128]{1,0:T(8,128)S(1)} %get-tuple-element.195), channel_id=1, source_target_pairs={{0,1},{1,0},{2,3},{3,2},{4,5},{5,4},{6,7},{7,6},{8,9},{9,8},{10,11... | collective-permute-start | bytes 12296 | tf_op jit(solution)/shard_map/ppermute | solution.py:535
  169.9 3.9 %collective-permute-done.46 = f32[8,128]{1,0:T(8,128)S(1)} collective-permute-done((f32[8,128]{1,0:T(8,128)S(1)}, f32[8,128]{1,0:T(8,128)S(1)}, u32[]{:S(2)}, u32[]{:S(2)}) %collective-permute-start.46) | collective-permute-done | bytes 4128 | tf_op jit(solution)/shard_map/ppermute | solution.py:535
  173.8 1.6 collective-permute-start.47
  175.4 0.9 shard_map.263
  176.4 1.5 shard_map.264
  178.3 0.7 shard_map.267
  179.0 1.3 shard_map.265
  (156 shorter events, 10.7 us)
Async XLA Ops:
  1.6 17.0 %collective-permute-start.1 = (bf16[128,1024]{1,0:T(8,128)(2,1)S(1)}, bf16[128,1024]{1,0:T(8,128)(2,1)S(1)}, u32[]{:S(2)}, u32[]{:S(2)}) collective-permute-start(bf16[128,1024]{1,0:T(8,128)(2,1)S(1)} %constant_dynamic-slice_fusion), channel_id=1, source_target_pairs={{0,2},{1,3},{2,0},{3,1},{4,6},{5,7},{6,4},{7,5},{8,10},{9,11},{10,... | collective-permute-start | bytes 786440 | tf_op jit(solution)/shard_map/ppermute | solution.py:535
  5.7 12.9 %collective-permute-start = (bf16[128,1024]{1,0:T(8,128)(2,1)S(1)}, bf16[128,1024]{1,0:T(8,128)(2,1)S(1)}, u32[]{:S(2)}, u32[]{:S(2)}) collective-permute-start(bf16[128,1024]{1,0:T(8,128)(2,1)S(1)} %constant_dynamic-slice_fusion), channel_id=1, source_target_pairs={{0,1},{1,0},{2,3},{3,2},{4,5},{5,4},{6,7},{7,6},{8,9},{9,8},{10,11... | collective-permute-start | bytes 786440 | tf_op jit(solution)/shard_map/ppermute | solution.py:535
  11.2 11.6 %collective-permute-start.6 = (bf16[384,256]{1,0:T(8,128)(2,1)}, bf16[384,256]{1,0:T(8,128)(2,1)S(1)}, u32[]{:S(2)}, u32[]{:S(2)}) collective-permute-start(bf16[384,256]{1,0:T(8,128)(2,1)} %get-tuple-element.115), channel_id=1, source_target_pairs={{0,24},{4,28},{8,16},{12,20},{16,8},{20,12},{24,0},{28,4},{1,25},{... | collective-permute-start | bytes 589832 | tf_op jit(solution)/shard_map/ppermute | solution.py:535
  13.6 9.1 %collective-permute-start.5 = (bf16[384,256]{1,0:T(8,128)(2,1)}, bf16[384,256]{1,0:T(8,128)(2,1)S(1)}, u32[]{:S(2)}, u32[]{:S(2)}) collective-permute-start(bf16[384,256]{1,0:T(8,128)(2,1)} %get-tuple-element.115), channel_id=1, source_target_pairs={{0,16},{4,20},{8,24},{12,28},{16,0},{20,4},{24,8},{28,12},{1,17},{... | collective-permute-start | bytes 589832 | tf_op jit(solution)/shard_map/ppermute | solution.py:535
  14.2 8.5 %collective-permute-start.4 = (bf16[384,256]{1,0:T(8,128)(2,1)}, bf16[384,256]{1,0:T(8,128)(2,1)S(1)}, u32[]{:S(2)}, u32[]{:S(2)}) collective-permute-start(bf16[384,256]{1,0:T(8,128)(2,1)} %get-tuple-element.115), channel_id=1, source_target_pairs={{0,8},{4,12},{8,0},{12,4},{16,24},{20,28},{24,16},{28,20},{1,9},{5... | collective-permute-start | bytes 589832 | tf_op jit(solution)/shard_map/ppermute | solution.py:535
  22.8 2.4 %collective-permute-start.7 = (bf16[1536,256]{1,0:T(8,128)(2,1)S(1)}, bf16[1536,256]{1,0:T(8,128)(2,1)S(1)}, u32[]{:S(2)}, u32[]{:S(2)}) collective-permute-start(bf16[1536,256]{1,0:T(8,128)(2,1)S(1)} %constant_dynamic-update-slice_fusion.refs_0_), channel_id=1, source_target_pairs={{0,4},{4,0},{8,12},{12,8},{16,20},{20,16},{24,28},{28,24},{1,5},{5... | collective-permute-start | bytes 2359304 | tf_op jit(solution)/shard_map/ppermute | solution.py:535
  22.9 7.5 %collective-permute-start.2 = (bf16[64,1024]{1,0:T(8,128)(2,1)S(1)}, bf16[64,1024]{1,0:T(8,128)(2,1)S(1)}, u32[]{:S(2)}, u32[]{:S(2)}) collective-permute-start(bf16[64,1024]{1,0:T(8,128)(2,1)S(1)} %slice.88), channel_id=1, source_target_pairs={{0,1},{1,0},{2,3},{3,2},{4,5},{5,4},{6,7},{7,6},{8,9},{9,8},{10,11... | collective-permute-start | bytes 393224 | tf_op jit(solution)/shard_map/ppermute | solution.py:535
  23.4 9.4 %collective-permute-start.3 = (bf16[64,1024]{1,0:T(8,128)(2,1)S(1)}, bf16[64,1024]{1,0:T(8,128)(2,1)S(1)}, u32[]{:S(2)}, u32[]{:S(2)}) collective-permute-start(bf16[64,1024]{1,0:T(8,128)(2,1)S(1)} %slice.89), channel_id=1, source_target_pairs={{0,2},{1,3},{2,0},{3,1},{4,6},{5,7},{6,4},{7,5},{8,10},{9,11},{10,... | collective-permute-start | bytes 393224 | tf_op jit(solution)/shard_map/ppermute | solution.py:535
  28.2 26.0 %copy-start.11 = (bf16[384,256]{1,0:T(8,128)(2,1)}, bf16[384,256]{1,0:T(8,128)(2,1)S(1)}, u32[]{:S(2)}) copy-start(bf16[384,256]{1,0:T(8,128)(2,1)S(1)} %get-tuple-element.116.refs_0_.refs_1_) | copy-start | bytes 589828
  28.2 24.1 %copy-start.13 = (bf16[256,1024]{1,0:T(8,128)(2,1)S(1)}, bf16[256,1024]{1,0:T(8,128)(2,1)}, u32[]{:S(2)}) copy-start(bf16[256,1024]{1,0:T(8,128)(2,1)} %w0_ref.3) | copy-start | bytes 1572868
  28.2 24.1 %copy-start.25 = (bf16[384,1024]{1,0:T(8,128)(2,1)S(1)}, bf16[384,1024]{1,0:T(8,128)(2,1)}, u32[]{:S(2)}) copy-start(bf16[384,1024]{1,0:T(8,128)(2,1)} %x_ref.5) | copy-start | bytes 2359300
  28.2 24.1 %copy-start.31 = (f32[1024]{0:T(1024)S(1)}, f32[1024]{0:T(1024)}, u32[]{:S(2)}) copy-start(f32[1024]{0:T(1024)} %param.24) | copy-start | bytes 12292
  33.0 19.3 %collective-permute-start.8 = (bf16[3,128,1024]{2,1,0:T(8,128)(2,1)S(1)}, bf16[3,128,1024]{2,1,0:T(8,128)(2,1)S(1)}, u32[]{:S(2)}, u32[]{:S(2)}) collective-permute-start(bf16[3,128,1024]{2,1,0:T(8,128)(2,1)S(1)} %pad_maximum_fusion.wm_ref), channel_id=1, source_target_pairs={{0,4},{4,0},{8,12},{12,8},{16,20},{20,16},{24,28},{28,24},{1,5},{5... | collective-permute-start | bytes 2359304 | tf_op jit(solution)/shard_map/ppermute | solution.py:535
  33.1 11.2 %collective-permute-start.10 = (bf16[384,256]{1,0:T(8,128)(2,1)S(1)}, bf16[384,256]{1,0:T(8,128)(2,1)S(1)}, u32[]{:S(2)}, u32[]{:S(2)}) collective-permute-start(bf16[384,256]{1,0:T(8,128)(2,1)S(1)} %get-tuple-element.116.refs_0_.refs_1_), channel_id=1, source_target_pairs={{0,2},{1,3},{2,0},{3,1},{4,6},{5,7},{6,4},{7,5},{8,10},{9,11},{10,... | collective-permute-start | bytes 589832 | tf_op jit(solution)/shard_map/ppermute | solution.py:535
  33.4 11.2 %collective-permute-start.9 = (bf16[384,256]{1,0:T(8,128)(2,1)S(1)}, bf16[384,256]{1,0:T(8,128)(2,1)S(1)}, u32[]{:S(2)}, u32[]{:S(2)}) collective-permute-start(bf16[384,256]{1,0:T(8,128)(2,1)S(1)} %get-tuple-element.116.refs_0_.refs_1_), channel_id=1, source_target_pairs={{0,1},{1,0},{2,3},{3,2},{4,5},{5,4},{6,7},{7,6},{8,9},{9,8},{10,11... | collective-permute-start | bytes 589832 | tf_op jit(solution)/shard_map/ppermute | solution.py:535
  44.3 10.0 %copy-start.3 = (bf16[384,256]{1,0:T(8,128)(2,1)}, bf16[384,256]{1,0:T(8,128)(2,1)S(1)}, u32[]{:S(2)}) copy-start(bf16[384,256]{1,0:T(8,128)(2,1)S(1)} %collective-permute-done.10.refs_2_.refs_3_) | copy-start | bytes 589828
  44.3 6.6 %collective-permute-start.11 = (bf16[192,256]{1,0:T(8,128)(2,1)S(1)}, bf16[192,256]{1,0:T(8,128)(2,1)S(1)}, u32[]{:S(2)}, u32[]{:S(2)}) collective-permute-start(bf16[192,256]{1,0:T(8,128)(2,1)S(1)} %slice.90), channel_id=1, source_target_pairs={{0,1},{1,0},{2,3},{3,2},{4,5},{5,4},{6,7},{7,6},{8,9},{9,8},{10,11... | collective-permute-start | bytes 294920 | tf_op jit(solution)/shard_map/ppermute | solution.py:535
  44.6 9.7 %copy-start.5 = (bf16[384,256]{1,0:T(8,128)(2,1)}, bf16[384,256]{1,0:T(8,128)(2,1)S(1)}, u32[]{:S(2)}) copy-start(bf16[384,256]{1,0:T(8,128)(2,1)S(1)} %collective-permute-done.9.refs_1_.refs_2_) | copy-start | bytes 589828
  44.6 7.7 %collective-permute-start.12 = (bf16[192,256]{1,0:T(8,128)(2,1)S(1)}, bf16[192,256]{1,0:T(8,128)(2,1)S(1)}, u32[]{:S(2)}, u32[]{:S(2)}) collective-permute-start(bf16[192,256]{1,0:T(8,128)(2,1)S(1)} %slice.91), channel_id=1, source_target_pairs={{0,2},{1,3},{2,0},{3,1},{4,6},{5,7},{6,4},{7,5},{8,10},{9,11},{10,... | collective-permute-start | bytes 294920 | tf_op jit(solution)/shard_map/ppermute | solution.py:535
  61.4 7.4 %collective-permute-start.13 = (bf16[48,1024]{1,0:T(8,128)(2,1)S(1)}, bf16[48,1024]{1,0:T(8,128)(2,1)S(1)}, u32[]{:S(2)}, u32[]{:S(2)}) collective-permute-start(bf16[48,1024]{1,0:T(8,128)(2,1)S(1)} %get-tuple-element.131), channel_id=1, source_target_pairs={{0,1},{1,0},{2,3},{3,2},{4,5},{5,4},{6,7},{7,6},{8,9},{9,8},{10,11... | collective-permute-start | bytes 294920 | tf_op jit(solution)/shard_map/ppermute | solution.py:535
  61.7 7.1 %collective-permute-start.14 = (bf16[48,1024]{1,0:T(8,128)(2,1)S(1)}, bf16[48,1024]{1,0:T(8,128)(2,1)S(1)}, u32[]{:S(2)}, u32[]{:S(2)}) collective-permute-start(bf16[48,1024]{1,0:T(8,128)(2,1)S(1)} %get-tuple-element.132), channel_id=1, source_target_pairs={{0,2},{1,3},{2,0},{3,1},{4,6},{5,7},{6,4},{7,5},{8,10},{9,11},{10,... | collective-permute-start | bytes 294920 | tf_op jit(solution)/shard_map/ppermute | solution.py:535
  68.9 8.2 %collective-permute-start.15 = (bf16[96,1024]{1,0:T(8,128)(2,1)S(1)}, bf16[96,1024]{1,0:T(8,128)(2,1)S(1)}, u32[]{:S(2)}, u32[]{:S(2)}) collective-permute-start(bf16[96,1024]{1,0:T(8,128)(2,1)S(1)} %get-tuple-element.133), channel_id=1, source_target_pairs={{0,1},{1,0},{2,3},{3,2},{4,5},{5,4},{6,7},{7,6},{8,9},{9,8},{10,11... | collective-permute-start | bytes 589832 | tf_op jit(solution)/shard_map/ppermute | solution.py:535
  69.1 9.6 %collective-permute-start.16 = (bf16[96,1024]{1,0:T(8,128)(2,1)S(1)}, bf16[96,1024]{1,0:T(8,128)(2,1)S(1)}, u32[]{:S(2)}, u32[]{:S(2)}) collective-permute-start(bf16[96,1024]{1,0:T(8,128)(2,1)S(1)} %get-tuple-element.134), channel_id=1, source_target_pairs={{0,2},{1,3},{2,0},{3,1},{4,6},{5,7},{6,4},{7,5},{8,10},{9,11},{10,... | collective-permute-start | bytes 589832 | tf_op jit(solution)/shard_map/ppermute | solution.py:535
  71.0 14.9 %collective-permute-start.20 = (bf16[512,3456]{1,0:T(8,128)(2,1)S(1)}, bf16[512,3456]{1,0:T(8,128)(2,1)S(1)}, u32[]{:S(2)}, u32[]{:S(2)}) collective-permute-start(bf16[512,3456]{1,0:T(8,128)(2,1)S(1)} %get-tuple-element.140), channel_id=1, source_target_pairs={{0,4},{4,0},{8,12},{12,8},{16,20},{20,16},{24,28},{28,24},{1,5},{5... | collective-permute-start | bytes 10616840 | tf_op jit(solution)/shard_map/ppermute | solution.py:535
  79.6 9.3 %collective-permute-start.21 = (bf16[96,256]{1,0:T(8,128)(2,1)S(1)}, bf16[96,256]{1,0:T(8,128)(2,1)S(1)}, u32[]{:S(2)}, u32[]{:S(2)}) collective-permute-start(bf16[96,256]{1,0:T(8,128)(2,1)S(1)} %get-tuple-element.145), channel_id=1, source_target_pairs={{0,1},{1,0},{2,3},{3,2},{4,5},{5,4},{6,7},{7,6},{8,9},{9,8},{10,11... | collective-permute-start | bytes 147464 | tf_op jit(solution)/shard_map/ppermute | solution.py:535
  80.1 10.4 %collective-permute-start.22 = (bf16[96,256]{1,0:T(8,128)(2,1)S(1)}, bf16[96,256]{1,0:T(8,128)(2,1)S(1)}, u32[]{:S(2)}, u32[]{:S(2)}) collective-permute-start(bf16[96,256]{1,0:T(8,128)(2,1)S(1)} %get-tuple-element.146), channel_id=1, source_target_pairs={{0,2},{1,3},{2,0},{3,1},{4,6},{5,7},{6,4},{7,5},{8,10},{9,11},{10,... | collective-permute-start | bytes 147464 | tf_op jit(solution)/shard_map/ppermute | solution.py:535
  82.7 9.3 %collective-permute-start.23 = (bf16[96,256]{1,0:T(8,128)(2,1)S(1)}, bf16[96,256]{1,0:T(8,128)(2,1)S(1)}, u32[]{:S(2)}, u32[]{:S(2)}) collective-permute-start(bf16[96,256]{1,0:T(8,128)(2,1)S(1)} %get-tuple-element.147), channel_id=1, source_target_pairs={{0,3},{1,2},{2,1},{3,0},{4,7},{5,6},{6,5},{7,4},{8,11},{9,10},{10,... | collective-permute-start | bytes 147464 | tf_op jit(solution)/shard_map/ppermute | solution.py:535
  85.6 17.8 %collective-permute-start.18 = (bf16[96,1280]{1,0:T(8,128)(2,1)S(1)}, bf16[96,1280]{1,0:T(8,128)(2,1)S(1)}, u32[]{:S(2)}, u32[]{:S(2)}) collective-permute-start(bf16[96,1280]{1,0:T(8,128)(2,1)S(1)} %get-tuple-element.138), channel_id=1, source_target_pairs={{0,2},{1,3},{2,0},{3,1},{4,6},{5,7},{6,4},{7,5},{8,10},{9,11},{10,... | collective-permute-start | bytes 737288 | tf_op jit(solution)/shard_map/ppermute | solution.py:535
  85.9 17.6 %collective-permute-start.17 = (bf16[96,1280]{1,0:T(8,128)(2,1)S(1)}, bf16[96,1280]{1,0:T(8,128)(2,1)S(1)}, u32[]{:S(2)}, u32[]{:S(2)}) collective-permute-start(bf16[96,1280]{1,0:T(8,128)(2,1)S(1)} %get-tuple-element.137), channel_id=1, source_target_pairs={{0,1},{1,0},{2,3},{3,2},{4,5},{5,4},{6,7},{7,6},{8,9},{9,8},{10,11... | collective-permute-start | bytes 737288 | tf_op jit(solution)/shard_map/ppermute | solution.py:535
  89.0 14.5 %collective-permute-start.19 = (bf16[96,1280]{1,0:T(8,128)(2,1)S(1)}, bf16[96,1280]{1,0:T(8,128)(2,1)S(1)}, u32[]{:S(2)}, u32[]{:S(2)}) collective-permute-start(bf16[96,1280]{1,0:T(8,128)(2,1)S(1)} %get-tuple-element.139), channel_id=1, source_target_pairs={{0,3},{1,2},{2,1},{3,0},{4,7},{5,6},{6,5},{7,4},{8,11},{9,10},{10,... | collective-permute-start | bytes 737288 | tf_op jit(solution)/shard_map/ppermute | solution.py:535
  90.5 25.3 %collective-permute-start.30 = (bf16[256,3456]{1,0:T(8,128)(2,1)S(1)}, bf16[256,3456]{1,0:T(8,128)(2,1)S(1)}, u32[]{:S(2)}, u32[]{:S(2)}) collective-permute-start(bf16[256,3456]{1,0:T(8,128)(2,1)S(1)} %slice_add_fusion), channel_id=1, source_target_pairs={{0,8},{4,20},{8,0},{12,28},{16,24},{20,4},{24,16},{28,12},{1,9},{5... | collective-permute-start | bytes 5308424 | tf_op jit(solution)/shard_map/ppermute | solution.py:540
  95.4 18.0 %copy-start.1 = (bf16[384,1024]{1,0:T(8,128)(2,1)S(1)}, bf16[384,1024]{1,0:T(8,128)(2,1)}, u32[]{:S(2)}) copy-start(bf16[384,1024]{1,0:T(8,128)(2,1)} %get-tuple-element.110.h_ref.refs_14_) | copy-start | bytes 2359300
  95.4 18.0 %copy-start.4 = (bf16[384,256]{1,0:T(8,128)(2,1)S(1)}, bf16[384,256]{1,0:T(8,128)(2,1)}, u32[]{:S(2)}) copy-start(bf16[384,256]{1,0:T(8,128)(2,1)} %copy-done.3) | copy-start | bytes 589828
  95.4 18.0 %copy-start.6 = (bf16[384,256]{1,0:T(8,128)(2,1)S(1)}, bf16[384,256]{1,0:T(8,128)(2,1)}, u32[]{:S(2)}) copy-start(bf16[384,256]{1,0:T(8,128)(2,1)} %copy-done.5) | copy-start | bytes 589828
  95.4 18.0 %copy-start.8 = (f32[384,128]{1,0:T(8,128)S(1)}, f32[384,128]{1,0:T(8,128)}, u32[]{:S(2)}) copy-start(f32[384,128]{1,0:T(8,128)} %get-tuple-element.111.cos_ref.refs_5_) | copy-start | bytes 589828
  95.4 18.0 %copy-start.10 = (f32[384,128]{1,0:T(8,128)S(1)}, f32[384,128]{1,0:T(8,128)}, u32[]{:S(2)}) copy-start(f32[384,128]{1,0:T(8,128)} %get-tuple-element.112.sin_ref.refs_6_) | copy-start | bytes 589828
  95.4 18.0 %copy-start.12 = (bf16[384,256]{1,0:T(8,128)(2,1)S(1)}, bf16[384,256]{1,0:T(8,128)(2,1)}, u32[]{:S(2)}) copy-start(bf16[384,256]{1,0:T(8,128)(2,1)} %copy-done.11) | copy-start | bytes 589828
  95.4 18.0 %copy-start.15 = (bf16[192,256]{1,0:T(8,128)(2,1)S(1)}, bf16[192,256]{1,0:T(8,128)(2,1)}, u32[]{:S(2)}) copy-start(bf16[192,256]{1,0:T(8,128)(2,1)} %copy-done.14) | copy-start | bytes 294916
  95.5 18.0 %copy-start.17 = (bf16[192,256]{1,0:T(8,128)(2,1)S(1)}, bf16[192,256]{1,0:T(8,128)(2,1)}, u32[]{:S(2)}) copy-start(bf16[192,256]{1,0:T(8,128)(2,1)} %copy-done.16) | copy-start | bytes 294916
  103.5 5.2 %collective-permute-start.26 = (bf16[1536,256]{1,0:T(8,128)(2,1)S(1)}, bf16[1536,256]{1,0:T(8,128)(2,1)S(1)}, u32[]{:S(2)}, u32[]{:S(2)}) collective-permute-start(bf16[1536,256]{1,0:T(8,128)(2,1)S(1)} %get-tuple-element.156), channel_id=1, source_target_pairs={{0,4},{4,0},{8,12},{12,8},{16,20},{20,16},{24,28},{28,24},{1,5},{5... | collective-permute-start | bytes 2359304 | tf_op jit(solution)/shard_map/ppermute | solution.py:535
  103.6 14.9 %collective-permute-start.25 = (bf16[96,1024]{1,0:T(8,128)(2,1)S(1)}, bf16[96,1024]{1,0:T(8,128)(2,1)S(1)}, u32[]{:S(2)}, u32[]{:S(2)}) collective-permute-start(bf16[96,1024]{1,0:T(8,128)(2,1)S(1)} %get-tuple-element.153.refs_0_), channel_id=1, source_target_pairs={{0,2},{1,3},{2,0},{3,1},{4,6},{5,7},{6,4},{7,5},{8,10},{9,11},{10,... | collective-permute-start | bytes 589832 | tf_op jit(solution)/shard_map/ppermute | solution.py:535
  108.7 10.6 %collective-permute-start.24 = (bf16[96,1024]{1,0:T(8,128)(2,1)S(1)}, bf16[96,1024]{1,0:T(8,128)(2,1)S(1)}, u32[]{:S(2)}, u32[]{:S(2)}) collective-permute-start(bf16[96,1024]{1,0:T(8,128)(2,1)S(1)} %get-tuple-element.153.refs_0_), channel_id=1, source_target_pairs={{0,1},{1,0},{2,3},{3,2},{4,5},{5,4},{6,7},{7,6},{8,9},{9,8},{10,11... | collective-permute-start | bytes 589832 | tf_op jit(solution)/shard_map/ppermute | solution.py:535
  108.8 11.9 %collective-permute-start.29 = (bf16[384,256]{1,0:T(8,128)(2,1)S(1)}, bf16[384,256]{1,0:T(8,128)(2,1)S(1)}, u32[]{:S(2)}, u32[]{:S(2)}) collective-permute-start(bf16[384,256]{1,0:T(8,128)(2,1)S(1)} %get-tuple-element.209), channel_id=1, source_target_pairs={{0,24},{4,28},{8,16},{12,20},{16,8},{20,12},{24,0},{28,4},{1,25},{... | collective-permute-start | bytes 589832 | tf_op jit(solution)/shard_map/ppermute | solution.py:535
  113.4 10.3 %collective-permute-start.28 = (bf16[384,256]{1,0:T(8,128)(2,1)S(1)}, bf16[384,256]{1,0:T(8,128)(2,1)S(1)}, u32[]{:S(2)}, u32[]{:S(2)}) collective-permute-start(bf16[384,256]{1,0:T(8,128)(2,1)S(1)} %get-tuple-element.210), channel_id=1, source_target_pairs={{0,16},{4,20},{8,24},{12,28},{16,0},{20,4},{24,8},{28,12},{1,17},{... | collective-permute-start | bytes 589832 | tf_op jit(solution)/shard_map/ppermute | solution.py:535
  115.8 7.9 %collective-permute-start.27 = (bf16[384,256]{1,0:T(8,128)(2,1)S(1)}, bf16[384,256]{1,0:T(8,128)(2,1)S(1)}, u32[]{:S(2)}, u32[]{:S(2)}) collective-permute-start(bf16[384,256]{1,0:T(8,128)(2,1)S(1)} %get-tuple-element.211), channel_id=1, source_target_pairs={{0,8},{4,12},{8,0},{12,4},{16,24},{20,28},{24,16},{28,20},{1,9},{5... | collective-permute-start | bytes 589832 | tf_op jit(solution)/shard_map/ppermute | solution.py:535
  118.6 2.0 %collective-permute-start.31 = (bf16[512,512]{1,0:T(8,128)(2,1)S(1)}, bf16[512,512]{1,0:T(8,128)(2,1)S(1)}, u32[]{:S(2)}, u32[]{:S(2)}) collective-permute-start(bf16[512,512]{1,0:T(8,128)(2,1)S(1)} %get-tuple-element.164), channel_id=1, source_target_pairs={{0,4},{4,0},{8,12},{12,8},{16,20},{20,16},{24,28},{28,24},{1,5},{5... | collective-permute-start | bytes 1572872 | tf_op jit(solution)/shard_map/ppermute | solution.py:535
  125.8 5.3 %collective-permute-start.32 = (bf16[48,1024]{1,0:T(8,128)(2,1)S(1)}, bf16[48,1024]{1,0:T(8,128)(2,1)S(1)}, u32[]{:S(2)}, u32[]{:S(2)}) collective-permute-start(bf16[48,1024]{1,0:T(8,128)(2,1)S(1)} %get-tuple-element.171), channel_id=1, source_target_pairs={{0,1},{1,0},{2,3},{3,2},{4,5},{5,4},{6,7},{7,6},{8,9},{9,8},{10,11... | collective-permute-start | bytes 294920 | tf_op jit(solution)/shard_map/ppermute | solution.py:535
  126.8 7.5 %collective-permute-start.33 = (bf16[48,1024]{1,0:T(8,128)(2,1)S(1)}, bf16[48,1024]{1,0:T(8,128)(2,1)S(1)}, u32[]{:S(2)}, u32[]{:S(2)}) collective-permute-start(bf16[48,1024]{1,0:T(8,128)(2,1)S(1)} %get-tuple-element.172), channel_id=1, source_target_pairs={{0,2},{1,3},{2,0},{3,1},{4,6},{5,7},{6,4},{7,5},{8,10},{9,11},{10,... | collective-permute-start | bytes 294920 | tf_op jit(solution)/shard_map/ppermute | solution.py:535
  134.3 5.2 %collective-permute-start.36 = (bf16[512,384]{1,0:T(8,128)(2,1)S(1)}, bf16[512,384]{1,0:T(8,128)(2,1)S(1)}, u32[]{:S(2)}, u32[]{:S(2)}) collective-permute-start(bf16[512,384]{1,0:T(8,128)(2,1)S(1)} %get-tuple-element.180), channel_id=1, source_target_pairs={{0,4},{4,0},{8,12},{12,8},{16,20},{20,16},{24,28},{28,24},{1,5},{5... | collective-permute-start | bytes 1179656 | tf_op jit(solution)/shard_map/ppermute | solution.py:535
  134.4 16.8 %collective-permute-start.38 = (bf16[96,1024]{1,0:T(8,128)(2,1)S(1)}, bf16[96,1024]{1,0:T(8,128)(2,1)S(1)}, u32[]{:S(2)}, u32[]{:S(2)}) collective-permute-start(bf16[96,1024]{1,0:T(8,128)(2,1)S(1)} %get-tuple-element.173), channel_id=1, source_target_pairs={{0,1},{1,0},{2,3},{3,2},{4,5},{5,4},{6,7},{7,6},{8,9},{9,8},{10,11... | collective-permute-start | bytes 589832 | tf_op jit(solution)/shard_map/ppermute | solution.py:535
  134.5 14.8 %collective-permute-start.35 = (bf16[48,1024]{1,0:T(8,128)(2,1)S(1)}, bf16[48,1024]{1,0:T(8,128)(2,1)S(1)}, u32[]{:S(2)}, u32[]{:S(2)}) collective-permute-start(bf16[48,1024]{1,0:T(8,128)(2,1)S(1)} %slice.83), channel_id=1, source_target_pairs={{0,2},{1,3},{2,0},{3,1},{4,6},{5,7},{6,4},{7,5},{8,10},{9,11},{10,... | collective-permute-start | bytes 294920 | tf_op jit(solution)/shard_map/ppermute | solution.py:535
  136.8 12.5 %collective-permute-start.34 = (bf16[48,1024]{1,0:T(8,128)(2,1)S(1)}, bf16[48,1024]{1,0:T(8,128)(2,1)S(1)}, u32[]{:S(2)}, u32[]{:S(2)}) collective-permute-start(bf16[48,1024]{1,0:T(8,128)(2,1)S(1)} %slice.82), channel_id=1, source_target_pairs={{0,1},{1,0},{2,3},{3,2},{4,5},{5,4},{6,7},{7,6},{8,9},{9,8},{10,11... | collective-permute-start | bytes 294920 | tf_op jit(solution)/shard_map/ppermute | solution.py:535
  137.0 14.3 %collective-permute-start.39 = (bf16[96,1024]{1,0:T(8,128)(2,1)S(1)}, bf16[96,1024]{1,0:T(8,128)(2,1)S(1)}, u32[]{:S(2)}, u32[]{:S(2)}) collective-permute-start(bf16[96,1024]{1,0:T(8,128)(2,1)S(1)} %get-tuple-element.187), channel_id=1, source_target_pairs={{0,2},{1,3},{2,0},{3,1},{4,6},{5,7},{6,4},{7,5},{8,10},{9,11},{10,... | collective-permute-start | bytes 589832 | tf_op jit(solution)/shard_map/ppermute | solution.py:535
  140.0 11.3 %copy-start.32 = (f32[1024]{0:T(1024)S(1)}, f32[1024]{0:T(1024)}, u32[]{:S(2)}) copy-start(f32[1024]{0:T(1024)} %param.17) | copy-start | bytes 12292
  140.0 8.5 %collective-permute-start.37 = (bf16[256,896]{1,0:T(8,128)(2,1)S(1)}, bf16[256,896]{1,0:T(8,128)(2,1)S(1)}, u32[]{:S(2)}, u32[]{:S(2)}) collective-permute-start(bf16[256,896]{1,0:T(8,128)(2,1)S(1)} %get-tuple-element.182), channel_id=1, source_target_pairs={{0,8},{4,20},{8,0},{12,28},{16,24},{20,4},{24,16},{28,12},{1,9},{5... | collective-permute-start | bytes 1376264 | tf_op jit(solution)/shard_map/ppermute | solution.py:540
  148.5 27.8 %collective-permute-start.40 = (bf16[128,3456]{1,0:T(8,128)(2,1)S(1)}, bf16[128,3456]{1,0:T(8,128)(2,1)S(1)}, u32[]{:S(2)}, u32[]{:S(2)}) collective-permute-start(bf16[128,3456]{1,0:T(8,128)(2,1)S(1)} %get-tuple-element.190), channel_id=1, source_target_pairs={{0,16},{4,12},{8,24},{12,4},{16,0},{20,28},{24,8},{28,20},{1,17},{... | collective-permute-start | bytes 2654216 | tf_op jit(solution)/shard_map/ppermute | solution.py:540
  149.3 15.3 %collective-permute-start.45 = (bf16[128,896]{1,0:T(8,128)(2,1)S(1)}, bf16[128,896]{1,0:T(8,128)(2,1)S(1)}, u32[]{:S(2)}, u32[]{:S(2)}) collective-permute-start(bf16[128,896]{1,0:T(8,128)(2,1)S(1)} %get-tuple-element.194), channel_id=1, source_target_pairs={{0,16},{4,12},{8,24},{12,4},{16,0},{20,28},{24,8},{28,20},{1,17},{... | collective-permute-start | bytes 688136 | tf_op jit(solution)/shard_map/ppermute | solution.py:540
  151.5 10.8 %collective-permute-start.42 = (bf16[96,1024]{1,0:T(8,128)(2,1)S(1)}, bf16[96,1024]{1,0:T(8,128)(2,1)S(1)}, u32[]{:S(2)}, u32[]{:S(2)}) collective-permute-start(bf16[96,1024]{1,0:T(8,128)(2,1)S(1)} %shard_map.262.refs_0_), channel_id=1, source_target_pairs={{0,2},{1,3},{2,0},{3,1},{4,6},{5,7},{6,4},{7,5},{8,10},{9,11},{10,... | collective-permute-start | bytes 589832 | tf_op jit(solution)/shard_map/ppermute | solution.py:535
  151.8 10.6 %collective-permute-start.41 = (bf16[96,1024]{1,0:T(8,128)(2,1)S(1)}, bf16[96,1024]{1,0:T(8,128)(2,1)S(1)}, u32[]{:S(2)}, u32[]{:S(2)}) collective-permute-start(bf16[96,1024]{1,0:T(8,128)(2,1)S(1)} %shard_map.262.refs_0_), channel_id=1, source_target_pairs={{0,1},{1,0},{2,3},{3,2},{4,5},{5,4},{6,7},{7,6},{8,9},{9,8},{10,11... | collective-permute-start | bytes 589832 | tf_op jit(solution)/shard_map/ppermute | solution.py:535
  162.3 16.7 %collective-permute-start.43 = (bf16[48,1024]{1,0:T(8,128)(2,1)S(1)}, bf16[48,1024]{1,0:T(8,128)(2,1)S(1)}, u32[]{:S(2)}, u32[]{:S(2)}) collective-permute-start(bf16[48,1024]{1,0:T(8,128)(2,1)S(1)} %slice.99), channel_id=1, source_target_pairs={{0,1},{1,0},{2,3},{3,2},{4,5},{5,4},{6,7},{7,6},{8,9},{9,8},{10,11... | collective-permute-start | bytes 294920 | tf_op jit(solution)/shard_map/ppermute | solution.py:535
  162.4 16.6 %collective-permute-start.44 = (bf16[48,1024]{1,0:T(8,128)(2,1)S(1)}, bf16[48,1024]{1,0:T(8,128)(2,1)S(1)}, u32[]{:S(2)}, u32[]{:S(2)}) collective-permute-start(bf16[48,1024]{1,0:T(8,128)(2,1)S(1)} %slice.100), channel_id=1, source_target_pairs={{0,2},{1,3},{2,0},{3,1},{4,6},{5,7},{6,4},{7,5},{8,10},{9,11},{10,... | collective-permute-start | bytes 294920 | tf_op jit(solution)/shard_map/ppermute | solution.py:535
  165.3 13.0 %collective-permute-start.48 = (bf16[256,128]{1,0:T(8,128)(2,1)S(1)}, bf16[256,128]{1,0:T(8,128)(2,1)S(1)}, u32[]{:S(2)}, u32[]{:S(2)}) collective-permute-start(bf16[256,128]{1,0:T(8,128)(2,1)S(1)} %get-tuple-element.196), channel_id=1, source_target_pairs={{0,0},{1,8},{2,16},{3,24},{4,4},{5,12},{6,20},{7,28},{8,1},{9,9},{... | collective-permute-start | bytes 196616 | tf_op jit(solution)/shard_map/ppermute | solution.py:826
  166.0 7.8 %collective-permute-start.46 = (f32[8,128]{1,0:T(8,128)S(1)}, f32[8,128]{1,0:T(8,128)S(1)}, u32[]{:S(2)}, u32[]{:S(2)}) collective-permute-start(f32[8,128]{1,0:T(8,128)S(1)} %get-tuple-element.195), channel_id=1, source_target_pairs={{0,1},{1,0},{2,3},{3,2},{4,5},{5,4},{6,7},{7,6},{8,9},{9,8},{10,11... | collective-permute-start | bytes 12296 | tf_op jit(solution)/shard_map/ppermute | solution.py:535
  173.8 4.5 %collective-permute-start.47 = (f32[8,128]{1,0:T(8,128)S(1)}, f32[8,128]{1,0:T(8,128)S(1)}, u32[]{:S(2)}, u32[]{:S(2)}) collective-permute-start(f32[8,128]{1,0:T(8,128)S(1)} %add.40.a_ref), channel_id=1, source_target_pairs={{0,2},{1,3},{2,0},{3,1},{4,6},{5,7},{6,4},{7,5},{8,10},{9,11},{10,... | collective-permute-start | bytes 12296 | tf_op jit(solution)/shard_map/ppermute | solution.py:535
  (25 other events, 106.4 us)

commit v5 on v4

--- a/solution.py
+++ b/solution.py
@@ -308,12 +308,17 @@
     store_around(acc_ref, dh_refs)
 
 
-def reduce_kernel(one_ref, two_ref, got_one_ref, got_two_ref, to_one_ref, to_two_ref):
+def reduce_kernel(one_ref, two_ref, got_one_ref, got_two_ref, *refs):
+    to_one_ref, to_two_ref = refs[-2:]
     half = got_one_ref.shape[0]
+    own = 2 * half
     to_one_ref[:half, :] = one_ref[:half, :]
-    to_one_ref[half:, :] = (one_ref[half:, :].astype(f32) + got_two_ref[...].astype(f32)).astype(bf16)
+    to_one_ref[half:own, :] = (one_ref[half:, :].astype(f32) + got_two_ref[...].astype(f32)).astype(bf16)
     to_two_ref[:half, :] = (two_ref[:half, :].astype(f32) + got_one_ref[...].astype(f32)).astype(bf16)
-    to_two_ref[half:, :] = two_ref[half:, :]
+    to_two_ref[half:own, :] = two_ref[half:, :]
+    if len(refs) > 2:
+        to_one_ref[own:, :] = refs[1][:half, :]
+        to_two_ref[own:, :] = refs[0][half:, :]
 
 
 def mid_kernel(g_ref, y_ref, gain_ref, w0_ref, wm_ref, wp_ref, *refs):
@@ -418,24 +423,27 @@
     gains_ref[2 * lots + 2 :, :] = jnp.zeros((gains_ref.shape[0] - 2 * lots - 2, 128), f32)
     if near:
         odd_ref, even_ref, hp_ref = refs[:3]
-        mine = lax.axis_index("ctx")
         for parity, out_ref in ((1, odd_ref), (0, even_ref)):
             gather_columns(parity, h_ref, hp_ref)
-            out_ref[:, :256] = dot(hp_ref[...], low_ref[...], TN).astype(bf16)
-            for at, chip in enumerate(block_order(parity)):
-                block = jnp.bitwise_xor(mine, 2 * chip + parity)
-                out_ref[128 * at : 128 * at + 128, 256:] = parted(gain_columns(gains_ref, block, lots))
+            out_ref[...] = dot(hp_ref[...], low_ref[...], TN).astype(bf16)
 
 
 def last_kernel(x_ref, dy_ref, gain_ref, *refs):
     dh_refs, out_ref = refs[:3], refs[3]
-    dh = sum(ref[...].astype(f32) for ref in dh_refs)
+    dh = sum(ref[: dy_ref.shape[0], :].astype(f32) for ref in dh_refs)
     x = x_ref[quarter(0, dy_ref.shape[0]), :].astype(f32)
     inverse = row_norm(x)
     z = x * inverse
     e = dh * gain_ref[...]
     inner = jnp.mean(e * z, axis=1, keepdims=True)
     out_ref[...] = (dy_ref[...] + inverse * (e - z * inner)).astype(bf16)
+
+
+def layer_join_kernel(own_ref, one_ref, two_ref, low_ref, high_ref, out_ref):
+    own = own_ref.shape[0]
+    for k, ref in enumerate((own_ref, one_ref, two_ref)):
+        out_ref[quarter(k, own), :] = ref[...]
+    out_ref[quarter(3, own), :] = jnp.concatenate([low_ref[own:, :], high_ref[own:, :]], axis=0)
 
 
 def join_kernel(*refs):
@@ -477,57 +485,47 @@
         out_ref[...] = total.T if i == 2 else total
 
 
-def joined(x):
-    x = x.astype(f32)
-    return x + pltpu.roll(x, 64, 1)
-
-
-def parted(x):
-    high = x.astype(bf16).astype(f32)
-    return jnp.where(lanes(x) < 64, high, x - high).astype(bf16)
-
-
-def gain_columns(gains_ref, block, lots):
-    row = lambda i: gains_ref[pl.ds(i, 1), :]
-    heads = jnp.where(lanes(row(0)) < 64, row(2 * lots), row(2 * lots + 1))
-    rows = jnp.concatenate([row(block), row(lots + block), heads, jnp.zeros((125, 128), f32)], axis=0)
-    total = rows.T
-    return total + pltpu.roll(total, 64, 1)
-
-
 def attn_grad_chip_kernel(q_ref, q_got_ref, kv_ref, kv_got_ref, here_ref, send_ref):
     half = here_ref.shape[0]
     for i, out_ref in enumerate((here_ref, send_ref)):
         row = slice(half * i, half * (i + 1))
         out_ref[:, :512] = (q_ref[row, :].astype(f32) + q_got_ref[row, :].astype(f32)).astype(bf16)
-        out_ref[:, 512:768] = (kv_ref[row, :256].astype(f32) + kv_got_ref[row, :256].astype(f32)).astype(bf16)
-        out_ref[:, 768:] = parted(joined(kv_ref[row, 256:]) + joined(kv_got_ref[row, 256:]))
+        out_ref[:, 512:] = (kv_ref[row, :].astype(f32) + kv_got_ref[row, :].astype(f32)).astype(bf16)
 
 
 def attn_grad_pass_kernel(keep_ref, got_ref, here_ref, send_ref):
     half = here_ref.shape[0]
     for i, out_ref in enumerate((here_ref, send_ref)):
         row = slice(half * i, half * (i + 1))
-        out_ref[:, :768] = (keep_ref[row, :768].astype(f32) + got_ref[row, :768].astype(f32)).astype(bf16)
-        out_ref[:, 768:] = parted(joined(keep_ref[row, 768:]) + joined(got_ref[row, 768:]))
-
-
-def attn_grad_sum_kernel(keep_ref, got_ref, q_ref, k_ref, v_ref, o_ref, gains_ref):
-    total = keep_ref[:, :768].astype(f32) + got_ref[:, :768].astype(f32)
+        out_ref[...] = (keep_ref[row, :].astype(f32) + got_ref[row, :].astype(f32)).astype(bf16)
+
+
+def attn_grad_sum_kernel(keep_ref, got_ref, q_ref, k_ref, v_ref, o_ref):
+    total = keep_ref[...].astype(f32) + got_ref[...].astype(f32)
     q_ref[...] = total[:, :256]
     o_ref[...] = total[:, 256:512].T.astype(bf16)
     k_ref[...] = total[:, 512:640]
     v_ref[...] = total[:, 640:]
-    gains_ref[...] = (joined(keep_ref[:, 768:]) + joined(got_ref[:, 768:])).T[:8]
 
 
 def gain_kernel(block, a_ref, b_ref, w_ref, one_ref, two_ref, q_ref, k_ref, out_ref):
     out_ref[...] = w_ref[...].astype(f32)
     total = a_ref[...] + b_ref[...]
-    one_ref[...] = total[0:1, :block]
-    two_ref[...] = total[1:2, :block]
-    q_ref[...] = total[2:3, :64]
-    k_ref[...] = total[2:3, 64:]
+    lots = (total.shape[0] - 8) // 2
+    q_ref[...] = total[2 * lots : 2 * lots + 1, :64]
+    k_ref[...] = total[2 * lots + 1 : 2 * lots + 2, :64]
+    mine = lax.axis_index("ctx")
+    row = mine * block // 128
+    at = lax.broadcasted_iota(jnp.int32, total.shape, 0)
+    for i, ref in enumerate((one_ref, two_ref)):
+        picked = jnp.sum(jnp.where(at == row + lots * i, total, 0.0), axis=0, keepdims=True)
+        if block < 128:
+            spots = lax.broadcasted_iota(jnp.int32, (128, block), 0)
+            want = lax.broadcasted_iota(jnp.int32, (128, block), 1) + mine * block % 128
+            picked = lax.dot_general(
+                picked, (spots == want).astype(f32), NN, precision=lax.Precision.HIGHEST
+            )
+        ref[...] = picked
 
 
 def swap(x, axis, k):
@@ -584,15 +582,15 @@
         from_one, from_two = lax.optimization_barrier((one, two, *first))[:2] if first else (one, two)
         return [x, one, two, swap(from_two[:half], "tp", 1), swap(from_one[half:], "tp", 2)]
 
-    def reduce(parts, *first):
+    def reduce(parts, *first, riders=()):
         here, one, two, far_low, far_high = parts
         got_one, got_two = swap(far_low, "tp", 1), swap(far_high, "tp", 2)
         if first:
             one = after(one, *first)
         to_one, to_two = call(
             reduce_kernel,
-            [one, two, got_one, got_two],
-            [shape(one.shape, bf16)] * 2,
+            [one, two, got_one, got_two, *riders],
+            [shape((own + (own // 2 if riders else 0), width), bf16)] * 2,
             work=1,
         )
         return [here, swap(to_one, "tp", 1), swap(to_two, "tp", 2)], to_one
@@ -752,47 +750,47 @@
         ],
         [shape((rows, 256), bf16), shape((gain_rows, 128), f32)]
         + quarters
-        + ([shape((4 * block, 384), bf16)] * 2 if near else []),
+        + ([shape((4 * block, 256), bf16)] * 2 if near else []),
         ([ordered] if near else []) + [pltpu.VMEM((rows, width), f32)],
     )
     kv_pre_low, gains = got[:2]
     one_parts = got[2:7]
-    one_got, token = reduce(one_parts)
+    gains = gains + swap(gains, "tp", 1)
+    one_got, token = reduce(one_parts, gains, riders=(layer_one, layer_two))
+    gains = gains + swap(gains, "tp", 2)
+    mixed_grad = after(mixed_grad, gains)
     if near:
         kv_odd, kv_even = got[7:]
         kv_odd = after(kv_odd, token)
         attn_here, attn_send = call(
             attn_grad_chip_kernel,
             [q_even, q_other, kv_even, swap(kv_odd, "ctx", 1)],
-            [shape((2 * block, 896), bf16)] * 2,
+            [shape((2 * block, 768), bf16)] * 2,
             work=1,
         )
         attn_here, attn_send = call(
             attn_grad_pass_kernel,
             [attn_here, swap_across(attn_send, 0)],
-            [shape((block, 896), bf16)] * 2,
+            [shape((block, 768), bf16)] * 2,
             work=1,
         )
         mixed_grad = after(mixed_grad, attn_here)
-    far_one, far_two, _ = lax.optimization_barrier((layer_one, layer_two, token))
-    half = own // 2
-    layer_parts = [
-        layer_own,
-        layer_one,
-        layer_two,
-        swap(far_two[:half], "tp", 1),
-        swap(far_one[half:], "tp", 2),
-    ]
-    mixed_grad = after(mixed_grad, *layer_parts[3:])
     input_own = call(
         last_kernel,
         [hidden_in, mixed_grad, gain_one, *one_got],
         [shape((own, width), bf16)],
     )[0]
-    input_parts = gather(input_own)
-    layer_parts[4] = after(layer_parts[4], input_own)
+    gains = after(gains, input_own)
+    gains = gains + swap(gains, "ctx", 1)
+    gains = gains + swap(gains, "ctx", 2)
+    input_parts = gather(input_own, gains)
+    steps = [1 << i for i in range(2, (n_ctx - 1).bit_length())]
+    for k in steps[:-1]:
+        gains = gains + swap(gains, "ctx", k)
+    last_gains = swap(gains, "ctx", steps[-1])
+    layer_parts = [after(layer_own, input_own), layer_one, layer_two, *one_got[1:]]
     layer_out = call(
-        join_kernel,
+        layer_join_kernel,
         layer_parts,
         [shape((rows, width), bf16)],
         work=1,
@@ -806,7 +804,7 @@
             [shape((block, units), f32), shape((block, units), f32), shape((units, block), f32)],
             work=1,
         )
-        query_w, key_w, value_w, out_w, gains = call(
+        query_w, key_w, value_w, out_w = call(
             attn_grad_sum_kernel,
             [after(attn_here, input_parts[1]), swap_across(attn_send, 1)],
             [
@@ -814,7 +812,6 @@
                 shape((block, 128), f32),
                 shape((block, 128), f32),
                 shape((256, block), bf16),
-                shape((8, 128), f32),
             ],
             work=1,
         )
@@ -839,18 +836,9 @@
         kv_w = scatter(h_one, kv_pre_low)
         key_w, value_w = kv_w[:, :128], kv_w[:, 128:]
 
-    if not near:
-        gains = lax.psum(gains, "ctx")
-        cut = lambda row: lax.dynamic_slice_in_dim(
-            gains[row : row + lots].reshape(width), mine * block, block, 0
-        )
-        heads = jnp.concatenate([gains[2 * lots, :64], gains[2 * lots + 1, :64]])
-        gains = jnp.stack([jnp.pad(cut(0), (0, 128 - block)), jnp.pad(cut(lots), (0, 128 - block)), heads])
-        gains = jnp.pad(gains, ((0, 5), (0, 0)))
-    gains = gains + swap(gains, "tp", 1)
     gain_one_sum, gain_two_sum, q_gain_sum, k_gain_sum, out_w = call(
         functools.partial(gain_kernel, block),
-        [gains, swap(gains, "tp", 2), out_w],
+        [gains, last_gains, out_w],
         [shape((1, block), f32)] * 2 + [shape((1, 64), f32)] * 2 + [shape(out_w.shape, f32)],
         work=1,
     )

time: 181 us -> 177 us (0.978)
  waiting for transfers between devices: 73.5 us -> 68.4 us
    ppermute x44 -> x45, waiting for transfers between devices: 66.1 us -> 59.1 us  [swap(): return lax.ppermute(x, axis, [(i, i ^ k) for i in range(size)])]
    ppermute x4, waiting for transfers between devices: 7.46 us -> 9.29 us  [swap_across(): lax.ppermute(x, 'ctx', [(i, i ^ 2 << (i + step) % 2) for i in range(size)])]
    ppermute x44 -> x45, starting transfers between devices: 56.9 us -> 57.7 us  [swap(): return lax.ppermute(x, axis, [(i, i ^ k) for i in range(size)])]
  transfers between devices with their start and end apart: 49 -> 50, of which waited for: 22 -> 22; matrix products, arithmetic and copies ran while one was open for 1% -> 1% of each run, Pallas kernels for 14% -> 14%
where the time goes in v5:
time: 177 us; the launch traced here: 176 us
  waiting for transfers between devices  68.4 us (39%)
  starting transfers between devices  62.9 us (36%)
  Pallas kernels  35.5 us (20%)
  local copies, waits for them, and re-layouts  6.51 us (4%)
    ppermute x45, waiting for transfers between devices, swap(): return lax.ppermute(x, axis, [(i, i ^ k) for i in range(size)])  59.1 us
    ppermute x45, starting transfers between devices, swap(): return lax.ppermute(x, axis, [(i, i ^ k) for i in range(size)])  57.7 us
    pallas_call x22, Pallas kernels, call(): pl.pallas_call(body, out_shape=outs, in_specs=in_specs, out_specs=out_spe...  35.5 us
    ppermute x4, waiting for transfers between devices, swap_across(): lax.ppermute(x, 'ctx', [(i, i ^ 2 << (i + step) % 2) for i in range(size)])  9.29 us
    unnamed x83, local copies, waits for them, and re-layouts  5.35 us
    ppermute x4, starting transfers between devices, swap_across(): lax.ppermute(x, 'ctx', [(i, i ^ 2 << (i + step) % 2) for i in range(size)])  4.59 us
  transfers between devices with their start and end apart: 50, of which 22 were waited for; matrix products, arithmetic and copies ran while one was open for 1% of the time, Pallas kernels for 14%

profile of v5, /device:TPU:0, one launch (start us, length us, event | category | flops | bytes accessed | tf_op | source)
XLA Modules:
  0.0 175.7 jit_solution(9274879842953689151)
XLA Ops:
  0.7 1.0 constant_dynamic-slice_fusion
  1.6 4.1 %collective-permute-start.1 = (bf16[128,1024]{1,0:T(8,128)(2,1)S(1)}, bf16[128,1024]{1,0:T(8,128)(2,1)S(1)}, u32[]{:S(2)}, u32[]{:S(2)}) collective-permute-start(bf16[128,1024]{1,0:T(8,128)(2,1)S(1)} %constant_dynamic-slice_fusion), channel_id=1, source_target_pairs={{0,2},{1,3},{2,0},{3,1},{4,6},{5,7},{6,4},{7,5},{8,10},{9,11},{10,... | collective-permute-start | bytes 786440 | tf_op jit(solution)/shard_map/ppermute | solution.py:533
  5.7 1.6 collective-permute-start
  7.3 3.9 %shard_map.246 = (bf16[384,1024]{1,0:T(8,128)(2,1)}, bf16[384,256]{1,0:T(8,128)(2,1)}, f32[384,128]{1,0:T(8,128)}, f32[384,128]{1,0:T(8,128)}, f32[384,128]{1,0:T(8,128)}) custom-call(s32[8]{0:T(128)} %starts_ref.5, bf16[384,1024]{1,0:T(8,128)(2,1)} %x_ref.5, f32[1,1024]{1,0:T(1,128)} %bitcast.16, bf16[1024,128]{1,0:T(8,128)(2,1)} %refs_8_.1, ...), custom_call_target="tpu_custom_call" | custom-call | flops 49999998976 | bytes 2888480 | tf_op jit(solution)/shard_map/pallas_call | solution.py:39
  11.2 2.4 %collective-permute-start.6 = (bf16[384,256]{1,0:T(8,128)(2,1)}, bf16[384,256]{1,0:T(8,128)(2,1)S(1)}, u32[]{:S(2)}, u32[]{:S(2)}) collective-permute-start(bf16[384,256]{1,0:T(8,128)(2,1)} %get-tuple-element.117), channel_id=1, source_target_pairs={{0,24},{4,28},{8,16},{12,20},{16,8},{20,12},{24,0},{28,4},{1,25},{... | collective-permute-start | bytes 589832 | tf_op jit(solution)/shard_map/ppermute | solution.py:533
  14.7 1.1 copy-done
  15.8 0.9 copy-done.7
  16.8 0.9 copy-done.9
  17.7 0.9 shard_map.247
  18.7 4.0 %collective-permute-done.4 = bf16[384,256]{1,0:T(8,128)(2,1)S(1)} collective-permute-done((bf16[384,256]{1,0:T(8,128)(2,1)}, bf16[384,256]{1,0:T(8,128)(2,1)S(1)}, u32[]{:S(2)}, u32[]{:S(2)}) %collective-permute-start.4) | collective-permute-done | bytes 196640 | tf_op jit(solution)/shard_map/ppermute | solution.py:533
  23.8 1.3 collective-permute-done.7.refs_1_
  25.2 2.2 %shard_map.248 = (bf16[384,256]{1,0:T(8,128)(2,1)S(1)}, f32[384,256]{1,0:T(8,128)S(1)}, f32[2,768]{1,0:T(2,128)S(1)}) custom-call(s32[8]{0:T(128)S(1)} %copy-done.33, bf16[1536,128]{1,0:T(8,128)(2,1)S(1)} %get-tuple-element.143.qpad_ref, bf16[1536,256]{1,0:T(8,128)(2,1)S(1)} %constant_dynamic-update-slice_fusion.refs_0_, ...), custom_call_target="tpu_custom_call" | custom-call | flops 49999998976 | bytes 2562080 | tf_op jit(solution)/shard_map/pallas_call | solution.py:39
  27.4 0.9 copy-done.27
  28.2 2.1 %collective-permute-done.2 = bf16[64,1024]{1,0:T(8,128)(2,1)S(1)} collective-permute-done((bf16[64,1024]{1,0:T(8,128)(2,1)S(1)}, bf16[64,1024]{1,0:T(8,128)(2,1)S(1)}, u32[]{:S(2)}, u32[]{:S(2)}) %collective-permute-start.2) | collective-permute-done | bytes 131104 | tf_op jit(solution)/shard_map/ppermute | solution.py:533
  30.4 2.5 %collective-permute-done.3 = bf16[64,1024]{1,0:T(8,128)(2,1)S(1)} collective-permute-done((bf16[64,1024]{1,0:T(8,128)(2,1)S(1)}, bf16[64,1024]{1,0:T(8,128)(2,1)S(1)}, u32[]{:S(2)}, u32[]{:S(2)}) %collective-permute-start.3) | collective-permute-done | bytes 131104 | tf_op jit(solution)/shard_map/ppermute | solution.py:533
  33.4 1.7 collective-permute-start.9
  35.1 9.3 %collective-permute-done.10.refs_2_.refs_3_ = bf16[384,256]{1,0:T(8,128)(2,1)S(1)} collective-permute-done((bf16[384,256]{1,0:T(8,128)(2,1)S(1)}, bf16[384,256]{1,0:T(8,128)(2,1)S(1)}, u32[]{:S(2)}, u32[]{:S(2)}) %collective-permute-start.10) | collective-permute-done | bytes 196640 | tf_op jit(solution)/shard_map/ppermute | solution.py:533
  44.6 2.9 %collective-permute-start.12 = (bf16[192,256]{1,0:T(8,128)(2,1)S(1)}, bf16[192,256]{1,0:T(8,128)(2,1)S(1)}, u32[]{:S(2)}, u32[]{:S(2)}) collective-permute-start(bf16[192,256]{1,0:T(8,128)(2,1)S(1)} %slice.83), channel_id=1, source_target_pairs={{0,2},{1,3},{2,0},{3,1},{4,6},{5,7},{6,4},{7,5},{8,10},{9,11},{10,... | collective-permute-start | bytes 294920 | tf_op jit(solution)/shard_map/ppermute | solution.py:533
  47.5 3.4 %collective-permute-done.11.refs_3_.refs_4_ = bf16[192,256]{1,0:T(8,128)(2,1)S(1)} collective-permute-done((bf16[192,256]{1,0:T(8,128)(2,1)S(1)}, bf16[192,256]{1,0:T(8,128)(2,1)S(1)}, u32[]{:S(2)}, u32[]{:S(2)}) %collective-permute-start.11) | collective-permute-done | bytes 98336 | tf_op jit(solution)/shard_map/ppermute | solution.py:533
  50.9 1.4 collective-permute-done.12.refs_4_.refs_5_
  52.4 1.8 %shard_map.249 = (bf16[384,1024]{1,0:T(8,128)(2,1)S(1)}, f32[96,1024]{1,0:T(8,128)S(1)}) custom-call(bf16[384,1024]{1,0:T(8,128)(2,1)S(1)} %copy-done.25, f32[1,1024]{1,0:T(1,128)S(1)} %bitcast.14, bf16[256,1024]{1,0:T(8,128)(2,1)S(1)} %copy-done.13, bf16[3,128,1024]{2,1,0:T(8,128)(2,1)S(1)} %pad_maximum_fusion.wm_ref, ...), custom_call_target="tpu_custom_call" | custom-call | flops 49999998976 | bytes 4853760 | tf_op jit(solution)/shard_map/pallas_call | solution.py:39
  55.6 5.8 %shard_map.250 = (bf16[384,1152]{1,0:T(8,128)(2,1)S(1)}, bf16[384,1152]{1,0:T(8,128)(2,1)S(1)}, bf16[384,1152]{1,0:T(8,128)(2,1)S(1)}, bf16[96,1024]{1,0:T(8,128...) custom-call(bf16[384,1024]{1,0:T(8,128)(2,1)S(1)} %get-tuple-element, ...), custom_call_target="tpu_custom_call" | custom-call | flops 49999998976 | bytes 12091392 | tf_op jit(solution)/shard_map/pallas_call | solution.py:39
  61.7 2.7 %collective-permute-start.14 = (bf16[48,1024]{1,0:T(8,128)(2,1)S(1)}, bf16[48,1024]{1,0:T(8,128)(2,1)S(1)}, u32[]{:S(2)}, u32[]{:S(2)}) collective-permute-start(bf16[48,1024]{1,0:T(8,128)(2,1)S(1)} %get-tuple-element.134), channel_id=1, source_target_pairs={{0,2},{1,3},{2,0},{3,1},{4,6},{5,7},{6,4},{7,5},{8,10},{9,11},{10,... | collective-permute-start | bytes 294920 | tf_op jit(solution)/shard_map/ppermute | solution.py:533
  64.4 4.3 %shard_map.251 = (bf16[512,3456]{1,0:T(8,128)(2,1)S(1)}, bf16[512,3456]{1,0:T(8,128)(2,1)S(1)}) custom-call(bf16[384,1024]{1,0:T(8,128)(2,1)S(1)} %get-tuple-element.124.h_ref, bf16[384,1024]{1,0:T(8,128)(2,1)S(1)} %copy-done.24, bf16[384,1152]{1,0:T(8,128)(2,1)S(1)} %get-tuple-element.125.act_ref, bf16[384,1152]{1,0:T(8,128)(2,1)S(1)} %get-tuple-element.128.dg_ref, ...), custom_call_target="tpu_custom_call" | custom-call | flops 49999998976 | bytes 11304960 | tf_op jit(solution)/shard_map/pallas_call | solution.py:39
  69.1 1.8 %collective-permute-start.16 = (bf16[96,1024]{1,0:T(8,128)(2,1)S(1)}, bf16[96,1024]{1,0:T(8,128)(2,1)S(1)}, u32[]{:S(2)}, u32[]{:S(2)}) collective-permute-start(bf16[96,1024]{1,0:T(8,128)(2,1)S(1)} %get-tuple-element.136), channel_id=1, source_target_pairs={{0,2},{1,3},{2,0},{3,1},{4,6},{5,7},{6,4},{7,5},{8,10},{9,11},{10,... | collective-permute-start | bytes 589832 | tf_op jit(solution)/shard_map/ppermute | solution.py:533
  70.9 6.2 %collective-permute-done.15.refs_1_ = bf16[96,1024]{1,0:T(8,128)(2,1)S(1)} collective-permute-done((bf16[96,1024]{1,0:T(8,128)(2,1)S(1)}, bf16[96,1024]{1,0:T(8,128)(2,1)S(1)}, u32[]{:S(2)}, u32[]{:S(2)}) %collective-permute-start.15) | collective-permute-done | bytes 196640 | tf_op jit(solution)/shard_map/ppermute | solution.py:533
  77.1 1.6 collective-permute-done.16.refs_2_
  78.7 0.9 shard_map.253
  80.1 2.6 %collective-permute-start.22 = (bf16[96,256]{1,0:T(8,128)(2,1)S(1)}, bf16[96,256]{1,0:T(8,128)(2,1)S(1)}, u32[]{:S(2)}, u32[]{:S(2)}) collective-permute-start(bf16[96,256]{1,0:T(8,128)(2,1)S(1)} %get-tuple-element.148), channel_id=1, source_target_pairs={{0,2},{1,3},{2,0},{3,1},{4,6},{5,7},{6,4},{7,5},{8,10},{9,11},{10,... | collective-permute-start | bytes 147464 | tf_op jit(solution)/shard_map/ppermute | solution.py:533
  82.7 1.4 collective-permute-start.23
  84.1 1.5 shard_map.254
  85.8 2.9 %collective-permute-start.17 = (bf16[96,1280]{1,0:T(8,128)(2,1)S(1)}, bf16[96,1280]{1,0:T(8,128)(2,1)S(1)}, u32[]{:S(2)}, u32[]{:S(2)}) collective-permute-start(bf16[96,1280]{1,0:T(8,128)(2,1)S(1)} %get-tuple-element.139), channel_id=1, source_target_pairs={{0,1},{1,0},{2,3},{3,2},{4,5},{5,4},{6,7},{7,6},{8,9},{9,8},{10,11... | collective-permute-start | bytes 737288 | tf_op jit(solution)/shard_map/ppermute | solution.py:533
  89.0 1.5 collective-permute-start.19
  90.4 1.5 collective-permute-start.30
  92.0 3.4 %shard_map.255 = (bf16[384,256]{1,0:T(8,128)(2,1)S(1)}, bf16[1536,256]{1,0:T(8,128)(2,1)S(1)}, bf16[1536,256]{1,0:T(8,128)(2,1)S(1)}) custom-call(s32[8]{0:T(128)S(1)} %copy-done.34, bf16[1536,128]{1,0:T(8,128)(2,1)S(1)} %copy-done.37, f32[384,256]{1,0:T(8,128)S(1)} %get-tuple-element.144.o32_ref, f32[2,768]{1,0:T(2,128)S(1)} %get-tuple-element.145.lse_ref, ...), custom_call_target="tpu_custom_call" | custom-call | flops 49999998976 | bytes 4331552 | tf_op jit(solution)/shard_map/pallas_call | solution.py:39
  95.5 8.0 %collective-permute-done.18.refs_2_ = bf16[96,1280]{1,0:T(8,128)(2,1)S(1)} collective-permute-done((bf16[96,1280]{1,0:T(8,128)(2,1)S(1)}, bf16[96,1280]{1,0:T(8,128)(2,1)S(1)}, u32[]{:S(2)}, u32[]{:S(2)}) %collective-permute-start.18) | collective-permute-done | bytes 245792 | tf_op jit(solution)/shard_map/ppermute | solution.py:533
  103.6 5.0 %collective-permute-start.29 = (bf16[96,1024]{1,0:T(8,128)(2,1)S(1)}, bf16[96,1024]{1,0:T(8,128)(2,1)S(1)}, u32[]{:S(2)}, u32[]{:S(2)}) collective-permute-start(bf16[96,1024]{1,0:T(8,128)(2,1)S(1)} %get-tuple-element.190.own_ref), channel_id=1, source_target_pairs={{0,2},{1,3},{2,0},{3,1},{4,6},{5,7},{6,4},{7,5},{8,10},{9,11},{10,... | collective-permute-start | bytes 589832 | tf_op jit(solution)/shard_map/ppermute | solution.py:533
  108.8 4.6 %collective-permute-start.27 = (bf16[384,256]{1,0:T(8,128)(2,1)S(1)}, bf16[384,256]{1,0:T(8,128)(2,1)S(1)}, u32[]{:S(2)}, u32[]{:S(2)}) collective-permute-start(bf16[384,256]{1,0:T(8,128)(2,1)S(1)} %get-tuple-element.213), channel_id=1, source_target_pairs={{0,24},{4,28},{8,16},{12,20},{16,8},{20,12},{24,0},{28,4},{1,25},{... | collective-permute-start | bytes 589832 | tf_op jit(solution)/shard_map/ppermute | solution.py:533
  113.5 2.3 %shard_map.257 = (bf16[384,256]{1,0:T(8,128)(2,1)}, f32[1,128]{1,0:T(1,128)S(1)}, f32[384,1024]{1,0:T(8,128)S(1)}, bf16[512,512]{1,0:T(8,128)(2,1)S(1)}, bf16[512,512]{1,0:T(8,128)(2,1)S(1)}) custom-call(bf16[384,256]{1,0:T(8,128)(2,1)S(1)} %get-tuple-element.164.dq_ref, f32[384,256]{1,0:T(8,128)S(1)} %get-tuple-element.165.qpre_ref, ...), custom_call_target="tpu_custom_call" | custom-call | flops 1 | bytes 6095616 | tf_op jit(solution)/shard_map/pallas_call | solution.py:39
  116.4 2.1 %collective-permute-done.29.refs_1_.two_ref = bf16[96,1024]{1,0:T(8,128)(2,1)S(1)} collective-permute-done((bf16[96,1024]{1,0:T(8,128)(2,1)S(1)}, bf16[96,1024]{1,0:T(8,128)(2,1)S(1)}, u32[]{:S(2)}, u32[]{:S(2)}) %collective-permute-start.29) | collective-permute-done | bytes 196640 | tf_op jit(solution)/shard_map/ppermute | solution.py:533
  119.3 1.2 collective-permute-done.31.q_got_ref
  120.6 3.0 %collective-permute-done.26.refs_2_ = bf16[384,256]{1,0:T(8,128)(2,1)S(1)} collective-permute-done((bf16[384,256]{1,0:T(8,128)(2,1)S(1)}, bf16[384,256]{1,0:T(8,128)(2,1)S(1)}, u32[]{:S(2)}, u32[]{:S(2)}) %collective-permute-start.26) | collective-permute-done | bytes 196640 | tf_op jit(solution)/shard_map/ppermute | solution.py:533
  123.7 2.5 %shard_map.258 = (bf16[384,256]{1,0:T(8,128)(2,1)}, f32[24,128]{1,0:T(8,128)S(1)}, bf16[96,1024]{1,0:T(8,128)(2,1)S(1)}, bf16[96,1024]{1,0:T(8,128)(2,1)S(1)}, b...) custom-call(bf16[384,256]{1,0:T(8,128)(2,1)S(1)} %get-tuple-element., ...), custom_call_target="tpu_custom_call" | custom-call | flops 49999998976 | bytes 6570752 | tf_op jit(solution)/shard_map/pallas_call | solution.py:39
  126.2 1.0 collective-permute-start.34
  127.2 1.1 collective-permute-start.35
  128.3 1.1 collective-permute-start.32
  129.4 2.7 %collective-permute-done.32 = f32[24,128]{1,0:T(8,128)S(1)} collective-permute-done((f32[24,128]{1,0:T(8,128)S(1)}, f32[24,128]{1,0:T(8,128)S(1)}, u32[]{:S(2)}, u32[]{:S(2)}) %collective-permute-start.32) | collective-permute-done | bytes 12320 | tf_op jit(solution)/shard_map/ppermute | solution.py:533
  132.1 2.5 %collective-permute-done.35.got_two_ref = bf16[48,1024]{1,0:T(8,128)(2,1)S(1)} collective-permute-done((bf16[48,1024]{1,0:T(8,128)(2,1)S(1)}, bf16[48,1024]{1,0:T(8,128)(2,1)S(1)}, u32[]{:S(2)}, u32[]{:S(2)}) %collective-permute-start.35) | collective-permute-done | bytes 98336 | tf_op jit(solution)/shard_map/ppermute | solution.py:533
  135.3 1.9 %collective-permute-start.38 = (bf16[144,1024]{1,0:T(8,128)(2,1)S(1)}, bf16[144,1024]{1,0:T(8,128)(2,1)S(1)}, u32[]{:S(2)}, u32[]{:S(2)}) collective-permute-start(bf16[144,1024]{1,0:T(8,128)(2,1)S(1)} %get-tuple-element.182), channel_id=1, source_target_pairs={{0,1},{1,0},{2,3},{3,2},{4,5},{5,4},{6,7},{7,6},{8,9},{9,8},{10,11... | collective-permute-start | bytes 884744 | tf_op jit(solution)/shard_map/ppermute | solution.py:533
  138.0 1.0 collective-permute-start.37
  139.1 1.6 collective-permute-start.40
  140.7 9.3 %collective-permute-done.37.got_ref = bf16[256,768]{1,0:T(8,128)(2,1)S(1)} collective-permute-done((bf16[256,768]{1,0:T(8,128)(2,1)S(1)}, bf16[256,768]{1,0:T(8,128)(2,1)S(1)}, u32[]{:S(2)}, u32[]{:S(2)}) %collective-permute-start.37) | collective-permute-done | bytes 393248 | tf_op jit(solution)/shard_map/ppermute | solution.py:538
  150.1 3.1 %collective-permute-done.39.refs_2_.high_ref = bf16[144,1024]{1,0:T(8,128)(2,1)S(1)} collective-permute-done((bf16[144,1024]{1,0:T(8,128)(2,1)S(1)}, bf16[144,1024]{1,0:T(8,128)(2,1)S(1)}, u32[]{:S(2)}, u32[]{:S(2)}) %collective-permute-start.39) | collective-permute-done | bytes 294944 | tf_op jit(solution)/shard_map/ppermute | solution.py:533
  153.9 2.4 %collective-permute-start.41 = (bf16[96,1024]{1,0:T(8,128)(2,1)S(1)}, bf16[96,1024]{1,0:T(8,128)(2,1)S(1)}, u32[]{:S(2)}, u32[]{:S(2)}) collective-permute-start(bf16[96,1024]{1,0:T(8,128)(2,1)S(1)} %shard_map.262.refs_0_), channel_id=1, source_target_pairs={{0,1},{1,0},{2,3},{3,2},{4,5},{5,4},{6,7},{7,6},{8,9},{9,8},{10,11... | collective-permute-start | bytes 589832 | tf_op jit(solution)/shard_map/ppermute | solution.py:533
  156.7 1.2 collective-permute-done.43
  157.9 1.4 collective-permute-start.44
  159.3 2.3 %collective-permute-done.44 = f32[24,128]{1,0:T(8,128)S(1)} collective-permute-done((f32[24,128]{1,0:T(8,128)S(1)}, f32[24,128]{1,0:T(8,128)S(1)}, u32[]{:S(2)}, u32[]{:S(2)}) %collective-permute-start.44) | collective-permute-done | bytes 12320 | tf_op jit(solution)/shard_map/ppermute | solution.py:533
  161.6 0.8 collective-permute-done.42.refs_2_
  162.4 2.5 %collective-permute-start.46 = (bf16[48,1024]{1,0:T(8,128)(2,1)S(1)}, bf16[48,1024]{1,0:T(8,128)(2,1)S(1)}, u32[]{:S(2)}, u32[]{:S(2)}) collective-permute-start(bf16[48,1024]{1,0:T(8,128)(2,1)S(1)} %slice.79), channel_id=1, source_target_pairs={{0,2},{1,3},{2,0},{3,1},{4,6},{5,7},{6,4},{7,5},{8,10},{9,11},{10,... | collective-permute-start | bytes 294920 | tf_op jit(solution)/shard_map/ppermute | solution.py:533
  165.2 0.7 shard_map.266
  166.6 4.8 %collective-permute-start.47 = (f32[24,128]{1,0:T(8,128)S(1)}, f32[24,128]{1,0:T(8,128)S(1)}, u32[]{:S(2)}, u32[]{:S(2)}) collective-permute-start(f32[24,128]{1,0:T(8,128)S(1)} %add.52.a_ref), channel_id=1, source_target_pairs={{0,16},{4,20},{8,24},{12,28},{16,0},{20,4},{24,8},{28,12},{1,17},{... | collective-permute-start | bytes 36872 | tf_op jit(solution)/shard_map/ppermute | solution.py:533
  171.4 0.9 shard_map.263
  172.3 1.5 shard_map.264
  174.5 1.3 shard_map.265
  (159 shorter events, 12.0 us)
Async XLA Ops:
  1.6 17.0 %collective-permute-start.1 = (bf16[128,1024]{1,0:T(8,128)(2,1)S(1)}, bf16[128,1024]{1,0:T(8,128)(2,1)S(1)}, u32[]{:S(2)}, u32[]{:S(2)}) collective-permute-start(bf16[128,1024]{1,0:T(8,128)(2,1)S(1)} %constant_dynamic-slice_fusion), channel_id=1, source_target_pairs={{0,2},{1,3},{2,0},{3,1},{4,6},{5,7},{6,4},{7,5},{8,10},{9,11},{10,... | collective-permute-start | bytes 786440 | tf_op jit(solution)/shard_map/ppermute | solution.py:533
  5.7 12.9 %collective-permute-start = (bf16[128,1024]{1,0:T(8,128)(2,1)S(1)}, bf16[128,1024]{1,0:T(8,128)(2,1)S(1)}, u32[]{:S(2)}, u32[]{:S(2)}) collective-permute-start(bf16[128,1024]{1,0:T(8,128)(2,1)S(1)} %constant_dynamic-slice_fusion), channel_id=1, source_target_pairs={{0,1},{1,0},{2,3},{3,2},{4,5},{5,4},{6,7},{7,6},{8,9},{9,8},{10,11... | collective-permute-start | bytes 786440 | tf_op jit(solution)/shard_map/ppermute | solution.py:533
  11.2 11.6 %collective-permute-start.6 = (bf16[384,256]{1,0:T(8,128)(2,1)}, bf16[384,256]{1,0:T(8,128)(2,1)S(1)}, u32[]{:S(2)}, u32[]{:S(2)}) collective-permute-start(bf16[384,256]{1,0:T(8,128)(2,1)} %get-tuple-element.117), channel_id=1, source_target_pairs={{0,24},{4,28},{8,16},{12,20},{16,8},{20,12},{24,0},{28,4},{1,25},{... | collective-permute-start | bytes 589832 | tf_op jit(solution)/shard_map/ppermute | solution.py:533
  13.6 9.1 %collective-permute-start.5 = (bf16[384,256]{1,0:T(8,128)(2,1)}, bf16[384,256]{1,0:T(8,128)(2,1)S(1)}, u32[]{:S(2)}, u32[]{:S(2)}) collective-permute-start(bf16[384,256]{1,0:T(8,128)(2,1)} %get-tuple-element.117), channel_id=1, source_target_pairs={{0,16},{4,20},{8,24},{12,28},{16,0},{20,4},{24,8},{28,12},{1,17},{... | collective-permute-start | bytes 589832 | tf_op jit(solution)/shard_map/ppermute | solution.py:533
  14.2 8.5 %collective-permute-start.4 = (bf16[384,256]{1,0:T(8,128)(2,1)}, bf16[384,256]{1,0:T(8,128)(2,1)S(1)}, u32[]{:S(2)}, u32[]{:S(2)}) collective-permute-start(bf16[384,256]{1,0:T(8,128)(2,1)} %get-tuple-element.117), channel_id=1, source_target_pairs={{0,8},{4,12},{8,0},{12,4},{16,24},{20,28},{24,16},{28,20},{1,9},{5... | collective-permute-start | bytes 589832 | tf_op jit(solution)/shard_map/ppermute | solution.py:533
  22.8 2.4 %collective-permute-start.7 = (bf16[1536,256]{1,0:T(8,128)(2,1)S(1)}, bf16[1536,256]{1,0:T(8,128)(2,1)S(1)}, u32[]{:S(2)}, u32[]{:S(2)}) collective-permute-start(bf16[1536,256]{1,0:T(8,128)(2,1)S(1)} %constant_dynamic-update-slice_fusion.refs_0_), channel_id=1, source_target_pairs={{0,4},{4,0},{8,12},{12,8},{16,20},{20,16},{24,28},{28,24},{1,5},{5... | collective-permute-start | bytes 2359304 | tf_op jit(solution)/shard_map/ppermute | solution.py:533
  22.9 7.5 %collective-permute-start.2 = (bf16[64,1024]{1,0:T(8,128)(2,1)S(1)}, bf16[64,1024]{1,0:T(8,128)(2,1)S(1)}, u32[]{:S(2)}, u32[]{:S(2)}) collective-permute-start(bf16[64,1024]{1,0:T(8,128)(2,1)S(1)} %slice.80), channel_id=1, source_target_pairs={{0,1},{1,0},{2,3},{3,2},{4,5},{5,4},{6,7},{7,6},{8,9},{9,8},{10,11... | collective-permute-start | bytes 393224 | tf_op jit(solution)/shard_map/ppermute | solution.py:533
  23.4 9.4 %collective-permute-start.3 = (bf16[64,1024]{1,0:T(8,128)(2,1)S(1)}, bf16[64,1024]{1,0:T(8,128)(2,1)S(1)}, u32[]{:S(2)}, u32[]{:S(2)}) collective-permute-start(bf16[64,1024]{1,0:T(8,128)(2,1)S(1)} %slice.81), channel_id=1, source_target_pairs={{0,2},{1,3},{2,0},{3,1},{4,6},{5,7},{6,4},{7,5},{8,10},{9,11},{10,... | collective-permute-start | bytes 393224 | tf_op jit(solution)/shard_map/ppermute | solution.py:533
  28.2 26.0 %copy-start.11 = (bf16[384,256]{1,0:T(8,128)(2,1)}, bf16[384,256]{1,0:T(8,128)(2,1)S(1)}, u32[]{:S(2)}) copy-start(bf16[384,256]{1,0:T(8,128)(2,1)S(1)} %get-tuple-element.118.refs_0_.refs_1_) | copy-start | bytes 589828
  28.2 24.1 %copy-start.13 = (bf16[256,1024]{1,0:T(8,128)(2,1)S(1)}, bf16[256,1024]{1,0:T(8,128)(2,1)}, u32[]{:S(2)}) copy-start(bf16[256,1024]{1,0:T(8,128)(2,1)} %w0_ref.3) | copy-start | bytes 1572868
  28.2 24.1 %copy-start.25 = (bf16[384,1024]{1,0:T(8,128)(2,1)S(1)}, bf16[384,1024]{1,0:T(8,128)(2,1)}, u32[]{:S(2)}) copy-start(bf16[384,1024]{1,0:T(8,128)(2,1)} %x_ref.5) | copy-start | bytes 2359300
  28.2 24.1 %copy-start.31 = (f32[1024]{0:T(1024)S(1)}, f32[1024]{0:T(1024)}, u32[]{:S(2)}) copy-start(f32[1024]{0:T(1024)} %param.24) | copy-start | bytes 12292
  33.0 19.3 %collective-permute-start.8 = (bf16[3,128,1024]{2,1,0:T(8,128)(2,1)S(1)}, bf16[3,128,1024]{2,1,0:T(8,128)(2,1)S(1)}, u32[]{:S(2)}, u32[]{:S(2)}) collective-permute-start(bf16[3,128,1024]{2,1,0:T(8,128)(2,1)S(1)} %pad_maximum_fusion.wm_ref), channel_id=1, source_target_pairs={{0,4},{4,0},{8,12},{12,8},{16,20},{20,16},{24,28},{28,24},{1,5},{5... | collective-permute-start | bytes 2359304 | tf_op jit(solution)/shard_map/ppermute | solution.py:533
  33.1 11.2 %collective-permute-start.10 = (bf16[384,256]{1,0:T(8,128)(2,1)S(1)}, bf16[384,256]{1,0:T(8,128)(2,1)S(1)}, u32[]{:S(2)}, u32[]{:S(2)}) collective-permute-start(bf16[384,256]{1,0:T(8,128)(2,1)S(1)} %get-tuple-element.118.refs_0_.refs_1_), channel_id=1, source_target_pairs={{0,2},{1,3},{2,0},{3,1},{4,6},{5,7},{6,4},{7,5},{8,10},{9,11},{10,... | collective-permute-start | bytes 589832 | tf_op jit(solution)/shard_map/ppermute | solution.py:533
  33.4 11.2 %collective-permute-start.9 = (bf16[384,256]{1,0:T(8,128)(2,1)S(1)}, bf16[384,256]{1,0:T(8,128)(2,1)S(1)}, u32[]{:S(2)}, u32[]{:S(2)}) collective-permute-start(bf16[384,256]{1,0:T(8,128)(2,1)S(1)} %get-tuple-element.118.refs_0_.refs_1_), channel_id=1, source_target_pairs={{0,1},{1,0},{2,3},{3,2},{4,5},{5,4},{6,7},{7,6},{8,9},{9,8},{10,11... | collective-permute-start | bytes 589832 | tf_op jit(solution)/shard_map/ppermute | solution.py:533
  44.3 10.0 %copy-start.3 = (bf16[384,256]{1,0:T(8,128)(2,1)}, bf16[384,256]{1,0:T(8,128)(2,1)S(1)}, u32[]{:S(2)}) copy-start(bf16[384,256]{1,0:T(8,128)(2,1)S(1)} %collective-permute-done.10.refs_2_.refs_3_) | copy-start | bytes 589828
  44.3 6.6 %collective-permute-start.11 = (bf16[192,256]{1,0:T(8,128)(2,1)S(1)}, bf16[192,256]{1,0:T(8,128)(2,1)S(1)}, u32[]{:S(2)}, u32[]{:S(2)}) collective-permute-start(bf16[192,256]{1,0:T(8,128)(2,1)S(1)} %slice.82), channel_id=1, source_target_pairs={{0,1},{1,0},{2,3},{3,2},{4,5},{5,4},{6,7},{7,6},{8,9},{9,8},{10,11... | collective-permute-start | bytes 294920 | tf_op jit(solution)/shard_map/ppermute | solution.py:533
  44.6 7.7 %collective-permute-start.12 = (bf16[192,256]{1,0:T(8,128)(2,1)S(1)}, bf16[192,256]{1,0:T(8,128)(2,1)S(1)}, u32[]{:S(2)}, u32[]{:S(2)}) collective-permute-start(bf16[192,256]{1,0:T(8,128)(2,1)S(1)} %slice.83), channel_id=1, source_target_pairs={{0,2},{1,3},{2,0},{3,1},{4,6},{5,7},{6,4},{7,5},{8,10},{9,11},{10,... | collective-permute-start | bytes 294920 | tf_op jit(solution)/shard_map/ppermute | solution.py:533
  61.4 7.4 %collective-permute-start.13 = (bf16[48,1024]{1,0:T(8,128)(2,1)S(1)}, bf16[48,1024]{1,0:T(8,128)(2,1)S(1)}, u32[]{:S(2)}, u32[]{:S(2)}) collective-permute-start(bf16[48,1024]{1,0:T(8,128)(2,1)S(1)} %get-tuple-element.133), channel_id=1, source_target_pairs={{0,1},{1,0},{2,3},{3,2},{4,5},{5,4},{6,7},{7,6},{8,9},{9,8},{10,11... | collective-permute-start | bytes 294920 | tf_op jit(solution)/shard_map/ppermute | solution.py:533
  61.7 7.1 %collective-permute-start.14 = (bf16[48,1024]{1,0:T(8,128)(2,1)S(1)}, bf16[48,1024]{1,0:T(8,128)(2,1)S(1)}, u32[]{:S(2)}, u32[]{:S(2)}) collective-permute-start(bf16[48,1024]{1,0:T(8,128)(2,1)S(1)} %get-tuple-element.134), channel_id=1, source_target_pairs={{0,2},{1,3},{2,0},{3,1},{4,6},{5,7},{6,4},{7,5},{8,10},{9,11},{10,... | collective-permute-start | bytes 294920 | tf_op jit(solution)/shard_map/ppermute | solution.py:533
  68.9 8.2 %collective-permute-start.15 = (bf16[96,1024]{1,0:T(8,128)(2,1)S(1)}, bf16[96,1024]{1,0:T(8,128)(2,1)S(1)}, u32[]{:S(2)}, u32[]{:S(2)}) collective-permute-start(bf16[96,1024]{1,0:T(8,128)(2,1)S(1)} %get-tuple-element.135), channel_id=1, source_target_pairs={{0,1},{1,0},{2,3},{3,2},{4,5},{5,4},{6,7},{7,6},{8,9},{9,8},{10,11... | collective-permute-start | bytes 589832 | tf_op jit(solution)/shard_map/ppermute | solution.py:533
  69.1 9.6 %collective-permute-start.16 = (bf16[96,1024]{1,0:T(8,128)(2,1)S(1)}, bf16[96,1024]{1,0:T(8,128)(2,1)S(1)}, u32[]{:S(2)}, u32[]{:S(2)}) collective-permute-start(bf16[96,1024]{1,0:T(8,128)(2,1)S(1)} %get-tuple-element.136), channel_id=1, source_target_pairs={{0,2},{1,3},{2,0},{3,1},{4,6},{5,7},{6,4},{7,5},{8,10},{9,11},{10,... | collective-permute-start | bytes 589832 | tf_op jit(solution)/shard_map/ppermute | solution.py:533
  70.9 14.9 %collective-permute-start.20 = (bf16[512,3456]{1,0:T(8,128)(2,1)S(1)}, bf16[512,3456]{1,0:T(8,128)(2,1)S(1)}, u32[]{:S(2)}, u32[]{:S(2)}) collective-permute-start(bf16[512,3456]{1,0:T(8,128)(2,1)S(1)} %get-tuple-element.142), channel_id=1, source_target_pairs={{0,4},{4,0},{8,12},{12,8},{16,20},{20,16},{24,28},{28,24},{1,5},{5... | collective-permute-start | bytes 10616840 | tf_op jit(solution)/shard_map/ppermute | solution.py:533
  79.6 9.3 %collective-permute-start.21 = (bf16[96,256]{1,0:T(8,128)(2,1)S(1)}, bf16[96,256]{1,0:T(8,128)(2,1)S(1)}, u32[]{:S(2)}, u32[]{:S(2)}) collective-permute-start(bf16[96,256]{1,0:T(8,128)(2,1)S(1)} %get-tuple-element.147), channel_id=1, source_target_pairs={{0,1},{1,0},{2,3},{3,2},{4,5},{5,4},{6,7},{7,6},{8,9},{9,8},{10,11... | collective-permute-start | bytes 147464 | tf_op jit(solution)/shard_map/ppermute | solution.py:533
  80.1 10.4 %collective-permute-start.22 = (bf16[96,256]{1,0:T(8,128)(2,1)S(1)}, bf16[96,256]{1,0:T(8,128)(2,1)S(1)}, u32[]{:S(2)}, u32[]{:S(2)}) collective-permute-start(bf16[96,256]{1,0:T(8,128)(2,1)S(1)} %get-tuple-element.148), channel_id=1, source_target_pairs={{0,2},{1,3},{2,0},{3,1},{4,6},{5,7},{6,4},{7,5},{8,10},{9,11},{10,... | collective-permute-start | bytes 147464 | tf_op jit(solution)/shard_map/ppermute | solution.py:533
  82.7 9.3 %collective-permute-start.23 = (bf16[96,256]{1,0:T(8,128)(2,1)S(1)}, bf16[96,256]{1,0:T(8,128)(2,1)S(1)}, u32[]{:S(2)}, u32[]{:S(2)}) collective-permute-start(bf16[96,256]{1,0:T(8,128)(2,1)S(1)} %get-tuple-element.149), channel_id=1, source_target_pairs={{0,3},{1,2},{2,1},{3,0},{4,7},{5,6},{6,5},{7,4},{8,11},{9,10},{10,... | collective-permute-start | bytes 147464 | tf_op jit(solution)/shard_map/ppermute | solution.py:533
  85.6 17.8 %collective-permute-start.18 = (bf16[96,1280]{1,0:T(8,128)(2,1)S(1)}, bf16[96,1280]{1,0:T(8,128)(2,1)S(1)}, u32[]{:S(2)}, u32[]{:S(2)}) collective-permute-start(bf16[96,1280]{1,0:T(8,128)(2,1)S(1)} %get-tuple-element.140), channel_id=1, source_target_pairs={{0,2},{1,3},{2,0},{3,1},{4,6},{5,7},{6,4},{7,5},{8,10},{9,11},{10,... | collective-permute-start | bytes 737288 | tf_op jit(solution)/shard_map/ppermute | solution.py:533
  85.8 17.6 %collective-permute-start.17 = (bf16[96,1280]{1,0:T(8,128)(2,1)S(1)}, bf16[96,1280]{1,0:T(8,128)(2,1)S(1)}, u32[]{:S(2)}, u32[]{:S(2)}) collective-permute-start(bf16[96,1280]{1,0:T(8,128)(2,1)S(1)} %get-tuple-element.139), channel_id=1, source_target_pairs={{0,1},{1,0},{2,3},{3,2},{4,5},{5,4},{6,7},{7,6},{8,9},{9,8},{10,11... | collective-permute-start | bytes 737288 | tf_op jit(solution)/shard_map/ppermute | solution.py:533
  89.0 14.5 %collective-permute-start.19 = (bf16[96,1280]{1,0:T(8,128)(2,1)S(1)}, bf16[96,1280]{1,0:T(8,128)(2,1)S(1)}, u32[]{:S(2)}, u32[]{:S(2)}) collective-permute-start(bf16[96,1280]{1,0:T(8,128)(2,1)S(1)} %get-tuple-element.141), channel_id=1, source_target_pairs={{0,3},{1,2},{2,1},{3,0},{4,7},{5,6},{6,5},{7,4},{8,11},{9,10},{10,... | collective-permute-start | bytes 737288 | tf_op jit(solution)/shard_map/ppermute | solution.py:533
  90.4 25.3 %collective-permute-start.30 = (bf16[256,3456]{1,0:T(8,128)(2,1)S(1)}, bf16[256,3456]{1,0:T(8,128)(2,1)S(1)}, u32[]{:S(2)}, u32[]{:S(2)}) collective-permute-start(bf16[256,3456]{1,0:T(8,128)(2,1)S(1)} %slice_add_fusion), channel_id=1, source_target_pairs={{0,8},{4,20},{8,0},{12,28},{16,24},{20,4},{24,16},{28,12},{1,9},{5... | collective-permute-start | bytes 5308424 | tf_op jit(solution)/shard_map/ppermute | solution.py:538
  95.4 18.0 %copy-start.1 = (bf16[384,1024]{1,0:T(8,128)(2,1)S(1)}, bf16[384,1024]{1,0:T(8,128)(2,1)}, u32[]{:S(2)}) copy-start(bf16[384,1024]{1,0:T(8,128)(2,1)} %get-tuple-element.112.h_ref.refs_14_) | copy-start | bytes 2359300
  95.4 18.0 %copy-start.4 = (bf16[384,256]{1,0:T(8,128)(2,1)S(1)}, bf16[384,256]{1,0:T(8,128)(2,1)}, u32[]{:S(2)}) copy-start(bf16[384,256]{1,0:T(8,128)(2,1)} %copy-done.3) | copy-start | bytes 589828
  95.4 18.0 %copy-start.6 = (bf16[384,256]{1,0:T(8,128)(2,1)S(1)}, bf16[384,256]{1,0:T(8,128)(2,1)}, u32[]{:S(2)}) copy-start(bf16[384,256]{1,0:T(8,128)(2,1)} %copy-done.5) | copy-start | bytes 589828
  95.4 18.0 %copy-start.8 = (f32[384,128]{1,0:T(8,128)S(1)}, f32[384,128]{1,0:T(8,128)}, u32[]{:S(2)}) copy-start(f32[384,128]{1,0:T(8,128)} %get-tuple-element.113.cos_ref.refs_5_) | copy-start | bytes 589828
  95.4 18.0 %copy-start.10 = (f32[384,128]{1,0:T(8,128)S(1)}, f32[384,128]{1,0:T(8,128)}, u32[]{:S(2)}) copy-start(f32[384,128]{1,0:T(8,128)} %get-tuple-element.114.sin_ref.refs_6_) | copy-start | bytes 589828
  95.4 18.0 %copy-start.12 = (bf16[384,256]{1,0:T(8,128)(2,1)S(1)}, bf16[384,256]{1,0:T(8,128)(2,1)}, u32[]{:S(2)}) copy-start(bf16[384,256]{1,0:T(8,128)(2,1)} %copy-done.11) | copy-start | bytes 589828
  95.4 18.0 %copy-start.15 = (bf16[192,256]{1,0:T(8,128)(2,1)S(1)}, bf16[192,256]{1,0:T(8,128)(2,1)}, u32[]{:S(2)}) copy-start(bf16[192,256]{1,0:T(8,128)(2,1)} %copy-done.14) | copy-start | bytes 294916
  95.4 18.0 %copy-start.17 = (bf16[192,256]{1,0:T(8,128)(2,1)S(1)}, bf16[192,256]{1,0:T(8,128)(2,1)}, u32[]{:S(2)}) copy-start(bf16[192,256]{1,0:T(8,128)(2,1)} %copy-done.16) | copy-start | bytes 294916
  103.5 5.2 %collective-permute-start.24 = (bf16[1536,256]{1,0:T(8,128)(2,1)S(1)}, bf16[1536,256]{1,0:T(8,128)(2,1)S(1)}, u32[]{:S(2)}, u32[]{:S(2)}) collective-permute-start(bf16[1536,256]{1,0:T(8,128)(2,1)S(1)} %get-tuple-element.159), channel_id=1, source_target_pairs={{0,4},{4,0},{8,12},{12,8},{16,20},{20,16},{24,28},{28,24},{1,5},{5... | collective-permute-start | bytes 2359304 | tf_op jit(solution)/shard_map/ppermute | solution.py:533
  103.6 14.9 %collective-permute-start.29 = (bf16[96,1024]{1,0:T(8,128)(2,1)S(1)}, bf16[96,1024]{1,0:T(8,128)(2,1)S(1)}, u32[]{:S(2)}, u32[]{:S(2)}) collective-permute-start(bf16[96,1024]{1,0:T(8,128)(2,1)S(1)} %get-tuple-element.190.own_ref), channel_id=1, source_target_pairs={{0,2},{1,3},{2,0},{3,1},{4,6},{5,7},{6,4},{7,5},{8,10},{9,11},{10,... | collective-permute-start | bytes 589832 | tf_op jit(solution)/shard_map/ppermute | solution.py:533
  108.7 10.6 %collective-permute-start.28 = (bf16[96,1024]{1,0:T(8,128)(2,1)S(1)}, bf16[96,1024]{1,0:T(8,128)(2,1)S(1)}, u32[]{:S(2)}, u32[]{:S(2)}) collective-permute-start(bf16[96,1024]{1,0:T(8,128)(2,1)S(1)} %get-tuple-element.190.own_ref), channel_id=1, source_target_pairs={{0,1},{1,0},{2,3},{3,2},{4,5},{5,4},{6,7},{7,6},{8,9},{9,8},{10,11... | collective-permute-start | bytes 589832 | tf_op jit(solution)/shard_map/ppermute | solution.py:533
  108.8 11.9 %collective-permute-start.27 = (bf16[384,256]{1,0:T(8,128)(2,1)S(1)}, bf16[384,256]{1,0:T(8,128)(2,1)S(1)}, u32[]{:S(2)}, u32[]{:S(2)}) collective-permute-start(bf16[384,256]{1,0:T(8,128)(2,1)S(1)} %get-tuple-element.213), channel_id=1, source_target_pairs={{0,24},{4,28},{8,16},{12,20},{16,8},{20,12},{24,0},{28,4},{1,25},{... | collective-permute-start | bytes 589832 | tf_op jit(solution)/shard_map/ppermute | solution.py:533
  113.4 10.3 %collective-permute-start.26 = (bf16[384,256]{1,0:T(8,128)(2,1)S(1)}, bf16[384,256]{1,0:T(8,128)(2,1)S(1)}, u32[]{:S(2)}, u32[]{:S(2)}) collective-permute-start(bf16[384,256]{1,0:T(8,128)(2,1)S(1)} %get-tuple-element.214), channel_id=1, source_target_pairs={{0,16},{4,20},{8,24},{12,28},{16,0},{20,4},{24,8},{28,12},{1,17},{... | collective-permute-start | bytes 589832 | tf_op jit(solution)/shard_map/ppermute | solution.py:533
  115.8 7.9 %collective-permute-start.25 = (bf16[384,256]{1,0:T(8,128)(2,1)S(1)}, bf16[384,256]{1,0:T(8,128)(2,1)S(1)}, u32[]{:S(2)}, u32[]{:S(2)}) collective-permute-start(bf16[384,256]{1,0:T(8,128)(2,1)S(1)} %get-tuple-element.215), channel_id=1, source_target_pairs={{0,8},{4,12},{8,0},{12,4},{16,24},{20,28},{24,16},{28,20},{1,9},{5... | collective-permute-start | bytes 589832 | tf_op jit(solution)/shard_map/ppermute | solution.py:533
  118.6 2.0 %collective-permute-start.31 = (bf16[512,512]{1,0:T(8,128)(2,1)S(1)}, bf16[512,512]{1,0:T(8,128)(2,1)S(1)}, u32[]{:S(2)}, u32[]{:S(2)}) collective-permute-start(bf16[512,512]{1,0:T(8,128)(2,1)S(1)} %get-tuple-element.167), channel_id=1, source_target_pairs={{0,4},{4,0},{8,12},{12,8},{16,20},{20,16},{24,28},{28,24},{1,5},{5... | collective-permute-start | bytes 1572872 | tf_op jit(solution)/shard_map/ppermute | solution.py:533
  126.2 5.9 %collective-permute-start.34 = (bf16[48,1024]{1,0:T(8,128)(2,1)S(1)}, bf16[48,1024]{1,0:T(8,128)(2,1)S(1)}, u32[]{:S(2)}, u32[]{:S(2)}) collective-permute-start(bf16[48,1024]{1,0:T(8,128)(2,1)S(1)} %get-tuple-element.180), channel_id=1, source_target_pairs={{0,1},{1,0},{2,3},{3,2},{4,5},{5,4},{6,7},{7,6},{8,9},{9,8},{10,11... | collective-permute-start | bytes 294920 | tf_op jit(solution)/shard_map/ppermute | solution.py:533
  127.2 7.4 %collective-permute-start.35 = (bf16[48,1024]{1,0:T(8,128)(2,1)S(1)}, bf16[48,1024]{1,0:T(8,128)(2,1)S(1)}, u32[]{:S(2)}, u32[]{:S(2)}) collective-permute-start(bf16[48,1024]{1,0:T(8,128)(2,1)S(1)} %get-tuple-element.181), channel_id=1, source_target_pairs={{0,2},{1,3},{2,0},{3,1},{4,6},{5,7},{6,4},{7,5},{8,10},{9,11},{10,... | collective-permute-start | bytes 294920 | tf_op jit(solution)/shard_map/ppermute | solution.py:533
  128.3 3.8 %collective-permute-start.32 = (f32[24,128]{1,0:T(8,128)S(1)}, f32[24,128]{1,0:T(8,128)S(1)}, u32[]{:S(2)}, u32[]{:S(2)}) collective-permute-start(f32[24,128]{1,0:T(8,128)S(1)} %get-tuple-element.172), channel_id=1, source_target_pairs={{0,1},{1,0},{2,3},{3,2},{4,5},{5,4},{6,7},{7,6},{8,9},{9,8},{10,11... | collective-permute-start | bytes 36872 | tf_op jit(solution)/shard_map/ppermute | solution.py:533
  134.7 3.1 %collective-permute-start.36 = (bf16[512,256]{1,0:T(8,128)(2,1)S(1)}, bf16[512,256]{1,0:T(8,128)(2,1)S(1)}, u32[]{:S(2)}, u32[]{:S(2)}) collective-permute-start(bf16[512,256]{1,0:T(8,128)(2,1)S(1)} %get-tuple-element.183), channel_id=1, source_target_pairs={{0,4},{4,0},{8,12},{12,8},{16,20},{20,16},{24,28},{28,24},{1,5},{5... | collective-permute-start | bytes 786440 | tf_op jit(solution)/shard_map/ppermute | solution.py:533
  134.8 5.9 %collective-permute-start.33 = (f32[24,128]{1,0:T(8,128)S(1)}, f32[24,128]{1,0:T(8,128)S(1)}, u32[]{:S(2)}, u32[]{:S(2)}) collective-permute-start(f32[24,128]{1,0:T(8,128)S(1)} %add.49), channel_id=1, source_target_pairs={{0,2},{1,3},{2,0},{3,1},{4,6},{5,7},{6,4},{7,5},{8,10},{9,11},{10,... | collective-permute-start | bytes 36872 | tf_op jit(solution)/shard_map/ppermute | solution.py:533
  135.3 17.9 %collective-permute-start.38 = (bf16[144,1024]{1,0:T(8,128)(2,1)S(1)}, bf16[144,1024]{1,0:T(8,128)(2,1)S(1)}, u32[]{:S(2)}, u32[]{:S(2)}) collective-permute-start(bf16[144,1024]{1,0:T(8,128)(2,1)S(1)} %get-tuple-element.182), channel_id=1, source_target_pairs={{0,1},{1,0},{2,3},{3,2},{4,5},{5,4},{6,7},{7,6},{8,9},{9,8},{10,11... | collective-permute-start | bytes 884744 | tf_op jit(solution)/shard_map/ppermute | solution.py:533
  137.1 16.1 %collective-permute-start.39 = (bf16[144,1024]{1,0:T(8,128)(2,1)S(1)}, bf16[144,1024]{1,0:T(8,128)(2,1)S(1)}, u32[]{:S(2)}, u32[]{:S(2)}) collective-permute-start(bf16[144,1024]{1,0:T(8,128)(2,1)S(1)} %get-tuple-element.189), channel_id=1, source_target_pairs={{0,2},{1,3},{2,0},{3,1},{4,6},{5,7},{6,4},{7,5},{8,10},{9,11},{10,... | collective-permute-start | bytes 884744 | tf_op jit(solution)/shard_map/ppermute | solution.py:533
  138.0 15.2 %copy-start.32 = (f32[1024]{0:T(1024)S(1)}, f32[1024]{0:T(1024)}, u32[]{:S(2)}) copy-start(f32[1024]{0:T(1024)} %param.17) | copy-start | bytes 12292
  138.0 12.0 %collective-permute-start.37 = (bf16[256,768]{1,0:T(8,128)(2,1)S(1)}, bf16[256,768]{1,0:T(8,128)(2,1)S(1)}, u32[]{:S(2)}, u32[]{:S(2)}) collective-permute-start(bf16[256,768]{1,0:T(8,128)(2,1)S(1)} %get-tuple-element.185), channel_id=1, source_target_pairs={{0,8},{4,20},{8,0},{12,28},{16,24},{20,4},{24,16},{28,12},{1,9},{5... | collective-permute-start | bytes 1179656 | tf_op jit(solution)/shard_map/ppermute | solution.py:538
  139.1 33.2 %collective-permute-start.40 = (bf16[128,3456]{1,0:T(8,128)(2,1)S(1)}, bf16[128,3456]{1,0:T(8,128)(2,1)S(1)}, u32[]{:S(2)}, u32[]{:S(2)}) collective-permute-start(bf16[128,3456]{1,0:T(8,128)(2,1)S(1)} %get-tuple-element.192), channel_id=1, source_target_pairs={{0,16},{4,12},{8,24},{12,4},{16,0},{20,28},{24,8},{28,20},{1,17},{... | collective-permute-start | bytes 2654216 | tf_op jit(solution)/shard_map/ppermute | solution.py:538
  153.5 9.0 %collective-permute-start.42 = (bf16[96,1024]{1,0:T(8,128)(2,1)S(1)}, bf16[96,1024]{1,0:T(8,128)(2,1)S(1)}, u32[]{:S(2)}, u32[]{:S(2)}) collective-permute-start(bf16[96,1024]{1,0:T(8,128)(2,1)S(1)} %shard_map.262.refs_0_), channel_id=1, source_target_pairs={{0,2},{1,3},{2,0},{3,1},{4,6},{5,7},{6,4},{7,5},{8,10},{9,11},{10,... | collective-permute-start | bytes 589832 | tf_op jit(solution)/shard_map/ppermute | solution.py:533
  153.9 8.6 %collective-permute-start.41 = (bf16[96,1024]{1,0:T(8,128)(2,1)S(1)}, bf16[96,1024]{1,0:T(8,128)(2,1)S(1)}, u32[]{:S(2)}, u32[]{:S(2)}) collective-permute-start(bf16[96,1024]{1,0:T(8,128)(2,1)S(1)} %shard_map.262.refs_0_), channel_id=1, source_target_pairs={{0,1},{1,0},{2,3},{3,2},{4,5},{5,4},{6,7},{7,6},{8,9},{9,8},{10,11... | collective-permute-start | bytes 589832 | tf_op jit(solution)/shard_map/ppermute | solution.py:533
  156.2 9.0 %collective-permute-start.48 = (bf16[128,768]{1,0:T(8,128)(2,1)S(1)}, bf16[128,768]{1,0:T(8,128)(2,1)S(1)}, u32[]{:S(2)}, u32[]{:S(2)}) collective-permute-start(bf16[128,768]{1,0:T(8,128)(2,1)S(1)} %get-tuple-element.199), channel_id=1, source_target_pairs={{0,16},{4,12},{8,24},{12,4},{16,0},{20,28},{24,8},{28,20},{1,17},{... | collective-permute-start | bytes 589832 | tf_op jit(solution)/shard_map/ppermute | solution.py:538
  156.7 1.2 collective-permute-start.43
  157.9 3.7 %collective-permute-start.44 = (f32[24,128]{1,0:T(8,128)S(1)}, f32[24,128]{1,0:T(8,128)S(1)}, u32[]{:S(2)}, u32[]{:S(2)}) collective-permute-start(f32[24,128]{1,0:T(8,128)S(1)} %add.51), channel_id=1, source_target_pairs={{0,8},{4,12},{8,0},{12,4},{16,24},{20,28},{24,16},{28,20},{1,9},{5... | collective-permute-start | bytes 36872 | tf_op jit(solution)/shard_map/ppermute | solution.py:533
  162.4 12.0 %collective-permute-start.46 = (bf16[48,1024]{1,0:T(8,128)(2,1)S(1)}, bf16[48,1024]{1,0:T(8,128)(2,1)S(1)}, u32[]{:S(2)}, u32[]{:S(2)}) collective-permute-start(bf16[48,1024]{1,0:T(8,128)(2,1)S(1)} %slice.79), channel_id=1, source_target_pairs={{0,2},{1,3},{2,0},{3,1},{4,6},{5,7},{6,4},{7,5},{8,10},{9,11},{10,... | collective-permute-start | bytes 294920 | tf_op jit(solution)/shard_map/ppermute | solution.py:533
  164.9 9.5 %collective-permute-start.45 = (bf16[48,1024]{1,0:T(8,128)(2,1)S(1)}, bf16[48,1024]{1,0:T(8,128)(2,1)S(1)}, u32[]{:S(2)}, u32[]{:S(2)}) collective-permute-start(bf16[48,1024]{1,0:T(8,128)(2,1)S(1)} %slice.78), channel_id=1, source_target_pairs={{0,1},{1,0},{2,3},{3,2},{4,5},{5,4},{6,7},{7,6},{8,9},{9,8},{10,11... | collective-permute-start | bytes 294920 | tf_op jit(solution)/shard_map/ppermute | solution.py:533
  165.9 7.9 %collective-permute-start.49 = (bf16[256,128]{1,0:T(8,128)(2,1)S(1)}, bf16[256,128]{1,0:T(8,128)(2,1)S(1)}, u32[]{:S(2)}, u32[]{:S(2)}) collective-permute-start(bf16[256,128]{1,0:T(8,128)(2,1)S(1)} %get-tuple-element.200), channel_id=1, source_target_pairs={{0,0},{1,8},{2,16},{3,24},{4,4},{5,12},{6,20},{7,28},{8,1},{9,9},{... | collective-permute-start | bytes 196616 | tf_op jit(solution)/shard_map/ppermute | solution.py:823
  166.6 7.2 %collective-permute-start.47 = (f32[24,128]{1,0:T(8,128)S(1)}, f32[24,128]{1,0:T(8,128)S(1)}, u32[]{:S(2)}, u32[]{:S(2)}) collective-permute-start(f32[24,128]{1,0:T(8,128)S(1)} %add.52.a_ref), channel_id=1, source_target_pairs={{0,16},{4,20},{8,24},{12,28},{16,0},{20,4},{24,8},{28,12},{1,17},{... | collective-permute-start | bytes 36872 | tf_op jit(solution)/shard_map/ppermute | solution.py:533
  (26 other events, 116.1 us)

commit v6 on v5

--- a/solution.py
+++ b/solution.py
@@ -806,7 +806,7 @@
         )
         query_w, key_w, value_w, out_w = call(
             attn_grad_sum_kernel,
-            [after(attn_here, input_parts[1]), swap_across(attn_send, 1)],
+            [after(attn_here, input_own), swap_across(attn_send, 1)],
             [
                 shape((block, 256), f32),
                 shape((block, 128), f32),

time: 177 us -> 177 us (level)
  no operation moved by 1% of the time
where the time goes in v6:
time: 177 us; the launch traced here: 176 us
  waiting for transfers between devices  68.4 us (39%)
  starting transfers between devices  62.9 us (36%)
  Pallas kernels  35.5 us (20%)
  local copies, waits for them, and re-layouts  6.51 us (4%)
    ppermute x45, waiting for transfers between devices, swap(): return lax.ppermute(x, axis, [(i, i ^ k) for i in range(size)])  59.1 us
    ppermute x45, starting transfers between devices, swap(): return lax.ppermute(x, axis, [(i, i ^ k) for i in range(size)])  57.7 us
    pallas_call x22, Pallas kernels, call(): pl.pallas_call(body, out_shape=outs, in_specs=in_specs, out_specs=out_spe...  35.5 us
    ppermute x4, waiting for transfers between devices, swap_across(): lax.ppermute(x, 'ctx', [(i, i ^ 2 << (i + step) % 2) for i in range(size)])  9.29 us
    unnamed x83, local copies, waits for them, and re-layouts  5.35 us
    ppermute x4, starting transfers between devices, swap_across(): lax.ppermute(x, 'ctx', [(i, i ^ 2 << (i + step) % 2) for i in range(size)])  4.59 us
  transfers between devices with their start and end apart: 50, of which 22 were waited for; matrix products, arithmetic and copies ran while one was open for 1% of the time, Pallas kernels for 14%

profile of v6, /device:TPU:0, one launch (start us, length us, event | category | flops | bytes accessed | tf_op | source)
XLA Modules:
  0.0 175.7 jit_solution(9274879842953689151)
XLA Ops:
  0.7 1.0 constant_dynamic-slice_fusion
  1.6 4.1 %collective-permute-start.1 = (bf16[128,1024]{1,0:T(8,128)(2,1)S(1)}, bf16[128,1024]{1,0:T(8,128)(2,1)S(1)}, u32[]{:S(2)}, u32[]{:S(2)}) collective-permute-start(bf16[128,1024]{1,0:T(8,128)(2,1)S(1)} %constant_dynamic-slice_fusion), channel_id=1, source_target_pairs={{0,2},{1,3},{2,0},{3,1},{4,6},{5,7},{6,4},{7,5},{8,10},{9,11},{10,... | collective-permute-start | bytes 786440 | tf_op jit(solution)/shard_map/ppermute | solution.py:533
  5.7 1.6 collective-permute-start
  7.3 3.9 %shard_map.246 = (bf16[384,1024]{1,0:T(8,128)(2,1)}, bf16[384,256]{1,0:T(8,128)(2,1)}, f32[384,128]{1,0:T(8,128)}, f32[384,128]{1,0:T(8,128)}, f32[384,128]{1,0:T(8,128)}) custom-call(s32[8]{0:T(128)} %starts_ref.5, bf16[384,1024]{1,0:T(8,128)(2,1)} %x_ref.5, f32[1,1024]{1,0:T(1,128)} %bitcast.16, bf16[1024,128]{1,0:T(8,128)(2,1)} %refs_8_.1, ...), custom_call_target="tpu_custom_call" | custom-call | flops 49999998976 | bytes 2888480 | tf_op jit(solution)/shard_map/pallas_call | solution.py:39
  11.2 2.4 %collective-permute-start.6 = (bf16[384,256]{1,0:T(8,128)(2,1)}, bf16[384,256]{1,0:T(8,128)(2,1)S(1)}, u32[]{:S(2)}, u32[]{:S(2)}) collective-permute-start(bf16[384,256]{1,0:T(8,128)(2,1)} %get-tuple-element.117), channel_id=1, source_target_pairs={{0,24},{4,28},{8,16},{12,20},{16,8},{20,12},{24,0},{28,4},{1,25},{... | collective-permute-start | bytes 589832 | tf_op jit(solution)/shard_map/ppermute | solution.py:533
  14.7 1.1 copy-done
  15.8 0.9 copy-done.7
  16.8 0.9 copy-done.9
  17.7 0.9 shard_map.247
  18.7 4.0 %collective-permute-done.4 = bf16[384,256]{1,0:T(8,128)(2,1)S(1)} collective-permute-done((bf16[384,256]{1,0:T(8,128)(2,1)}, bf16[384,256]{1,0:T(8,128)(2,1)S(1)}, u32[]{:S(2)}, u32[]{:S(2)}) %collective-permute-start.4) | collective-permute-done | bytes 196640 | tf_op jit(solution)/shard_map/ppermute | solution.py:533
  23.8 1.3 collective-permute-done.7.refs_1_
  25.2 2.2 %shard_map.248 = (bf16[384,256]{1,0:T(8,128)(2,1)S(1)}, f32[384,256]{1,0:T(8,128)S(1)}, f32[2,768]{1,0:T(2,128)S(1)}) custom-call(s32[8]{0:T(128)S(1)} %copy-done.33, bf16[1536,128]{1,0:T(8,128)(2,1)S(1)} %get-tuple-element.143.qpad_ref, bf16[1536,256]{1,0:T(8,128)(2,1)S(1)} %constant_dynamic-update-slice_fusion.refs_0_, ...), custom_call_target="tpu_custom_call" | custom-call | flops 49999998976 | bytes 2562080 | tf_op jit(solution)/shard_map/pallas_call | solution.py:39
  27.4 0.9 copy-done.27
  28.2 2.1 %collective-permute-done.2 = bf16[64,1024]{1,0:T(8,128)(2,1)S(1)} collective-permute-done((bf16[64,1024]{1,0:T(8,128)(2,1)S(1)}, bf16[64,1024]{1,0:T(8,128)(2,1)S(1)}, u32[]{:S(2)}, u32[]{:S(2)}) %collective-permute-start.2) | collective-permute-done | bytes 131104 | tf_op jit(solution)/shard_map/ppermute | solution.py:533
  30.4 2.5 %collective-permute-done.3 = bf16[64,1024]{1,0:T(8,128)(2,1)S(1)} collective-permute-done((bf16[64,1024]{1,0:T(8,128)(2,1)S(1)}, bf16[64,1024]{1,0:T(8,128)(2,1)S(1)}, u32[]{:S(2)}, u32[]{:S(2)}) %collective-permute-start.3) | collective-permute-done | bytes 131104 | tf_op jit(solution)/shard_map/ppermute | solution.py:533
  33.4 1.7 collective-permute-start.9
  35.1 9.3 %collective-permute-done.10.refs_2_.refs_3_ = bf16[384,256]{1,0:T(8,128)(2,1)S(1)} collective-permute-done((bf16[384,256]{1,0:T(8,128)(2,1)S(1)}, bf16[384,256]{1,0:T(8,128)(2,1)S(1)}, u32[]{:S(2)}, u32[]{:S(2)}) %collective-permute-start.10) | collective-permute-done | bytes 196640 | tf_op jit(solution)/shard_map/ppermute | solution.py:533
  44.6 2.9 %collective-permute-start.12 = (bf16[192,256]{1,0:T(8,128)(2,1)S(1)}, bf16[192,256]{1,0:T(8,128)(2,1)S(1)}, u32[]{:S(2)}, u32[]{:S(2)}) collective-permute-start(bf16[192,256]{1,0:T(8,128)(2,1)S(1)} %slice.83), channel_id=1, source_target_pairs={{0,2},{1,3},{2,0},{3,1},{4,6},{5,7},{6,4},{7,5},{8,10},{9,11},{10,... | collective-permute-start | bytes 294920 | tf_op jit(solution)/shard_map/ppermute | solution.py:533
  47.5 3.4 %collective-permute-done.11.refs_3_.refs_4_ = bf16[192,256]{1,0:T(8,128)(2,1)S(1)} collective-permute-done((bf16[192,256]{1,0:T(8,128)(2,1)S(1)}, bf16[192,256]{1,0:T(8,128)(2,1)S(1)}, u32[]{:S(2)}, u32[]{:S(2)}) %collective-permute-start.11) | collective-permute-done | bytes 98336 | tf_op jit(solution)/shard_map/ppermute | solution.py:533
  50.9 1.4 collective-permute-done.12.refs_4_.refs_5_
  52.4 1.8 %shard_map.249 = (bf16[384,1024]{1,0:T(8,128)(2,1)S(1)}, f32[96,1024]{1,0:T(8,128)S(1)}) custom-call(bf16[384,1024]{1,0:T(8,128)(2,1)S(1)} %copy-done.25, f32[1,1024]{1,0:T(1,128)S(1)} %bitcast.14, bf16[256,1024]{1,0:T(8,128)(2,1)S(1)} %copy-done.13, bf16[3,128,1024]{2,1,0:T(8,128)(2,1)S(1)} %pad_maximum_fusion.wm_ref, ...), custom_call_target="tpu_custom_call" | custom-call | flops 49999998976 | bytes 4853760 | tf_op jit(solution)/shard_map/pallas_call | solution.py:39
  55.6 5.8 %shard_map.250 = (bf16[384,1152]{1,0:T(8,128)(2,1)S(1)}, bf16[384,1152]{1,0:T(8,128)(2,1)S(1)}, bf16[384,1152]{1,0:T(8,128)(2,1)S(1)}, bf16[96,1024]{1,0:T(8,128...) custom-call(bf16[384,1024]{1,0:T(8,128)(2,1)S(1)} %get-tuple-element, ...), custom_call_target="tpu_custom_call" | custom-call | flops 49999998976 | bytes 12091392 | tf_op jit(solution)/shard_map/pallas_call | solution.py:39
  61.7 2.7 %collective-permute-start.14 = (bf16[48,1024]{1,0:T(8,128)(2,1)S(1)}, bf16[48,1024]{1,0:T(8,128)(2,1)S(1)}, u32[]{:S(2)}, u32[]{:S(2)}) collective-permute-start(bf16[48,1024]{1,0:T(8,128)(2,1)S(1)} %get-tuple-element.134), channel_id=1, source_target_pairs={{0,2},{1,3},{2,0},{3,1},{4,6},{5,7},{6,4},{7,5},{8,10},{9,11},{10,... | collective-permute-start | bytes 294920 | tf_op jit(solution)/shard_map/ppermute | solution.py:533
  64.4 4.3 %shard_map.251 = (bf16[512,3456]{1,0:T(8,128)(2,1)S(1)}, bf16[512,3456]{1,0:T(8,128)(2,1)S(1)}) custom-call(bf16[384,1024]{1,0:T(8,128)(2,1)S(1)} %get-tuple-element.124.h_ref, bf16[384,1024]{1,0:T(8,128)(2,1)S(1)} %copy-done.24, bf16[384,1152]{1,0:T(8,128)(2,1)S(1)} %get-tuple-element.125.act_ref, bf16[384,1152]{1,0:T(8,128)(2,1)S(1)} %get-tuple-element.128.dg_ref, ...), custom_call_target="tpu_custom_call" | custom-call | flops 49999998976 | bytes 11304960 | tf_op jit(solution)/shard_map/pallas_call | solution.py:39
  69.1 1.8 %collective-permute-start.16 = (bf16[96,1024]{1,0:T(8,128)(2,1)S(1)}, bf16[96,1024]{1,0:T(8,128)(2,1)S(1)}, u32[]{:S(2)}, u32[]{:S(2)}) collective-permute-start(bf16[96,1024]{1,0:T(8,128)(2,1)S(1)} %get-tuple-element.136), channel_id=1, source_target_pairs={{0,2},{1,3},{2,0},{3,1},{4,6},{5,7},{6,4},{7,5},{8,10},{9,11},{10,... | collective-permute-start | bytes 589832 | tf_op jit(solution)/shard_map/ppermute | solution.py:533
  70.9 6.2 %collective-permute-done.15.refs_1_ = bf16[96,1024]{1,0:T(8,128)(2,1)S(1)} collective-permute-done((bf16[96,1024]{1,0:T(8,128)(2,1)S(1)}, bf16[96,1024]{1,0:T(8,128)(2,1)S(1)}, u32[]{:S(2)}, u32[]{:S(2)}) %collective-permute-start.15) | collective-permute-done | bytes 196640 | tf_op jit(solution)/shard_map/ppermute | solution.py:533
  77.1 1.6 collective-permute-done.16.refs_2_
  78.7 0.9 shard_map.253
  80.1 2.6 %collective-permute-start.22 = (bf16[96,256]{1,0:T(8,128)(2,1)S(1)}, bf16[96,256]{1,0:T(8,128)(2,1)S(1)}, u32[]{:S(2)}, u32[]{:S(2)}) collective-permute-start(bf16[96,256]{1,0:T(8,128)(2,1)S(1)} %get-tuple-element.148), channel_id=1, source_target_pairs={{0,2},{1,3},{2,0},{3,1},{4,6},{5,7},{6,4},{7,5},{8,10},{9,11},{10,... | collective-permute-start | bytes 147464 | tf_op jit(solution)/shard_map/ppermute | solution.py:533
  82.7 1.4 collective-permute-start.23
  84.1 1.5 shard_map.254
  85.8 2.9 %collective-permute-start.17 = (bf16[96,1280]{1,0:T(8,128)(2,1)S(1)}, bf16[96,1280]{1,0:T(8,128)(2,1)S(1)}, u32[]{:S(2)}, u32[]{:S(2)}) collective-permute-start(bf16[96,1280]{1,0:T(8,128)(2,1)S(1)} %get-tuple-element.139), channel_id=1, source_target_pairs={{0,1},{1,0},{2,3},{3,2},{4,5},{5,4},{6,7},{7,6},{8,9},{9,8},{10,11... | collective-permute-start | bytes 737288 | tf_op jit(solution)/shard_map/ppermute | solution.py:533
  89.0 1.5 collective-permute-start.19
  90.4 1.5 collective-permute-start.30
  92.0 3.4 %shard_map.255 = (bf16[384,256]{1,0:T(8,128)(2,1)S(1)}, bf16[1536,256]{1,0:T(8,128)(2,1)S(1)}, bf16[1536,256]{1,0:T(8,128)(2,1)S(1)}) custom-call(s32[8]{0:T(128)S(1)} %copy-done.34, bf16[1536,128]{1,0:T(8,128)(2,1)S(1)} %copy-done.37, f32[384,256]{1,0:T(8,128)S(1)} %get-tuple-element.144.o32_ref, f32[2,768]{1,0:T(2,128)S(1)} %get-tuple-element.145.lse_ref, ...), custom_call_target="tpu_custom_call" | custom-call | flops 49999998976 | bytes 4331552 | tf_op jit(solution)/shard_map/pallas_call | solution.py:39
  95.5 8.0 %collective-permute-done.18.refs_2_ = bf16[96,1280]{1,0:T(8,128)(2,1)S(1)} collective-permute-done((bf16[96,1280]{1,0:T(8,128)(2,1)S(1)}, bf16[96,1280]{1,0:T(8,128)(2,1)S(1)}, u32[]{:S(2)}, u32[]{:S(2)}) %collective-permute-start.18) | collective-permute-done | bytes 245792 | tf_op jit(solution)/shard_map/ppermute | solution.py:533
  103.6 5.0 %collective-permute-start.29 = (bf16[96,1024]{1,0:T(8,128)(2,1)S(1)}, bf16[96,1024]{1,0:T(8,128)(2,1)S(1)}, u32[]{:S(2)}, u32[]{:S(2)}) collective-permute-start(bf16[96,1024]{1,0:T(8,128)(2,1)S(1)} %get-tuple-element.190.own_ref), channel_id=1, source_target_pairs={{0,2},{1,3},{2,0},{3,1},{4,6},{5,7},{6,4},{7,5},{8,10},{9,11},{10,... | collective-permute-start | bytes 589832 | tf_op jit(solution)/shard_map/ppermute | solution.py:533
  108.8 4.6 %collective-permute-start.27 = (bf16[384,256]{1,0:T(8,128)(2,1)S(1)}, bf16[384,256]{1,0:T(8,128)(2,1)S(1)}, u32[]{:S(2)}, u32[]{:S(2)}) collective-permute-start(bf16[384,256]{1,0:T(8,128)(2,1)S(1)} %get-tuple-element.213), channel_id=1, source_target_pairs={{0,24},{4,28},{8,16},{12,20},{16,8},{20,12},{24,0},{28,4},{1,25},{... | collective-permute-start | bytes 589832 | tf_op jit(solution)/shard_map/ppermute | solution.py:533
  113.5 2.3 %shard_map.257 = (bf16[384,256]{1,0:T(8,128)(2,1)}, f32[1,128]{1,0:T(1,128)S(1)}, f32[384,1024]{1,0:T(8,128)S(1)}, bf16[512,512]{1,0:T(8,128)(2,1)S(1)}, bf16[512,512]{1,0:T(8,128)(2,1)S(1)}) custom-call(bf16[384,256]{1,0:T(8,128)(2,1)S(1)} %get-tuple-element.164.dq_ref, f32[384,256]{1,0:T(8,128)S(1)} %get-tuple-element.165.qpre_ref, ...), custom_call_target="tpu_custom_call" | custom-call | flops 1 | bytes 6095616 | tf_op jit(solution)/shard_map/pallas_call | solution.py:39
  116.4 2.1 %collective-permute-done.29.refs_1_.two_ref = bf16[96,1024]{1,0:T(8,128)(2,1)S(1)} collective-permute-done((bf16[96,1024]{1,0:T(8,128)(2,1)S(1)}, bf16[96,1024]{1,0:T(8,128)(2,1)S(1)}, u32[]{:S(2)}, u32[]{:S(2)}) %collective-permute-start.29) | collective-permute-done | bytes 196640 | tf_op jit(solution)/shard_map/ppermute | solution.py:533
  119.3 1.2 collective-permute-done.31.q_got_ref
  120.6 3.0 %collective-permute-done.26.refs_2_ = bf16[384,256]{1,0:T(8,128)(2,1)S(1)} collective-permute-done((bf16[384,256]{1,0:T(8,128)(2,1)S(1)}, bf16[384,256]{1,0:T(8,128)(2,1)S(1)}, u32[]{:S(2)}, u32[]{:S(2)}) %collective-permute-start.26) | collective-permute-done | bytes 196640 | tf_op jit(solution)/shard_map/ppermute | solution.py:533
  123.7 2.5 %shard_map.258 = (bf16[384,256]{1,0:T(8,128)(2,1)}, f32[24,128]{1,0:T(8,128)S(1)}, bf16[96,1024]{1,0:T(8,128)(2,1)S(1)}, bf16[96,1024]{1,0:T(8,128)(2,1)S(1)}, b...) custom-call(bf16[384,256]{1,0:T(8,128)(2,1)S(1)} %get-tuple-element., ...), custom_call_target="tpu_custom_call" | custom-call | flops 49999998976 | bytes 6570752 | tf_op jit(solution)/shard_map/pallas_call | solution.py:39
  126.2 1.0 collective-permute-start.34
  127.2 1.1 collective-permute-start.35
  128.3 1.1 collective-permute-start.32
  129.4 2.7 %collective-permute-done.32 = f32[24,128]{1,0:T(8,128)S(1)} collective-permute-done((f32[24,128]{1,0:T(8,128)S(1)}, f32[24,128]{1,0:T(8,128)S(1)}, u32[]{:S(2)}, u32[]{:S(2)}) %collective-permute-start.32) | collective-permute-done | bytes 12320 | tf_op jit(solution)/shard_map/ppermute | solution.py:533
  132.1 2.5 %collective-permute-done.35.got_two_ref = bf16[48,1024]{1,0:T(8,128)(2,1)S(1)} collective-permute-done((bf16[48,1024]{1,0:T(8,128)(2,1)S(1)}, bf16[48,1024]{1,0:T(8,128)(2,1)S(1)}, u32[]{:S(2)}, u32[]{:S(2)}) %collective-permute-start.35) | collective-permute-done | bytes 98336 | tf_op jit(solution)/shard_map/ppermute | solution.py:533
  135.3 1.9 %collective-permute-start.38 = (bf16[144,1024]{1,0:T(8,128)(2,1)S(1)}, bf16[144,1024]{1,0:T(8,128)(2,1)S(1)}, u32[]{:S(2)}, u32[]{:S(2)}) collective-permute-start(bf16[144,1024]{1,0:T(8,128)(2,1)S(1)} %get-tuple-element.182), channel_id=1, source_target_pairs={{0,1},{1,0},{2,3},{3,2},{4,5},{5,4},{6,7},{7,6},{8,9},{9,8},{10,11... | collective-permute-start | bytes 884744 | tf_op jit(solution)/shard_map/ppermute | solution.py:533
  138.0 1.0 collective-permute-start.37
  139.1 1.6 collective-permute-start.40
  140.7 9.3 %collective-permute-done.37.got_ref = bf16[256,768]{1,0:T(8,128)(2,1)S(1)} collective-permute-done((bf16[256,768]{1,0:T(8,128)(2,1)S(1)}, bf16[256,768]{1,0:T(8,128)(2,1)S(1)}, u32[]{:S(2)}, u32[]{:S(2)}) %collective-permute-start.37) | collective-permute-done | bytes 393248 | tf_op jit(solution)/shard_map/ppermute | solution.py:538
  150.1 3.1 %collective-permute-done.39.refs_2_.high_ref = bf16[144,1024]{1,0:T(8,128)(2,1)S(1)} collective-permute-done((bf16[144,1024]{1,0:T(8,128)(2,1)S(1)}, bf16[144,1024]{1,0:T(8,128)(2,1)S(1)}, u32[]{:S(2)}, u32[]{:S(2)}) %collective-permute-start.39) | collective-permute-done | bytes 294944 | tf_op jit(solution)/shard_map/ppermute | solution.py:533
  153.9 2.4 %collective-permute-start.41 = (bf16[96,1024]{1,0:T(8,128)(2,1)S(1)}, bf16[96,1024]{1,0:T(8,128)(2,1)S(1)}, u32[]{:S(2)}, u32[]{:S(2)}) collective-permute-start(bf16[96,1024]{1,0:T(8,128)(2,1)S(1)} %shard_map.262.refs_0_), channel_id=1, source_target_pairs={{0,1},{1,0},{2,3},{3,2},{4,5},{5,4},{6,7},{7,6},{8,9},{9,8},{10,11... | collective-permute-start | bytes 589832 | tf_op jit(solution)/shard_map/ppermute | solution.py:533
  156.7 1.2 collective-permute-done.43
  157.9 1.4 collective-permute-start.44
  159.3 2.3 %collective-permute-done.44 = f32[24,128]{1,0:T(8,128)S(1)} collective-permute-done((f32[24,128]{1,0:T(8,128)S(1)}, f32[24,128]{1,0:T(8,128)S(1)}, u32[]{:S(2)}, u32[]{:S(2)}) %collective-permute-start.44) | collective-permute-done | bytes 12320 | tf_op jit(solution)/shard_map/ppermute | solution.py:533
  161.6 0.8 collective-permute-done.42.refs_2_
  162.4 2.5 %collective-permute-start.46 = (bf16[48,1024]{1,0:T(8,128)(2,1)S(1)}, bf16[48,1024]{1,0:T(8,128)(2,1)S(1)}, u32[]{:S(2)}, u32[]{:S(2)}) collective-permute-start(bf16[48,1024]{1,0:T(8,128)(2,1)S(1)} %slice.79), channel_id=1, source_target_pairs={{0,2},{1,3},{2,0},{3,1},{4,6},{5,7},{6,4},{7,5},{8,10},{9,11},{10,... | collective-permute-start | bytes 294920 | tf_op jit(solution)/shard_map/ppermute | solution.py:533
  165.2 0.7 shard_map.266
  166.6 4.8 %collective-permute-start.47 = (f32[24,128]{1,0:T(8,128)S(1)}, f32[24,128]{1,0:T(8,128)S(1)}, u32[]{:S(2)}, u32[]{:S(2)}) collective-permute-start(f32[24,128]{1,0:T(8,128)S(1)} %add.52.a_ref), channel_id=1, source_target_pairs={{0,16},{4,20},{8,24},{12,28},{16,0},{20,4},{24,8},{28,12},{1,17},{... | collective-permute-start | bytes 36872 | tf_op jit(solution)/shard_map/ppermute | solution.py:533
  171.4 0.9 shard_map.263
  172.3 1.5 shard_map.264
  174.5 1.3 shard_map.265
  (159 shorter events, 12.0 us)
Async XLA Ops:
  1.6 17.0 %collective-permute-start.1 = (bf16[128,1024]{1,0:T(8,128)(2,1)S(1)}, bf16[128,1024]{1,0:T(8,128)(2,1)S(1)}, u32[]{:S(2)}, u32[]{:S(2)}) collective-permute-start(bf16[128,1024]{1,0:T(8,128)(2,1)S(1)} %constant_dynamic-slice_fusion), channel_id=1, source_target_pairs={{0,2},{1,3},{2,0},{3,1},{4,6},{5,7},{6,4},{7,5},{8,10},{9,11},{10,... | collective-permute-start | bytes 786440 | tf_op jit(solution)/shard_map/ppermute | solution.py:533
  5.7 12.9 %collective-permute-start = (bf16[128,1024]{1,0:T(8,128)(2,1)S(1)}, bf16[128,1024]{1,0:T(8,128)(2,1)S(1)}, u32[]{:S(2)}, u32[]{:S(2)}) collective-permute-start(bf16[128,1024]{1,0:T(8,128)(2,1)S(1)} %constant_dynamic-slice_fusion), channel_id=1, source_target_pairs={{0,1},{1,0},{2,3},{3,2},{4,5},{5,4},{6,7},{7,6},{8,9},{9,8},{10,11... | collective-permute-start | bytes 786440 | tf_op jit(solution)/shard_map/ppermute | solution.py:533
  11.2 11.6 %collective-permute-start.6 = (bf16[384,256]{1,0:T(8,128)(2,1)}, bf16[384,256]{1,0:T(8,128)(2,1)S(1)}, u32[]{:S(2)}, u32[]{:S(2)}) collective-permute-start(bf16[384,256]{1,0:T(8,128)(2,1)} %get-tuple-element.117), channel_id=1, source_target_pairs={{0,24},{4,28},{8,16},{12,20},{16,8},{20,12},{24,0},{28,4},{1,25},{... | collective-permute-start | bytes 589832 | tf_op jit(solution)/shard_map/ppermute | solution.py:533
  13.6 9.1 %collective-permute-start.5 = (bf16[384,256]{1,0:T(8,128)(2,1)}, bf16[384,256]{1,0:T(8,128)(2,1)S(1)}, u32[]{:S(2)}, u32[]{:S(2)}) collective-permute-start(bf16[384,256]{1,0:T(8,128)(2,1)} %get-tuple-element.117), channel_id=1, source_target_pairs={{0,16},{4,20},{8,24},{12,28},{16,0},{20,4},{24,8},{28,12},{1,17},{... | collective-permute-start | bytes 589832 | tf_op jit(solution)/shard_map/ppermute | solution.py:533
  14.2 8.5 %collective-permute-start.4 = (bf16[384,256]{1,0:T(8,128)(2,1)}, bf16[384,256]{1,0:T(8,128)(2,1)S(1)}, u32[]{:S(2)}, u32[]{:S(2)}) collective-permute-start(bf16[384,256]{1,0:T(8,128)(2,1)} %get-tuple-element.117), channel_id=1, source_target_pairs={{0,8},{4,12},{8,0},{12,4},{16,24},{20,28},{24,16},{28,20},{1,9},{5... | collective-permute-start | bytes 589832 | tf_op jit(solution)/shard_map/ppermute | solution.py:533
  22.8 2.4 %collective-permute-start.7 = (bf16[1536,256]{1,0:T(8,128)(2,1)S(1)}, bf16[1536,256]{1,0:T(8,128)(2,1)S(1)}, u32[]{:S(2)}, u32[]{:S(2)}) collective-permute-start(bf16[1536,256]{1,0:T(8,128)(2,1)S(1)} %constant_dynamic-update-slice_fusion.refs_0_), channel_id=1, source_target_pairs={{0,4},{4,0},{8,12},{12,8},{16,20},{20,16},{24,28},{28,24},{1,5},{5... | collective-permute-start | bytes 2359304 | tf_op jit(solution)/shard_map/ppermute | solution.py:533
  22.9 7.5 %collective-permute-start.2 = (bf16[64,1024]{1,0:T(8,128)(2,1)S(1)}, bf16[64,1024]{1,0:T(8,128)(2,1)S(1)}, u32[]{:S(2)}, u32[]{:S(2)}) collective-permute-start(bf16[64,1024]{1,0:T(8,128)(2,1)S(1)} %slice.80), channel_id=1, source_target_pairs={{0,1},{1,0},{2,3},{3,2},{4,5},{5,4},{6,7},{7,6},{8,9},{9,8},{10,11... | collective-permute-start | bytes 393224 | tf_op jit(solution)/shard_map/ppermute | solution.py:533
  23.4 9.4 %collective-permute-start.3 = (bf16[64,1024]{1,0:T(8,128)(2,1)S(1)}, bf16[64,1024]{1,0:T(8,128)(2,1)S(1)}, u32[]{:S(2)}, u32[]{:S(2)}) collective-permute-start(bf16[64,1024]{1,0:T(8,128)(2,1)S(1)} %slice.81), channel_id=1, source_target_pairs={{0,2},{1,3},{2,0},{3,1},{4,6},{5,7},{6,4},{7,5},{8,10},{9,11},{10,... | collective-permute-start | bytes 393224 | tf_op jit(solution)/shard_map/ppermute | solution.py:533
  28.2 26.0 %copy-start.11 = (bf16[384,256]{1,0:T(8,128)(2,1)}, bf16[384,256]{1,0:T(8,128)(2,1)S(1)}, u32[]{:S(2)}) copy-start(bf16[384,256]{1,0:T(8,128)(2,1)S(1)} %get-tuple-element.118.refs_0_.refs_1_) | copy-start | bytes 589828
  28.2 24.1 %copy-start.13 = (bf16[256,1024]{1,0:T(8,128)(2,1)S(1)}, bf16[256,1024]{1,0:T(8,128)(2,1)}, u32[]{:S(2)}) copy-start(bf16[256,1024]{1,0:T(8,128)(2,1)} %w0_ref.3) | copy-start | bytes 1572868
  28.2 24.1 %copy-start.25 = (bf16[384,1024]{1,0:T(8,128)(2,1)S(1)}, bf16[384,1024]{1,0:T(8,128)(2,1)}, u32[]{:S(2)}) copy-start(bf16[384,1024]{1,0:T(8,128)(2,1)} %x_ref.5) | copy-start | bytes 2359300
  28.2 24.1 %copy-start.31 = (f32[1024]{0:T(1024)S(1)}, f32[1024]{0:T(1024)}, u32[]{:S(2)}) copy-start(f32[1024]{0:T(1024)} %param.24) | copy-start | bytes 12292
  33.0 19.3 %collective-permute-start.8 = (bf16[3,128,1024]{2,1,0:T(8,128)(2,1)S(1)}, bf16[3,128,1024]{2,1,0:T(8,128)(2,1)S(1)}, u32[]{:S(2)}, u32[]{:S(2)}) collective-permute-start(bf16[3,128,1024]{2,1,0:T(8,128)(2,1)S(1)} %pad_maximum_fusion.wm_ref), channel_id=1, source_target_pairs={{0,4},{4,0},{8,12},{12,8},{16,20},{20,16},{24,28},{28,24},{1,5},{5... | collective-permute-start | bytes 2359304 | tf_op jit(solution)/shard_map/ppermute | solution.py:533
  33.1 11.2 %collective-permute-start.10 = (bf16[384,256]{1,0:T(8,128)(2,1)S(1)}, bf16[384,256]{1,0:T(8,128)(2,1)S(1)}, u32[]{:S(2)}, u32[]{:S(2)}) collective-permute-start(bf16[384,256]{1,0:T(8,128)(2,1)S(1)} %get-tuple-element.118.refs_0_.refs_1_), channel_id=1, source_target_pairs={{0,2},{1,3},{2,0},{3,1},{4,6},{5,7},{6,4},{7,5},{8,10},{9,11},{10,... | collective-permute-start | bytes 589832 | tf_op jit(solution)/shard_map/ppermute | solution.py:533
  33.4 11.2 %collective-permute-start.9 = (bf16[384,256]{1,0:T(8,128)(2,1)S(1)}, bf16[384,256]{1,0:T(8,128)(2,1)S(1)}, u32[]{:S(2)}, u32[]{:S(2)}) collective-permute-start(bf16[384,256]{1,0:T(8,128)(2,1)S(1)} %get-tuple-element.118.refs_0_.refs_1_), channel_id=1, source_target_pairs={{0,1},{1,0},{2,3},{3,2},{4,5},{5,4},{6,7},{7,6},{8,9},{9,8},{10,11... | collective-permute-start | bytes 589832 | tf_op jit(solution)/shard_map/ppermute | solution.py:533
  44.3 10.0 %copy-start.3 = (bf16[384,256]{1,0:T(8,128)(2,1)}, bf16[384,256]{1,0:T(8,128)(2,1)S(1)}, u32[]{:S(2)}) copy-start(bf16[384,256]{1,0:T(8,128)(2,1)S(1)} %collective-permute-done.10.refs_2_.refs_3_) | copy-start | bytes 589828
  44.3 6.6 %collective-permute-start.11 = (bf16[192,256]{1,0:T(8,128)(2,1)S(1)}, bf16[192,256]{1,0:T(8,128)(2,1)S(1)}, u32[]{:S(2)}, u32[]{:S(2)}) collective-permute-start(bf16[192,256]{1,0:T(8,128)(2,1)S(1)} %slice.82), channel_id=1, source_target_pairs={{0,1},{1,0},{2,3},{3,2},{4,5},{5,4},{6,7},{7,6},{8,9},{9,8},{10,11... | collective-permute-start | bytes 294920 | tf_op jit(solution)/shard_map/ppermute | solution.py:533
  44.6 7.7 %collective-permute-start.12 = (bf16[192,256]{1,0:T(8,128)(2,1)S(1)}, bf16[192,256]{1,0:T(8,128)(2,1)S(1)}, u32[]{:S(2)}, u32[]{:S(2)}) collective-permute-start(bf16[192,256]{1,0:T(8,128)(2,1)S(1)} %slice.83), channel_id=1, source_target_pairs={{0,2},{1,3},{2,0},{3,1},{4,6},{5,7},{6,4},{7,5},{8,10},{9,11},{10,... | collective-permute-start | bytes 294920 | tf_op jit(solution)/shard_map/ppermute | solution.py:533
  61.4 7.4 %collective-permute-start.13 = (bf16[48,1024]{1,0:T(8,128)(2,1)S(1)}, bf16[48,1024]{1,0:T(8,128)(2,1)S(1)}, u32[]{:S(2)}, u32[]{:S(2)}) collective-permute-start(bf16[48,1024]{1,0:T(8,128)(2,1)S(1)} %get-tuple-element.133), channel_id=1, source_target_pairs={{0,1},{1,0},{2,3},{3,2},{4,5},{5,4},{6,7},{7,6},{8,9},{9,8},{10,11... | collective-permute-start | bytes 294920 | tf_op jit(solution)/shard_map/ppermute | solution.py:533
  61.7 7.1 %collective-permute-start.14 = (bf16[48,1024]{1,0:T(8,128)(2,1)S(1)}, bf16[48,1024]{1,0:T(8,128)(2,1)S(1)}, u32[]{:S(2)}, u32[]{:S(2)}) collective-permute-start(bf16[48,1024]{1,0:T(8,128)(2,1)S(1)} %get-tuple-element.134), channel_id=1, source_target_pairs={{0,2},{1,3},{2,0},{3,1},{4,6},{5,7},{6,4},{7,5},{8,10},{9,11},{10,... | collective-permute-start | bytes 294920 | tf_op jit(solution)/shard_map/ppermute | solution.py:533
  68.9 8.2 %collective-permute-start.15 = (bf16[96,1024]{1,0:T(8,128)(2,1)S(1)}, bf16[96,1024]{1,0:T(8,128)(2,1)S(1)}, u32[]{:S(2)}, u32[]{:S(2)}) collective-permute-start(bf16[96,1024]{1,0:T(8,128)(2,1)S(1)} %get-tuple-element.135), channel_id=1, source_target_pairs={{0,1},{1,0},{2,3},{3,2},{4,5},{5,4},{6,7},{7,6},{8,9},{9,8},{10,11... | collective-permute-start | bytes 589832 | tf_op jit(solution)/shard_map/ppermute | solution.py:533
  69.1 9.6 %collective-permute-start.16 = (bf16[96,1024]{1,0:T(8,128)(2,1)S(1)}, bf16[96,1024]{1,0:T(8,128)(2,1)S(1)}, u32[]{:S(2)}, u32[]{:S(2)}) collective-permute-start(bf16[96,1024]{1,0:T(8,128)(2,1)S(1)} %get-tuple-element.136), channel_id=1, source_target_pairs={{0,2},{1,3},{2,0},{3,1},{4,6},{5,7},{6,4},{7,5},{8,10},{9,11},{10,... | collective-permute-start | bytes 589832 | tf_op jit(solution)/shard_map/ppermute | solution.py:533
  70.9 14.9 %collective-permute-start.20 = (bf16[512,3456]{1,0:T(8,128)(2,1)S(1)}, bf16[512,3456]{1,0:T(8,128)(2,1)S(1)}, u32[]{:S(2)}, u32[]{:S(2)}) collective-permute-start(bf16[512,3456]{1,0:T(8,128)(2,1)S(1)} %get-tuple-element.142), channel_id=1, source_target_pairs={{0,4},{4,0},{8,12},{12,8},{16,20},{20,16},{24,28},{28,24},{1,5},{5... | collective-permute-start | bytes 10616840 | tf_op jit(solution)/shard_map/ppermute | solution.py:533
  79.6 9.3 %collective-permute-start.21 = (bf16[96,256]{1,0:T(8,128)(2,1)S(1)}, bf16[96,256]{1,0:T(8,128)(2,1)S(1)}, u32[]{:S(2)}, u32[]{:S(2)}) collective-permute-start(bf16[96,256]{1,0:T(8,128)(2,1)S(1)} %get-tuple-element.147), channel_id=1, source_target_pairs={{0,1},{1,0},{2,3},{3,2},{4,5},{5,4},{6,7},{7,6},{8,9},{9,8},{10,11... | collective-permute-start | bytes 147464 | tf_op jit(solution)/shard_map/ppermute | solution.py:533
  80.1 10.4 %collective-permute-start.22 = (bf16[96,256]{1,0:T(8,128)(2,1)S(1)}, bf16[96,256]{1,0:T(8,128)(2,1)S(1)}, u32[]{:S(2)}, u32[]{:S(2)}) collective-permute-start(bf16[96,256]{1,0:T(8,128)(2,1)S(1)} %get-tuple-element.148), channel_id=1, source_target_pairs={{0,2},{1,3},{2,0},{3,1},{4,6},{5,7},{6,4},{7,5},{8,10},{9,11},{10,... | collective-permute-start | bytes 147464 | tf_op jit(solution)/shard_map/ppermute | solution.py:533
  82.7 9.3 %collective-permute-start.23 = (bf16[96,256]{1,0:T(8,128)(2,1)S(1)}, bf16[96,256]{1,0:T(8,128)(2,1)S(1)}, u32[]{:S(2)}, u32[]{:S(2)}) collective-permute-start(bf16[96,256]{1,0:T(8,128)(2,1)S(1)} %get-tuple-element.149), channel_id=1, source_target_pairs={{0,3},{1,2},{2,1},{3,0},{4,7},{5,6},{6,5},{7,4},{8,11},{9,10},{10,... | collective-permute-start | bytes 147464 | tf_op jit(solution)/shard_map/ppermute | solution.py:533
  85.6 17.8 %collective-permute-start.18 = (bf16[96,1280]{1,0:T(8,128)(2,1)S(1)}, bf16[96,1280]{1,0:T(8,128)(2,1)S(1)}, u32[]{:S(2)}, u32[]{:S(2)}) collective-permute-start(bf16[96,1280]{1,0:T(8,128)(2,1)S(1)} %get-tuple-element.140), channel_id=1, source_target_pairs={{0,2},{1,3},{2,0},{3,1},{4,6},{5,7},{6,4},{7,5},{8,10},{9,11},{10,... | collective-permute-start | bytes 737288 | tf_op jit(solution)/shard_map/ppermute | solution.py:533
  85.8 17.6 %collective-permute-start.17 = (bf16[96,1280]{1,0:T(8,128)(2,1)S(1)}, bf16[96,1280]{1,0:T(8,128)(2,1)S(1)}, u32[]{:S(2)}, u32[]{:S(2)}) collective-permute-start(bf16[96,1280]{1,0:T(8,128)(2,1)S(1)} %get-tuple-element.139), channel_id=1, source_target_pairs={{0,1},{1,0},{2,3},{3,2},{4,5},{5,4},{6,7},{7,6},{8,9},{9,8},{10,11... | collective-permute-start | bytes 737288 | tf_op jit(solution)/shard_map/ppermute | solution.py:533
  89.0 14.5 %collective-permute-start.19 = (bf16[96,1280]{1,0:T(8,128)(2,1)S(1)}, bf16[96,1280]{1,0:T(8,128)(2,1)S(1)}, u32[]{:S(2)}, u32[]{:S(2)}) collective-permute-start(bf16[96,1280]{1,0:T(8,128)(2,1)S(1)} %get-tuple-element.141), channel_id=1, source_target_pairs={{0,3},{1,2},{2,1},{3,0},{4,7},{5,6},{6,5},{7,4},{8,11},{9,10},{10,... | collective-permute-start | bytes 737288 | tf_op jit(solution)/shard_map/ppermute | solution.py:533
  90.4 25.3 %collective-permute-start.30 = (bf16[256,3456]{1,0:T(8,128)(2,1)S(1)}, bf16[256,3456]{1,0:T(8,128)(2,1)S(1)}, u32[]{:S(2)}, u32[]{:S(2)}) collective-permute-start(bf16[256,3456]{1,0:T(8,128)(2,1)S(1)} %slice_add_fusion), channel_id=1, source_target_pairs={{0,8},{4,20},{8,0},{12,28},{16,24},{20,4},{24,16},{28,12},{1,9},{5... | collective-permute-start | bytes 5308424 | tf_op jit(solution)/shard_map/ppermute | solution.py:538
  95.4 18.0 %copy-start.1 = (bf16[384,1024]{1,0:T(8,128)(2,1)S(1)}, bf16[384,1024]{1,0:T(8,128)(2,1)}, u32[]{:S(2)}) copy-start(bf16[384,1024]{1,0:T(8,128)(2,1)} %get-tuple-element.112.h_ref.refs_14_) | copy-start | bytes 2359300
  95.4 18.0 %copy-start.4 = (bf16[384,256]{1,0:T(8,128)(2,1)S(1)}, bf16[384,256]{1,0:T(8,128)(2,1)}, u32[]{:S(2)}) copy-start(bf16[384,256]{1,0:T(8,128)(2,1)} %copy-done.3) | copy-start | bytes 589828
  95.4 18.0 %copy-start.6 = (bf16[384,256]{1,0:T(8,128)(2,1)S(1)}, bf16[384,256]{1,0:T(8,128)(2,1)}, u32[]{:S(2)}) copy-start(bf16[384,256]{1,0:T(8,128)(2,1)} %copy-done.5) | copy-start | bytes 589828
  95.4 18.0 %copy-start.8 = (f32[384,128]{1,0:T(8,128)S(1)}, f32[384,128]{1,0:T(8,128)}, u32[]{:S(2)}) copy-start(f32[384,128]{1,0:T(8,128)} %get-tuple-element.113.cos_ref.refs_5_) | copy-start | bytes 589828
  95.4 18.0 %copy-start.10 = (f32[384,128]{1,0:T(8,128)S(1)}, f32[384,128]{1,0:T(8,128)}, u32[]{:S(2)}) copy-start(f32[384,128]{1,0:T(8,128)} %get-tuple-element.114.sin_ref.refs_6_) | copy-start | bytes 589828
  95.4 18.0 %copy-start.12 = (bf16[384,256]{1,0:T(8,128)(2,1)S(1)}, bf16[384,256]{1,0:T(8,128)(2,1)}, u32[]{:S(2)}) copy-start(bf16[384,256]{1,0:T(8,128)(2,1)} %copy-done.11) | copy-start | bytes 589828
  95.4 18.0 %copy-start.15 = (bf16[192,256]{1,0:T(8,128)(2,1)S(1)}, bf16[192,256]{1,0:T(8,128)(2,1)}, u32[]{:S(2)}) copy-start(bf16[192,256]{1,0:T(8,128)(2,1)} %copy-done.14) | copy-start | bytes 294916
  95.4 18.0 %copy-start.17 = (bf16[192,256]{1,0:T(8,128)(2,1)S(1)}, bf16[192,256]{1,0:T(8,128)(2,1)}, u32[]{:S(2)}) copy-start(bf16[192,256]{1,0:T(8,128)(2,1)} %copy-done.16) | copy-start | bytes 294916
  103.5 5.2 %collective-permute-start.24 = (bf16[1536,256]{1,0:T(8,128)(2,1)S(1)}, bf16[1536,256]{1,0:T(8,128)(2,1)S(1)}, u32[]{:S(2)}, u32[]{:S(2)}) collective-permute-start(bf16[1536,256]{1,0:T(8,128)(2,1)S(1)} %get-tuple-element.159), channel_id=1, source_target_pairs={{0,4},{4,0},{8,12},{12,8},{16,20},{20,16},{24,28},{28,24},{1,5},{5... | collective-permute-start | bytes 2359304 | tf_op jit(solution)/shard_map/ppermute | solution.py:533
  103.6 14.9 %collective-permute-start.29 = (bf16[96,1024]{1,0:T(8,128)(2,1)S(1)}, bf16[96,1024]{1,0:T(8,128)(2,1)S(1)}, u32[]{:S(2)}, u32[]{:S(2)}) collective-permute-start(bf16[96,1024]{1,0:T(8,128)(2,1)S(1)} %get-tuple-element.190.own_ref), channel_id=1, source_target_pairs={{0,2},{1,3},{2,0},{3,1},{4,6},{5,7},{6,4},{7,5},{8,10},{9,11},{10,... | collective-permute-start | bytes 589832 | tf_op jit(solution)/shard_map/ppermute | solution.py:533
  108.7 10.6 %collective-permute-start.28 = (bf16[96,1024]{1,0:T(8,128)(2,1)S(1)}, bf16[96,1024]{1,0:T(8,128)(2,1)S(1)}, u32[]{:S(2)}, u32[]{:S(2)}) collective-permute-start(bf16[96,1024]{1,0:T(8,128)(2,1)S(1)} %get-tuple-element.190.own_ref), channel_id=1, source_target_pairs={{0,1},{1,0},{2,3},{3,2},{4,5},{5,4},{6,7},{7,6},{8,9},{9,8},{10,11... | collective-permute-start | bytes 589832 | tf_op jit(solution)/shard_map/ppermute | solution.py:533
  108.8 11.9 %collective-permute-start.27 = (bf16[384,256]{1,0:T(8,128)(2,1)S(1)}, bf16[384,256]{1,0:T(8,128)(2,1)S(1)}, u32[]{:S(2)}, u32[]{:S(2)}) collective-permute-start(bf16[384,256]{1,0:T(8,128)(2,1)S(1)} %get-tuple-element.213), channel_id=1, source_target_pairs={{0,24},{4,28},{8,16},{12,20},{16,8},{20,12},{24,0},{28,4},{1,25},{... | collective-permute-start | bytes 589832 | tf_op jit(solution)/shard_map/ppermute | solution.py:533
  113.4 10.3 %collective-permute-start.26 = (bf16[384,256]{1,0:T(8,128)(2,1)S(1)}, bf16[384,256]{1,0:T(8,128)(2,1)S(1)}, u32[]{:S(2)}, u32[]{:S(2)}) collective-permute-start(bf16[384,256]{1,0:T(8,128)(2,1)S(1)} %get-tuple-element.214), channel_id=1, source_target_pairs={{0,16},{4,20},{8,24},{12,28},{16,0},{20,4},{24,8},{28,12},{1,17},{... | collective-permute-start | bytes 589832 | tf_op jit(solution)/shard_map/ppermute | solution.py:533
  115.8 7.9 %collective-permute-start.25 = (bf16[384,256]{1,0:T(8,128)(2,1)S(1)}, bf16[384,256]{1,0:T(8,128)(2,1)S(1)}, u32[]{:S(2)}, u32[]{:S(2)}) collective-permute-start(bf16[384,256]{1,0:T(8,128)(2,1)S(1)} %get-tuple-element.215), channel_id=1, source_target_pairs={{0,8},{4,12},{8,0},{12,4},{16,24},{20,28},{24,16},{28,20},{1,9},{5... | collective-permute-start | bytes 589832 | tf_op jit(solution)/shard_map/ppermute | solution.py:533
  118.6 2.0 %collective-permute-start.31 = (bf16[512,512]{1,0:T(8,128)(2,1)S(1)}, bf16[512,512]{1,0:T(8,128)(2,1)S(1)}, u32[]{:S(2)}, u32[]{:S(2)}) collective-permute-start(bf16[512,512]{1,0:T(8,128)(2,1)S(1)} %get-tuple-element.167), channel_id=1, source_target_pairs={{0,4},{4,0},{8,12},{12,8},{16,20},{20,16},{24,28},{28,24},{1,5},{5... | collective-permute-start | bytes 1572872 | tf_op jit(solution)/shard_map/ppermute | solution.py:533
  126.2 5.9 %collective-permute-start.34 = (bf16[48,1024]{1,0:T(8,128)(2,1)S(1)}, bf16[48,1024]{1,0:T(8,128)(2,1)S(1)}, u32[]{:S(2)}, u32[]{:S(2)}) collective-permute-start(bf16[48,1024]{1,0:T(8,128)(2,1)S(1)} %get-tuple-element.180), channel_id=1, source_target_pairs={{0,1},{1,0},{2,3},{3,2},{4,5},{5,4},{6,7},{7,6},{8,9},{9,8},{10,11... | collective-permute-start | bytes 294920 | tf_op jit(solution)/shard_map/ppermute | solution.py:533
  127.2 7.4 %collective-permute-start.35 = (bf16[48,1024]{1,0:T(8,128)(2,1)S(1)}, bf16[48,1024]{1,0:T(8,128)(2,1)S(1)}, u32[]{:S(2)}, u32[]{:S(2)}) collective-permute-start(bf16[48,1024]{1,0:T(8,128)(2,1)S(1)} %get-tuple-element.181), channel_id=1, source_target_pairs={{0,2},{1,3},{2,0},{3,1},{4,6},{5,7},{6,4},{7,5},{8,10},{9,11},{10,... | collective-permute-start | bytes 294920 | tf_op jit(solution)/shard_map/ppermute | solution.py:533
  128.3 3.8 %collective-permute-start.32 = (f32[24,128]{1,0:T(8,128)S(1)}, f32[24,128]{1,0:T(8,128)S(1)}, u32[]{:S(2)}, u32[]{:S(2)}) collective-permute-start(f32[24,128]{1,0:T(8,128)S(1)} %get-tuple-element.172), channel_id=1, source_target_pairs={{0,1},{1,0},{2,3},{3,2},{4,5},{5,4},{6,7},{7,6},{8,9},{9,8},{10,11... | collective-permute-start | bytes 36872 | tf_op jit(solution)/shard_map/ppermute | solution.py:533
  134.7 3.1 %collective-permute-start.36 = (bf16[512,256]{1,0:T(8,128)(2,1)S(1)}, bf16[512,256]{1,0:T(8,128)(2,1)S(1)}, u32[]{:S(2)}, u32[]{:S(2)}) collective-permute-start(bf16[512,256]{1,0:T(8,128)(2,1)S(1)} %get-tuple-element.183), channel_id=1, source_target_pairs={{0,4},{4,0},{8,12},{12,8},{16,20},{20,16},{24,28},{28,24},{1,5},{5... | collective-permute-start | bytes 786440 | tf_op jit(solution)/shard_map/ppermute | solution.py:533
  134.8 5.9 %collective-permute-start.33 = (f32[24,128]{1,0:T(8,128)S(1)}, f32[24,128]{1,0:T(8,128)S(1)}, u32[]{:S(2)}, u32[]{:S(2)}) collective-permute-start(f32[24,128]{1,0:T(8,128)S(1)} %add.49), channel_id=1, source_target_pairs={{0,2},{1,3},{2,0},{3,1},{4,6},{5,7},{6,4},{7,5},{8,10},{9,11},{10,... | collective-permute-start | bytes 36872 | tf_op jit(solution)/shard_map/ppermute | solution.py:533
  135.3 17.9 %collective-permute-start.38 = (bf16[144,1024]{1,0:T(8,128)(2,1)S(1)}, bf16[144,1024]{1,0:T(8,128)(2,1)S(1)}, u32[]{:S(2)}, u32[]{:S(2)}) collective-permute-start(bf16[144,1024]{1,0:T(8,128)(2,1)S(1)} %get-tuple-element.182), channel_id=1, source_target_pairs={{0,1},{1,0},{2,3},{3,2},{4,5},{5,4},{6,7},{7,6},{8,9},{9,8},{10,11... | collective-permute-start | bytes 884744 | tf_op jit(solution)/shard_map/ppermute | solution.py:533
  137.1 16.1 %collective-permute-start.39 = (bf16[144,1024]{1,0:T(8,128)(2,1)S(1)}, bf16[144,1024]{1,0:T(8,128)(2,1)S(1)}, u32[]{:S(2)}, u32[]{:S(2)}) collective-permute-start(bf16[144,1024]{1,0:T(8,128)(2,1)S(1)} %get-tuple-element.189), channel_id=1, source_target_pairs={{0,2},{1,3},{2,0},{3,1},{4,6},{5,7},{6,4},{7,5},{8,10},{9,11},{10,... | collective-permute-start | bytes 884744 | tf_op jit(solution)/shard_map/ppermute | solution.py:533
  138.0 15.2 %copy-start.32 = (f32[1024]{0:T(1024)S(1)}, f32[1024]{0:T(1024)}, u32[]{:S(2)}) copy-start(f32[1024]{0:T(1024)} %param.17) | copy-start | bytes 12292
  138.0 12.0 %collective-permute-start.37 = (bf16[256,768]{1,0:T(8,128)(2,1)S(1)}, bf16[256,768]{1,0:T(8,128)(2,1)S(1)}, u32[]{:S(2)}, u32[]{:S(2)}) collective-permute-start(bf16[256,768]{1,0:T(8,128)(2,1)S(1)} %get-tuple-element.185), channel_id=1, source_target_pairs={{0,8},{4,20},{8,0},{12,28},{16,24},{20,4},{24,16},{28,12},{1,9},{5... | collective-permute-start | bytes 1179656 | tf_op jit(solution)/shard_map/ppermute | solution.py:538
  139.1 33.2 %collective-permute-start.40 = (bf16[128,3456]{1,0:T(8,128)(2,1)S(1)}, bf16[128,3456]{1,0:T(8,128)(2,1)S(1)}, u32[]{:S(2)}, u32[]{:S(2)}) collective-permute-start(bf16[128,3456]{1,0:T(8,128)(2,1)S(1)} %get-tuple-element.192), channel_id=1, source_target_pairs={{0,16},{4,12},{8,24},{12,4},{16,0},{20,28},{24,8},{28,20},{1,17},{... | collective-permute-start | bytes 2654216 | tf_op jit(solution)/shard_map/ppermute | solution.py:538
  153.5 9.0 %collective-permute-start.42 = (bf16[96,1024]{1,0:T(8,128)(2,1)S(1)}, bf16[96,1024]{1,0:T(8,128)(2,1)S(1)}, u32[]{:S(2)}, u32[]{:S(2)}) collective-permute-start(bf16[96,1024]{1,0:T(8,128)(2,1)S(1)} %shard_map.262.refs_0_), channel_id=1, source_target_pairs={{0,2},{1,3},{2,0},{3,1},{4,6},{5,7},{6,4},{7,5},{8,10},{9,11},{10,... | collective-permute-start | bytes 589832 | tf_op jit(solution)/shard_map/ppermute | solution.py:533
  153.9 8.6 %collective-permute-start.41 = (bf16[96,1024]{1,0:T(8,128)(2,1)S(1)}, bf16[96,1024]{1,0:T(8,128)(2,1)S(1)}, u32[]{:S(2)}, u32[]{:S(2)}) collective-permute-start(bf16[96,1024]{1,0:T(8,128)(2,1)S(1)} %shard_map.262.refs_0_), channel_id=1, source_target_pairs={{0,1},{1,0},{2,3},{3,2},{4,5},{5,4},{6,7},{7,6},{8,9},{9,8},{10,11... | collective-permute-start | bytes 589832 | tf_op jit(solution)/shard_map/ppermute | solution.py:533
  156.2 9.0 %collective-permute-start.48 = (bf16[128,768]{1,0:T(8,128)(2,1)S(1)}, bf16[128,768]{1,0:T(8,128)(2,1)S(1)}, u32[]{:S(2)}, u32[]{:S(2)}) collective-permute-start(bf16[128,768]{1,0:T(8,128)(2,1)S(1)} %get-tuple-element.199), channel_id=1, source_target_pairs={{0,16},{4,12},{8,24},{12,4},{16,0},{20,28},{24,8},{28,20},{1,17},{... | collective-permute-start | bytes 589832 | tf_op jit(solution)/shard_map/ppermute | solution.py:538
  156.7 1.2 collective-permute-start.43
  157.9 3.7 %collective-permute-start.44 = (f32[24,128]{1,0:T(8,128)S(1)}, f32[24,128]{1,0:T(8,128)S(1)}, u32[]{:S(2)}, u32[]{:S(2)}) collective-permute-start(f32[24,128]{1,0:T(8,128)S(1)} %add.51), channel_id=1, source_target_pairs={{0,8},{4,12},{8,0},{12,4},{16,24},{20,28},{24,16},{28,20},{1,9},{5... | collective-permute-start | bytes 36872 | tf_op jit(solution)/shard_map/ppermute | solution.py:533
  162.4 12.0 %collective-permute-start.46 = (bf16[48,1024]{1,0:T(8,128)(2,1)S(1)}, bf16[48,1024]{1,0:T(8,128)(2,1)S(1)}, u32[]{:S(2)}, u32[]{:S(2)}) collective-permute-start(bf16[48,1024]{1,0:T(8,128)(2,1)S(1)} %slice.79), channel_id=1, source_target_pairs={{0,2},{1,3},{2,0},{3,1},{4,6},{5,7},{6,4},{7,5},{8,10},{9,11},{10,... | collective-permute-start | bytes 294920 | tf_op jit(solution)/shard_map/ppermute | solution.py:533
  164.9 9.5 %collective-permute-start.45 = (bf16[48,1024]{1,0:T(8,128)(2,1)S(1)}, bf16[48,1024]{1,0:T(8,128)(2,1)S(1)}, u32[]{:S(2)}, u32[]{:S(2)}) collective-permute-start(bf16[48,1024]{1,0:T(8,128)(2,1)S(1)} %slice.78), channel_id=1, source_target_pairs={{0,1},{1,0},{2,3},{3,2},{4,5},{5,4},{6,7},{7,6},{8,9},{9,8},{10,11... | collective-permute-start | bytes 294920 | tf_op jit(solution)/shard_map/ppermute | solution.py:533
  165.9 7.9 %collective-permute-start.49 = (bf16[256,128]{1,0:T(8,128)(2,1)S(1)}, bf16[256,128]{1,0:T(8,128)(2,1)S(1)}, u32[]{:S(2)}, u32[]{:S(2)}) collective-permute-start(bf16[256,128]{1,0:T(8,128)(2,1)S(1)} %get-tuple-element.200), channel_id=1, source_target_pairs={{0,0},{1,8},{2,16},{3,24},{4,4},{5,12},{6,20},{7,28},{8,1},{9,9},{... | collective-permute-start | bytes 196616 | tf_op jit(solution)/shard_map/ppermute | solution.py:823
  166.6 7.2 %collective-permute-start.47 = (f32[24,128]{1,0:T(8,128)S(1)}, f32[24,128]{1,0:T(8,128)S(1)}, u32[]{:S(2)}, u32[]{:S(2)}) collective-permute-start(f32[24,128]{1,0:T(8,128)S(1)} %add.52.a_ref), channel_id=1, source_target_pairs={{0,16},{4,20},{8,24},{12,28},{16,0},{20,4},{24,8},{28,12},{1,17},{... | collective-permute-start | bytes 36872 | tf_op jit(solution)/shard_map/ppermute | solution.py:533
  (26 other events, 116.1 us)
